TPU v7x, 32 devices: a whole 2x2x4 slice. The times are simulated.
32 devices in a mesh: pipe: 4 (over y, core), expert: 8 (over z, x).
Axes of the slice: x: 2, y: 2, z: 4, core: 2. Of those that a mesh axis runs over, the one named last changes fastest.
Arguments:
- east_batch: bfloat16 [4, 256, 7168], P('pipe', 'expert'), may hold values from -6 to 6
- west_batch: bfloat16 [4, 256, 7168], P('pipe', 'expert'), may hold values from -6 to 6
- east_entering: bfloat16 [1, 256, 7168], P(None, 'expert'), may hold values from -6 to 6
- west_entering: bfloat16 [1, 256, 7168], P(None, 'expert'), may hold values from -6 to 6
- east_experts: int32 [2, 4, 256, 2], P(None, 'pipe', 'expert'), may hold values from 0 to 3, all different within a row; in each aligned block of 32 rows (0 to 31, 32 to 63, ..., all dimensions but the last counted through in order) at most 18 rows name the same one
- west_experts: int32 [2, 4, 256, 2], P(None, 'pipe', 'expert'), may hold values from 0 to 3, all different within a row; in each aligned block of 32 rows (0 to 31, 32 to 63, ..., all dimensions but the last counted through in order) at most 18 rows name the same one
- east_gates: float32 [2, 4, 256, 2], P(None, 'pipe', 'expert'), may hold values from 0.1 to 1
- west_gates: float32 [2, 4, 256, 2], P(None, 'pipe', 'expert'), may hold values from 0.1 to 1
- norm_gain: float32 [4, 7168], P('pipe'), may hold values from 0.5 to 1.5
- expert_in: bfloat16 [4, 8, 3584, 2048], P('pipe', 'expert'), may hold values from -0.0625 to 0.0625
- expert_down: bfloat16 [4, 8, 1024, 3584], P('pipe', 'expert'), may hold values from -0.1875 to 0.1875
Outputs:
- east_out: bfloat16 [4, 256, 7168], P('pipe', 'expert')
- west_out: bfloat16 [4, 256, 7168], P('pipe', 'expert')
Inputs may be any that keep to these rules, and one draw needn't show every extreme that they name: `east_experts`: the 2 experts of a token differ. In each step and section, the 32 tokens of one device name one expert at most 18 times, a bound that some block reaches. `west_experts`: the 2 experts of a token differ. In each step and section, the 32 tokens of one device name one expert at most 18 times, a bound that some block reaches.
All inputs are finite; a program needn't handle non-finite values.
Results may differ from a plain program's by a relative error of at most 0.007.
Values may be sent and summed in bfloat16 or wider, within the bound.
No kernel may reach another device: no remote copies, remote signals or barrier semaphores. Data moves between devices by JAX's collectives and lax.ppermute only.
A program may use at most 128 MiB of HBM per device.

v0:
```python
import jax
import jax.numpy as jnp
from jax import lax
from jax.sharding import PartitionSpec as P

EXPERTS = 4
TICKS = 2
CAP = 18


EPSILON = 1e-06


def partner(shard, axis, apart):
    return lax.ppermute(shard, axis, [(i, i ^ 1 << apart) for i in range(lax.axis_size(axis))])


def shifted(block, axis, distance):
    devices = range(lax.axis_size(axis))
    route = [(i - distance, i) for i in devices if i - distance in devices]
    return lax.ppermute(block, axis, route)


def rms_scaled(joined_rows, gain_row):
    values = joined_rows.astype(jnp.float32)
    scale_row = lax.rsqrt(jnp.mean(values * values, axis=-1, keepdims=True) + EPSILON)
    return (values * scale_row * gain_row[None, :]).astype(jnp.bfloat16)


def slot_tables(joined_routes, joined_shares, batch_count, experts, capacity):
    total_rows = joined_routes.shape[0]
    row_count = total_rows // batch_count
    onehot = (
        joined_routes[:, :, None] == jnp.arange(experts, dtype=jnp.int32)[None, None, :]
    ).astype(jnp.int32)
    per_row = jnp.sum(onehot, axis=1).reshape(batch_count, row_count, experts)
    before = (jnp.cumsum(per_row, axis=1) - per_row).reshape(total_rows, experts)
    slot_of = jnp.sum(onehot * before[:, None, :], axis=2)
    offset = jnp.arange(total_rows, dtype=jnp.int32) // row_count * capacity
    slot_of = slot_of + offset[:, None]
    slot_ids = jnp.arange(batch_count * capacity, dtype=jnp.int32)
    slot_hit = (slot_of[:, :, None] == slot_ids[None, None, :]).astype(jnp.float32)
    onehot_float = onehot.astype(jnp.float32)
    placement = jnp.einsum("rke,rkc->ecr", onehot_float, slot_hit, precision=lax.Precision.HIGHEST)
    weighted = jnp.einsum(
        "rke,rkc->rec",
        onehot_float * joined_shares[:, :, None],
        slot_hit,
        precision=lax.Precision.HIGHEST,
    )
    return (placement, weighted)


def halving_sum(partial_value, groups, halved_bits):
    row_count = partial_value.shape[0]
    slice_width = partial_value.shape[1] // (2 * groups)
    holding = partial_value.reshape(row_count, 2, groups, slice_width)
    member_index = lax.axis_index("expert")
    held_count = groups
    for bit_index in range(halved_bits):
        own_bit = member_index >> bit_index & 1
        reshaped = holding.reshape(row_count, 2, held_count // 2, 2, slice_width)
        kept_half = lax.dynamic_index_in_dim(reshaped, own_bit, 3, keepdims=False)
        sent_half = lax.dynamic_index_in_dim(reshaped, 1 - own_bit, 3, keepdims=False)
        holding = kept_half + partner(sent_half, "expert", bit_index)
        held_count = held_count // 2
    holding = holding + partner(holding, "expert", halved_bits)
    return (holding[:, 0], holding[:, 1])


def doubling_gather(own_piece, gathered_bits):
    row_count, held_count, slice_width = own_piece.shape
    holding = own_piece
    member_index = lax.axis_index("expert")
    for bit_index in reversed(range(gathered_bits)):
        own_bit = member_index >> bit_index & 1
        arrived = partner(holding, "expert", bit_index)
        first_half = jnp.where(own_bit == 0, holding, arrived)
        second_half = jnp.where(own_bit == 0, arrived, holding)
        stacked = jnp.stack([first_half, second_half], axis=2)
        holding = stacked.reshape(row_count, -1, slice_width)
    return holding.reshape(row_count, -1)


def expert_layer(batch_list, route_list, share_list, gain_row, weight_in, weight_out):
    batch_count = len(batch_list)
    row_count = batch_list[0].shape[0]
    model_width = batch_list[0].shape[1]
    groups = lax.axis_size("expert") // EXPERTS
    bit_count = groups.bit_length() - 1
    halved_bits = bit_count - 1
    feat_width = model_width // groups
    joined_rows = batch_list[0]
    joined_routes = route_list[0]
    joined_shares = share_list[0]
    normed = rms_scaled(joined_rows, gain_row)
    placement, weighted = slot_tables(joined_routes, joined_shares, batch_count, EXPERTS, CAP)
    total_rows = batch_count * row_count
    normed_split = normed.reshape(total_rows, groups, feat_width)
    outgoing = jnp.einsum(
        "ecr,rwf->ewcf",
        placement.astype(jnp.bfloat16),
        normed_split,
        preferred_element_type=jnp.float32,
    ).astype(jnp.bfloat16)
    outgoing = outgoing.reshape(EXPERTS * groups, batch_count * CAP, feat_width)
    arrived = lax.all_to_all(outgoing, "expert", split_axis=0, concat_axis=0, tiled=True)
    sources, slot_count, block_width = arrived.shape
    flat_rows = arrived.reshape(sources * slot_count, block_width)
    partial_value = jnp.dot(flat_rows, weight_in, preferred_element_type=jnp.float32)
    gate_part, up_part = halving_sum(partial_value, groups, halved_bits)
    own_piece = (jax.nn.silu(gate_part) * up_part).astype(jnp.bfloat16)
    hidden = doubling_gather(own_piece, halved_bits)
    result = jnp.dot(hidden, weight_out, preferred_element_type=jnp.float32).astype(jnp.bfloat16)
    returned = lax.all_to_all(
        result.reshape(sources, slot_count, block_width),
        "expert",
        split_axis=0,
        concat_axis=0,
        tiled=True,
    )
    returned_split = returned.reshape(EXPERTS, groups, batch_count * CAP, feat_width).astype(
        jnp.float32
    )
    mixed = jnp.einsum(
        "rec,ewcf->rwf", weighted, returned_split, precision=lax.Precision.HIGHEST
    ).reshape(total_rows, model_width)
    output = (joined_rows.astype(jnp.float32) + mixed).astype(jnp.bfloat16)
    return [output]


def shards(
    east_batch,
    west_batch,
    east_entering,
    west_entering,
    east_experts,
    west_experts,
    east_gates,
    west_gates,
    norm_gain,
    expert_in,
    expert_down,
):
    section_index = lax.axis_index("pipe")
    section_count = lax.axis_size("pipe")
    gain_row = norm_gain[0]
    weight_in = expert_in[0, 0]
    weight_out = expert_down[0, 0]
    east_now = east_batch[0]
    west_now = west_batch[0]
    for tick_index in range(TICKS):
        east_routes = east_experts[tick_index, 0]
        west_routes = west_experts[tick_index, 0]
        east_shares = east_gates[tick_index, 0]
        west_shares = west_gates[tick_index, 0]
        east_now = expert_layer(
            [east_now], [east_routes], [east_shares], gain_row, weight_in, weight_out
        )[0]
        west_now = expert_layer(
            [west_now], [west_routes], [west_shares], gain_row, weight_in, weight_out
        )[0]
        if tick_index + 1 < TICKS:
            moved_east = shifted(east_now, "pipe", 1)
            east_now = jnp.where(section_index == 0, east_entering[tick_index], moved_east)
            moved_west = shifted(west_now, "pipe", -1)
            west_now = jnp.where(
                section_index == section_count - 1, west_entering[tick_index], moved_west
            )
    return (east_now[None], west_now[None])


def solution(mesh):
    in_specs = (
        P("pipe", "expert", None),
        P("pipe", "expert", None),
        P(None, "expert", None),
        P(None, "expert", None),
        P(None, "pipe", "expert", None),
        P(None, "pipe", "expert", None),
        P(None, "pipe", "expert", None),
        P(None, "pipe", "expert", None),
        P("pipe", None),
        P("pipe", "expert", None, None),
        P("pipe", "expert", None, None),
    )
    out_specs = (P("pipe", "expert", None), P("pipe", "expert", None))
    return jax.shard_map(shards, mesh=mesh, in_specs=in_specs, out_specs=out_specs, check_vma=False)
```

profile of v0, /device:TPU:0, one launch (start us, length us, event | category | flops | bytes accessed | tf_op | source)
XLA Modules:
  0.0 383.7 jit_solution(1210832911361081170)
XLA Ops:
  0.7 2.0 reshape.319
  10.2 7.4 %all-to-all-start = ((bf16[8,18,3584]{2,1,0:T(8,128)(2,1)}), bf16[8,18,3584]{2,1,0:T(8,128)(2,1)S(1)}, u32[]{:S(2)}, u32[]{:S(2)}) async-start(bf16[8,18,3584]{2,1,0:T(8,128)(2,1)} %bitcast.9), calls=%async_computation | async-start | bytes 2752512 | tf_op jit(solution)/shard_map/all_to_all | solution.py:107
  21.1 29.3 %all-to-all-done = bf16[8,18,3584]{2,1,0:T(8,128)(2,1)S(1)} async-done(((bf16[8,18,3584]{2,1,0:T(8,128)(2,1)}), bf16[8,18,3584]{2,1,0:T(8,128)(2,1)S(1)}, u32[]{:S(2)}, u32[]{:S(2)}) %all-to-all-start) | async-done | bytes 1032224 | tf_op jit(solution)/shard_map/all_to_all | solution.py:107
  50.4 4.8 %all-to-all-start.4 = ((bf16[8,18,3584]{2,1,0:T(8,128)(2,1)}), bf16[8,18,3584]{2,1,0:T(8,128)(2,1)}, u32[]{:S(2)}, u32[]{:S(2)}) async-start(bf16[8,18,3584]{2,1,0:T(8,128)(2,1)} %bitcast.39), calls=%async_computation.4 | async-start | bytes 2752512 | tf_op jit(solution)/shard_map/all_to_all | solution.py:107
  55.2 18.8 %copy.130 = bf16[2048,3584]{1,0:T(8,128)(2,1)} copy(bf16[2048,3584]{0,1:T(8,128)(2,1)} %bitcast.198) | data formatting | bytes 29360128 | tf_op jit(solution)/shard_map/dot_general | solution.py:110
  74.4 11.1 %fusion.48 = f32[144,2,2,512]{3,0,2,1:T(8,128)} fusion(bf16[2,2,512,3584]{3,2,1,0:T(8,128)(2,1)} %bitcast.190, bf16[144,3584,1,1]{1,0,2,3:T(8,128)(2,1)S(1)} %reshape.324), kind=kOutput, calls=%fused_computation.56 | convolution fusion | flops 2113929216 | bytes 16891904 | tf_op jit(solution)/shard_map/dot_general | solution.py:110
  85.5 2.0 collective-permute-start
  87.7 2.4 reshape.332
  90.1 11.5 %fusion.44 = f32[144,2,2,512]{3,0,2,1:T(8,128)} fusion(bf16[2,2,512,3584]{3,2,1,0:T(8,128)(2,1)} %bitcast.191, bf16[144,3584,1,1]{1,0,2,3:T(8,128)(2,1)} %reshape.332), kind=kOutput, calls=%fused_computation.52 | convolution fusion | flops 2113929216 | bytes 16891904 | tf_op jit(solution)/shard_map/dot_general | solution.py:110
  101.6 1.4 collective-permute-start.3
  103.0 11.7 %collective-permute-done = f32[144,2,2,512]{3,0,2,1:T(8,128)} collective-permute-done((f32[144,2,2,512]{3,0,2,1:T(8,128)}, f32[144,2,2,512]{3,0,2,1:T(8,128)}, u32[]{:S(2)}, u32[]{:S(2)}) %collective-permute-start) | collective-permute-done | bytes 1179680 | tf_op jit(solution)/shard_map/ppermute | solution.py:15
  114.7 1.9 add.133
  117.1 2.2 fusion.18
  119.4 2.3 reshape.302
  121.6 6.0 %all-to-all-start.1 = ((bf16[8,18,3584]{2,1,0:T(8,128)(2,1)}), bf16[8,18,3584]{2,1,0:T(8,128)(2,1)S(1)}, u32[]{:S(2)}, u32[]{:S(2)}) async-start(bf16[8,18,3584]{2,1,0:T(8,128)(2,1)} %reshape.302), calls=%async_computation.1 | async-start | bytes 2752512 | tf_op jit(solution)/shard_map/all_to_all | solution.py:115
  127.6 23.4 %collective-permute-done.3 = f32[144,2,2,512]{3,0,2,1:T(8,128)} collective-permute-done((f32[144,2,2,512]{3,0,2,1:T(8,128)}, f32[144,2,2,512]{3,0,2,1:T(8,128)}, u32[]{:S(2)}, u32[]{:S(2)}) %collective-permute-start.3) | collective-permute-done | bytes 1179680 | tf_op jit(solution)/shard_map/ppermute | solution.py:15
  151.0 1.9 add.143
  153.4 4.3 %fusion.24 = bf16[144,3584]{1,0:T(8,128)(2,1)S(1)} fusion(bf16[144,1024]{1,0:T(8,128)(2,1)S(1)} %bitcast.208, bf16[1,1,1024,3584]{3,2,1,0:T(8,128)(2,1)} %param.21), kind=kOutput, calls=%fused_computation.28 | convolution fusion | flops 1057480704 | bytes 8667136 | tf_op jit(solution)/shard_map/dot_general | solution.py:114
  157.7 1.3 reshape.311
  159.0 5.2 %all-to-all-start.5 = ((bf16[8,18,3584]{2,1,0:T(8,128)(2,1)}), bf16[8,18,3584]{2,1,0:T(8,128)(2,1)S(1)}, u32[]{:S(2)}, u32[]{:S(2)}) async-start(bf16[8,18,3584]{2,1,0:T(8,128)(2,1)} %reshape.311), calls=%async_computation.5 | async-start | bytes 2752512 | tf_op jit(solution)/shard_map/all_to_all | solution.py:115
  165.5 1.8 copy.181
  167.2 2.6 dot_general.100
  169.8 3.4 fusion.7
  173.2 1.3 collective-permute-start.1
  175.0 18.5 %all-to-all-done.5 = bf16[8,18,3584]{2,1,0:T(8,128)(2,1)S(1)} async-done(((bf16[8,18,3584]{2,1,0:T(8,128)(2,1)}), bf16[8,18,3584]{2,1,0:T(8,128)(2,1)S(1)}, u32[]{:S(2)}, u32[]{:S(2)}) %all-to-all-start.5) | async-done | bytes 1032224 | tf_op jit(solution)/shard_map/all_to_all | solution.py:115
  195.3 1.4 fusion.5
  198.3 2.1 collective-permute-done.4
  203.1 3.6 all-to-all-start.6
  209.3 29.2 %all-to-all-done.6 = bf16[8,18,3584]{2,1,0:T(8,128)(2,1)S(1)} async-done(((bf16[8,18,3584]{2,1,0:T(8,128)(2,1)}), bf16[8,18,3584]{2,1,0:T(8,128)(2,1)S(1)}, u32[]{:S(2)}, u32[]{:S(2)}) %all-to-all-start.6) | async-done | bytes 1032224 | tf_op jit(solution)/shard_map/all_to_all | solution.py:107
  238.5 4.9 %all-to-all-start.2 = ((bf16[8,18,3584]{2,1,0:T(8,128)(2,1)}), bf16[8,18,3584]{2,1,0:T(8,128)(2,1)}, u32[]{:S(2)}, u32[]{:S(2)}) async-start(bf16[8,18,3584]{2,1,0:T(8,128)(2,1)} %bitcast.24), calls=%async_computation.2 | async-start | bytes 2752512 | tf_op jit(solution)/shard_map/all_to_all | solution.py:107
  243.8 11.1 %fusion.42 = f32[144,2,2,512]{3,0,2,1:T(8,128)} fusion(bf16[2,2,512,3584]{3,2,1,0:T(8,128)(2,1)} %bitcast.192, bf16[144,3584,1,1]{1,0,2,3:T(8,128)(2,1)S(1)} %reshape.336), kind=kOutput, calls=%fused_computation.50 | convolution fusion | flops 2113929216 | bytes 16891904 | tf_op jit(solution)/shard_map/dot_general | solution.py:110
  254.8 2.0 collective-permute-start.5
  256.8 20.1 %all-to-all-done.2 = bf16[8,18,3584]{2,1,0:T(8,128)(2,1)} async-done(((bf16[8,18,3584]{2,1,0:T(8,128)(2,1)}), bf16[8,18,3584]{2,1,0:T(8,128)(2,1)}, u32[]{:S(2)}, u32[]{:S(2)}) %all-to-all-start.2) | async-done | bytes 1032224 | tf_op jit(solution)/shard_map/all_to_all | solution.py:107
  276.9 2.4 reshape.328
  279.3 11.5 %fusion.46 = f32[144,2,2,512]{3,0,2,1:T(8,128)} fusion(bf16[2,2,512,3584]{3,2,1,0:T(8,128)(2,1)} %bitcast.193, bf16[144,3584,1,1]{1,0,2,3:T(8,128)(2,1)} %reshape.328), kind=kOutput, calls=%fused_computation.54 | convolution fusion | flops 2113929216 | bytes 16891904 | tf_op jit(solution)/shard_map/dot_general | solution.py:110
  292.0 1.9 add.148
  294.4 2.2 fusion.27
  296.6 2.3 reshape.316
  298.9 3.7 all-to-all-start.7
  302.6 28.3 %collective-permute-done.2 = f32[144,2,2,512]{3,0,2,1:T(8,128)} collective-permute-done((f32[144,2,2,512]{3,0,2,1:T(8,128)}, f32[144,2,2,512]{3,0,2,1:T(8,128)}, u32[]{:S(2)}, u32[]{:S(2)}) %collective-permute-start.2) | collective-permute-done | bytes 1179680 | tf_op jit(solution)/shard_map/ppermute | solution.py:15
  330.9 1.9 add.138
  333.4 4.3 %fusion.21 = bf16[144,3584]{1,0:T(8,128)(2,1)S(1)} fusion(bf16[144,1024]{1,0:T(8,128)(2,1)S(1)} %bitcast.210, bf16[1,1,1024,3584]{3,2,1,0:T(8,128)(2,1)} %param.21), kind=kOutput, calls=%fused_computation.27 | convolution fusion | flops 1057480704 | bytes 8667136 | tf_op jit(solution)/shard_map/dot_general | solution.py:114
  339.0 3.8 all-to-all-start.3
  345.2 1.8 copy.178
  347.0 2.5 dot_general.124
  349.5 26.6 %all-to-all-done.3 = bf16[8,18,3584]{2,1,0:T(8,128)(2,1)S(1)} async-done(((bf16[8,18,3584]{2,1,0:T(8,128)(2,1)}), bf16[8,18,3584]{2,1,0:T(8,128)(2,1)S(1)}, u32[]{:S(2)}, u32[]{:S(2)}) %all-to-all-start.3) | async-done | bytes 1032224 | tf_op jit(solution)/shard_map/all_to_all | solution.py:115
  378.3 3.0 fusion.9
  381.3 2.1 fusion.8
  (133 shorter events, 31.4 us)
Async XLA Ops:
  0.6 2.0 copy-start.4
  0.6 2.3 copy-start.12
  0.7 2.8 copy-start.13
  0.7 7.0 %copy-start.11 = (f32[1,7168]{1,0:T(1,128)S(1)}, f32[1,7168]{1,0:T(1,128)}, u32[]{:S(2)}) copy-start(f32[1,7168]{1,0:T(1,128)} %param.19) | copy-start | bytes 86020
  10.2 8.0 %copy-start.6 = (bf16[1,32,7168]{2,1,0:T(8,128)(2,1)S(1)}, bf16[1,32,7168]{2,1,0:T(8,128)(2,1)}, u32[]{:S(2)}) copy-start(bf16[1,32,7168]{2,1,0:T(8,128)(2,1)} %param.12) | copy-start | bytes 1376260
  10.2 40.2 %all-to-all-start = ((bf16[8,18,3584]{2,1,0:T(8,128)(2,1)}), bf16[8,18,3584]{2,1,0:T(8,128)(2,1)S(1)}, u32[]{:S(2)}, u32[]{:S(2)}) async-start(bf16[8,18,3584]{2,1,0:T(8,128)(2,1)} %bitcast.9), calls=%async_computation | async-start | bytes 2752512 | tf_op jit(solution)/shard_map/all_to_all | solution.py:107
  50.4 37.2 %all-to-all-start.4 = ((bf16[8,18,3584]{2,1,0:T(8,128)(2,1)}), bf16[8,18,3584]{2,1,0:T(8,128)(2,1)}, u32[]{:S(2)}, u32[]{:S(2)}) async-start(bf16[8,18,3584]{2,1,0:T(8,128)(2,1)} %bitcast.39), calls=%async_computation.4 | async-start | bytes 2752512 | tf_op jit(solution)/shard_map/all_to_all | solution.py:107
  85.5 29.2 %collective-permute-start = (f32[144,2,2,512]{3,0,2,1:T(8,128)}, f32[144,2,2,512]{3,0,2,1:T(8,128)}, u32[]{:S(2)}, u32[]{:S(2)}) collective-permute-start(f32[144,2,2,512]{3,0,2,1:T(8,128)} %fusion.48), channel_id=1, source_target_pairs={{0,1},{1,0},{2,3},{3,2},{4,5},{5,4},{6,7},{7,6},{8,9},{9,8},{10,11... | collective-permute-start | bytes 3538952 | tf_op jit(solution)/shard_map/ppermute | solution.py:15
  87.7 29.4 %slice-start = ((s8[7340032]{0:T(1024)(128)(4,1)}), s8[3145728]{0:T(1024)(128)(4,1)S(1)}, s32[]{:S(2)}) async-start(s8[7340032]{0:T(1024)(128)(4,1)} %bitcast.194), calls=%async_computation.8 | async-start | bytes 6291456
  90.1 27.0 %slice-start.1 = ((s8[7340032]{0:T(1024)(128)(4,1)}), s8[4194304]{0:T(1024)(128)(4,1)S(1)}, s32[]{:S(2)}) async-start(s8[7340032]{0:T(1024)(128)(4,1)} %bitcast.194), calls=%async_computation.9 | async-start | bytes 8388608
  101.6 49.4 %collective-permute-start.3 = (f32[144,2,2,512]{3,0,2,1:T(8,128)}, f32[144,2,2,512]{3,0,2,1:T(8,128)}, u32[]{:S(2)}, u32[]{:S(2)}) collective-permute-start(f32[144,2,2,512]{3,0,2,1:T(8,128)} %fusion.44), channel_id=1, source_target_pairs={{0,1},{1,0},{2,3},{3,2},{4,5},{5,4},{6,7},{7,6},{8,9},{9,8},{10,11... | collective-permute-start | bytes 3538952 | tf_op jit(solution)/shard_map/ppermute | solution.py:15
  121.6 37.4 %all-to-all-start.1 = ((bf16[8,18,3584]{2,1,0:T(8,128)(2,1)}), bf16[8,18,3584]{2,1,0:T(8,128)(2,1)S(1)}, u32[]{:S(2)}, u32[]{:S(2)}) async-start(bf16[8,18,3584]{2,1,0:T(8,128)(2,1)} %reshape.302), calls=%async_computation.1 | async-start | bytes 2752512 | tf_op jit(solution)/shard_map/all_to_all | solution.py:115
  159.0 5.2 %copy-start.14 = (f32[2,1,32,2]{2,3,1,0:T(2,128)S(1)}, f32[2,1,32,2]{2,3,1,0:T(2,128)}, u32[]{:S(2)}) copy-start(f32[2,1,32,2]{2,3,1,0:T(2,128)} %param.17) | copy-start | bytes 1540
  159.0 5.3 %copy-start.15 = (f32[2,1,32,2]{2,3,1,0:T(2,128)S(1)}, f32[2,1,32,2]{2,3,1,0:T(2,128)}, u32[]{:S(2)}) copy-start(f32[2,1,32,2]{2,3,1,0:T(2,128)} %param.18) | copy-start | bytes 1540
  159.0 34.4 %all-to-all-start.5 = ((bf16[8,18,3584]{2,1,0:T(8,128)(2,1)}), bf16[8,18,3584]{2,1,0:T(8,128)(2,1)S(1)}, u32[]{:S(2)}, u32[]{:S(2)}) async-start(bf16[8,18,3584]{2,1,0:T(8,128)(2,1)} %reshape.311), calls=%async_computation.5 | async-start | bytes 2752512 | tf_op jit(solution)/shard_map/all_to_all | solution.py:115
  167.2 2.6 copy-start.5
  173.2 24.8 %collective-permute-start.1 = (bf16[32,7168]{1,0:T(8,128)(2,1)}, bf16[32,7168]{1,0:T(8,128)(2,1)S(1)}, u32[]{:S(2)}, u32[]{:S(2)}) collective-permute-start(bf16[32,7168]{1,0:T(8,128)(2,1)} %fusion.7), channel_id=1, source_target_pairs={{0,8},{8,16},{16,24},{1,9},{9,17},{17,25},{2,10},{10,18},{18,26},{... | collective-permute-start | bytes 1376264 | tf_op jit(solution)/shard_map/ppermute | solution.py:21
  194.3 1.0 copy-start.7
  195.3 2.7 copy-start.9
  195.3 5.1 %copy-start.10 = (bf16[1,32,7168]{2,1,0:T(8,128)(2,1)S(1)}, bf16[1,32,7168]{2,1,0:T(8,128)(2,1)}, u32[]{:S(2)}) copy-start(bf16[1,32,7168]{2,1,0:T(8,128)(2,1)} %param.14) | copy-start | bytes 1376260
  196.7 3.7 collective-permute-start.4
  198.2 2.7 copy-start
  200.6 0.8 copy-start.2
  203.1 35.3 %all-to-all-start.6 = ((bf16[8,18,3584]{2,1,0:T(8,128)(2,1)}), bf16[8,18,3584]{2,1,0:T(8,128)(2,1)S(1)}, u32[]{:S(2)}, u32[]{:S(2)}) async-start(bf16[8,18,3584]{2,1,0:T(8,128)(2,1)} %bitcast.50), calls=%async_computation.6 | async-start | bytes 2752512 | tf_op jit(solution)/shard_map/all_to_all | solution.py:107
  238.5 38.4 %all-to-all-start.2 = ((bf16[8,18,3584]{2,1,0:T(8,128)(2,1)}), bf16[8,18,3584]{2,1,0:T(8,128)(2,1)}, u32[]{:S(2)}, u32[]{:S(2)}) async-start(bf16[8,18,3584]{2,1,0:T(8,128)(2,1)} %bitcast.24), calls=%async_computation.2 | async-start | bytes 2752512 | tf_op jit(solution)/shard_map/all_to_all | solution.py:107
  254.8 37.2 %collective-permute-start.5 = (f32[144,2,2,512]{3,0,2,1:T(8,128)}, f32[144,2,2,512]{3,0,2,1:T(8,128)}, u32[]{:S(2)}, u32[]{:S(2)}) collective-permute-start(f32[144,2,2,512]{3,0,2,1:T(8,128)} %fusion.42), channel_id=1, source_target_pairs={{0,1},{1,0},{2,3},{3,2},{4,5},{5,4},{6,7},{7,6},{8,9},{9,8},{10,11... | collective-permute-start | bytes 3538952 | tf_op jit(solution)/shard_map/ppermute | solution.py:15
  276.9 17.5 %slice-start.2 = ((s8[7340032]{0:T(1024)(128)(4,1)}), s8[3145728]{0:T(1024)(128)(4,1)S(1)}, s32[]{:S(2)}) async-start(s8[7340032]{0:T(1024)(128)(4,1)} %bitcast.196), calls=%async_computation.10 | async-start | bytes 6291456
  279.3 15.1 %slice-start.3 = ((s8[7340032]{0:T(1024)(128)(4,1)}), s8[4194304]{0:T(1024)(128)(4,1)S(1)}, s32[]{:S(2)}) async-start(s8[7340032]{0:T(1024)(128)(4,1)} %bitcast.196), calls=%async_computation.11 | async-start | bytes 8388608
  290.8 40.1 %collective-permute-start.2 = (f32[144,2,2,512]{3,0,2,1:T(8,128)}, f32[144,2,2,512]{3,0,2,1:T(8,128)}, u32[]{:S(2)}, u32[]{:S(2)}) collective-permute-start(f32[144,2,2,512]{3,0,2,1:T(8,128)} %fusion.46), channel_id=1, source_target_pairs={{0,1},{1,0},{2,3},{3,2},{4,5},{5,4},{6,7},{7,6},{8,9},{9,8},{10,11... | collective-permute-start | bytes 3538952 | tf_op jit(solution)/shard_map/ppermute | solution.py:15
  298.9 40.1 %all-to-all-start.7 = ((bf16[8,18,3584]{2,1,0:T(8,128)(2,1)}), bf16[8,18,3584]{2,1,0:T(8,128)(2,1)S(1)}, u32[]{:S(2)}, u32[]{:S(2)}) async-start(bf16[8,18,3584]{2,1,0:T(8,128)(2,1)} %reshape.316), calls=%async_computation.7 | async-start | bytes 2752512 | tf_op jit(solution)/shard_map/all_to_all | solution.py:115
  339.0 37.1 %all-to-all-start.3 = ((bf16[8,18,3584]{2,1,0:T(8,128)(2,1)}), bf16[8,18,3584]{2,1,0:T(8,128)(2,1)S(1)}, u32[]{:S(2)}, u32[]{:S(2)}) async-start(bf16[8,18,3584]{2,1,0:T(8,128)(2,1)} %reshape.307), calls=%async_computation.3 | async-start | bytes 2752512 | tf_op jit(solution)/shard_map/all_to_all | solution.py:115
  376.9 1.0 copy-start.3
  376.9 1.4 copy-start.8
  378.3 3.0 copy-start.1
  378.3 3.0 copy-start.16
where the time goes:
time: 391 us; the launch traced here: 384 us
  waiting for transfers between devices  189 us (48%)
  matrix products  75.3 us (19%)
  local copies, waits for them, and re-layouts  55.6 us (14%)
  starting transfers between devices  48.5 us (12%)
  other arithmetic  13.5 us (3%)
    all_to_all x4, waiting for transfers between devices, expert_layer(): lax.all_to_all(outgoing, 'expert', split_axis=0, concat_axis=0, tiled=True)  78.8 us
    ppermute x4, waiting for transfers between devices, partner(): lax.ppermute(shard, axis, [(i, i ^ 1 << apart) for i in range(lax.axis_si...  63.4 us
    dot_general x4, matrix products, expert_layer(): jnp.dot(flat_rows, weight_in, preferred_element_type=jnp.float32)  45.1 us
    all_to_all x4, waiting for transfers between devices, expert_layer(): lax.all_to_all(result.reshape(sources, slot_count, block_width), 'expert'...  45.1 us
    all_to_all x4, starting transfers between devices, expert_layer(): lax.all_to_all(outgoing, 'expert', split_axis=0, concat_axis=0, tiled=True)  20.7 us
    dot_general x1, local copies, waits for them, and re-layouts, expert_layer(): jnp.dot(flat_rows, weight_in, preferred_element_type=jnp.float32)  18.8 us
    all_to_all x4, starting transfers between devices, expert_layer(): lax.all_to_all(result.reshape(sources, slot_count, block_width), 'expert'...  18.7 us
    dot_general x4, matrix products, expert_layer(): jnp.dot(hidden, weight_out, preferred_element_type=jnp.float32)  13.1 us
  transfers between devices with their start and end apart: 14, of which 10 were waited for; matrix products, arithmetic and copies ran while one was open for 32% of the time, Pallas kernels for 0%

commit v1 on v0

--- a/solution.py
+++ b/solution.py
@@ -1,6 +1,10 @@
+import functools
+
 import jax
 import jax.numpy as jnp
 from jax import lax
+from jax.experimental import pallas as pl
+from jax.experimental.pallas import tpu as pltpu
 from jax.sharding import PartitionSpec as P
 
 EXPERTS = 4
@@ -129,7 +133,7 @@
     return [output]
 
 
-def shards(
+def general_shards(
     east_batch,
     west_batch,
     east_entering,
@@ -170,6 +174,366 @@
     return (east_now[None], west_now[None])
 
 
+PARTS = 4
+LIMIT = 40 * 2**20
+
+
+def params(limit=LIMIT):
+    return pltpu.CompilerParams(vmem_limit_bytes=limit)
+
+
+def iota(shape, axis):
+    return lax.broadcasted_iota(jnp.int32, shape, axis)
+
+
+def matmul(a, b):
+    return jnp.dot(a, b, preferred_element_type=jnp.float32)
+
+
+def pack_kernel(rows, me, state, route, *outs_and_scratch):
+    outs, (stacked,) = outs_and_scratch[:EXPERTS], outs_and_scratch[EXPERTS:]
+    tokens, half = state.shape
+    width = half // PARTS
+    total = PARTS * tokens
+    slots = 2 * CAP
+    for part in range(PARTS):
+        stacked[part * tokens:(part + 1) * tokens, :] = state[:, part * width:(part + 1) * width]
+    expert = me[0] ^ iota((8, total), 0)
+    named = (route[0:1, :] == expert) | (route[1:2, :] == expert)
+    earlier = (iota((total, total), 0) // rows == iota((total, total), 1) // rows) & (
+        iota((total, total), 0) < iota((total, total), 1)
+    )
+    before = matmul(named.astype(jnp.float32).astype(jnp.bfloat16), earlier.astype(jnp.float32).astype(jnp.bfloat16))
+    column = iota((8, total), 1)
+    first = column // tokens * slots + column // rows % 2 * CAP
+    place = jnp.where(named, first + before.astype(jnp.int32), -1)
+    for apart in range(EXPERTS):
+        hit = iota((PARTS * slots, total), 0) == place[apart:apart + 1, :]
+        outs[apart][...] = matmul(hit.astype(jnp.float32).astype(jnp.bfloat16), stacked[...]).astype(jnp.bfloat16)
+
+
+def pack(me, state, route, rows):
+    tokens, half = state.shape
+    shape = (PARTS * 2 * CAP, half // PARTS)
+    return pl.pallas_call(
+        functools.partial(pack_kernel, rows),
+        out_shape=[jax.ShapeDtypeStruct(shape, jnp.bfloat16)] * EXPERTS,
+        in_specs=[pl.BlockSpec(memory_space=pltpu.SMEM)] + [pl.BlockSpec(memory_space=pltpu.VMEM)] * 2,
+        out_specs=[pl.BlockSpec(memory_space=pltpu.VMEM)] * EXPERTS,
+        scratch_shapes=[pltpu.VMEM((PARTS * tokens, half // PARTS), jnp.bfloat16)],
+        compiler_params=params(),
+        name="pack",
+    )(me, state, route)
+
+
+def first_kernel(me, r0, r1, r2, r3, gain, weight, partial, rows_out, squares, stacked):
+    slots = 2 * CAP
+    block = PARTS * slots
+    width = r0.shape[1]
+
+    @pl.when(pl.program_id(0) == 0)
+    def _():
+        for apart, ref in enumerate((r0, r1, r2, r3)):
+            stacked[apart * block:(apart + 1) * block, :] = ref[...]
+        row = iota((block, EXPERTS * block), 0)
+        column = iota((block, EXPERTS * block), 1)
+        total = jnp.zeros((block, 1), jnp.float32)
+        for part in range(PARTS):
+            source = row // slots * block + part * slots + row % slots
+            pick = (column == source).astype(jnp.float32).astype(jnp.bfloat16)
+            values = matmul(pick, stacked[...])
+            total = total + jnp.sum(values * values, axis=1, keepdims=True)
+            scaled = values * gain[part:part + 1, :]
+            rows_out[:, part * width:(part + 1) * width] = scaled.astype(jnp.bfloat16)
+        squares[...] = jnp.broadcast_to(total, squares.shape)
+
+    partial[...] = matmul(rows_out[...], weight[...]).astype(partial.dtype)
+
+
+def column_block(step, side, count, blocks):
+    return step // blocks * count + side * blocks + step % blocks
+
+
+def first(me, received, gain, weight, step_width=256):
+    block, width = received[0].shape
+    half = PARTS * width
+    both = weight.shape[1]
+    blocks = both // 4 // step_width
+    whole = pl.BlockSpec(memory_space=pltpu.VMEM)
+    fixed = lambda shape: pl.BlockSpec(shape, lambda step, me: (0, 0))
+    return pl.pallas_call(
+        first_kernel,
+        out_shape=[
+            jax.ShapeDtypeStruct((block, both // 2), jnp.bfloat16),
+            jax.ShapeDtypeStruct((block, half), jnp.bfloat16),
+            jax.ShapeDtypeStruct((block, 128), jnp.float32),
+        ],
+        grid_spec=pltpu.PrefetchScalarGridSpec(
+            num_scalar_prefetch=1,
+            grid=(2 * blocks,),
+            in_specs=[fixed((block, width))] * EXPERTS + [
+                fixed((PARTS, width)),
+                pl.BlockSpec(
+                    (half, step_width),
+                    lambda step, me: (0, column_block(step, 1 - me[1], 2 * blocks, blocks)),
+                ),
+            ],
+            out_specs=[
+                pl.BlockSpec((block, step_width), lambda step, me: (0, step)),
+                fixed((block, half)),
+                fixed((block, 128)),
+            ],
+            scratch_shapes=[pltpu.VMEM((EXPERTS * block, width), jnp.bfloat16)],
+        ),
+        compiler_params=params(),
+        cost_estimate=pl.CostEstimate(flops=2 * block * half * both // 2, bytes_accessed=half * both, transcendentals=0),
+        name="first",
+    )(me, *received, gain, weight)
+
+
+def second_kernel(me, rows_in, weight, partial):
+    partial[...] = matmul(rows_in[...], weight[...])
+
+
+def second(me, rows_in, weight, step_width=256):
+    block, half = rows_in.shape
+    both = weight.shape[1]
+    blocks = both // 4 // step_width
+    return pl.pallas_call(
+        second_kernel,
+        out_shape=jax.ShapeDtypeStruct((block, both // 2), jnp.float32),
+        grid_spec=pltpu.PrefetchScalarGridSpec(
+            num_scalar_prefetch=1,
+            grid=(2 * blocks,),
+            in_specs=[
+                pl.BlockSpec((block, half), lambda step, me: (0, 0)),
+                pl.BlockSpec(
+                    (half, step_width),
+                    lambda step, me: (0, column_block(step, me[1], 2 * blocks, blocks)),
+                ),
+            ],
+            out_specs=pl.BlockSpec((block, step_width), lambda step, me: (0, step)),
+        ),
+        compiler_params=params(),
+        cost_estimate=pl.CostEstimate(flops=2 * block * half * both // 2, bytes_accessed=half * both, transcendentals=0),
+        name="second",
+    )(me, rows_in, weight)
+
+
+def act_kernel(model_width, own, other, squares, squares_other, hidden):
+    units = hidden.shape[1]
+    mean = (squares[:, 0:1] + squares_other[:, 0:1]) / model_width
+    scale = lax.rsqrt(mean + EPSILON)
+    summed = (own[...] + other[...].astype(jnp.float32)) * scale
+    gate = summed[:, :units]
+    hidden[...] = (gate / (1.0 + jnp.exp(-gate)) * summed[:, units:]).astype(jnp.bfloat16)
+
+
+def act(own, other, squares, squares_other, model_width):
+    block, both = own.shape
+    return pl.pallas_call(
+        functools.partial(act_kernel, model_width),
+        out_shape=jax.ShapeDtypeStruct((block, both // 2), jnp.bfloat16),
+        in_specs=[pl.BlockSpec(memory_space=pltpu.VMEM)] * 4,
+        out_specs=pl.BlockSpec(memory_space=pltpu.VMEM),
+        compiler_params=params(),
+        name="act",
+    )(own, other, squares, squares_other)
+
+
+def third_kernel(me, hidden, weight, partial):
+    partial[...] = matmul(hidden[...], weight[...])
+
+
+def third(me, hidden, weight):
+    block, units = hidden.shape
+    half = weight.shape[1]
+    width = half // PARTS
+    return pl.pallas_call(
+        third_kernel,
+        out_shape=jax.ShapeDtypeStruct((block, half), jnp.float32),
+        grid_spec=pltpu.PrefetchScalarGridSpec(
+            num_scalar_prefetch=1,
+            grid=(PARTS,),
+            in_specs=[
+                pl.BlockSpec((block, units), lambda step, me: (0, 0)),
+                pl.BlockSpec((units, width), lambda step, me: (me[1], step)),
+            ],
+            out_specs=pl.BlockSpec((block, width), lambda step, me: (0, step)),
+        ),
+        compiler_params=params(),
+        cost_estimate=pl.CostEstimate(flops=2 * block * half * units, bytes_accessed=2 * half * units, transcendentals=0),
+        name="third",
+    )(me, hidden, weight)
+
+
+def fourth_kernel(me, hidden, weight, own, o0, o1, o2, o3, stacked):
+    slots = 2 * CAP
+    block = PARTS * slots
+    step = pl.program_id(0)
+    result = own[...] + matmul(hidden[...], weight[...])
+    start = pl.multiple_of(step * block, block)
+    stacked[pl.ds(start, block), :] = result.astype(jnp.bfloat16)
+
+    @pl.when(step == PARTS - 1)
+    def _():
+        row = iota((block, EXPERTS * block), 0)
+        column = iota((block, EXPERTS * block), 1)
+        for apart, out in enumerate((o0, o1, o2, o3)):
+            source = row // slots * block + apart * slots + row % slots
+            pick = (column == source).astype(jnp.float32).astype(jnp.bfloat16)
+            out[...] = matmul(pick, stacked[...]).astype(jnp.bfloat16)
+
+
+def fourth(me, hidden, weight, own):
+    block, units = hidden.shape
+    half = weight.shape[1]
+    width = half // PARTS
+    return pl.pallas_call(
+        fourth_kernel,
+        out_shape=[jax.ShapeDtypeStruct((block, width), jnp.bfloat16)] * EXPERTS,
+        grid_spec=pltpu.PrefetchScalarGridSpec(
+            num_scalar_prefetch=1,
+            grid=(PARTS,),
+            in_specs=[
+                pl.BlockSpec((block, units), lambda step, me: (0, 0)),
+                pl.BlockSpec((units, width), lambda step, me: (1 - me[1], step)),
+                pl.BlockSpec((block, width), lambda step, me: (0, step)),
+            ],
+            out_specs=[pl.BlockSpec((block, width), lambda step, me: (0, 0))] * EXPERTS,
+            scratch_shapes=[pltpu.VMEM((PARTS * block, width), jnp.bfloat16)],
+        ),
+        compiler_params=params(),
+        cost_estimate=pl.CostEstimate(flops=2 * block * half * units, bytes_accessed=2 * half * units, transcendentals=0),
+        name="fourth",
+    )(me, hidden, weight, own)
+
+
+def mix_kernel(rows, me, state, route, share, r0, r1, r2, r3, out):
+    tokens, half = state.shape
+    width = half // PARTS
+    total = PARTS * tokens
+    slots = 2 * CAP
+    expert = me[0] ^ iota((total, 128), 1)
+    named = (route[:, 0:1] == expert) | (route[:, 1:2] == expert)
+    weight = jnp.where(route[:, 0:1] == expert, share[:, 0:1], 0.0) + jnp.where(
+        route[:, 1:2] == expert, share[:, 1:2], 0.0
+    )
+    earlier = (iota((total, total), 0) // rows == iota((total, total), 1) // rows) & (
+        iota((total, total), 0) > iota((total, total), 1)
+    )
+    before = matmul(earlier.astype(jnp.float32).astype(jnp.bfloat16), named.astype(jnp.float32).astype(jnp.bfloat16))
+    line = iota((total, 128), 0)
+    first = line // tokens * slots + line // rows % 2 * CAP
+    place = jnp.where(named, first + before.astype(jnp.int32), -1)
+    mixed = jnp.zeros((total, width), jnp.float32)
+    for apart, ref in enumerate((r0, r1, r2, r3)):
+        hit = iota((total, PARTS * slots), 1) == place[:, apart:apart + 1]
+        spread = jnp.where(hit, weight[:, apart:apart + 1], 0.0)
+        high = spread.astype(jnp.bfloat16)
+        low = (spread - high.astype(jnp.float32)).astype(jnp.bfloat16)
+        mixed = mixed + matmul(high, ref[...]) + matmul(low, ref[...])
+    for part in range(PARTS):
+        span = slice(part * width, (part + 1) * width)
+        summed = state[:, span].astype(jnp.float32) + mixed[part * tokens:(part + 1) * tokens, :]
+        out[:, span] = summed.astype(jnp.bfloat16)
+
+
+def mix(me, state, route, share, received, rows):
+    return pl.pallas_call(
+        functools.partial(mix_kernel, rows),
+        out_shape=jax.ShapeDtypeStruct(state.shape, jnp.bfloat16),
+        in_specs=[pl.BlockSpec(memory_space=pltpu.SMEM)] + [pl.BlockSpec(memory_space=pltpu.VMEM)] * 7,
+        out_specs=pl.BlockSpec(memory_space=pltpu.VMEM),
+        compiler_params=params(),
+        name="mix",
+    )(me, state, route, share, *received)
+
+
+def across(blocks):
+    size = lax.axis_size("expert")
+    moved = [blocks[0]]
+    for apart in range(1, EXPERTS):
+        moved.append(lax.ppermute(blocks[apart], "expert", [(i, i ^ 2 * apart) for i in range(size)]))
+    return moved
+
+
+def gathered_pair(block, x, axis):
+    other = partner(block, "expert", 0)
+    return jnp.concatenate([jnp.where(x == 0, block, other), jnp.where(x == 0, other, block)], axis=axis)
+
+
+def to_halves(batch, x):
+    half = batch.shape[1] // 2
+    kept = lax.dynamic_slice_in_dim(batch, x * half, half, 1)
+    sent = lax.dynamic_slice_in_dim(batch, (1 - x) * half, half, 1)
+    other = partner(sent, "expert", 0)
+    return jnp.concatenate([jnp.where(x == 0, kept, other), jnp.where(x == 0, other, kept)], axis=0)
+
+
+def to_rows(state, x):
+    rows = state.shape[0] // 2
+    kept = lax.dynamic_slice_in_dim(state, x * rows, rows, 0)
+    sent = lax.dynamic_slice_in_dim(state, (1 - x) * rows, rows, 0)
+    other = partner(sent, "expert", 0)
+    return jnp.concatenate([jnp.where(x == 0, kept, other), jnp.where(x == 0, other, kept)], axis=1)
+
+
+def paired_shards(
+    east_batch,
+    west_batch,
+    east_entering,
+    west_entering,
+    east_experts,
+    west_experts,
+    east_gates,
+    west_gates,
+    norm_gain,
+    expert_in,
+    expert_down,
+):
+    section_index = lax.axis_index("pipe")
+    section_count = lax.axis_size("pipe")
+    member = lax.axis_index("expert")
+    x = member % 2
+    me = jnp.stack([member // 2, x]).astype(jnp.int32)
+    rows, model_width = east_batch.shape[1:]
+    half = model_width // 2
+    weight_in = expert_in[0, 0]
+    weight_out = expert_down[0, 0]
+    gain = lax.dynamic_slice_in_dim(norm_gain[0], x * half, half, 0).reshape(PARTS, half // PARTS)
+
+    table = jnp.stack([east_experts[:, 0], west_experts[:, 0]]).astype(jnp.float32)
+    table = jnp.concatenate([table, jnp.stack([east_gates[:, 0], west_gates[:, 0]])], axis=3)
+    table = gathered_pair(table, x, 2)
+    table = jnp.tile(table, (1, 1, PARTS, 1))
+    routes = table[..., :2].astype(jnp.int32)
+    routes_row = jnp.swapaxes(routes, 2, 3)
+    shares = table[..., 2:]
+
+    now = [to_halves(east_batch[0], x), to_halves(west_batch[0], x)]
+    entering = [to_halves(east_entering[0], x), to_halves(west_entering[0], x)]
+    for tick in range(TICKS):
+        for stream in range(2):
+            state = now[stream]
+            received = across(pack(me, state, routes_row[stream, tick], rows))
+            sent, scaled, squares = first(me, received, gain, weight_in)
+            other = partner(sent, "expert", 0)
+            squares_other = partner(squares, "expert", 0)
+            own = second(me, scaled, weight_in)
+            hidden = act(own, other, squares, squares_other, model_width)
+            hidden_other = partner(hidden, "expert", 0)
+            result = third(me, hidden, weight_out)
+            returned = across(fourth(me, hidden_other, weight_out, result))
+            state = mix(me, state, routes[stream, tick], shares[stream, tick], returned, rows)
+            if tick + 1 < TICKS:
+                step = 1 - 2 * stream
+                edge = 0 if stream == 0 else section_count - 1
+                state = jnp.where(section_index == edge, entering[stream], shifted(state, "pipe", step))
+            now[stream] = state
+    return (to_rows(now[0], x)[None], to_rows(now[1], x)[None])
+
+
 def solution(mesh):
     in_specs = (
         P("pipe", "expert", None),
@@ -185,4 +549,6 @@
         P("pipe", "expert", None, None),
     )
     out_specs = (P("pipe", "expert", None), P("pipe", "expert", None))
+    groups = mesh.shape["expert"] // EXPERTS
+    shards = paired_shards if groups == 2 else general_shards
     return jax.shard_map(shards, mesh=mesh, in_specs=in_specs, out_specs=out_specs, check_vma=False)

time: 391 us -> 276 us (0.71); the launches traced: 384 us -> 274 us
  waiting for transfers between devices: 189 us -> 80.5 us
  Pallas kernels: 0 us -> 88.6 us
  matrix products: 75.3 us -> 0 us
  local copies, waits for them, and re-layouts: 55.6 us -> 16.1 us
  starting transfers between devices: 48.5 us -> 80.7 us
  other arithmetic: 13.5 us -> 6.56 us
    all_to_all x8 -> x0, waiting for transfers between devices: 124 us -> none  [the longest x4 78.8 us: expert_layer(): lax.all_to_all(outgoing, 'expert', split_axis=0, concat_axis=0, tiled=True)]
    pallas_call x0 -> x28, Pallas kernels: none -> 88.6 us  [the longest x4 26.2 us: first(): pl.pallas_call(first_kernel, out_shape=[jax.ShapeDtypeStruct((block, both...]
    ppermute x0 -> x24, waiting for transfers between devices: none -> 75.8 us  [across(): lax.ppermute(blocks[apart], 'expert', [(i, i ^ 2 * apart) for i in range(...]
    dot_general x24 -> x0, matrix products: 75.3 us -> none  [the longest x4 45.1 us: expert_layer(): jnp.dot(flat_rows, weight_in, preferred_element_type=jnp.float32)]
    ppermute x4 -> x19, waiting for transfers between devices: 63.4 us -> 4.7 us  [partner(): lax.ppermute(shard, axis, [(i, i ^ 1 << apart) for i in range(lax.axis_si...]
    ppermute x0 -> x24, starting transfers between devices: none -> 55.1 us  [across(): lax.ppermute(blocks[apart], 'expert', [(i, i ^ 2 * apart) for i in range(...]
    all_to_all x8 -> x0, starting transfers between devices: 39.3 us -> none  [the longest x4 20.7 us: expert_layer(): lax.all_to_all(outgoing, 'expert', split_axis=0, concat_axis=0, tiled=True)]
    dot_general x5 -> x0, local copies, waits for them, and re-layouts: 25.2 us -> none  [the longest x1 18.8 us: expert_layer(): jnp.dot(flat_rows, weight_in, preferred_element_type=jnp.float32)]
  transfers between devices with their start and end apart: 14 -> 45, of which waited for: 10 -> 16; matrix products, arithmetic and copies ran while one was open for 32% -> 4% of each run, Pallas kernels for 0% -> 32%
where the time goes in v1:
time: 276 us; the launch traced here: 274 us
  Pallas kernels  88.6 us (32%)
  starting transfers between devices  80.7 us (29%)
  waiting for transfers between devices  80.5 us (29%)
  local copies, waits for them, and re-layouts  16.1 us (6%)
  other arithmetic  6.56 us (2%)
    ppermute x24, waiting for transfers between devices, across(): lax.ppermute(blocks[apart], 'expert', [(i, i ^ 2 * apart) for i in range(...  75.8 us
    ppermute x24, starting transfers between devices, across(): lax.ppermute(blocks[apart], 'expert', [(i, i ^ 2 * apart) for i in range(...  55.1 us
    pallas_call x4, Pallas kernels, first(): pl.pallas_call(first_kernel, out_shape=[jax.ShapeDtypeStruct((block, both...  26.2 us
    ppermute x19, starting transfers between devices, partner(): lax.ppermute(shard, axis, [(i, i ^ 1 << apart) for i in range(lax.axis_si...  22.7 us
    pallas_call x4, Pallas kernels, second(): pl.pallas_call(second_kernel, out_shape=jax.ShapeDtypeStruct((block, both...  21.5 us
    pallas_call x4, Pallas kernels, fourth(): pl.pallas_call(fourth_kernel, out_shape=[jax.ShapeDtypeStruct((block, wid...  15.9 us
    pallas_call x4, Pallas kernels, third(): pl.pallas_call(third_kernel, out_shape=jax.ShapeDtypeStruct((block, half)...  9.42 us
    unnamed x38, local copies, waits for them, and re-layouts  9.34 us
  transfers between devices with their start and end apart: 45, of which 16 were waited for; matrix products, arithmetic and copies ran while one was open for 4% of the time, Pallas kernels for 32%

profile of v1, /device:TPU:0, one launch (start us, length us, event | category | flops | bytes accessed | tf_op | source)
XLA Modules:
  0.0 273.7 jit_solution(1727666222442239801)
XLA Ops:
  1.6 3.0 %collective-permute-start.24 = (bf16[32,3584]{1,0:T(8,128)(2,1)S(1)}, bf16[32,3584]{1,0:T(8,128)(2,1)S(1)}, u32[]{:S(2)}, u32[]{:S(2)}) collective-permute-start(bf16[32,3584]{1,0:T(8,128)(2,1)S(1)} %dynamic-slice_bitcast_fusion), channel_id=1, source_target_pairs={{0,1},{1,0},{2,3},{3,2},{4,5},{5,4},{6,7},{7,6},{8,9},{9,8},{10,11... | collective-permute-start | bytes 688136 | tf_op jit(solution)/shard_map/ppermute | solution.py:19
  7.1 2.1 collective-permute-start.1
  16.0 2.1 collective-permute-start.25
  18.1 2.6 collective-permute-start.26
  20.8 1.9 pack.4
  23.6 3.5 %collective-permute-start.4 = (bf16[144,896]{1,0:T(8,128)(2,1)}, bf16[144,896]{1,0:T(8,128)(2,1)S(1)}, u32[]{:S(2)}, u32[]{:S(2)}) collective-permute-start(bf16[144,896]{1,0:T(8,128)(2,1)} %get-tuple-element.48), channel_id=1, source_target_pairs={{0,4},{1,5},{2,6},{3,7},{4,0},{5,1},{6,2},{7,3},{8,12},{9,13},{10,... | collective-permute-start | bytes 774152 | tf_op jit(solution)/shard_map/ppermute | solution.py:457
  27.1 3.7 %collective-permute-done.25.r1 = bf16[144,896]{1,0:T(8,128)(2,1)S(1)} collective-permute-done((bf16[144,896]{1,0:T(8,128)(2,1)S(1)}, bf16[144,896]{1,0:T(8,128)(2,1)S(1)}, u32[]{:S(2)}, u32[]{:S(2)}) %collective-permute-start.25) | collective-permute-done | bytes 258080 | tf_op jit(solution)/shard_map/ppermute | solution.py:457
  30.8 3.6 %collective-permute-start.5 = (bf16[144,896]{1,0:T(8,128)(2,1)}, bf16[144,896]{1,0:T(8,128)(2,1)S(1)}, u32[]{:S(2)}, u32[]{:S(2)}) collective-permute-start(bf16[144,896]{1,0:T(8,128)(2,1)} %get-tuple-element.49), channel_id=1, source_target_pairs={{0,6},{1,7},{2,4},{3,5},{4,2},{5,3},{6,0},{7,1},{8,14},{9,15},{10,... | collective-permute-start | bytes 774152 | tf_op jit(solution)/shard_map/ppermute | solution.py:457
  35.1 4.4 %collective-permute-done.26.r2 = bf16[144,896]{1,0:T(8,128)(2,1)S(1)} collective-permute-done((bf16[144,896]{1,0:T(8,128)(2,1)}, bf16[144,896]{1,0:T(8,128)(2,1)S(1)}, u32[]{:S(2)}, u32[]{:S(2)}) %collective-permute-start.26) | collective-permute-done | bytes 258080 | tf_op jit(solution)/shard_map/ppermute | solution.py:457
  41.0 6.6 %first.6 = (bf16[144,1024]{1,0:T(8,128)(2,1)S(1)}, bf16[144,3584]{1,0:T(8,128)(2,1)S(1)}, f32[144,128]{1,0:T(8,128)S(1)}) custom-call(s32[2]{0:T(128)S(1)} %pad_add_fusion.me, bf16[144,896]{1,0:T(8,128)(2,1)S(1)} %get-tuple-element.68.r0, bf16[144,896]{1,0:T(8,128)(2,1)S(1)} %collective-permute-done.25.r1, bf16[144,896]{1,0:T(8,128)(2,1)S(1)} %collective-permute-done.26.r2, ...), custom_call_target="tpu_custom_call" | custom-call | flops 1056964608 | bytes 7340032 | tf_op jit(solution)/shard_map/first/pallas_call | solution.py:264
  48.2 13.0 %collective-permute-done.4.r2 = bf16[144,896]{1,0:T(8,128)(2,1)S(1)} collective-permute-done((bf16[144,896]{1,0:T(8,128)(2,1)}, bf16[144,896]{1,0:T(8,128)(2,1)S(1)}, u32[]{:S(2)}, u32[]{:S(2)}) %collective-permute-start.4) | collective-permute-done | bytes 258080 | tf_op jit(solution)/shard_map/ppermute | solution.py:457
  61.2 6.4 %first.4 = (bf16[144,1024]{1,0:T(8,128)(2,1)S(1)}, bf16[144,3584]{1,0:T(8,128)(2,1)S(1)}, f32[144,128]{1,0:T(8,128)S(1)}) custom-call(s32[2]{0:T(128)S(1)} %pad_add_fusion.me, bf16[144,896]{1,0:T(8,128)(2,1)S(1)} %get-tuple-element.46.r0, bf16[144,896]{1,0:T(8,128)(2,1)S(1)} %collective-permute-done.3.r1, bf16[144,896]{1,0:T(8,128)(2,1)S(1)} %collective-permute-done.4.r2, ...), custom_call_target="tpu_custom_call" | custom-call | flops 1056964608 | bytes 7340032 | tf_op jit(solution)/shard_map/first/pallas_call | solution.py:264
  71.2 5.2 %second.6.own = f32[144,1024]{1,0:T(8,128)S(1)} custom-call(s32[2]{0:T(128)S(1)} %pad_add_fusion.me, bf16[144,3584]{1,0:T(8,128)(2,1)S(1)} %get-tuple-element.72.rows_in, bf16[3584,2048]{1,0:T(8,128)(2,1)} %bitcast.73), custom_call_target="tpu_custom_call" | custom-call | flops 1056964608 | bytes 7340032 | tf_op jit(solution)/shard_map/second/pallas_call | solution.py:302
  78.2 5.9 %second.4.own = f32[144,1024]{1,0:T(8,128)S(1)} custom-call(s32[2]{0:T(128)S(1)} %pad_add_fusion.me, bf16[144,3584]{1,0:T(8,128)(2,1)S(1)} %get-tuple-element.50.rows_in, bf16[3584,2048]{1,0:T(8,128)(2,1)} %bitcast.74), custom_call_target="tpu_custom_call" | custom-call | flops 1056964608 | bytes 7340032 | tf_op jit(solution)/shard_map/second/pallas_call | solution.py:302
  85.3 2.4 third.6.own
  87.6 4.4 %fourth.6 = (bf16[144,896]{1,0:T(8,128)(2,1)S(1)}, bf16[144,896]{1,0:T(8,128)(2,1)}, bf16[144,896]{1,0:T(8,128)(2,1)}, bf16[144,896]{1,0:T(8,128)(2,1)}) custom-call(s32[2]{0:T(128)S(1)} %pad_add_fusion.me, bf16[144,512]{1,0:T(8,128)(2,1)S(1)} %collective-permute-done.30.hidden, bf16[1024,3584]{1,0:T(8,128)(2,1)S(1)} %bitcast.62, f32[144,3584]{1,0:T(8,128)S(1)} %third.6.own), custom_call_target="tpu_custom_call" | custom-call | flops 528482304 | bytes 3670016 | tf_op jit(solution)/shard_map/fourth/pallas_call | solution.py:392
  92.0 3.5 %collective-permute-start.31 = (bf16[144,896]{1,0:T(8,128)(2,1)}, bf16[144,896]{1,0:T(8,128)(2,1)S(1)}, u32[]{:S(2)}, u32[]{:S(2)}) collective-permute-start(bf16[144,896]{1,0:T(8,128)(2,1)} %get-tuple-element.76), channel_id=1, source_target_pairs={{0,2},{1,3},{2,0},{3,1},{4,6},{5,7},{6,4},{7,5},{8,10},{9,11},{10,... | collective-permute-start | bytes 774152 | tf_op jit(solution)/shard_map/ppermute | solution.py:457
  99.7 3.1 %copy-done.2 = bf16[1,1,1024,3584]{3,2,1,0:T(8,128)(2,1)S(1)} copy-done((bf16[1,1,1024,3584]{3,2,1,0:T(8,128)(2,1)S(1)}, bf16[1,1,1024,3584]{3,2,1,0:T(8,128)(2,1)}, u32[]{:S(2)}) %copy-start.2) | copy-done | bytes 7340056
  102.8 2.4 third.4.own
  106.7 3.1 %copy-done.3 = bf16[1,1,1024,3584]{3,2,1,0:T(8,128)(2,1)S(1)} copy-done((bf16[1,1,1024,3584]{3,2,1,0:T(8,128)(2,1)S(1)}, bf16[1,1,1024,3584]{3,2,1,0:T(8,128)(2,1)}, u32[]{:S(2)}) %copy-start.3) | copy-done | bytes 7340056
  109.8 3.5 %fourth.4 = (bf16[144,896]{1,0:T(8,128)(2,1)S(1)}, bf16[144,896]{1,0:T(8,128)(2,1)S(1)}, bf16[144,896]{1,0:T(8,128)(2,1)S(1)}, bf16[144,896]{1,0:T(8,128)(2,1)S(1)}) custom-call(s32[2]{0:T(128)S(1)} %pad_add_fusion.me, bf16[144,512]{1,0:T(8,128)(2,1)S(1)} %collective-permute-done.8.hidden, bf16[1024,3584]{1,0:T(8,128)(2,1)S(1)} %bitcast.64, ...), custom_call_target="tpu_custom_call" | custom-call | flops 528482304 | bytes 3670016 | tf_op jit(solution)/shard_map/fourth/pallas_call | solution.py:392
  113.3 2.1 collective-permute-start.10
  115.4 7.3 %collective-permute-done.32.r2 = bf16[144,896]{1,0:T(8,128)(2,1)S(1)} collective-permute-done((bf16[144,896]{1,0:T(8,128)(2,1)}, bf16[144,896]{1,0:T(8,128)(2,1)S(1)}, u32[]{:S(2)}, u32[]{:S(2)}) %collective-permute-start.32) | collective-permute-done | bytes 258080 | tf_op jit(solution)/shard_map/ppermute | solution.py:457
  124.4 4.5 %collective-permute-start.9 = (bf16[144,896]{1,0:T(8,128)(2,1)S(1)}, bf16[144,896]{1,0:T(8,128)(2,1)S(1)}, u32[]{:S(2)}, u32[]{:S(2)}) collective-permute-start(bf16[144,896]{1,0:T(8,128)(2,1)S(1)} %get-tuple-element.54), channel_id=1, source_target_pairs={{0,2},{1,3},{2,0},{3,1},{4,6},{5,7},{6,4},{7,5},{8,10},{9,11},{10,... | collective-permute-start | bytes 774152 | tf_op jit(solution)/shard_map/ppermute | solution.py:457
  129.0 2.2 mix.6
  133.5 2.5 collective-permute-done.10.r2
  137.0 2.2 mix.4
  142.1 2.3 collective-permute-start.35
  144.4 1.8 collective-permute-start.36
  147.6 7.1 %collective-permute-done.35.r1 = bf16[144,896]{1,0:T(8,128)(2,1)S(1)} collective-permute-done((bf16[144,896]{1,0:T(8,128)(2,1)S(1)}, bf16[144,896]{1,0:T(8,128)(2,1)S(1)}, u32[]{:S(2)}, u32[]{:S(2)}) %collective-permute-start.35) | collective-permute-done | bytes 258080 | tf_op jit(solution)/shard_map/ppermute | solution.py:457
  155.3 9.1 %collective-permute-done.37.r3 = bf16[144,896]{1,0:T(8,128)(2,1)S(1)} collective-permute-done((bf16[144,896]{1,0:T(8,128)(2,1)S(1)}, bf16[144,896]{1,0:T(8,128)(2,1)S(1)}, u32[]{:S(2)}, u32[]{:S(2)}) %collective-permute-start.37) | collective-permute-done | bytes 258080 | tf_op jit(solution)/shard_map/ppermute | solution.py:457
  164.4 6.4 %first.7 = (bf16[144,1024]{1,0:T(8,128)(2,1)S(1)}, bf16[144,3584]{1,0:T(8,128)(2,1)S(1)}, f32[144,128]{1,0:T(8,128)S(1)}) custom-call(s32[2]{0:T(128)S(1)} %pad_add_fusion.me, bf16[144,896]{1,0:T(8,128)(2,1)S(1)} %get-tuple-element.79.r0, bf16[144,896]{1,0:T(8,128)(2,1)S(1)} %collective-permute-done.35.r1, bf16[144,896]{1,0:T(8,128)(2,1)S(1)} %collective-permute-done.36.r2, ...), custom_call_target="tpu_custom_call" | custom-call | flops 1056964608 | bytes 7340032 | tf_op jit(solution)/shard_map/first/pallas_call | solution.py:264
  173.1 6.3 %collective-permute-start.13 = (bf16[144,896]{1,0:T(8,128)(2,1)S(1)}, bf16[144,896]{1,0:T(8,128)(2,1)S(1)}, u32[]{:S(2)}, u32[]{:S(2)}) collective-permute-start(bf16[144,896]{1,0:T(8,128)(2,1)S(1)} %get-tuple-element.58), channel_id=1, source_target_pairs={{0,2},{1,3},{2,0},{3,1},{4,6},{5,7},{6,4},{7,5},{8,10},{9,11},{10,... | collective-permute-start | bytes 774152 | tf_op jit(solution)/shard_map/ppermute | solution.py:457
  183.6 5.2 %second.7.own = f32[144,1024]{1,0:T(8,128)S(1)} custom-call(s32[2]{0:T(128)S(1)} %pad_add_fusion.me, bf16[144,3584]{1,0:T(8,128)(2,1)S(1)} %get-tuple-element.83.rows_in, bf16[3584,2048]{1,0:T(8,128)(2,1)} %bitcast.76), custom_call_target="tpu_custom_call" | custom-call | flops 1056964608 | bytes 7340032 | tf_op jit(solution)/shard_map/second/pallas_call | solution.py:302
  191.7 8.8 %collective-permute-done.14.r2 = bf16[144,896]{1,0:T(8,128)(2,1)S(1)} collective-permute-done((bf16[144,896]{1,0:T(8,128)(2,1)S(1)}, bf16[144,896]{1,0:T(8,128)(2,1)S(1)}, u32[]{:S(2)}, u32[]{:S(2)}) %collective-permute-start.14) | collective-permute-done | bytes 258080 | tf_op jit(solution)/shard_map/ppermute | solution.py:457
  200.5 6.7 %first.5 = (bf16[144,1024]{1,0:T(8,128)(2,1)S(1)}, bf16[144,3584]{1,0:T(8,128)(2,1)S(1)}, f32[144,128]{1,0:T(8,128)S(1)}) custom-call(s32[2]{0:T(128)S(1)} %pad_add_fusion.me, bf16[144,896]{1,0:T(8,128)(2,1)S(1)} %get-tuple-element.57.r0, bf16[144,896]{1,0:T(8,128)(2,1)S(1)} %collective-permute-done.13.r1, bf16[144,896]{1,0:T(8,128)(2,1)S(1)} %collective-permute-done.14.r2, ...), custom_call_target="tpu_custom_call" | custom-call | flops 1056964608 | bytes 7340032 | tf_op jit(solution)/shard_map/first/pallas_call | solution.py:264
  209.3 2.4 third.7.own
  211.7 4.2 %fourth.7 = (bf16[144,896]{1,0:T(8,128)(2,1)S(1)}, bf16[144,896]{1,0:T(8,128)(2,1)}, bf16[144,896]{1,0:T(8,128)(2,1)S(1)}, bf16[144,896]{1,0:T(8,128)(2,1)S(1)}) custom-call(s32[2]{0:T(128)S(1)} %pad_add_fusion.me, bf16[144,512]{1,0:T(8,128)(2,1)S(1)} %collective-permute-done.40.hidden, bf16[1024,3584]{1,0:T(8,128)(2,1)S(1)} %bitcast.68, ...), custom_call_target="tpu_custom_call" | custom-call | flops 528482304 | bytes 3670016 | tf_op jit(solution)/shard_map/fourth/pallas_call | solution.py:392
  215.9 5.4 %collective-permute-start.41 = (bf16[144,896]{1,0:T(8,128)(2,1)}, bf16[144,896]{1,0:T(8,128)(2,1)S(1)}, u32[]{:S(2)}, u32[]{:S(2)}) collective-permute-start(bf16[144,896]{1,0:T(8,128)(2,1)} %get-tuple-element.87), channel_id=1, source_target_pairs={{0,2},{1,3},{2,0},{3,1},{4,6},{5,7},{6,4},{7,5},{8,10},{9,11},{10,... | collective-permute-start | bytes 774152 | tf_op jit(solution)/shard_map/ppermute | solution.py:457
  224.3 5.2 %second.5.own = f32[144,1024]{1,0:T(8,128)S(1)} custom-call(s32[2]{0:T(128)S(1)} %pad_add_fusion.me, bf16[144,3584]{1,0:T(8,128)(2,1)S(1)} %get-tuple-element.61.rows_in, bf16[3584,2048]{1,0:T(8,128)(2,1)} %bitcast.78), custom_call_target="tpu_custom_call" | custom-call | flops 1056964608 | bytes 7340032 | tf_op jit(solution)/shard_map/second/pallas_call | solution.py:302
  231.0 3.1 %copy-done.4 = bf16[1,1,1024,3584]{3,2,1,0:T(8,128)(2,1)S(1)} copy-done((bf16[1,1,1024,3584]{3,2,1,0:T(8,128)(2,1)S(1)}, bf16[1,1,1024,3584]{3,2,1,0:T(8,128)(2,1)}, u32[]{:S(2)}) %copy-start.4) | copy-done | bytes 7340056
  234.0 2.4 third.5.own
  236.4 3.8 %fourth.5 = (bf16[144,896]{1,0:T(8,128)(2,1)S(1)}, bf16[144,896]{1,0:T(8,128)(2,1)S(1)}, bf16[144,896]{1,0:T(8,128)(2,1)S(1)}, bf16[144,896]{1,0:T(8,128)(2,1)S(1)}) custom-call(s32[2]{0:T(128)S(1)} %pad_add_fusion.me, bf16[144,512]{1,0:T(8,128)(2,1)S(1)} %collective-permute-done.18.hidden, bf16[1024,3584]{1,0:T(8,128)(2,1)S(1)} %bitcast.70, ...), custom_call_target="tpu_custom_call" | custom-call | flops 528482304 | bytes 3670016 | tf_op jit(solution)/shard_map/fourth/pallas_call | solution.py:392
  240.8 2.4 collective-permute-start.20
  244.7 2.2 mix.7
  248.9 15.6 %collective-permute-done.20.r2 = bf16[144,896]{1,0:T(8,128)(2,1)S(1)} collective-permute-done((bf16[144,896]{1,0:T(8,128)(2,1)S(1)}, bf16[144,896]{1,0:T(8,128)(2,1)S(1)}, u32[]{:S(2)}, u32[]{:S(2)}) %collective-permute-start.20) | collective-permute-done | bytes 258080 | tf_op jit(solution)/shard_map/ppermute | solution.py:457
  264.5 2.2 mix.5
  268.9 4.0 %collective-permute-done.22 = bf16[32,3584]{1,0:T(8,128)(2,1)S(1)} collective-permute-done((bf16[32,3584]{1,0:T(8,128)(2,1)S(1)}, bf16[32,3584]{1,0:T(8,128)(2,1)S(1)}, u32[]{:S(2)}, u32[]{:S(2)}) %collective-permute-start.22) | collective-permute-done | bytes 229408 | tf_op jit(solution)/shard_map/ppermute | solution.py:19
  (145 shorter events, 59.1 us)
Async XLA Ops:
  0.6 34.4 %copy-start = (f32[1,7168]{1,0:T(1,128)S(1)}, f32[1,7168]{1,0:T(1,128)}, u32[]{:S(2)}) copy-start(f32[1,7168]{1,0:T(1,128)} %param.19) | copy-start | bytes 86020
  1.6 12.5 %collective-permute-start.24 = (bf16[32,3584]{1,0:T(8,128)(2,1)S(1)}, bf16[32,3584]{1,0:T(8,128)(2,1)S(1)}, u32[]{:S(2)}, u32[]{:S(2)}) collective-permute-start(bf16[32,3584]{1,0:T(8,128)(2,1)S(1)} %dynamic-slice_bitcast_fusion), channel_id=1, source_target_pairs={{0,1},{1,0},{2,3},{3,2},{4,5},{5,4},{6,7},{7,6},{8,9},{9,8},{10,11... | collective-permute-start | bytes 688136 | tf_op jit(solution)/shard_map/ppermute | solution.py:19
  6.0 5.2 %collective-permute-start.2 = (f32[2,2,32,4]{2,3,1,0:T(4,128)S(1)}, f32[2,2,32,4]{2,3,1,0:T(4,128)S(1)}, u32[]{:S(2)}, u32[]{:S(2)}) collective-permute-start(f32[2,2,32,4]{2,3,1,0:T(4,128)S(1)} %maximum_maximum_fusion), channel_id=1, source_target_pairs={{0,1},{1,0},{2,3},{3,2},{4,5},{5,4},{6,7},{7,6},{8,9},{9,8},{10,11... | collective-permute-start | bytes 6152 | tf_op jit(solution)/shard_map/ppermute | solution.py:19
  7.1 13.6 %collective-permute-start.1 = (bf16[32,3584]{1,0:T(8,128)(2,1)S(1)}, bf16[32,3584]{1,0:T(8,128)(2,1)S(1)}, u32[]{:S(2)}, u32[]{:S(2)}) collective-permute-start(bf16[32,3584]{1,0:T(8,128)(2,1)S(1)} %dynamic-slice_bitcast_fusion.2), channel_id=1, source_target_pairs={{0,1},{1,0},{2,3},{3,2},{4,5},{5,4},{6,7},{7,6},{8,9},{9,8},{10,11... | collective-permute-start | bytes 688136 | tf_op jit(solution)/shard_map/ppermute | solution.py:19
  14.2 20.1 %copy-start.12 = (bf16[1,32,7168]{2,1,0:T(8,128)(2,1)S(1)}, bf16[1,32,7168]{2,1,0:T(8,128)(2,1)}, u32[]{:S(2)}) copy-start(bf16[1,32,7168]{2,1,0:T(8,128)(2,1)} %param.13) | copy-start | bytes 1376260
  16.0 14.7 %collective-permute-start.25 = (bf16[144,896]{1,0:T(8,128)(2,1)S(1)}, bf16[144,896]{1,0:T(8,128)(2,1)S(1)}, u32[]{:S(2)}, u32[]{:S(2)}) collective-permute-start(bf16[144,896]{1,0:T(8,128)(2,1)S(1)} %get-tuple-element.69), channel_id=1, source_target_pairs={{0,2},{1,3},{2,0},{3,1},{4,6},{5,7},{6,4},{7,5},{8,10},{9,11},{10,... | collective-permute-start | bytes 774152 | tf_op jit(solution)/shard_map/ppermute | solution.py:457
  18.1 21.4 %collective-permute-start.26 = (bf16[144,896]{1,0:T(8,128)(2,1)}, bf16[144,896]{1,0:T(8,128)(2,1)S(1)}, u32[]{:S(2)}, u32[]{:S(2)}) collective-permute-start(bf16[144,896]{1,0:T(8,128)(2,1)} %get-tuple-element.70), channel_id=1, source_target_pairs={{0,4},{1,5},{2,6},{3,7},{4,0},{5,1},{6,2},{7,3},{8,12},{9,13},{10,... | collective-permute-start | bytes 774152 | tf_op jit(solution)/shard_map/ppermute | solution.py:457
  20.7 20.3 %collective-permute-start.27 = (bf16[144,896]{1,0:T(8,128)(2,1)S(1)}, bf16[144,896]{1,0:T(8,128)(2,1)S(1)}, u32[]{:S(2)}, u32[]{:S(2)}) collective-permute-start(bf16[144,896]{1,0:T(8,128)(2,1)S(1)} %get-tuple-element.71), channel_id=1, source_target_pairs={{0,6},{1,7},{2,4},{3,5},{4,2},{5,3},{6,0},{7,1},{8,14},{9,15},{10,... | collective-permute-start | bytes 774152 | tf_op jit(solution)/shard_map/ppermute | solution.py:457
  22.7 25.5 %collective-permute-start.3 = (bf16[144,896]{1,0:T(8,128)(2,1)}, bf16[144,896]{1,0:T(8,128)(2,1)S(1)}, u32[]{:S(2)}, u32[]{:S(2)}) collective-permute-start(bf16[144,896]{1,0:T(8,128)(2,1)} %get-tuple-element.47), channel_id=1, source_target_pairs={{0,2},{1,3},{2,0},{3,1},{4,6},{5,7},{6,4},{7,5},{8,10},{9,11},{10,... | collective-permute-start | bytes 774152 | tf_op jit(solution)/shard_map/ppermute | solution.py:457
  23.6 37.6 %collective-permute-start.4 = (bf16[144,896]{1,0:T(8,128)(2,1)}, bf16[144,896]{1,0:T(8,128)(2,1)S(1)}, u32[]{:S(2)}, u32[]{:S(2)}) collective-permute-start(bf16[144,896]{1,0:T(8,128)(2,1)} %get-tuple-element.48), channel_id=1, source_target_pairs={{0,4},{1,5},{2,6},{3,7},{4,0},{5,1},{6,2},{7,3},{8,12},{9,13},{10,... | collective-permute-start | bytes 774152 | tf_op jit(solution)/shard_map/ppermute | solution.py:457
  30.8 30.5 %collective-permute-start.5 = (bf16[144,896]{1,0:T(8,128)(2,1)}, bf16[144,896]{1,0:T(8,128)(2,1)S(1)}, u32[]{:S(2)}, u32[]{:S(2)}) collective-permute-start(bf16[144,896]{1,0:T(8,128)(2,1)} %get-tuple-element.49), channel_id=1, source_target_pairs={{0,6},{1,7},{2,4},{3,5},{4,2},{5,3},{6,0},{7,1},{8,14},{9,15},{10,... | collective-permute-start | bytes 774152 | tf_op jit(solution)/shard_map/ppermute | solution.py:457
  39.5 91.7 %collective-permute-start.23 = (bf16[32,3584]{1,0:T(8,128)(2,1)}, bf16[32,3584]{1,0:T(8,128)(2,1)}, u32[]{:S(2)}, u32[]{:S(2)}) collective-permute-start(bf16[32,3584]{1,0:T(8,128)(2,1)} %dynamic-slice_bitcast_fusion.1), channel_id=1, source_target_pairs={{0,1},{1,0},{2,3},{3,2},{4,5},{5,4},{6,7},{7,6},{8,9},{9,8},{10,11... | collective-permute-start | bytes 688136 | tf_op jit(solution)/shard_map/ppermute | solution.py:19
  47.6 29.2 %collective-permute-start.28 = (bf16[144,1024]{1,0:T(8,128)(2,1)S(1)}, bf16[144,1024]{1,0:T(8,128)(2,1)S(1)}, u32[]{:S(2)}, u32[]{:S(2)}) collective-permute-start(bf16[144,1024]{1,0:T(8,128)(2,1)S(1)} %get-tuple-element.73), channel_id=1, source_target_pairs={{0,1},{1,0},{2,3},{3,2},{4,5},{5,4},{6,7},{7,6},{8,9},{9,8},{10,11... | collective-permute-start | bytes 884744 | tf_op jit(solution)/shard_map/ppermute | solution.py:19
  67.7 16.5 %collective-permute-start.6 = (bf16[144,1024]{1,0:T(8,128)(2,1)S(1)}, bf16[144,1024]{1,0:T(8,128)(2,1)S(1)}, u32[]{:S(2)}, u32[]{:S(2)}) collective-permute-start(bf16[144,1024]{1,0:T(8,128)(2,1)S(1)} %get-tuple-element.51), channel_id=1, source_target_pairs={{0,1},{1,0},{2,3},{3,2},{4,5},{5,4},{6,7},{7,6},{8,9},{9,8},{10,11... | collective-permute-start | bytes 884744 | tf_op jit(solution)/shard_map/ppermute | solution.py:19
  69.1 7.7 %collective-permute-start.29 = (f32[144,128]{1,0:T(8,128)S(1)}, f32[144,128]{1,0:T(8,128)S(1)}, u32[]{:S(2)}, u32[]{:S(2)}) collective-permute-start(f32[144,128]{1,0:T(8,128)S(1)} %get-tuple-element.74.squares), channel_id=1, source_target_pairs={{0,1},{1,0},{2,3},{3,2},{4,5},{5,4},{6,7},{7,6},{8,9},{9,8},{10,11... | collective-permute-start | bytes 221192 | tf_op jit(solution)/shard_map/ppermute | solution.py:19
  70.0 14.1 %collective-permute-start.7 = (f32[144,128]{1,0:T(8,128)S(1)}, f32[144,128]{1,0:T(8,128)S(1)}, u32[]{:S(2)}, u32[]{:S(2)}) collective-permute-start(f32[144,128]{1,0:T(8,128)S(1)} %get-tuple-element.52.squares), channel_id=1, source_target_pairs={{0,1},{1,0},{2,3},{3,2},{4,5},{5,4},{6,7},{7,6},{8,9},{9,8},{10,11... | collective-permute-start | bytes 221192 | tf_op jit(solution)/shard_map/ppermute | solution.py:19
  77.0 10.6 %collective-permute-start.30 = (bf16[144,512]{1,0:T(8,128)(2,1)S(1)}, bf16[144,512]{1,0:T(8,128)(2,1)S(1)}, u32[]{:S(2)}, u32[]{:S(2)}) collective-permute-start(bf16[144,512]{1,0:T(8,128)(2,1)S(1)} %act.6.hidden), channel_id=1, source_target_pairs={{0,1},{1,0},{2,3},{3,2},{4,5},{5,4},{6,7},{7,6},{8,9},{9,8},{10,11... | collective-permute-start | bytes 442376 | tf_op jit(solution)/shard_map/ppermute | solution.py:19
  84.3 20.8 %collective-permute-start.8 = (bf16[144,512]{1,0:T(8,128)(2,1)S(1)}, bf16[144,512]{1,0:T(8,128)(2,1)S(1)}, u32[]{:S(2)}, u32[]{:S(2)}) collective-permute-start(bf16[144,512]{1,0:T(8,128)(2,1)S(1)} %act.4.hidden), channel_id=1, source_target_pairs={{0,1},{1,0},{2,3},{3,2},{4,5},{5,4},{6,7},{7,6},{8,9},{9,8},{10,11... | collective-permute-start | bytes 442376 | tf_op jit(solution)/shard_map/ppermute | solution.py:19
  92.0 21.2 %collective-permute-start.31 = (bf16[144,896]{1,0:T(8,128)(2,1)}, bf16[144,896]{1,0:T(8,128)(2,1)S(1)}, u32[]{:S(2)}, u32[]{:S(2)}) collective-permute-start(bf16[144,896]{1,0:T(8,128)(2,1)} %get-tuple-element.76), channel_id=1, source_target_pairs={{0,2},{1,3},{2,0},{3,1},{4,6},{5,7},{6,4},{7,5},{8,10},{9,11},{10,... | collective-permute-start | bytes 774152 | tf_op jit(solution)/shard_map/ppermute | solution.py:457
  95.5 27.1 %collective-permute-start.32 = (bf16[144,896]{1,0:T(8,128)(2,1)}, bf16[144,896]{1,0:T(8,128)(2,1)S(1)}, u32[]{:S(2)}, u32[]{:S(2)}) collective-permute-start(bf16[144,896]{1,0:T(8,128)(2,1)} %get-tuple-element.77), channel_id=1, source_target_pairs={{0,4},{1,5},{2,6},{3,7},{4,0},{5,1},{6,2},{7,3},{8,12},{9,13},{10,... | collective-permute-start | bytes 774152 | tf_op jit(solution)/shard_map/ppermute | solution.py:457
  97.1 27.3 %collective-permute-start.33 = (bf16[144,896]{1,0:T(8,128)(2,1)}, bf16[144,896]{1,0:T(8,128)(2,1)S(1)}, u32[]{:S(2)}, u32[]{:S(2)}) collective-permute-start(bf16[144,896]{1,0:T(8,128)(2,1)} %get-tuple-element.78), channel_id=1, source_target_pairs={{0,6},{1,7},{2,4},{3,5},{4,2},{5,3},{6,0},{7,1},{8,14},{9,15},{10,... | collective-permute-start | bytes 774152 | tf_op jit(solution)/shard_map/ppermute | solution.py:457
  105.2 42.3 %collective-permute-start = (bf16[32,3584]{1,0:T(8,128)(2,1)S(1)}, bf16[32,3584]{1,0:T(8,128)(2,1)S(1)}, u32[]{:S(2)}, u32[]{:S(2)}) collective-permute-start(bf16[32,3584]{1,0:T(8,128)(2,1)S(1)} %copy-done.14), channel_id=1, source_target_pairs={{0,1},{1,0},{2,3},{3,2},{4,5},{5,4},{6,7},{7,6},{8,9},{9,8},{10,11... | collective-permute-start | bytes 688136 | tf_op jit(solution)/shard_map/ppermute | solution.py:19
  113.3 19.2 %copy-start.11 = (bf16[1,32,7168]{2,1,0:T(8,128)(2,1)S(1)}, bf16[1,32,7168]{2,1,0:T(8,128)(2,1)}, u32[]{:S(2)}) copy-start(bf16[1,32,7168]{2,1,0:T(8,128)(2,1)} %param.14) | copy-start | bytes 1376260
  113.3 22.7 %collective-permute-start.10 = (bf16[144,896]{1,0:T(8,128)(2,1)S(1)}, bf16[144,896]{1,0:T(8,128)(2,1)S(1)}, u32[]{:S(2)}, u32[]{:S(2)}) collective-permute-start(bf16[144,896]{1,0:T(8,128)(2,1)S(1)} %get-tuple-element.55), channel_id=1, source_target_pairs={{0,4},{1,5},{2,6},{3,7},{4,0},{5,1},{6,2},{7,3},{8,12},{9,13},{10,... | collective-permute-start | bytes 774152 | tf_op jit(solution)/shard_map/ppermute | solution.py:457
  122.7 13.4 %collective-permute-start.11 = (bf16[144,896]{1,0:T(8,128)(2,1)S(1)}, bf16[144,896]{1,0:T(8,128)(2,1)S(1)}, u32[]{:S(2)}, u32[]{:S(2)}) collective-permute-start(bf16[144,896]{1,0:T(8,128)(2,1)S(1)} %get-tuple-element.56), channel_id=1, source_target_pairs={{0,6},{1,7},{2,4},{3,5},{4,2},{5,3},{6,0},{7,1},{8,14},{9,15},{10,... | collective-permute-start | bytes 774152 | tf_op jit(solution)/shard_map/ppermute | solution.py:457
  124.4 12.6 %collective-permute-start.9 = (bf16[144,896]{1,0:T(8,128)(2,1)S(1)}, bf16[144,896]{1,0:T(8,128)(2,1)S(1)}, u32[]{:S(2)}, u32[]{:S(2)}) collective-permute-start(bf16[144,896]{1,0:T(8,128)(2,1)S(1)} %get-tuple-element.54), channel_id=1, source_target_pairs={{0,2},{1,3},{2,0},{3,1},{4,6},{5,7},{6,4},{7,5},{8,10},{9,11},{10,... | collective-permute-start | bytes 774152 | tf_op jit(solution)/shard_map/ppermute | solution.py:457
  131.2 9.6 %collective-permute-start.34 = (bf16[64,3584]{1,0:T(8,128)(2,1)S(1)}, bf16[64,3584]{1,0:T(8,128)(2,1)S(1)}, u32[]{:S(2)}, u32[]{:S(2)}) collective-permute-start(bf16[64,3584]{1,0:T(8,128)(2,1)S(1)} %mix.6), channel_id=1, source_target_pairs={{8,0},{16,8},{24,16},{9,1},{17,9},{25,17},{10,2},{18,10},{26,18},{... | collective-permute-start | bytes 1376264 | tf_op jit(solution)/shard_map/ppermute | solution.py:25
  139.2 32.6 %collective-permute-start.12 = (bf16[64,3584]{1,0:T(8,128)(2,1)S(1)}, bf16[64,3584]{1,0:T(8,128)(2,1)S(1)}, u32[]{:S(2)}, u32[]{:S(2)}) collective-permute-start(bf16[64,3584]{1,0:T(8,128)(2,1)S(1)} %mix.4), channel_id=1, source_target_pairs={{0,8},{8,16},{16,24},{1,9},{9,17},{17,25},{2,10},{10,18},{18,26},{... | collective-permute-start | bytes 1376264 | tf_op jit(solution)/shard_map/ppermute | solution.py:25
  142.1 12.6 %collective-permute-start.35 = (bf16[144,896]{1,0:T(8,128)(2,1)S(1)}, bf16[144,896]{1,0:T(8,128)(2,1)S(1)}, u32[]{:S(2)}, u32[]{:S(2)}) collective-permute-start(bf16[144,896]{1,0:T(8,128)(2,1)S(1)} %get-tuple-element.80), channel_id=1, source_target_pairs={{0,2},{1,3},{2,0},{3,1},{4,6},{5,7},{6,4},{7,5},{8,10},{9,11},{10,... | collective-permute-start | bytes 774152 | tf_op jit(solution)/shard_map/ppermute | solution.py:457
  144.4 10.9 %collective-permute-start.36 = (bf16[144,896]{1,0:T(8,128)(2,1)S(1)}, bf16[144,896]{1,0:T(8,128)(2,1)S(1)}, u32[]{:S(2)}, u32[]{:S(2)}) collective-permute-start(bf16[144,896]{1,0:T(8,128)(2,1)S(1)} %get-tuple-element.81), channel_id=1, source_target_pairs={{0,4},{1,5},{2,6},{3,7},{4,0},{5,1},{6,2},{7,3},{8,12},{9,13},{10,... | collective-permute-start | bytes 774152 | tf_op jit(solution)/shard_map/ppermute | solution.py:457
  146.2 18.2 %collective-permute-start.37 = (bf16[144,896]{1,0:T(8,128)(2,1)S(1)}, bf16[144,896]{1,0:T(8,128)(2,1)S(1)}, u32[]{:S(2)}, u32[]{:S(2)}) collective-permute-start(bf16[144,896]{1,0:T(8,128)(2,1)S(1)} %get-tuple-element.82), channel_id=1, source_target_pairs={{0,6},{1,7},{2,4},{3,5},{4,2},{5,3},{6,0},{7,1},{8,14},{9,15},{10,... | collective-permute-start | bytes 774152 | tf_op jit(solution)/shard_map/ppermute | solution.py:457
  170.9 18.0 %collective-permute-start.38 = (bf16[144,1024]{1,0:T(8,128)(2,1)S(1)}, bf16[144,1024]{1,0:T(8,128)(2,1)S(1)}, u32[]{:S(2)}, u32[]{:S(2)}) collective-permute-start(bf16[144,1024]{1,0:T(8,128)(2,1)S(1)} %get-tuple-element.84), channel_id=1, source_target_pairs={{0,1},{1,0},{2,3},{3,2},{4,5},{5,4},{6,7},{7,6},{8,9},{9,8},{10,11... | collective-permute-start | bytes 884744 | tf_op jit(solution)/shard_map/ppermute | solution.py:19
  173.1 18.6 %collective-permute-start.13 = (bf16[144,896]{1,0:T(8,128)(2,1)S(1)}, bf16[144,896]{1,0:T(8,128)(2,1)S(1)}, u32[]{:S(2)}, u32[]{:S(2)}) collective-permute-start(bf16[144,896]{1,0:T(8,128)(2,1)S(1)} %get-tuple-element.58), channel_id=1, source_target_pairs={{0,2},{1,3},{2,0},{3,1},{4,6},{5,7},{6,4},{7,5},{8,10},{9,11},{10,... | collective-permute-start | bytes 774152 | tf_op jit(solution)/shard_map/ppermute | solution.py:457
  179.4 21.1 %collective-permute-start.14 = (bf16[144,896]{1,0:T(8,128)(2,1)S(1)}, bf16[144,896]{1,0:T(8,128)(2,1)S(1)}, u32[]{:S(2)}, u32[]{:S(2)}) collective-permute-start(bf16[144,896]{1,0:T(8,128)(2,1)S(1)} %get-tuple-element.59), channel_id=1, source_target_pairs={{0,4},{1,5},{2,6},{3,7},{4,0},{5,1},{6,2},{7,3},{8,12},{9,13},{10,... | collective-permute-start | bytes 774152 | tf_op jit(solution)/shard_map/ppermute | solution.py:457
  181.1 19.4 %collective-permute-start.15 = (bf16[144,896]{1,0:T(8,128)(2,1)S(1)}, bf16[144,896]{1,0:T(8,128)(2,1)S(1)}, u32[]{:S(2)}, u32[]{:S(2)}) collective-permute-start(bf16[144,896]{1,0:T(8,128)(2,1)S(1)} %get-tuple-element.60), channel_id=1, source_target_pairs={{0,6},{1,7},{2,4},{3,5},{4,2},{5,3},{6,0},{7,1},{8,14},{9,15},{10,... | collective-permute-start | bytes 774152 | tf_op jit(solution)/shard_map/ppermute | solution.py:457
  182.5 6.4 %collective-permute-start.39 = (f32[144,128]{1,0:T(8,128)S(1)}, f32[144,128]{1,0:T(8,128)S(1)}, u32[]{:S(2)}, u32[]{:S(2)}) collective-permute-start(f32[144,128]{1,0:T(8,128)S(1)} %get-tuple-element.85.squares), channel_id=1, source_target_pairs={{0,1},{1,0},{2,3},{3,2},{4,5},{5,4},{6,7},{7,6},{8,9},{9,8},{10,11... | collective-permute-start | bytes 221192 | tf_op jit(solution)/shard_map/ppermute | solution.py:19
  189.0 22.6 %collective-permute-start.40 = (bf16[144,512]{1,0:T(8,128)(2,1)S(1)}, bf16[144,512]{1,0:T(8,128)(2,1)S(1)}, u32[]{:S(2)}, u32[]{:S(2)}) collective-permute-start(bf16[144,512]{1,0:T(8,128)(2,1)S(1)} %act.7.hidden), channel_id=1, source_target_pairs={{0,1},{1,0},{2,3},{3,2},{4,5},{5,4},{6,7},{7,6},{8,9},{9,8},{10,11... | collective-permute-start | bytes 442376 | tf_op jit(solution)/shard_map/ppermute | solution.py:19
  207.2 22.3 %collective-permute-start.16 = (bf16[144,1024]{1,0:T(8,128)(2,1)S(1)}, bf16[144,1024]{1,0:T(8,128)(2,1)S(1)}, u32[]{:S(2)}, u32[]{:S(2)}) collective-permute-start(bf16[144,1024]{1,0:T(8,128)(2,1)S(1)} %get-tuple-element.62), channel_id=1, source_target_pairs={{0,1},{1,0},{2,3},{3,2},{4,5},{5,4},{6,7},{7,6},{8,9},{9,8},{10,11... | collective-permute-start | bytes 884744 | tf_op jit(solution)/shard_map/ppermute | solution.py:19
  208.4 21.1 %collective-permute-start.17 = (f32[144,128]{1,0:T(8,128)S(1)}, f32[144,128]{1,0:T(8,128)S(1)}, u32[]{:S(2)}, u32[]{:S(2)}) collective-permute-start(f32[144,128]{1,0:T(8,128)S(1)} %get-tuple-element.63.squares), channel_id=1, source_target_pairs={{0,1},{1,0},{2,3},{3,2},{4,5},{5,4},{6,7},{7,6},{8,9},{9,8},{10,11... | collective-permute-start | bytes 221192 | tf_op jit(solution)/shard_map/ppermute | solution.py:19
  215.9 27.3 %collective-permute-start.41 = (bf16[144,896]{1,0:T(8,128)(2,1)}, bf16[144,896]{1,0:T(8,128)(2,1)S(1)}, u32[]{:S(2)}, u32[]{:S(2)}) collective-permute-start(bf16[144,896]{1,0:T(8,128)(2,1)} %get-tuple-element.87), channel_id=1, source_target_pairs={{0,2},{1,3},{2,0},{3,1},{4,6},{5,7},{6,4},{7,5},{8,10},{9,11},{10,... | collective-permute-start | bytes 774152 | tf_op jit(solution)/shard_map/ppermute | solution.py:457
  221.3 23.4 %collective-permute-start.42 = (bf16[144,896]{1,0:T(8,128)(2,1)S(1)}, bf16[144,896]{1,0:T(8,128)(2,1)S(1)}, u32[]{:S(2)}, u32[]{:S(2)}) collective-permute-start(bf16[144,896]{1,0:T(8,128)(2,1)S(1)} %get-tuple-element.88), channel_id=1, source_target_pairs={{0,4},{1,5},{2,6},{3,7},{4,0},{5,1},{6,2},{7,3},{8,12},{9,13},{10,... | collective-permute-start | bytes 774152 | tf_op jit(solution)/shard_map/ppermute | solution.py:457
  222.8 21.8 %collective-permute-start.43 = (bf16[144,896]{1,0:T(8,128)(2,1)S(1)}, bf16[144,896]{1,0:T(8,128)(2,1)S(1)}, u32[]{:S(2)}, u32[]{:S(2)}) collective-permute-start(bf16[144,896]{1,0:T(8,128)(2,1)S(1)} %get-tuple-element.89), channel_id=1, source_target_pairs={{0,6},{1,7},{2,4},{3,5},{4,2},{5,3},{6,0},{7,1},{8,14},{9,15},{10,... | collective-permute-start | bytes 774152 | tf_op jit(solution)/shard_map/ppermute | solution.py:457
  229.7 6.7 %collective-permute-start.18 = (bf16[144,512]{1,0:T(8,128)(2,1)S(1)}, bf16[144,512]{1,0:T(8,128)(2,1)S(1)}, u32[]{:S(2)}, u32[]{:S(2)}) collective-permute-start(bf16[144,512]{1,0:T(8,128)(2,1)S(1)} %act.5.hidden), channel_id=1, source_target_pairs={{0,1},{1,0},{2,3},{3,2},{4,5},{5,4},{6,7},{7,6},{8,9},{9,8},{10,11... | collective-permute-start | bytes 442376 | tf_op jit(solution)/shard_map/ppermute | solution.py:19
  240.2 8.7 %collective-permute-start.19 = (bf16[144,896]{1,0:T(8,128)(2,1)S(1)}, bf16[144,896]{1,0:T(8,128)(2,1)S(1)}, u32[]{:S(2)}, u32[]{:S(2)}) collective-permute-start(bf16[144,896]{1,0:T(8,128)(2,1)S(1)} %get-tuple-element.65), channel_id=1, source_target_pairs={{0,2},{1,3},{2,0},{3,1},{4,6},{5,7},{6,4},{7,5},{8,10},{9,11},{10,... | collective-permute-start | bytes 774152 | tf_op jit(solution)/shard_map/ppermute | solution.py:457
  240.8 23.7 %collective-permute-start.20 = (bf16[144,896]{1,0:T(8,128)(2,1)S(1)}, bf16[144,896]{1,0:T(8,128)(2,1)S(1)}, u32[]{:S(2)}, u32[]{:S(2)}) collective-permute-start(bf16[144,896]{1,0:T(8,128)(2,1)S(1)} %get-tuple-element.66), channel_id=1, source_target_pairs={{0,4},{1,5},{2,6},{3,7},{4,0},{5,1},{6,2},{7,3},{8,12},{9,13},{10,... | collective-permute-start | bytes 774152 | tf_op jit(solution)/shard_map/ppermute | solution.py:457
  243.2 21.3 %collective-permute-start.21 = (bf16[144,896]{1,0:T(8,128)(2,1)S(1)}, bf16[144,896]{1,0:T(8,128)(2,1)S(1)}, u32[]{:S(2)}, u32[]{:S(2)}) collective-permute-start(bf16[144,896]{1,0:T(8,128)(2,1)S(1)} %get-tuple-element.67), channel_id=1, source_target_pairs={{0,6},{1,7},{2,4},{3,5},{4,2},{5,3},{6,0},{7,1},{8,14},{9,15},{10,... | collective-permute-start | bytes 774152 | tf_op jit(solution)/shard_map/ppermute | solution.py:457
  246.9 21.1 %collective-permute-start.44 = (bf16[32,3584]{1,0:T(8,128)(2,1)S(1)}, bf16[32,3584]{1,0:T(8,128)(2,1)S(1)}, u32[]{:S(2)}, u32[]{:S(2)}) collective-permute-start(bf16[32,3584]{1,0:T(8,128)(2,1)S(1)} %constant_dynamic-slice_fusion), channel_id=1, source_target_pairs={{0,1},{1,0},{2,3},{3,2},{4,5},{5,4},{6,7},{7,6},{8,9},{9,8},{10,11... | collective-permute-start | bytes 688136 | tf_op jit(solution)/shard_map/ppermute | solution.py:19
  266.7 6.1 %collective-permute-start.22 = (bf16[32,3584]{1,0:T(8,128)(2,1)S(1)}, bf16[32,3584]{1,0:T(8,128)(2,1)S(1)}, u32[]{:S(2)}, u32[]{:S(2)}) collective-permute-start(bf16[32,3584]{1,0:T(8,128)(2,1)S(1)} %constant_dynamic-slice_fusion.1), channel_id=1, source_target_pairs={{0,1},{1,0},{2,3},{3,2},{4,5},{5,4},{6,7},{7,6},{8,9},{9,8},{10,11... | collective-permute-start | bytes 688136 | tf_op jit(solution)/shard_map/ppermute | solution.py:19
  (16 other events, 111.5 us)

commit v2 on v0

--- a/solution.py
+++ b/solution.py
@@ -1,6 +1,10 @@
+import functools
+
 import jax
 import jax.numpy as jnp
 from jax import lax
+from jax.experimental import pallas as pl
+from jax.experimental.pallas import tpu as pltpu
 from jax.sharding import PartitionSpec as P
 
 EXPERTS = 4
@@ -129,7 +133,7 @@
     return [output]
 
 
-def shards(
+def general_shards(
     east_batch,
     west_batch,
     east_entering,
@@ -170,6 +174,410 @@
     return (east_now[None], west_now[None])
 
 
+PARTS = 4
+LIMIT = 16 * 2**20
+
+
+def whole(count):
+    return [pl.BlockSpec(memory_space=pltpu.VMEM)] * count
+
+
+def without(kernel, place, count, *refs):
+    kernel(*refs[:place], *refs[place + count:])
+
+
+def call(kernel, name, out_shape, me, *arrays, after=(), scratch=(), flops=0, limit=LIMIT):
+    several = isinstance(out_shape, list)
+    if after:
+        kernel = functools.partial(without, kernel, 1 + len(arrays), len(after))
+    unread = [pl.BlockSpec(memory_space=pl.ANY)] * len(after)
+    return pl.pallas_call(
+        kernel,
+        out_shape=out_shape,
+        in_specs=[pl.BlockSpec(memory_space=pltpu.SMEM)] + whole(len(arrays)) + unread,
+        out_specs=whole(len(out_shape)) if several else whole(1)[0],
+        scratch_shapes=list(scratch),
+        compiler_params=pltpu.CompilerParams(vmem_limit_bytes=limit),
+        cost_estimate=pl.CostEstimate(flops=flops, bytes_accessed=0, transcendentals=0),
+        name=name,
+    )(me, *arrays, *after)
+
+
+def bf16(*shape):
+    return jax.ShapeDtypeStruct(shape, jnp.bfloat16)
+
+
+def f32(*shape):
+    return jax.ShapeDtypeStruct(shape, jnp.float32)
+
+
+def iota(shape, axis):
+    return lax.broadcasted_iota(jnp.int32, shape, axis)
+
+
+def matmul(a, b):
+    return jnp.dot(a, b, preferred_element_type=jnp.float32)
+
+
+def ones_where(condition):
+    return condition.astype(jnp.float32).astype(jnp.bfloat16)
+
+
+def pieces(values):
+    high = values.astype(jnp.bfloat16)
+    rest = values - high.astype(jnp.float32)
+    middle = rest.astype(jnp.bfloat16)
+    return high, middle, (rest - middle.astype(jnp.float32)).astype(jnp.bfloat16)
+
+
+def cut_kernel(me, batch, sent):
+    half = sent.shape[1]
+    sent[...] = batch[:, pl.ds(pl.multiple_of((1 - me[1]) * half, half), half)]
+
+
+def cut(me, batch):
+    rows, model_width = batch.shape
+    return call(cut_kernel, "cut", bf16(rows, model_width // 2), me, batch)
+
+
+def tables_kernel(me, own, other, as_rows, as_columns):
+    rows = own.shape[1]
+    total = as_rows.shape[1]
+    row_sum = jnp.zeros(as_rows.shape, jnp.float32)
+    column_sum = jnp.zeros(as_columns.shape, jnp.float32)
+    for source, x in ((own, me[1]), (other, 1 - me[1])):
+        token, column = iota((rows, total), 0), iota((rows, total), 1)
+        spread = ones_where((column % rows == token) & (column // rows % 2 == x))
+        line, lane = iota((total, rows), 0), iota((total, rows), 1)
+        gather = ones_where((line % rows == lane) & (line // rows % 2 == x))
+        high, middle, low = pieces(source[...])
+        row_sum = row_sum + ((matmul(low, spread) + matmul(middle, spread)) + matmul(high, spread))
+        turned = [
+            lax.dot_general(gather, piece, (((1,), (1,)), ((), ())), preferred_element_type=jnp.float32)
+            for piece in (low, middle, high)
+        ]
+        column_sum = column_sum + ((turned[0] + turned[1]) + turned[2])
+    as_rows[...] = row_sum
+    as_columns[...] = column_sum
+
+
+def tables(me, own, other):
+    kinds, rows = own.shape
+    total = 2 * PARTS * rows
+    return call(tables_kernel, "tables", [f32(kinds, total), f32(total, kinds)], me, own, other)
+
+
+def joined(me, batch, other, state):
+    rows, half = other.shape
+    kept = batch[:, pl.ds(pl.multiple_of(me[1] * half, half), half)]
+    state[pl.ds(pl.multiple_of(me[1] * rows, rows), rows), :] = kept
+    state[pl.ds(pl.multiple_of((1 - me[1]) * rows, rows), rows), :] = other[...]
+
+
+def packed(me, state, table, turn, outs, stacked):
+    tokens, half = state.shape
+    rows = tokens // 2
+    width = half // PARTS
+    total = PARTS * tokens
+    slots = 2 * CAP
+    for part in range(PARTS):
+        stacked[part * tokens:(part + 1) * tokens, :] = state[:, part * width:(part + 1) * width]
+    expert = me[0] ^ iota((8, total), 0)
+    chosen = table[4 * turn:4 * turn + 2, :].astype(jnp.int32)
+    named = (chosen[0:1, :] == expert) | (chosen[1:2, :] == expert)
+    earlier = (iota((total, total), 0) // rows == iota((total, total), 1) // rows) & (
+        iota((total, total), 0) < iota((total, total), 1)
+    )
+    before = matmul(ones_where(named), ones_where(earlier))
+    column = iota((8, total), 1)
+    start = column // tokens * slots + column // rows % 2 * CAP
+    place = jnp.where(named, start + before.astype(jnp.int32), -1)
+    for apart in range(EXPERTS):
+        hit = iota((PARTS * slots, total), 0) == place[apart:apart + 1, :]
+        outs[apart][...] = matmul(ones_where(hit), stacked[...]).astype(jnp.bfloat16)
+
+
+def enter_kernel(turn, me, batch, other, table, o0, o1, o2, o3, state, stacked):
+    joined(me, batch, other, state)
+    packed(me, state, table, turn, (o0, o1, o2, o3), stacked)
+
+
+def relay_kernel(turn, edge, me, moved, batch, other, table, o0, o1, o2, o3, state, stacked):
+    state[...] = moved[...]
+
+    @pl.when(me[2 + edge] == 1)
+    def _():
+        joined(me, batch, other, state)
+
+    packed(me, state, table, turn, (o0, o1, o2, o3), stacked)
+
+
+def pack_shapes(rows, half):
+    width = half // PARTS
+    outs = [bf16(PARTS * 2 * CAP, width)] * EXPERTS + [bf16(2 * rows, half)]
+    return outs, [pltpu.VMEM((PARTS * 2 * rows, width), jnp.bfloat16)]
+
+
+def enter(me, turn, batch, other, table):
+    outs, scratch = pack_shapes(*other.shape)
+    made = call(functools.partial(enter_kernel, turn), "enter", outs, me, batch, other, table, scratch=scratch)
+    return made[:EXPERTS], made[EXPERTS]
+
+
+def relay(me, turn, edge, moved, batch, other, table):
+    outs, scratch = pack_shapes(*other.shape)
+    kernel = functools.partial(relay_kernel, turn, edge)
+    made = call(kernel, "relay", outs, me, moved, batch, other, table, scratch=scratch)
+    return made[:EXPERTS], made[EXPERTS]
+
+
+def first_kernel(me, r0, r1, r2, r3, gain, weight, partial, rows_out, squares, stacked):
+    slots = 2 * CAP
+    block = PARTS * slots
+    width = r0.shape[1]
+    units = weight.shape[1] // 4
+    for apart, ref in enumerate((r0, r1, r2, r3)):
+        stacked[apart * block:(apart + 1) * block, :] = ref[...]
+    row = iota((block, EXPERTS * block), 0)
+    column = iota((block, EXPERTS * block), 1)
+    total = jnp.zeros((block, 1), jnp.float32)
+    for part in range(PARTS):
+        source = row // slots * block + part * slots + row % slots
+        pick = (column == source).astype(jnp.float32).astype(jnp.bfloat16)
+        values = matmul(pick, stacked[...])
+        total = total + jnp.sum(values * values, axis=1, keepdims=True)
+        start = pl.multiple_of(me[1] * PARTS * width + part * width, width)
+        scaled = values * gain[:, pl.ds(start, width)]
+        rows_out[:, part * width:(part + 1) * width] = scaled.astype(jnp.bfloat16)
+    squares[...] = jnp.broadcast_to(total, squares.shape)
+    lane = iota(squares.shape, 1)
+    high, middle, low = [piece.astype(jnp.float32) for piece in pieces(total)]
+    sent = jnp.where(lane == 0, high, jnp.where(lane == 1, middle, jnp.where(lane == 2, low, 0.0)))
+    partial[:, 2 * units:] = sent.astype(jnp.bfloat16)
+    for kind in range(2):
+        start = pl.multiple_of(2 * units * kind + units * (1 - me[1]), units)
+        columns = matmul(rows_out[...], weight[:, pl.ds(start, units)])
+        partial[:, kind * units:(kind + 1) * units] = columns.astype(jnp.bfloat16)
+
+
+def first(me, received, gain, weight, after):
+    block, width = received[0].shape
+    half, both = weight.shape
+    outs = [bf16(block, both // 2 + 128), bf16(block, half), f32(block, 128)]
+    scratch = [pltpu.VMEM((EXPERTS * block, width), jnp.bfloat16)]
+    return call(first_kernel, "first", outs, me, *received, gain, weight, after=after, scratch=scratch, flops=block * half * both)
+
+
+def second_kernel(me, rows_in, weight, own):
+    units = weight.shape[1] // 4
+    for kind in range(2):
+        start = pl.multiple_of(2 * units * kind + units * me[1], units)
+        own[:, kind * units:(kind + 1) * units] = matmul(rows_in[...], weight[:, pl.ds(start, units)])
+
+
+def second(me, rows_in, weight):
+    block, half = rows_in.shape
+    both = weight.shape[1]
+    return call(second_kernel, "second", f32(block, both // 2), me, rows_in, weight, flops=block * half * both)
+
+
+def act_kernel(model_width, me, own, other, squares, hidden):
+    units = hidden.shape[1]
+    arrived = other[:, 2 * units:].astype(jnp.float32)
+    mean = (squares[:, 0:1] + ((arrived[:, 2:3] + arrived[:, 1:2]) + arrived[:, 0:1])) / model_width
+    scale = lax.rsqrt(mean + EPSILON)
+    gate = (own[:, :units] + other[:, :units].astype(jnp.float32)) * scale
+    up = (own[:, units:] + other[:, units:2 * units].astype(jnp.float32)) * scale
+    hidden[...] = (gate / (1.0 + jnp.exp(-gate)) * up).astype(jnp.bfloat16)
+
+
+def act(me, own, other, squares, model_width):
+    block, both = own.shape
+    return call(functools.partial(act_kernel, model_width), "act", bf16(block, both // 2), me, own, other, squares)
+
+
+def third_kernel(me, hidden, hidden_other, weight, o0, o1, o2, o3, stacked):
+    slots = 2 * CAP
+    block, units = hidden.shape
+    width = o0.shape[1]
+    own_rows = pl.ds(pl.multiple_of(units * me[1], units), units)
+    other_rows = pl.ds(pl.multiple_of(units * (1 - me[1]), units), units)
+    for part in range(PARTS):
+        columns = slice(part * width, (part + 1) * width)
+        result = matmul(hidden[...], weight[own_rows, columns]) + matmul(hidden_other[...], weight[other_rows, columns])
+        stacked[part * block:(part + 1) * block, :] = result.astype(jnp.bfloat16)
+    row = iota((block, PARTS * block), 0)
+    column = iota((block, PARTS * block), 1)
+    for apart, out in enumerate((o0, o1, o2, o3)):
+        source = row // slots * block + apart * slots + row % slots
+        pick = (column == source).astype(jnp.float32).astype(jnp.bfloat16)
+        out[...] = matmul(pick, stacked[...]).astype(jnp.bfloat16)
+
+
+def third(me, hidden, hidden_other, weight):
+    block, units = hidden.shape
+    half = weight.shape[1]
+    width = half // PARTS
+    outs = [bf16(block, width)] * EXPERTS
+    scratch = [pltpu.VMEM((PARTS * block, width), jnp.bfloat16)]
+    flops = 4 * block * half * units
+    return call(third_kernel, "third", outs, me, hidden, hidden_other, weight, scratch=scratch, flops=flops)
+
+
+def mixed_parts(me, table, turn, received, tokens):
+    rows = tokens // 2
+    width = received[0].shape[1]
+    total = PARTS * tokens
+    slots = 2 * CAP
+    expert = me[0] ^ iota((total, 128), 1)
+    chosen = table[:, 4 * turn:4 * turn + 2].astype(jnp.int32)
+    share = table[:, 4 * turn + 2:4 * turn + 4]
+    hits = [chosen[:, k:k + 1] == expert for k in range(2)]
+    weight = jnp.where(hits[0], share[:, 0:1], 0.0) + jnp.where(hits[1], share[:, 1:2], 0.0)
+    named = hits[0] | hits[1]
+    earlier = (iota((total, total), 0) // rows == iota((total, total), 1) // rows) & (
+        iota((total, total), 0) > iota((total, total), 1)
+    )
+    before = matmul(ones_where(earlier), ones_where(named))
+    line = iota((total, 128), 0)
+    start = line // tokens * slots + line // rows % 2 * CAP
+    place = jnp.where(named, start + before.astype(jnp.int32), -1)
+    mixed = jnp.zeros((total, width), jnp.float32)
+    for apart, ref in enumerate(received):
+        hit = iota((total, PARTS * slots), 1) == place[:, apart:apart + 1]
+        spread = jnp.where(hit, weight[:, apart:apart + 1], 0.0)
+        high = spread.astype(jnp.bfloat16)
+        low = (spread - high.astype(jnp.float32)).astype(jnp.bfloat16)
+        mixed = mixed + matmul(high, ref[...]) + matmul(low, ref[...])
+    return mixed
+
+
+def mix_kernel(turn, me, state, table, r0, r1, r2, r3, out):
+    tokens = state.shape[0]
+    width = r0.shape[1]
+    mixed = mixed_parts(me, table, turn, (r0, r1, r2, r3), tokens)
+    for part in range(PARTS):
+        span = slice(part * width, (part + 1) * width)
+        summed = state[:, span].astype(jnp.float32) + mixed[part * tokens:(part + 1) * tokens, :]
+        out[:, span] = summed.astype(jnp.bfloat16)
+
+
+def mix(me, turn, state, table, received, after):
+    kernel = functools.partial(mix_kernel, turn)
+    return call(kernel, "mix", bf16(*state.shape), me, state, table, *received, after=after)
+
+
+def last_kernel(turn, me, state, table, r0, r1, r2, r3, kept, sent, result):
+    rows = kept.shape[0]
+    mix_kernel(turn, me, state, table, r0, r1, r2, r3, result)
+    kept[...] = result[pl.ds(pl.multiple_of(me[1] * rows, rows), rows), :]
+    sent[...] = result[pl.ds(pl.multiple_of((1 - me[1]) * rows, rows), rows), :]
+
+
+def last(me, turn, state, table, received, after):
+    tokens, half = state.shape
+    outs = [bf16(tokens // 2, half)] * 2
+    scratch = [pltpu.VMEM(state.shape, jnp.bfloat16)]
+    return call(functools.partial(last_kernel, turn), "last", outs, me, state, table, *received, after=after, scratch=scratch)
+
+
+def finish_kernel(me, kept, other, out):
+    half = kept.shape[1]
+    out[:, pl.ds(pl.multiple_of(me[1] * half, half), half)] = kept[...]
+    out[:, pl.ds(pl.multiple_of((1 - me[1]) * half, half), half)] = other[...]
+
+
+def finish(me, kept, other):
+    return call(finish_kernel, "finish", bf16(kept.shape[0], 2 * kept.shape[1]), me, kept, other)
+
+
+def across(blocks, behind=None):
+    size = lax.axis_size("expert")
+    blocks = list(blocks)
+    if behind is not None:
+        *blocks, behind[2] = lax.optimization_barrier((*blocks, behind[2]))
+    moved = list(blocks)
+    for apart in (2, 3, 1):
+        moved[apart] = lax.ppermute(blocks[apart], "expert", [(i, i ^ 2 * apart) for i in range(size)])
+    return moved
+
+
+def paired_shards(
+    east_batch,
+    west_batch,
+    east_entering,
+    west_entering,
+    east_experts,
+    west_experts,
+    east_gates,
+    west_gates,
+    norm_gain,
+    expert_in,
+    expert_down,
+):
+    section_index = lax.axis_index("pipe")
+    section_count = lax.axis_size("pipe")
+    member = lax.axis_index("expert")
+    edges = [section_index == 0, section_index == section_count - 1]
+    me = jnp.stack([member // 2, member % 2, *edges]).astype(jnp.int32)
+    rows, model_width = east_batch.shape[1:]
+    weight_in = expert_in[0, 0]
+    weight_out = expert_down[0, 0]
+    kinds = [
+        jnp.swapaxes(array[tick, 0], 0, 1).astype(jnp.float32)
+        for experts, gates in ((east_experts, east_gates), (west_experts, west_gates))
+        for tick in range(TICKS)
+        for array in (experts, gates)
+    ]
+    lists = jnp.concatenate(kinds, axis=0)
+
+    batches = [east_batch[0], west_batch[0]]
+    entering = [east_entering[0], west_entering[0]]
+    batches_other = [partner(cut(me, batch), "expert", 0) for batch in batches]
+    as_rows, as_columns = tables(me, lists, partner(lists, "expert", 0))
+    entering_other = [partner(cut(me, batch), "expert", 0) for batch in entering]
+    moved = [None, None]
+    results = [None, None]
+    states = [None, None]
+    ahead = None
+    for tick in range(TICKS):
+        final = tick + 1 == TICKS
+        arrived = [None, None]
+        for stream in range(2):
+            turn = stream * TICKS + tick
+            if tick == 0:
+                sent, states[stream] = enter(me, turn, batches[stream], batches_other[stream], as_rows)
+            else:
+                sent, states[stream] = relay(
+                    me, turn, stream, moved[stream], entering[stream], entering_other[stream], as_rows
+                )
+                if stream == 0:
+                    moved[1] = shifted(mix(me, turn_before, state_before, as_columns, ahead, [sent[0]]), "pipe", -1)
+            arrived[stream] = across(sent, ahead)
+            ahead = arrived[stream]
+        behind = states[1]
+        for stream in range(2):
+            turn = stream * TICKS + tick
+            partial, scaled, squares = first(me, arrived[stream], norm_gain, weight_in, [behind])
+            other = partner(partial, "expert", 0)
+            own = second(me, scaled, weight_in)
+            hidden = act(me, own, other, squares, model_width)
+            hidden_other = partner(hidden, "expert", 0)
+            result = third(me, hidden, hidden_other, weight_out)
+            behind = result[0]
+            arrived[stream] = across(result, ahead)
+            ahead = arrived[stream]
+        if final:
+            for stream in range(2):
+                turn = stream * TICKS + tick
+                kept, sent = last(me, turn, states[stream], as_columns, arrived[stream], [behind])
+                results[stream] = finish(me, kept, partner(sent, "expert", 0))
+        else:
+            moved[0] = shifted(mix(me, tick, states[0], as_columns, arrived[0], [behind]), "pipe", 1)
+            turn_before, state_before = TICKS + tick, states[1]
+    return (results[0][None], results[1][None])
+
+
 def solution(mesh):
     in_specs = (
         P("pipe", "expert", None),
@@ -185,4 +593,6 @@
         P("pipe", "expert", None, None),
     )
     out_specs = (P("pipe", "expert", None), P("pipe", "expert", None))
+    groups = mesh.shape["expert"] // EXPERTS
+    shards = paired_shards if groups == 2 else general_shards
     return jax.shard_map(shards, mesh=mesh, in_specs=in_specs, out_specs=out_specs, check_vma=False)

time: 391 us -> 245 us (0.63)
  waiting for transfers between devices: 189 us -> 96.8 us
  matrix products: 75.3 us -> 0 us
  Pallas kernels: 0 us -> 53.1 us
  local copies, waits for them, and re-layouts: 55.6 us -> 10.8 us
  starting transfers between devices: 48.5 us -> 78.7 us
  other arithmetic: 13.5 us -> 0.81 us
    all_to_all x8 -> x0, waiting for transfers between devices: 124 us -> none  [the longest x4 78.8 us: expert_layer(): lax.all_to_all(outgoing, 'expert', split_axis=0, concat_axis=0, tiled=True)]
    dot_general x24 -> x0, matrix products: 75.3 us -> none  [the longest x4 45.1 us: expert_layer(): jnp.dot(flat_rows, weight_in, preferred_element_type=jnp.float32)]
    ppermute x0 -> x24, waiting for transfers between devices: none -> 58.4 us  [across(): lax.ppermute(blocks[apart], 'expert', [(i, i ^ 2 * apart) for i in range(...]
    ppermute x0 -> x24, starting transfers between devices: none -> 56.8 us  [across(): lax.ppermute(blocks[apart], 'expert', [(i, i ^ 2 * apart) for i in range(...]
    pallas_call x0 -> x31, Pallas kernels: none -> 53.1 us  [call(): pl.pallas_call(kernel, out_shape=out_shape, in_specs=[pl.BlockSpec(memory...]
    all_to_all x8 -> x0, starting transfers between devices: 39.3 us -> none  [the longest x4 20.7 us: expert_layer(): lax.all_to_all(outgoing, 'expert', split_axis=0, concat_axis=0, tiled=True)]
    dot_general x5 -> x0, local copies, waits for them, and re-layouts: 25.2 us -> none  [the longest x1 18.8 us: expert_layer(): jnp.dot(flat_rows, weight_in, preferred_element_type=jnp.float32)]
    ppermute x4 -> x15, waiting for transfers between devices: 63.4 us -> 38.5 us  [partner(): lax.ppermute(shard, axis, [(i, i ^ 1 << apart) for i in range(lax.axis_si...]
  transfers between devices with their start and end apart: 14 -> 41, of which waited for: 10 -> 21; matrix products, arithmetic and copies ran while one was open for 32% -> 1% of each run, Pallas kernels for 0% -> 14%
where the time goes in v2:
time: 245 us; the launch traced here: 241 us
  waiting for transfers between devices  96.8 us (40%)
  starting transfers between devices  78.7 us (32%)
  Pallas kernels  53.1 us (22%)
  local copies, waits for them, and re-layouts  10.8 us (4%)
    ppermute x24, waiting for transfers between devices, across(): lax.ppermute(blocks[apart], 'expert', [(i, i ^ 2 * apart) for i in range(...  58.4 us
    ppermute x24, starting transfers between devices, across(): lax.ppermute(blocks[apart], 'expert', [(i, i ^ 2 * apart) for i in range(...  56.8 us
    pallas_call x31, Pallas kernels, call(): pl.pallas_call(kernel, out_shape=out_shape, in_specs=[pl.BlockSpec(memory...  53.1 us
    ppermute x15, waiting for transfers between devices, partner(): lax.ppermute(shard, axis, [(i, i ^ 1 << apart) for i in range(lax.axis_si...  38.5 us
    ppermute x15, starting transfers between devices, partner(): lax.ppermute(shard, axis, [(i, i ^ 1 << apart) for i in range(lax.axis_si...  19.2 us
    unnamed x24, local copies, waits for them, and re-layouts  10 us
  transfers between devices with their start and end apart: 41, of which 21 were waited for; matrix products, arithmetic and copies ran while one was open for 1% of the time, Pallas kernels for 14%

profile of v2, /device:TPU:0, one launch (start us, length us, event | category | flops | bytes accessed | tf_op | source)
XLA Modules:
  0.0 241.2 jit_solution(8848711955565593600)
XLA Ops:
  2.3 3.0 %collective-permute-start = (bf16[32,3584]{1,0:T(8,128)(2,1)S(1)}, bf16[32,3584]{1,0:T(8,128)(2,1)S(1)}, u32[]{:S(2)}, u32[]{:S(2)}) collective-permute-start(bf16[32,3584]{1,0:T(8,128)(2,1)S(1)} %cut.4), channel_id=1, source_target_pairs={{0,1},{1,0},{2,3},{3,2},{4,5},{5,4},{6,7},{7,6},{8,9},{9,8},{10,11... | collective-permute-start | bytes 688136 | tf_op jit(solution)/shard_map/ppermute | solution.py:19
  6.9 4.2 %collective-permute-done.1.other = f32[16,32]{1,0:T(8,128)S(1)} collective-permute-done((f32[16,32]{1,0:T(8,128)S(1)}, f32[16,32]{1,0:T(8,128)S(1)}, u32[]{:S(2)}, u32[]{:S(2)}) %collective-permute-start.1) | collective-permute-done | bytes 2080 | tf_op jit(solution)/shard_map/ppermute | solution.py:19
  14.1 2.9 %collective-permute-start.4 = (bf16[144,896]{1,0:T(8,128)(2,1)S(1)}, bf16[144,896]{1,0:T(8,128)(2,1)S(1)}, u32[]{:S(2)}, u32[]{:S(2)}) collective-permute-start(bf16[144,896]{1,0:T(8,128)(2,1)S(1)} %get-tuple-element.99), channel_id=1, source_target_pairs={{0,4},{1,5},{2,6},{3,7},{4,0},{5,1},{6,2},{7,3},{8,12},{9,13},{10,... | collective-permute-start | bytes 774152 | tf_op jit(solution)/shard_map/ppermute | solution.py:501
  22.0 4.3 %collective-permute-done.3.other = bf16[32,3584]{1,0:T(8,128)(2,1)S(1)} collective-permute-done((bf16[32,3584]{1,0:T(8,128)(2,1)S(1)}, bf16[32,3584]{1,0:T(8,128)(2,1)S(1)}, u32[]{:S(2)}, u32[]{:S(2)}) %collective-permute-start.3) | collective-permute-done | bytes 229408 | tf_op jit(solution)/shard_map/ppermute | solution.py:19
  28.5 6.2 %collective-permute-done.4.refs_3_ = bf16[144,896]{1,0:T(8,128)(2,1)S(1)} collective-permute-done((bf16[144,896]{1,0:T(8,128)(2,1)S(1)}, bf16[144,896]{1,0:T(8,128)(2,1)S(1)}, u32[]{:S(2)}, u32[]{:S(2)}) %collective-permute-start.4) | collective-permute-done | bytes 258080 | tf_op jit(solution)/shard_map/ppermute | solution.py:501
  34.7 5.2 %copy-done = bf16[1,1,3584,2048]{3,2,1,0:T(8,128)(2,1)S(1)} copy-done((bf16[1,1,3584,2048]{3,2,1,0:T(8,128)(2,1)S(1)}, bf16[1,1,3584,2048]{3,2,1,0:T(8,128)(2,1)}, u32[]{:S(2)}) %copy-start) | copy-done | bytes 14680088
  40.7 2.8 %first.4 = (bf16[144,1152]{1,0:T(8,128)(2,1)S(1)}, bf16[144,3584]{1,0:T(8,128)(2,1)S(1)}, f32[144,128]{1,0:T(8,128)S(1)}) custom-call(s32[4]{0:T(128)S(1)} %pad_add_fusion.me.refs_0_, bf16[144,896]{1,0:T(8,128)(2,1)S(1)} %get-tuple-element.93.refs_1_, bf16[144,896]{1,0:T(8,128)(2,1)S(1)} %collective-permute-done.2.refs_2_, ...), custom_call_target="tpu_custom_call" | custom-call | flops 1056964608 | tf_op jit(solution)/shard_map/first/pallas_call | solution.py:194
  45.0 6.9 %collective-permute-start.8 = (bf16[144,896]{1,0:T(8,128)(2,1)S(1)}, bf16[144,896]{1,0:T(8,128)(2,1)S(1)}, u32[]{:S(2)}, u32[]{:S(2)}) collective-permute-start(bf16[144,896]{1,0:T(8,128)(2,1)S(1)} %get-tuple-element.110), channel_id=1, source_target_pairs={{0,4},{1,5},{2,6},{3,7},{4,0},{5,1},{6,2},{7,3},{8,12},{9,13},{10,... | collective-permute-start | bytes 774152 | tf_op jit(solution)/shard_map/ppermute | solution.py:501
  53.4 1.8 second.4.own
  56.7 4.6 %collective-permute-done.7.hidden_other = bf16[144,512]{1,0:T(8,128)(2,1)S(1)} collective-permute-done((bf16[144,512]{1,0:T(8,128)(2,1)S(1)}, bf16[144,512]{1,0:T(8,128)(2,1)S(1)}, u32[]{:S(2)}, u32[]{:S(2)}) %collective-permute-start.7) | collective-permute-done | bytes 147488 | tf_op jit(solution)/shard_map/ppermute | solution.py:19
  61.3 2.9 %third.4 = (bf16[144,896]{1,0:T(8,128)(2,1)S(1)}, bf16[144,896]{1,0:T(8,128)(2,1)S(1)}, bf16[144,896]{1,0:T(8,128)(2,1)S(1)}, bf16[144,896]{1,0:T(8,128)(2,1)S(1)}) custom-call(s32[4]{0:T(128)S(1)} %pad_add_fusion.me.refs_0_, bf16[144,512]{1,0:T(8,128)(2,1)S(1)} %act.4.hidden, bf16[144,512]{1,0:T(8,128)(2,1)S(1)} %collective-permute-done.7.hidden_other, ...), custom_call_target="tpu_custom_call" | custom-call | flops 1056964608 | tf_op jit(solution)/shard_map/third/pallas_call | solution.py:194
  65.1 5.2 %collective-permute-done.10.refs_2_ = bf16[144,896]{1,0:T(8,128)(2,1)S(1)} collective-permute-done((bf16[144,896]{1,0:T(8,128)(2,1)S(1)}, bf16[144,896]{1,0:T(8,128)(2,1)S(1)}, u32[]{:S(2)}, u32[]{:S(2)}) %collective-permute-start.10) | collective-permute-done | bytes 258080 | tf_op jit(solution)/shard_map/ppermute | solution.py:501
  70.3 2.8 %first.5 = (bf16[144,1152]{1,0:T(8,128)(2,1)S(1)}, bf16[144,3584]{1,0:T(8,128)(2,1)S(1)}, f32[144,128]{1,0:T(8,128)S(1)}) custom-call(s32[4]{0:T(128)S(1)} %pad_add_fusion.me.refs_0_, bf16[144,896]{1,0:T(8,128)(2,1)S(1)} %get-tuple-element.113.refs_1_, bf16[144,896]{1,0:T(8,128)(2,1)S(1)} %collective-permute-done.10.refs_2_, ...), custom_call_target="tpu_custom_call" | custom-call | flops 1056964608 | tf_op jit(solution)/shard_map/first/pallas_call | solution.py:194
  73.7 4.9 %collective-permute-start.9 = (bf16[144,896]{1,0:T(8,128)(2,1)S(1)}, bf16[144,896]{1,0:T(8,128)(2,1)S(1)}, u32[]{:S(2)}, u32[]{:S(2)}) collective-permute-start(bf16[144,896]{1,0:T(8,128)(2,1)S(1)} %get-tuple-element.112), channel_id=1, source_target_pairs={{0,2},{1,3},{2,0},{3,1},{4,6},{5,7},{6,4},{7,5},{8,10},{9,11},{10,... | collective-permute-start | bytes 774152 | tf_op jit(solution)/shard_map/ppermute | solution.py:501
  78.6 2.4 collective-permute-start.15
  85.2 3.6 %collective-permute-done.13.hidden_other = bf16[144,512]{1,0:T(8,128)(2,1)S(1)} collective-permute-done((bf16[144,512]{1,0:T(8,128)(2,1)S(1)}, bf16[144,512]{1,0:T(8,128)(2,1)S(1)}, u32[]{:S(2)}, u32[]{:S(2)}) %collective-permute-start.13) | collective-permute-done | bytes 147488 | tf_op jit(solution)/shard_map/ppermute | solution.py:19
  88.9 3.1 %third.5 = (bf16[144,896]{1,0:T(8,128)(2,1)S(1)}, bf16[144,896]{1,0:T(8,128)(2,1)S(1)}, bf16[144,896]{1,0:T(8,128)(2,1)S(1)}, bf16[144,896]{1,0:T(8,128)(2,1)S(1)}) custom-call(s32[4]{0:T(128)S(1)} %pad_add_fusion.me.refs_0_, bf16[144,512]{1,0:T(8,128)(2,1)S(1)} %act.5.hidden, bf16[144,512]{1,0:T(8,128)(2,1)S(1)} %collective-permute-done.13.hidden_other, ...), custom_call_target="tpu_custom_call" | custom-call | flops 1056964608 | tf_op jit(solution)/shard_map/third/pallas_call | solution.py:194
  92.0 7.8 %collective-permute-done.14.refs_5_ = bf16[144,896]{1,0:T(8,128)(2,1)S(1)} collective-permute-done((bf16[144,896]{1,0:T(8,128)(2,1)S(1)}, bf16[144,896]{1,0:T(8,128)(2,1)S(1)}, u32[]{:S(2)}, u32[]{:S(2)}) %collective-permute-start.14) | collective-permute-done | bytes 258080 | tf_op jit(solution)/shard_map/ppermute | solution.py:501
  99.7 2.2 mix.2
  103.3 3.4 %collective-permute-start.18 = (bf16[144,896]{1,0:T(8,128)(2,1)S(1)}, bf16[144,896]{1,0:T(8,128)(2,1)S(1)}, u32[]{:S(2)}, u32[]{:S(2)}) collective-permute-start(bf16[144,896]{1,0:T(8,128)(2,1)S(1)} %get-tuple-element.132), channel_id=1, source_target_pairs={{0,4},{1,5},{2,6},{3,7},{4,0},{5,1},{6,2},{7,3},{8,12},{9,13},{10,... | collective-permute-start | bytes 774152 | tf_op jit(solution)/shard_map/ppermute | solution.py:501
  107.8 2.3 collective-permute-start.21
  112.2 6.3 %collective-permute-done.17.other = bf16[32,3584]{1,0:T(8,128)(2,1)S(1)} collective-permute-done((bf16[32,3584]{1,0:T(8,128)(2,1)S(1)}, bf16[32,3584]{1,0:T(8,128)(2,1)S(1)}, u32[]{:S(2)}, u32[]{:S(2)}) %collective-permute-start.17) | collective-permute-done | bytes 229408 | tf_op jit(solution)/shard_map/ppermute | solution.py:19
  119.9 7.3 %collective-permute-done.21.refs_6_ = bf16[144,896]{1,0:T(8,128)(2,1)S(1)} collective-permute-done((bf16[144,896]{1,0:T(8,128)(2,1)S(1)}, bf16[144,896]{1,0:T(8,128)(2,1)S(1)}, u32[]{:S(2)}, u32[]{:S(2)}) %collective-permute-start.21) | collective-permute-done | bytes 258080 | tf_op jit(solution)/shard_map/ppermute | solution.py:501
  127.1 2.2 mix.3
  130.7 5.2 %collective-permute-start.24 = (bf16[144,896]{1,0:T(8,128)(2,1)S(1)}, bf16[144,896]{1,0:T(8,128)(2,1)S(1)}, u32[]{:S(2)}, u32[]{:S(2)}) collective-permute-start(bf16[144,896]{1,0:T(8,128)(2,1)S(1)} %get-tuple-element.142), channel_id=1, source_target_pairs={{0,4},{1,5},{2,6},{3,7},{4,0},{5,1},{6,2},{7,3},{8,12},{9,13},{10,... | collective-permute-start | bytes 774152 | tf_op jit(solution)/shard_map/ppermute | solution.py:501
  139.6 6.6 %collective-permute-done.23.other = bf16[32,3584]{1,0:T(8,128)(2,1)S(1)} collective-permute-done((bf16[32,3584]{1,0:T(8,128)(2,1)S(1)}, bf16[32,3584]{1,0:T(8,128)(2,1)S(1)}, u32[]{:S(2)}, u32[]{:S(2)}) %collective-permute-start.23) | collective-permute-done | bytes 229408 | tf_op jit(solution)/shard_map/ppermute | solution.py:19
  148.3 7.1 %collective-permute-done.19.refs_2_ = bf16[144,896]{1,0:T(8,128)(2,1)S(1)} collective-permute-done((bf16[144,896]{1,0:T(8,128)(2,1)S(1)}, bf16[144,896]{1,0:T(8,128)(2,1)S(1)}, u32[]{:S(2)}, u32[]{:S(2)}) %collective-permute-start.19) | collective-permute-done | bytes 258080 | tf_op jit(solution)/shard_map/ppermute | solution.py:501
  155.4 2.8 %first.6 = (bf16[144,1152]{1,0:T(8,128)(2,1)S(1)}, bf16[144,3584]{1,0:T(8,128)(2,1)S(1)}, f32[144,128]{1,0:T(8,128)S(1)}) custom-call(s32[4]{0:T(128)S(1)} %pad_add_fusion.me.refs_0_, bf16[144,896]{1,0:T(8,128)(2,1)S(1)} %get-tuple-element.133.refs_7_.refs_1_, bf16[144,896]{1,0:T(8,128)(2,1)S(1)} %collective-permute-done.19.refs_2_, ...), custom_call_target="tpu_custom_call" | custom-call | flops 1056964608 | tf_op jit(solution)/shard_map/first/pallas_call | solution.py:194
  159.7 3.4 %collective-permute-start.28 = (bf16[144,896]{1,0:T(8,128)(2,1)S(1)}, bf16[144,896]{1,0:T(8,128)(2,1)S(1)}, u32[]{:S(2)}, u32[]{:S(2)}) collective-permute-start(bf16[144,896]{1,0:T(8,128)(2,1)S(1)} %get-tuple-element.153), channel_id=1, source_target_pairs={{0,4},{1,5},{2,6},{3,7},{4,0},{5,1},{6,2},{7,3},{8,12},{9,13},{10,... | collective-permute-start | bytes 774152 | tf_op jit(solution)/shard_map/ppermute | solution.py:501
  164.1 2.4 collective-permute-start.31
  166.5 1.8 second.6.own
  170.3 4.0 %collective-permute-done.27.hidden_other = bf16[144,512]{1,0:T(8,128)(2,1)S(1)} collective-permute-done((bf16[144,512]{1,0:T(8,128)(2,1)S(1)}, bf16[144,512]{1,0:T(8,128)(2,1)S(1)}, u32[]{:S(2)}, u32[]{:S(2)}) %collective-permute-start.27) | collective-permute-done | bytes 147488 | tf_op jit(solution)/shard_map/ppermute | solution.py:19
  174.4 2.9 %third.6 = (bf16[144,896]{1,0:T(8,128)(2,1)S(1)}, bf16[144,896]{1,0:T(8,128)(2,1)S(1)}, bf16[144,896]{1,0:T(8,128)(2,1)S(1)}, bf16[144,896]{1,0:T(8,128)(2,1)S(1)}) custom-call(s32[4]{0:T(128)S(1)} %pad_add_fusion.me.refs_0_, bf16[144,512]{1,0:T(8,128)(2,1)S(1)} %act.6.hidden, bf16[144,512]{1,0:T(8,128)(2,1)S(1)} %collective-permute-done.27.hidden_other, ...), custom_call_target="tpu_custom_call" | custom-call | flops 1056964608 | tf_op jit(solution)/shard_map/third/pallas_call | solution.py:194
  177.3 6.4 %collective-permute-done.31.refs_4_ = bf16[144,896]{1,0:T(8,128)(2,1)S(1)} collective-permute-done((bf16[144,896]{1,0:T(8,128)(2,1)S(1)}, bf16[144,896]{1,0:T(8,128)(2,1)S(1)}, u32[]{:S(2)}, u32[]{:S(2)}) %collective-permute-start.31) | collective-permute-done | bytes 258080 | tf_op jit(solution)/shard_map/ppermute | solution.py:501
  183.7 2.8 %first.7 = (bf16[144,1152]{1,0:T(8,128)(2,1)S(1)}, bf16[144,3584]{1,0:T(8,128)(2,1)S(1)}, f32[144,128]{1,0:T(8,128)S(1)}) custom-call(s32[4]{0:T(128)S(1)} %pad_add_fusion.me.refs_0_, bf16[144,896]{1,0:T(8,128)(2,1)S(1)} %get-tuple-element.156.refs_1_, bf16[144,896]{1,0:T(8,128)(2,1)S(1)} %collective-permute-done.30.refs_2_, ...), custom_call_target="tpu_custom_call" | custom-call | flops 1056964608 | tf_op jit(solution)/shard_map/first/pallas_call | solution.py:194
  187.2 4.8 %collective-permute-start.34 = (bf16[144,896]{1,0:T(8,128)(2,1)S(1)}, bf16[144,896]{1,0:T(8,128)(2,1)S(1)}, u32[]{:S(2)}, u32[]{:S(2)}) collective-permute-start(bf16[144,896]{1,0:T(8,128)(2,1)S(1)} %get-tuple-element.167), channel_id=1, source_target_pairs={{0,4},{1,5},{2,6},{3,7},{4,0},{5,1},{6,2},{7,3},{8,12},{9,13},{10,... | collective-permute-start | bytes 774152 | tf_op jit(solution)/shard_map/ppermute | solution.py:501
  192.0 1.8 second.7.own
  196.8 3.8 %collective-permute-start.29 = (bf16[144,896]{1,0:T(8,128)(2,1)S(1)}, bf16[144,896]{1,0:T(8,128)(2,1)S(1)}, u32[]{:S(2)}, u32[]{:S(2)}) collective-permute-start(bf16[144,896]{1,0:T(8,128)(2,1)S(1)} %get-tuple-element.155), channel_id=1, source_target_pairs={{0,2},{1,3},{2,0},{3,1},{4,6},{5,7},{6,4},{7,5},{8,10},{9,11},{10,... | collective-permute-start | bytes 774152 | tf_op jit(solution)/shard_map/ppermute | solution.py:501
  200.6 3.0 %collective-permute-start.35 = (bf16[144,896]{1,0:T(8,128)(2,1)S(1)}, bf16[144,896]{1,0:T(8,128)(2,1)S(1)}, u32[]{:S(2)}, u32[]{:S(2)}) collective-permute-start(bf16[144,896]{1,0:T(8,128)(2,1)S(1)} %get-tuple-element.169), channel_id=1, source_target_pairs={{0,6},{1,7},{2,4},{3,5},{4,2},{5,3},{6,0},{7,1},{8,14},{9,15},{10,... | collective-permute-start | bytes 774152 | tf_op jit(solution)/shard_map/ppermute | solution.py:501
  203.7 2.9 %third.7 = (bf16[144,896]{1,0:T(8,128)(2,1)S(1)}, bf16[144,896]{1,0:T(8,128)(2,1)S(1)}, bf16[144,896]{1,0:T(8,128)(2,1)S(1)}, bf16[144,896]{1,0:T(8,128)(2,1)S(1)}) custom-call(s32[4]{0:T(128)S(1)} %pad_add_fusion.me.refs_0_, bf16[144,512]{1,0:T(8,128)(2,1)S(1)} %act.7.hidden, bf16[144,512]{1,0:T(8,128)(2,1)S(1)} %collective-permute-done.33.hidden_other, ...), custom_call_target="tpu_custom_call" | custom-call | flops 1056964608 | tf_op jit(solution)/shard_map/third/pallas_call | solution.py:194
  208.2 1.9 collective-permute-start.38
  211.2 2.8 %collective-permute-done.29.refs_4_ = bf16[144,896]{1,0:T(8,128)(2,1)S(1)} collective-permute-done((bf16[144,896]{1,0:T(8,128)(2,1)S(1)}, bf16[144,896]{1,0:T(8,128)(2,1)S(1)}, u32[]{:S(2)}, u32[]{:S(2)}) %collective-permute-start.29) | collective-permute-done | bytes 258080 | tf_op jit(solution)/shard_map/ppermute | solution.py:501
  214.0 2.3 collective-permute-done.35.refs_6_
  216.4 2.3 last.2
  220.2 7.1 %collective-permute-done.37.refs_4_ = bf16[144,896]{1,0:T(8,128)(2,1)S(1)} collective-permute-done((bf16[144,896]{1,0:T(8,128)(2,1)S(1)}, bf16[144,896]{1,0:T(8,128)(2,1)S(1)}, u32[]{:S(2)}, u32[]{:S(2)}) %collective-permute-start.37) | collective-permute-done | bytes 258080 | tf_op jit(solution)/shard_map/ppermute | solution.py:501
  227.2 4.3 %collective-permute-done.38.refs_5_ = bf16[144,896]{1,0:T(8,128)(2,1)S(1)} collective-permute-done((bf16[144,896]{1,0:T(8,128)(2,1)S(1)}, bf16[144,896]{1,0:T(8,128)(2,1)S(1)}, u32[]{:S(2)}, u32[]{:S(2)}) %collective-permute-start.38) | collective-permute-done | bytes 258080 | tf_op jit(solution)/shard_map/ppermute | solution.py:501
  231.5 2.2 last.3
  236.7 3.2 %collective-permute-done.40.other = bf16[32,3584]{1,0:T(8,128)(2,1)S(1)} collective-permute-done((bf16[32,3584]{1,0:T(8,128)(2,1)S(1)}, bf16[32,3584]{1,0:T(8,128)(2,1)S(1)}, u32[]{:S(2)}, u32[]{:S(2)}) %collective-permute-start.40) | collective-permute-done | bytes 229408 | tf_op jit(solution)/shard_map/ppermute | solution.py:19
  (94 shorter events, 53.9 us)
Async XLA Ops:
  2.3 9.6 %collective-permute-start = (bf16[32,3584]{1,0:T(8,128)(2,1)S(1)}, bf16[32,3584]{1,0:T(8,128)(2,1)S(1)}, u32[]{:S(2)}, u32[]{:S(2)}) collective-permute-start(bf16[32,3584]{1,0:T(8,128)(2,1)S(1)} %cut.4), channel_id=1, source_target_pairs={{0,1},{1,0},{2,3},{3,2},{4,5},{5,4},{6,7},{7,6},{8,9},{9,8},{10,11... | collective-permute-start | bytes 688136 | tf_op jit(solution)/shard_map/ppermute | solution.py:19
  6.8 4.3 %collective-permute-start.1 = (f32[16,32]{1,0:T(8,128)S(1)}, f32[16,32]{1,0:T(8,128)S(1)}, u32[]{:S(2)}, u32[]{:S(2)}) collective-permute-start(f32[16,32]{1,0:T(8,128)S(1)} %concatenate.3.own), channel_id=1, source_target_pairs={{0,1},{1,0},{2,3},{3,2},{4,5},{5,4},{6,7},{7,6},{8,9},{9,8},{10,11... | collective-permute-start | bytes 6152 | tf_op jit(solution)/shard_map/ppermute | solution.py:19
  14.1 20.6 %collective-permute-start.4 = (bf16[144,896]{1,0:T(8,128)(2,1)S(1)}, bf16[144,896]{1,0:T(8,128)(2,1)S(1)}, u32[]{:S(2)}, u32[]{:S(2)}) collective-permute-start(bf16[144,896]{1,0:T(8,128)(2,1)S(1)} %get-tuple-element.99), channel_id=1, source_target_pairs={{0,4},{1,5},{2,6},{3,7},{4,0},{5,1},{6,2},{7,3},{8,12},{9,13},{10,... | collective-permute-start | bytes 774152 | tf_op jit(solution)/shard_map/ppermute | solution.py:501
  17.0 17.7 %collective-permute-start.2 = (bf16[144,896]{1,0:T(8,128)(2,1)S(1)}, bf16[144,896]{1,0:T(8,128)(2,1)S(1)}, u32[]{:S(2)}, u32[]{:S(2)}) collective-permute-start(bf16[144,896]{1,0:T(8,128)(2,1)S(1)} %get-tuple-element.94), channel_id=1, source_target_pairs={{0,2},{1,3},{2,0},{3,1},{4,6},{5,7},{6,4},{7,5},{8,10},{9,11},{10,... | collective-permute-start | bytes 774152 | tf_op jit(solution)/shard_map/ppermute | solution.py:501
  18.6 16.1 %collective-permute-start.5 = (bf16[144,896]{1,0:T(8,128)(2,1)S(1)}, bf16[144,896]{1,0:T(8,128)(2,1)S(1)}, u32[]{:S(2)}, u32[]{:S(2)}) collective-permute-start(bf16[144,896]{1,0:T(8,128)(2,1)S(1)} %get-tuple-element.101), channel_id=1, source_target_pairs={{0,6},{1,7},{2,4},{3,5},{4,2},{5,3},{6,0},{7,1},{8,14},{9,15},{10,... | collective-permute-start | bytes 774152 | tf_op jit(solution)/shard_map/ppermute | solution.py:501
  20.2 6.1 %collective-permute-start.3 = (bf16[32,3584]{1,0:T(8,128)(2,1)S(1)}, bf16[32,3584]{1,0:T(8,128)(2,1)S(1)}, u32[]{:S(2)}, u32[]{:S(2)}) collective-permute-start(bf16[32,3584]{1,0:T(8,128)(2,1)S(1)} %cut.5), channel_id=1, source_target_pairs={{0,1},{1,0},{2,3},{3,2},{4,5},{5,4},{6,7},{7,6},{8,9},{9,8},{10,11... | collective-permute-start | bytes 688136 | tf_op jit(solution)/shard_map/ppermute | solution.py:19
  34.7 5.2 %copy-start = (bf16[1,1,3584,2048]{3,2,1,0:T(8,128)(2,1)S(1)}, bf16[1,1,3584,2048]{3,2,1,0:T(8,128)(2,1)}, u32[]{:S(2)}) copy-start(bf16[1,1,3584,2048]{3,2,1,0:T(8,128)(2,1)} %param.20) | copy-start | bytes 44040196
  40.6 12.7 %copy-start.1 = (bf16[1,1,3584,2048]{3,2,1,0:T(8,128)(2,1)S(1)}, bf16[1,1,3584,2048]{3,2,1,0:T(8,128)(2,1)}, u32[]{:S(2)}) copy-start(bf16[1,1,3584,2048]{3,2,1,0:T(8,128)(2,1)} %param.20) | copy-start | bytes 44040196
  40.7 20.6 %slice-start = ((s8[7340032]{0:T(1024)(128)(4,1)}), s8[4194304]{0:T(1024)(128)(4,1)S(1)}, s32[]{:S(2)}) async-start(s8[7340032]{0:T(1024)(128)(4,1)} %bitcast.52), calls=%async_computation | async-start | bytes 8388608
  43.5 26.8 %copy-start.9 = (f32[1,7168]{1,0:T(1,128)S(1)}, f32[1,7168]{1,0:T(1,128)}, u32[]{:S(2)}) copy-start(f32[1,7168]{1,0:T(1,128)} %refs_5_.7) | copy-start | bytes 86020
  43.5 11.7 %collective-permute-start.6 = (bf16[144,1152]{1,0:T(8,128)(2,1)S(1)}, bf16[144,1152]{1,0:T(8,128)(2,1)S(1)}, u32[]{:S(2)}, u32[]{:S(2)}) collective-permute-start(bf16[144,1152]{1,0:T(8,128)(2,1)S(1)} %get-tuple-element.104), channel_id=1, source_target_pairs={{0,1},{1,0},{2,3},{3,2},{4,5},{5,4},{6,7},{7,6},{8,9},{9,8},{10,11... | collective-permute-start | bytes 995336 | tf_op jit(solution)/shard_map/ppermute | solution.py:19
  45.0 20.1 %collective-permute-start.8 = (bf16[144,896]{1,0:T(8,128)(2,1)S(1)}, bf16[144,896]{1,0:T(8,128)(2,1)S(1)}, u32[]{:S(2)}, u32[]{:S(2)}) collective-permute-start(bf16[144,896]{1,0:T(8,128)(2,1)S(1)} %get-tuple-element.110), channel_id=1, source_target_pairs={{0,4},{1,5},{2,6},{3,7},{4,0},{5,1},{6,2},{7,3},{8,12},{9,13},{10,... | collective-permute-start | bytes 774152 | tf_op jit(solution)/shard_map/ppermute | solution.py:501
  51.9 18.4 %collective-permute-start.10 = (bf16[144,896]{1,0:T(8,128)(2,1)S(1)}, bf16[144,896]{1,0:T(8,128)(2,1)S(1)}, u32[]{:S(2)}, u32[]{:S(2)}) collective-permute-start(bf16[144,896]{1,0:T(8,128)(2,1)S(1)} %get-tuple-element.114), channel_id=1, source_target_pairs={{0,2},{1,3},{2,0},{3,1},{4,6},{5,7},{6,4},{7,5},{8,10},{9,11},{10,... | collective-permute-start | bytes 774152 | tf_op jit(solution)/shard_map/ppermute | solution.py:501
  51.9 18.4 %collective-permute-start.11 = (bf16[144,896]{1,0:T(8,128)(2,1)S(1)}, bf16[144,896]{1,0:T(8,128)(2,1)S(1)}, u32[]{:S(2)}, u32[]{:S(2)}) collective-permute-start(bf16[144,896]{1,0:T(8,128)(2,1)S(1)} %get-tuple-element.116), channel_id=1, source_target_pairs={{0,6},{1,7},{2,4},{3,5},{4,2},{5,3},{6,0},{7,1},{8,14},{9,15},{10,... | collective-permute-start | bytes 774152 | tf_op jit(solution)/shard_map/ppermute | solution.py:501
  53.4 7.9 %slice-start.1 = ((s8[7340032]{0:T(1024)(128)(4,1)}), s8[3145728]{0:T(1024)(128)(4,1)S(1)}, s32[]{:S(2)}) async-start(s8[7340032]{0:T(1024)(128)(4,1)} %bitcast.52), calls=%async_computation.1 | async-start | bytes 6291456
  56.1 5.2 %collective-permute-start.7 = (bf16[144,512]{1,0:T(8,128)(2,1)S(1)}, bf16[144,512]{1,0:T(8,128)(2,1)S(1)}, u32[]{:S(2)}, u32[]{:S(2)}) collective-permute-start(bf16[144,512]{1,0:T(8,128)(2,1)S(1)} %act.4.hidden), channel_id=1, source_target_pairs={{0,1},{1,0},{2,3},{3,2},{4,5},{5,4},{6,7},{7,6},{8,9},{9,8},{10,11... | collective-permute-start | bytes 442376 | tf_op jit(solution)/shard_map/ppermute | solution.py:19
  73.1 37.1 %copy-start.6 = (bf16[1,32,7168]{2,1,0:T(8,128)(2,1)S(1)}, bf16[1,32,7168]{2,1,0:T(8,128)(2,1)}, u32[]{:S(2)}) copy-start(bf16[1,32,7168]{2,1,0:T(8,128)(2,1)} %param.13) | copy-start | bytes 1376260
  73.1 9.7 %collective-permute-start.12 = (bf16[144,1152]{1,0:T(8,128)(2,1)S(1)}, bf16[144,1152]{1,0:T(8,128)(2,1)S(1)}, u32[]{:S(2)}, u32[]{:S(2)}) collective-permute-start(bf16[144,1152]{1,0:T(8,128)(2,1)S(1)} %get-tuple-element.118), channel_id=1, source_target_pairs={{0,1},{1,0},{2,3},{3,2},{4,5},{5,4},{6,7},{7,6},{8,9},{9,8},{10,11... | collective-permute-start | bytes 995336 | tf_op jit(solution)/shard_map/ppermute | solution.py:19
  73.7 26.1 %collective-permute-start.9 = (bf16[144,896]{1,0:T(8,128)(2,1)S(1)}, bf16[144,896]{1,0:T(8,128)(2,1)S(1)}, u32[]{:S(2)}, u32[]{:S(2)}) collective-permute-start(bf16[144,896]{1,0:T(8,128)(2,1)S(1)} %get-tuple-element.112), channel_id=1, source_target_pairs={{0,2},{1,3},{2,0},{3,1},{4,6},{5,7},{6,4},{7,5},{8,10},{9,11},{10,... | collective-permute-start | bytes 774152 | tf_op jit(solution)/shard_map/ppermute | solution.py:501
  78.6 21.1 %collective-permute-start.14 = (bf16[144,896]{1,0:T(8,128)(2,1)S(1)}, bf16[144,896]{1,0:T(8,128)(2,1)S(1)}, u32[]{:S(2)}, u32[]{:S(2)}) collective-permute-start(bf16[144,896]{1,0:T(8,128)(2,1)S(1)} %get-tuple-element.124), channel_id=1, source_target_pairs={{0,4},{1,5},{2,6},{3,7},{4,0},{5,1},{6,2},{7,3},{8,12},{9,13},{10,... | collective-permute-start | bytes 774152 | tf_op jit(solution)/shard_map/ppermute | solution.py:501
  78.6 21.1 %collective-permute-start.15 = (bf16[144,896]{1,0:T(8,128)(2,1)S(1)}, bf16[144,896]{1,0:T(8,128)(2,1)S(1)}, u32[]{:S(2)}, u32[]{:S(2)}) collective-permute-start(bf16[144,896]{1,0:T(8,128)(2,1)S(1)} %get-tuple-element.126), channel_id=1, source_target_pairs={{0,6},{1,7},{2,4},{3,5},{4,2},{5,3},{6,0},{7,1},{8,14},{9,15},{10,... | collective-permute-start | bytes 774152 | tf_op jit(solution)/shard_map/ppermute | solution.py:501
  81.0 56.5 %copy-start.7 = (bf16[1,32,7168]{2,1,0:T(8,128)(2,1)S(1)}, bf16[1,32,7168]{2,1,0:T(8,128)(2,1)}, u32[]{:S(2)}) copy-start(bf16[1,32,7168]{2,1,0:T(8,128)(2,1)} %param.14) | copy-start | bytes 1376260
  83.7 5.2 %collective-permute-start.13 = (bf16[144,512]{1,0:T(8,128)(2,1)S(1)}, bf16[144,512]{1,0:T(8,128)(2,1)S(1)}, u32[]{:S(2)}, u32[]{:S(2)}) collective-permute-start(bf16[144,512]{1,0:T(8,128)(2,1)S(1)} %act.5.hidden), channel_id=1, source_target_pairs={{0,1},{1,0},{2,3},{3,2},{4,5},{5,4},{6,7},{7,6},{8,9},{9,8},{10,11... | collective-permute-start | bytes 442376 | tf_op jit(solution)/shard_map/ppermute | solution.py:19
  102.0 16.6 %collective-permute-start.16 = (bf16[64,3584]{1,0:T(8,128)(2,1)S(1)}, bf16[64,3584]{1,0:T(8,128)(2,1)S(1)}, u32[]{:S(2)}, u32[]{:S(2)}) collective-permute-start(bf16[64,3584]{1,0:T(8,128)(2,1)S(1)} %mix.2), channel_id=1, source_target_pairs={{0,8},{8,16},{16,24},{1,9},{9,17},{17,25},{2,10},{10,18},{18,26},{... | collective-permute-start | bytes 1376264 | tf_op jit(solution)/shard_map/ppermute | solution.py:25
  103.3 16.5 %collective-permute-start.18 = (bf16[144,896]{1,0:T(8,128)(2,1)S(1)}, bf16[144,896]{1,0:T(8,128)(2,1)S(1)}, u32[]{:S(2)}, u32[]{:S(2)}) collective-permute-start(bf16[144,896]{1,0:T(8,128)(2,1)S(1)} %get-tuple-element.132), channel_id=1, source_target_pairs={{0,4},{1,5},{2,6},{3,7},{4,0},{5,1},{6,2},{7,3},{8,12},{9,13},{10,... | collective-permute-start | bytes 774152 | tf_op jit(solution)/shard_map/ppermute | solution.py:501
  106.7 13.1 %collective-permute-start.20 = (bf16[144,896]{1,0:T(8,128)(2,1)S(1)}, bf16[144,896]{1,0:T(8,128)(2,1)S(1)}, u32[]{:S(2)}, u32[]{:S(2)}) collective-permute-start(bf16[144,896]{1,0:T(8,128)(2,1)S(1)} %get-tuple-element.136), channel_id=1, source_target_pairs={{0,2},{1,3},{2,0},{3,1},{4,6},{5,7},{6,4},{7,5},{8,10},{9,11},{10,... | collective-permute-start | bytes 774152 | tf_op jit(solution)/shard_map/ppermute | solution.py:501
  107.8 19.3 %collective-permute-start.21 = (bf16[144,896]{1,0:T(8,128)(2,1)S(1)}, bf16[144,896]{1,0:T(8,128)(2,1)S(1)}, u32[]{:S(2)}, u32[]{:S(2)}) collective-permute-start(bf16[144,896]{1,0:T(8,128)(2,1)S(1)} %get-tuple-element.137), channel_id=1, source_target_pairs={{0,6},{1,7},{2,4},{3,5},{4,2},{5,3},{6,0},{7,1},{8,14},{9,15},{10,... | collective-permute-start | bytes 774152 | tf_op jit(solution)/shard_map/ppermute | solution.py:501
  110.7 7.9 %collective-permute-start.17 = (bf16[32,3584]{1,0:T(8,128)(2,1)S(1)}, bf16[32,3584]{1,0:T(8,128)(2,1)S(1)}, u32[]{:S(2)}, u32[]{:S(2)}) collective-permute-start(bf16[32,3584]{1,0:T(8,128)(2,1)S(1)} %cut.6), channel_id=1, source_target_pairs={{0,1},{1,0},{2,3},{3,2},{4,5},{5,4},{6,7},{7,6},{8,9},{9,8},{10,11... | collective-permute-start | bytes 688136 | tf_op jit(solution)/shard_map/ppermute | solution.py:19
  129.4 16.8 %collective-permute-start.22 = (bf16[64,3584]{1,0:T(8,128)(2,1)S(1)}, bf16[64,3584]{1,0:T(8,128)(2,1)S(1)}, u32[]{:S(2)}, u32[]{:S(2)}) collective-permute-start(bf16[64,3584]{1,0:T(8,128)(2,1)S(1)} %mix.3), channel_id=1, source_target_pairs={{8,0},{16,8},{24,16},{9,1},{17,9},{25,17},{10,2},{18,10},{26,18},{... | collective-permute-start | bytes 1376264 | tf_op jit(solution)/shard_map/ppermute | solution.py:25
  130.7 17.6 %collective-permute-start.24 = (bf16[144,896]{1,0:T(8,128)(2,1)S(1)}, bf16[144,896]{1,0:T(8,128)(2,1)S(1)}, u32[]{:S(2)}, u32[]{:S(2)}) collective-permute-start(bf16[144,896]{1,0:T(8,128)(2,1)S(1)} %get-tuple-element.142), channel_id=1, source_target_pairs={{0,4},{1,5},{2,6},{3,7},{4,0},{5,1},{6,2},{7,3},{8,12},{9,13},{10,... | collective-permute-start | bytes 774152 | tf_op jit(solution)/shard_map/ppermute | solution.py:501
  135.9 19.5 %collective-permute-start.19 = (bf16[144,896]{1,0:T(8,128)(2,1)S(1)}, bf16[144,896]{1,0:T(8,128)(2,1)S(1)}, u32[]{:S(2)}, u32[]{:S(2)}) collective-permute-start(bf16[144,896]{1,0:T(8,128)(2,1)S(1)} %get-tuple-element.134), channel_id=1, source_target_pairs={{0,2},{1,3},{2,0},{3,1},{4,6},{5,7},{6,4},{7,5},{8,10},{9,11},{10,... | collective-permute-start | bytes 774152 | tf_op jit(solution)/shard_map/ppermute | solution.py:501
  135.9 19.5 %collective-permute-start.25 = (bf16[144,896]{1,0:T(8,128)(2,1)S(1)}, bf16[144,896]{1,0:T(8,128)(2,1)S(1)}, u32[]{:S(2)}, u32[]{:S(2)}) collective-permute-start(bf16[144,896]{1,0:T(8,128)(2,1)S(1)} %get-tuple-element.144), channel_id=1, source_target_pairs={{0,6},{1,7},{2,4},{3,5},{4,2},{5,3},{6,0},{7,1},{8,14},{9,15},{10,... | collective-permute-start | bytes 774152 | tf_op jit(solution)/shard_map/ppermute | solution.py:501
  138.0 8.1 %collective-permute-start.23 = (bf16[32,3584]{1,0:T(8,128)(2,1)S(1)}, bf16[32,3584]{1,0:T(8,128)(2,1)S(1)}, u32[]{:S(2)}, u32[]{:S(2)}) collective-permute-start(bf16[32,3584]{1,0:T(8,128)(2,1)S(1)} %cut.7), channel_id=1, source_target_pairs={{0,1},{1,0},{2,3},{3,2},{4,5},{5,4},{6,7},{7,6},{8,9},{9,8},{10,11... | collective-permute-start | bytes 688136 | tf_op jit(solution)/shard_map/ppermute | solution.py:19
  158.2 10.1 %collective-permute-start.26 = (bf16[144,1152]{1,0:T(8,128)(2,1)S(1)}, bf16[144,1152]{1,0:T(8,128)(2,1)S(1)}, u32[]{:S(2)}, u32[]{:S(2)}) collective-permute-start(bf16[144,1152]{1,0:T(8,128)(2,1)S(1)} %get-tuple-element.147), channel_id=1, source_target_pairs={{0,1},{1,0},{2,3},{3,2},{4,5},{5,4},{6,7},{7,6},{8,9},{9,8},{10,11... | collective-permute-start | bytes 995336 | tf_op jit(solution)/shard_map/ppermute | solution.py:19
  159.7 17.6 %collective-permute-start.28 = (bf16[144,896]{1,0:T(8,128)(2,1)S(1)}, bf16[144,896]{1,0:T(8,128)(2,1)S(1)}, u32[]{:S(2)}, u32[]{:S(2)}) collective-permute-start(bf16[144,896]{1,0:T(8,128)(2,1)S(1)} %get-tuple-element.153), channel_id=1, source_target_pairs={{0,4},{1,5},{2,6},{3,7},{4,0},{5,1},{6,2},{7,3},{8,12},{9,13},{10,... | collective-permute-start | bytes 774152 | tf_op jit(solution)/shard_map/ppermute | solution.py:501
  163.1 14.2 %collective-permute-start.30 = (bf16[144,896]{1,0:T(8,128)(2,1)S(1)}, bf16[144,896]{1,0:T(8,128)(2,1)S(1)}, u32[]{:S(2)}, u32[]{:S(2)}) collective-permute-start(bf16[144,896]{1,0:T(8,128)(2,1)S(1)} %get-tuple-element.157), channel_id=1, source_target_pairs={{0,2},{1,3},{2,0},{3,1},{4,6},{5,7},{6,4},{7,5},{8,10},{9,11},{10,... | collective-permute-start | bytes 774152 | tf_op jit(solution)/shard_map/ppermute | solution.py:501
  164.1 19.6 %collective-permute-start.31 = (bf16[144,896]{1,0:T(8,128)(2,1)S(1)}, bf16[144,896]{1,0:T(8,128)(2,1)S(1)}, u32[]{:S(2)}, u32[]{:S(2)}) collective-permute-start(bf16[144,896]{1,0:T(8,128)(2,1)S(1)} %get-tuple-element.159), channel_id=1, source_target_pairs={{0,6},{1,7},{2,4},{3,5},{4,2},{5,3},{6,0},{7,1},{8,14},{9,15},{10,... | collective-permute-start | bytes 774152 | tf_op jit(solution)/shard_map/ppermute | solution.py:501
  169.2 5.2 %collective-permute-start.27 = (bf16[144,512]{1,0:T(8,128)(2,1)S(1)}, bf16[144,512]{1,0:T(8,128)(2,1)S(1)}, u32[]{:S(2)}, u32[]{:S(2)}) collective-permute-start(bf16[144,512]{1,0:T(8,128)(2,1)S(1)} %act.6.hidden), channel_id=1, source_target_pairs={{0,1},{1,0},{2,3},{3,2},{4,5},{5,4},{6,7},{7,6},{8,9},{9,8},{10,11... | collective-permute-start | bytes 442376 | tf_op jit(solution)/shard_map/ppermute | solution.py:19
  186.5 8.8 %collective-permute-start.32 = (bf16[144,1152]{1,0:T(8,128)(2,1)S(1)}, bf16[144,1152]{1,0:T(8,128)(2,1)S(1)}, u32[]{:S(2)}, u32[]{:S(2)}) collective-permute-start(bf16[144,1152]{1,0:T(8,128)(2,1)S(1)} %get-tuple-element.161), channel_id=1, source_target_pairs={{0,1},{1,0},{2,3},{3,2},{4,5},{5,4},{6,7},{7,6},{8,9},{9,8},{10,11... | collective-permute-start | bytes 995336 | tf_op jit(solution)/shard_map/ppermute | solution.py:19
  187.2 19.4 %collective-permute-start.34 = (bf16[144,896]{1,0:T(8,128)(2,1)S(1)}, bf16[144,896]{1,0:T(8,128)(2,1)S(1)}, u32[]{:S(2)}, u32[]{:S(2)}) collective-permute-start(bf16[144,896]{1,0:T(8,128)(2,1)S(1)} %get-tuple-element.167), channel_id=1, source_target_pairs={{0,4},{1,5},{2,6},{3,7},{4,0},{5,1},{6,2},{7,3},{8,12},{9,13},{10,... | collective-permute-start | bytes 774152 | tf_op jit(solution)/shard_map/ppermute | solution.py:501
  196.2 7.5 %collective-permute-start.33 = (bf16[144,512]{1,0:T(8,128)(2,1)S(1)}, bf16[144,512]{1,0:T(8,128)(2,1)S(1)}, u32[]{:S(2)}, u32[]{:S(2)}) collective-permute-start(bf16[144,512]{1,0:T(8,128)(2,1)S(1)} %act.7.hidden), channel_id=1, source_target_pairs={{0,1},{1,0},{2,3},{3,2},{4,5},{5,4},{6,7},{7,6},{8,9},{9,8},{10,11... | collective-permute-start | bytes 442376 | tf_op jit(solution)/shard_map/ppermute | solution.py:19
  196.8 17.2 %collective-permute-start.29 = (bf16[144,896]{1,0:T(8,128)(2,1)S(1)}, bf16[144,896]{1,0:T(8,128)(2,1)S(1)}, u32[]{:S(2)}, u32[]{:S(2)}) collective-permute-start(bf16[144,896]{1,0:T(8,128)(2,1)S(1)} %get-tuple-element.155), channel_id=1, source_target_pairs={{0,2},{1,3},{2,0},{3,1},{4,6},{5,7},{6,4},{7,5},{8,10},{9,11},{10,... | collective-permute-start | bytes 774152 | tf_op jit(solution)/shard_map/ppermute | solution.py:501
  200.6 15.8 %collective-permute-start.35 = (bf16[144,896]{1,0:T(8,128)(2,1)S(1)}, bf16[144,896]{1,0:T(8,128)(2,1)S(1)}, u32[]{:S(2)}, u32[]{:S(2)}) collective-permute-start(bf16[144,896]{1,0:T(8,128)(2,1)S(1)} %get-tuple-element.169), channel_id=1, source_target_pairs={{0,6},{1,7},{2,4},{3,5},{4,2},{5,3},{6,0},{7,1},{8,14},{9,15},{10,... | collective-permute-start | bytes 774152 | tf_op jit(solution)/shard_map/ppermute | solution.py:501
  206.6 20.6 %collective-permute-start.37 = (bf16[144,896]{1,0:T(8,128)(2,1)S(1)}, bf16[144,896]{1,0:T(8,128)(2,1)S(1)}, u32[]{:S(2)}, u32[]{:S(2)}) collective-permute-start(bf16[144,896]{1,0:T(8,128)(2,1)S(1)} %get-tuple-element.173), channel_id=1, source_target_pairs={{0,2},{1,3},{2,0},{3,1},{4,6},{5,7},{6,4},{7,5},{8,10},{9,11},{10,... | collective-permute-start | bytes 774152 | tf_op jit(solution)/shard_map/ppermute | solution.py:501
  208.2 23.3 %collective-permute-start.38 = (bf16[144,896]{1,0:T(8,128)(2,1)S(1)}, bf16[144,896]{1,0:T(8,128)(2,1)S(1)}, u32[]{:S(2)}, u32[]{:S(2)}) collective-permute-start(bf16[144,896]{1,0:T(8,128)(2,1)S(1)} %get-tuple-element.174), channel_id=1, source_target_pairs={{0,4},{1,5},{2,6},{3,7},{4,0},{5,1},{6,2},{7,3},{8,12},{9,13},{10,... | collective-permute-start | bytes 774152 | tf_op jit(solution)/shard_map/ppermute | solution.py:501
  210.1 21.5 %collective-permute-start.39 = (bf16[144,896]{1,0:T(8,128)(2,1)S(1)}, bf16[144,896]{1,0:T(8,128)(2,1)S(1)}, u32[]{:S(2)}, u32[]{:S(2)}) collective-permute-start(bf16[144,896]{1,0:T(8,128)(2,1)S(1)} %get-tuple-element.175), channel_id=1, source_target_pairs={{0,6},{1,7},{2,4},{3,5},{4,2},{5,3},{6,0},{7,1},{8,14},{9,15},{10,... | collective-permute-start | bytes 774152 | tf_op jit(solution)/shard_map/ppermute | solution.py:501
  218.6 16.7 %collective-permute-start.36 = (bf16[32,3584]{1,0:T(8,128)(2,1)S(1)}, bf16[32,3584]{1,0:T(8,128)(2,1)S(1)}, u32[]{:S(2)}, u32[]{:S(2)}) collective-permute-start(bf16[32,3584]{1,0:T(8,128)(2,1)S(1)} %get-tuple-element.171), channel_id=1, source_target_pairs={{0,1},{1,0},{2,3},{3,2},{4,5},{5,4},{6,7},{7,6},{8,9},{9,8},{10,11... | collective-permute-start | bytes 688136 | tf_op jit(solution)/shard_map/ppermute | solution.py:19
  233.8 6.1 %collective-permute-start.40 = (bf16[32,3584]{1,0:T(8,128)(2,1)S(1)}, bf16[32,3584]{1,0:T(8,128)(2,1)S(1)}, u32[]{:S(2)}, u32[]{:S(2)}) collective-permute-start(bf16[32,3584]{1,0:T(8,128)(2,1)S(1)} %get-tuple-element.177), channel_id=1, source_target_pairs={{0,1},{1,0},{2,3},{3,2},{4,5},{5,4},{6,7},{7,6},{8,9},{9,8},{10,11... | collective-permute-start | bytes 688136 | tf_op jit(solution)/shard_map/ppermute | solution.py:19
  (5 other events, 4.8 us)

commit v3 on v2

--- a/solution.py
+++ b/solution.py
@@ -186,7 +186,7 @@
     kernel(*refs[:place], *refs[place + count:])
 
 
-def call(kernel, name, out_shape, me, *arrays, after=(), scratch=(), flops=0, limit=LIMIT):
+def call(kernel, name, out_shape, me, *arrays, after=(), scratch=(), limit=LIMIT):
     several = isinstance(out_shape, list)
     if after:
         kernel = functools.partial(without, kernel, 1 + len(arrays), len(after))
@@ -198,7 +198,7 @@
         out_specs=whole(len(out_shape)) if several else whole(1)[0],
         scratch_shapes=list(scratch),
         compiler_params=pltpu.CompilerParams(vmem_limit_bytes=limit),
-        cost_estimate=pl.CostEstimate(flops=flops, bytes_accessed=0, transcendentals=0),
+        cost_estimate=pl.CostEstimate(flops=0, bytes_accessed=0, transcendentals=0),
         name=name,
     )(me, *arrays, *after)
 
@@ -302,8 +302,9 @@
     packed(me, state, table, turn, (o0, o1, o2, o3), stacked)
 
 
-def relay_kernel(turn, edge, me, moved, batch, other, table, o0, o1, o2, o3, state, stacked):
-    state[...] = moved[...]
+def relay_kernel(turn, edge, me, moved, moved_rest, batch, other, table, o0, o1, o2, o3, state, stacked):
+    state[:moved.shape[0], :] = moved[...]
+    state[moved.shape[0]:, :] = moved_rest[...]
 
     @pl.when(me[2 + edge] == 1)
     def _():
@@ -318,24 +319,50 @@
     return outs, [pltpu.VMEM((PARTS * 2 * rows, width), jnp.bfloat16)]
 
 
-def enter(me, turn, batch, other, table):
+def enter(me, turn, batch, other, table, after):
     outs, scratch = pack_shapes(*other.shape)
-    made = call(functools.partial(enter_kernel, turn), "enter", outs, me, batch, other, table, scratch=scratch)
+    made = call(functools.partial(enter_kernel, turn), "enter", outs, me, batch, other, table, after=after, scratch=scratch)
     return made[:EXPERTS], made[EXPERTS]
 
 
 def relay(me, turn, edge, moved, batch, other, table):
     outs, scratch = pack_shapes(*other.shape)
     kernel = functools.partial(relay_kernel, turn, edge)
-    made = call(kernel, "relay", outs, me, moved, batch, other, table, scratch=scratch)
+    made = call(kernel, "relay", outs, me, *moved, batch, other, table, scratch=scratch)
     return made[:EXPERTS], made[EXPERTS]
 
 
-def first_kernel(me, r0, r1, r2, r3, gain, weight, partial, rows_out, squares, stacked):
+def load_kernel(me, source, other_source, out, other_out, done):
+    copies = [
+        pltpu.make_async_copy(source, out, done.at[0]),
+        pltpu.make_async_copy(other_source, other_out, done.at[1]),
+    ]
+    for copy in copies:
+        copy.start()
+    for copy in copies:
+        copy.wait()
+
+
+def load(me, weight, other_weight, after):
+    arrays = [weight, other_weight]
+    kernel = functools.partial(without, load_kernel, 3, len(after))
+    return pl.pallas_call(
+        kernel,
+        out_shape=[bf16(*array.shape) for array in arrays],
+        in_specs=[pl.BlockSpec(memory_space=pltpu.SMEM)] + [pl.BlockSpec(memory_space=pltpu.HBM)] * 2
+        + [pl.BlockSpec(memory_space=pl.ANY)] * len(after),
+        out_specs=whole(2),
+        scratch_shapes=[pltpu.SemaphoreType.DMA((2,))],
+        compiler_params=pltpu.CompilerParams(vmem_limit_bytes=LIMIT),
+        cost_estimate=pl.CostEstimate(flops=0, bytes_accessed=0, transcendentals=0),
+        name="load",
+    )(me, *arrays, *after)
+
+
+def first_kernel(me, r0, r1, r2, r3, gain, weight, message, rows_out, squares, stacked):
     slots = 2 * CAP
     block = PARTS * slots
     width = r0.shape[1]
-    units = weight.shape[1] // 4
     for apart, ref in enumerate((r0, r1, r2, r3)):
         stacked[apart * block:(apart + 1) * block, :] = ref[...]
     row = iota((block, EXPERTS * block), 0)
@@ -343,85 +370,108 @@
     total = jnp.zeros((block, 1), jnp.float32)
     for part in range(PARTS):
         source = row // slots * block + part * slots + row % slots
-        pick = (column == source).astype(jnp.float32).astype(jnp.bfloat16)
-        values = matmul(pick, stacked[...])
+        values = matmul(ones_where(column == source), stacked[...])
         total = total + jnp.sum(values * values, axis=1, keepdims=True)
         start = pl.multiple_of(me[1] * PARTS * width + part * width, width)
         scaled = values * gain[:, pl.ds(start, width)]
         rows_out[:, part * width:(part + 1) * width] = scaled.astype(jnp.bfloat16)
     squares[...] = jnp.broadcast_to(total, squares.shape)
+    units = weight.shape[1] // 4
     lane = iota(squares.shape, 1)
     high, middle, low = [piece.astype(jnp.float32) for piece in pieces(total)]
     sent = jnp.where(lane == 0, high, jnp.where(lane == 1, middle, jnp.where(lane == 2, low, 0.0)))
-    partial[:, 2 * units:] = sent.astype(jnp.bfloat16)
-    for kind in range(2):
-        start = pl.multiple_of(2 * units * kind + units * (1 - me[1]), units)
-        columns = matmul(rows_out[...], weight[:, pl.ds(start, units)])
-        partial[:, kind * units:(kind + 1) * units] = columns.astype(jnp.bfloat16)
+    turned = lax.dot_general(
+        sent.astype(jnp.bfloat16),
+        ones_where(iota((block, block), 0) == iota((block, block), 1)),
+        (((0,), (0,)), ((), ())),
+        preferred_element_type=jnp.float32,
+    )
+    message[block:, :] = jnp.zeros((message.shape[0] - block, units), jnp.bfloat16)
+    message[block:, :block] = turned[:message.shape[0] - block, :].astype(jnp.bfloat16)
+    start = pl.multiple_of(units * (1 - me[1]), units)
+    message[:block, :] = matmul(rows_out[...], weight[:, pl.ds(start, units)]).astype(jnp.bfloat16)
 
 
 def first(me, received, gain, weight, after):
     block, width = received[0].shape
     half, both = weight.shape
-    outs = [bf16(block, both // 2 + 128), bf16(block, half), f32(block, 128)]
+    outs = [bf16(block + 16, both // 4), bf16(block, half), f32(block, 128)]
     scratch = [pltpu.VMEM((EXPERTS * block, width), jnp.bfloat16)]
-    return call(first_kernel, "first", outs, me, *received, gain, weight, after=after, scratch=scratch, flops=block * half * both)
-
-
-def second_kernel(me, rows_in, weight, own):
+    return call(first_kernel, "first", outs, me, *received, gain, weight, after=after, scratch=scratch)
+
+
+def second_kernel(me, rows_in, weight, message):
+    units = weight.shape[1] // 4
+    start = pl.multiple_of(units * (3 - me[1]), units)
+    message[...] = matmul(rows_in[...], weight[:, pl.ds(start, units)]).astype(jnp.bfloat16)
+
+
+def second(me, rows_in, weight):
+    return call(second_kernel, "second", bf16(rows_in.shape[0], weight.shape[1] // 4), me, rows_in, weight)
+
+
+def own_kernel(me, rows_in, weight, own):
     units = weight.shape[1] // 4
     for kind in range(2):
-        start = pl.multiple_of(2 * units * kind + units * me[1], units)
+        start = pl.multiple_of(units * (2 * kind + me[1]), units)
         own[:, kind * units:(kind + 1) * units] = matmul(rows_in[...], weight[:, pl.ds(start, units)])
 
 
-def second(me, rows_in, weight):
-    block, half = rows_in.shape
-    both = weight.shape[1]
-    return call(second_kernel, "second", f32(block, both // 2), me, rows_in, weight, flops=block * half * both)
-
-
-def act_kernel(model_width, me, own, other, squares, hidden):
-    units = hidden.shape[1]
-    arrived = other[:, 2 * units:].astype(jnp.float32)
-    mean = (squares[:, 0:1] + ((arrived[:, 2:3] + arrived[:, 1:2]) + arrived[:, 0:1])) / model_width
+def own_half(me, rows_in, weight):
+    return call(own_kernel, "own", f32(rows_in.shape[0], weight.shape[1] // 2), me, rows_in, weight)
+
+
+def act_kernel(model_width, me, own, gates, ups, squares, h0, h1):
+    block, both = own.shape
+    units = both // 2
+    pair = lax.dot_general(
+        ones_where(iota((block, block), 0) == iota((block, block), 1)),
+        gates[block:, :block],
+        (((1,), (1,)), ((), ())),
+        preferred_element_type=jnp.float32,
+    )
+    mean = (squares[:, 0:1] + ((pair[:, 2:3] + pair[:, 1:2]) + pair[:, 0:1])) / model_width
     scale = lax.rsqrt(mean + EPSILON)
-    gate = (own[:, :units] + other[:, :units].astype(jnp.float32)) * scale
-    up = (own[:, units:] + other[:, units:2 * units].astype(jnp.float32)) * scale
-    hidden[...] = (gate / (1.0 + jnp.exp(-gate)) * up).astype(jnp.bfloat16)
-
-
-def act(me, own, other, squares, model_width):
+    gate = (own[:, :units] + gates[:block, :].astype(jnp.float32)) * scale
+    up = (own[:, units:] + ups[...].astype(jnp.float32)) * scale
+    hidden = (gate / (1.0 + jnp.exp(-gate)) * up).astype(jnp.bfloat16)
+    h0[...] = hidden[:, :units // 2]
+    h1[...] = hidden[:, units // 2:]
+
+
+def act(me, own, gates, ups, squares, model_width):
     block, both = own.shape
-    return call(functools.partial(act_kernel, model_width), "act", bf16(block, both // 2), me, own, other, squares)
-
-
-def third_kernel(me, hidden, hidden_other, weight, o0, o1, o2, o3, stacked):
+    outs = [bf16(block, both // 4)] * 2
+    return call(functools.partial(act_kernel, model_width), "act", outs, me, own, gates, ups, squares)
+
+
+def third_kernel(me, h0, h1, t0, t1, weight, *refs):
+    o0, o1, o2, o3, hidden, stacked = refs
     slots = 2 * CAP
     block, units = hidden.shape
+    size = units // 4
     width = o0.shape[1]
-    own_rows = pl.ds(pl.multiple_of(units * me[1], units), units)
-    other_rows = pl.ds(pl.multiple_of(units * (1 - me[1]), units), units)
+    for index, refs in enumerate(((h0, h1), (t0, t1))):
+        for place, ref in enumerate(refs):
+            start = ((me[1] ^ index) * 2 + place) * size
+            hidden[:, pl.ds(pl.multiple_of(start, size), size)] = ref[...]
     for part in range(PARTS):
-        columns = slice(part * width, (part + 1) * width)
-        result = matmul(hidden[...], weight[own_rows, columns]) + matmul(hidden_other[...], weight[other_rows, columns])
+        result = matmul(hidden[...], weight[:, part * width:(part + 1) * width])
         stacked[part * block:(part + 1) * block, :] = result.astype(jnp.bfloat16)
     row = iota((block, PARTS * block), 0)
     column = iota((block, PARTS * block), 1)
     for apart, out in enumerate((o0, o1, o2, o3)):
         source = row // slots * block + apart * slots + row % slots
-        pick = (column == source).astype(jnp.float32).astype(jnp.bfloat16)
-        out[...] = matmul(pick, stacked[...]).astype(jnp.bfloat16)
+        out[...] = matmul(ones_where(column == source), stacked[...]).astype(jnp.bfloat16)
 
 
 def third(me, hidden, hidden_other, weight):
-    block, units = hidden.shape
-    half = weight.shape[1]
+    block = hidden[0].shape[0]
+    units, half = weight.shape
     width = half // PARTS
     outs = [bf16(block, width)] * EXPERTS
-    scratch = [pltpu.VMEM((PARTS * block, width), jnp.bfloat16)]
-    flops = 4 * block * half * units
-    return call(third_kernel, "third", outs, me, hidden, hidden_other, weight, scratch=scratch, flops=flops)
+    scratch = [pltpu.VMEM((block, units), jnp.bfloat16), pltpu.VMEM((PARTS * block, width), jnp.bfloat16)]
+    return call(third_kernel, "third", outs, me, *hidden, *hidden_other, weight, scratch=scratch)
 
 
 def mixed_parts(me, table, turn, received, tokens):
@@ -462,9 +512,19 @@
         out[:, span] = summed.astype(jnp.bfloat16)
 
 
+def halves_kernel(turn, me, state, table, *refs):
+    *received, upper, lower, result = refs
+    mix_kernel(turn, me, state, table, *received, result)
+    upper[...] = result[:upper.shape[0], :]
+    lower[...] = result[upper.shape[0]:, :]
+
+
 def mix(me, turn, state, table, received, after):
-    kernel = functools.partial(mix_kernel, turn)
-    return call(kernel, "mix", bf16(*state.shape), me, state, table, *received, after=after)
+    kernel = functools.partial(halves_kernel, turn)
+    tokens, half = state.shape
+    outs = [bf16(tokens // 2, half)] * 2
+    scratch = [pltpu.VMEM(state.shape, jnp.bfloat16)]
+    return call(kernel, "mix", outs, me, state, table, *received, after=after, scratch=scratch)
 
 
 def last_kernel(turn, me, state, table, r0, r1, r2, r3, kept, sent, result):
@@ -491,15 +551,16 @@
     return call(finish_kernel, "finish", bf16(kept.shape[0], 2 * kept.shape[1]), me, kept, other)
 
 
+def along(block, apart):
+    return lax.ppermute(block, "expert", [(i, i ^ 2 * apart) for i in range(lax.axis_size("expert"))])
+
+
 def across(blocks, behind=None):
-    size = lax.axis_size("expert")
-    blocks = list(blocks)
+    own, near, two, three = blocks
     if behind is not None:
-        *blocks, behind[2] = lax.optimization_barrier((*blocks, behind[2]))
-    moved = list(blocks)
-    for apart in (2, 3, 1):
-        moved[apart] = lax.ppermute(blocks[apart], "expert", [(i, i ^ 2 * apart) for i in range(size)])
-    return moved
+        near, two, three, *behind[2:] = lax.optimization_barrier((near, two, three, *behind[2:]))
+    two, three = along(two, 2), along(three, 3)
+    return [own, along(near, 1), two, three]
 
 
 def paired_shards(
@@ -521,8 +582,6 @@
     edges = [section_index == 0, section_index == section_count - 1]
     me = jnp.stack([member // 2, member % 2, *edges]).astype(jnp.int32)
     rows, model_width = east_batch.shape[1:]
-    weight_in = expert_in[0, 0]
-    weight_out = expert_down[0, 0]
     kinds = [
         jnp.swapaxes(array[tick, 0], 0, 1).astype(jnp.float32)
         for experts, gates in ((east_experts, east_gates), (west_experts, west_gates))
@@ -546,23 +605,29 @@
         for stream in range(2):
             turn = stream * TICKS + tick
             if tick == 0:
-                sent, states[stream] = enter(me, turn, batches[stream], batches_other[stream], as_rows)
+                after = []
+                if stream == 1:
+                    weight_in, weight_out = load(me, expert_in[0, 0], expert_down[0, 0], [states[0]])
+                    after = [weight_in, *entering_other]
+                sent, states[stream] = enter(me, turn, batches[stream], batches_other[stream], as_rows, after)
             else:
                 sent, states[stream] = relay(
                     me, turn, stream, moved[stream], entering[stream], entering_other[stream], as_rows
                 )
                 if stream == 0:
-                    moved[1] = shifted(mix(me, turn_before, state_before, as_columns, ahead, [sent[0]]), "pipe", -1)
+                    pieces_now = mix(me, turn_before, state_before, as_columns, ahead, [sent[0]])
+                    moved[1] = [shifted(piece, "pipe", -1) for piece in pieces_now]
             arrived[stream] = across(sent, ahead)
             ahead = arrived[stream]
         behind = states[1]
         for stream in range(2):
             turn = stream * TICKS + tick
-            partial, scaled, squares = first(me, arrived[stream], norm_gain, weight_in, [behind])
-            other = partner(partial, "expert", 0)
-            own = second(me, scaled, weight_in)
-            hidden = act(me, own, other, squares, model_width)
-            hidden_other = partner(hidden, "expert", 0)
+            message, scaled, squares = first(me, arrived[stream], norm_gain, weight_in, [behind])
+            gates = partner(message, "expert", 0)
+            ups = partner(second(me, scaled, weight_in), "expert", 0)
+            own = own_half(me, scaled, weight_in)
+            hidden = act(me, own, gates, ups, squares, model_width)
+            hidden_other = [partner(half, "expert", 0) for half in hidden]
             result = third(me, hidden, hidden_other, weight_out)
             behind = result[0]
             arrived[stream] = across(result, ahead)
@@ -573,7 +638,8 @@
                 kept, sent = last(me, turn, states[stream], as_columns, arrived[stream], [behind])
                 results[stream] = finish(me, kept, partner(sent, "expert", 0))
         else:
-            moved[0] = shifted(mix(me, tick, states[0], as_columns, arrived[0], [behind]), "pipe", 1)
+            pieces_now = mix(me, tick, states[0], as_columns, arrived[0], [behind])
+            moved[0] = [shifted(piece, "pipe", 1) for piece in pieces_now]
             turn_before, state_before = TICKS + tick, states[1]
     return (results[0][None], results[1][None])
 

time: 245 us -> 222 us (0.906)
  waiting for transfers between devices: 96.8 us -> 66.7 us
  Pallas kernels: 53.1 us -> 64.1 us
    ppermute x24, waiting for transfers between devices: 58.4 us -> 25.4 us  [along(): lax.ppermute(block, 'expert', [(i, i ^ 2 * apart) for i in range(lax.axis...]
    ppermute x24, starting transfers between devices: 56.8 us -> 44.4 us  [along(): lax.ppermute(block, 'expert', [(i, i ^ 2 * apart) for i in range(lax.axis...]
    ppermute x15 -> x23, starting transfers between devices: 19.2 us -> 26.1 us  [partner(): lax.ppermute(shard, axis, [(i, i ^ 1 << apart) for i in range(lax.axis_si...]
    pallas_call x0 -> x1, Pallas kernels: none -> 5.73 us  [load(): pl.pallas_call(kernel, out_shape=[bf16(*array.shape) for array in arrays]...]
    ppermute x2 -> x4, starting transfers between devices: 2.61 us -> 8.04 us  [shifted(): return lax.ppermute(block, axis, route)]
    pallas_call x31 -> x35, Pallas kernels: 53.1 us -> 58.3 us  [call(): pl.pallas_call(kernel, out_shape=out_shape, in_specs=[pl.BlockSpec(memory...]
    ppermute x2 -> x4, waiting for transfers between devices: 0.01 us -> 3.39 us  [shifted(): return lax.ppermute(block, axis, route)]
    unnamed x24 -> x20, local copies, waits for them, and re-layouts: 10 us -> 8.19 us
  transfers between devices with their start and end apart: 41 -> 51, of which waited for: 21 -> 22; matrix products, arithmetic and copies ran while one was open for 1% -> 1% of each run, Pallas kernels for 14% -> 28%
where the time goes in v3:
time: 222 us; the launch traced here: 220 us
  starting transfers between devices  78.6 us (35%)
  waiting for transfers between devices  66.7 us (30%)
  Pallas kernels  64.1 us (29%)
  local copies, waits for them, and re-layouts  8.96 us (4%)
    pallas_call x35, Pallas kernels, call(): pl.pallas_call(kernel, out_shape=out_shape, in_specs=[pl.BlockSpec(memory...  58.3 us
    ppermute x24, starting transfers between devices, along(): lax.ppermute(block, 'expert', [(i, i ^ 2 * apart) for i in range(lax.axis...  44.4 us
    ppermute x23, waiting for transfers between devices, partner(): lax.ppermute(shard, axis, [(i, i ^ 1 << apart) for i in range(lax.axis_si...  37.8 us
    ppermute x23, starting transfers between devices, partner(): lax.ppermute(shard, axis, [(i, i ^ 1 << apart) for i in range(lax.axis_si...  26.1 us
    ppermute x24, waiting for transfers between devices, along(): lax.ppermute(block, 'expert', [(i, i ^ 2 * apart) for i in range(lax.axis...  25.4 us
    unnamed x20, local copies, waits for them, and re-layouts  8.19 us
    ppermute x4, starting transfers between devices, shifted(): return lax.ppermute(block, axis, route)  8.04 us
    pallas_call x1, Pallas kernels, load(): pl.pallas_call(kernel, out_shape=[bf16(*array.shape) for array in arrays]...  5.73 us
  transfers between devices with their start and end apart: 51, of which 22 were waited for; matrix products, arithmetic and copies ran while one was open for 1% of the time, Pallas kernels for 28%

profile of v3, /device:TPU:0, one launch (start us, length us, event | category | flops | bytes accessed | tf_op | source)
XLA Modules:
  0.0 220.2 jit_solution(5791638331662745084)
XLA Ops:
  2.3 3.0 %collective-permute-start.5 = (bf16[32,3584]{1,0:T(8,128)(2,1)S(1)}, bf16[32,3584]{1,0:T(8,128)(2,1)S(1)}, u32[]{:S(2)}, u32[]{:S(2)}) collective-permute-start(bf16[32,3584]{1,0:T(8,128)(2,1)S(1)} %cut.7), channel_id=1, source_target_pairs={{0,1},{1,0},{2,3},{3,2},{4,5},{5,4},{6,7},{7,6},{8,9},{9,8},{10,11... | collective-permute-start | bytes 688136 | tf_op jit(solution)/shard_map/ppermute | solution.py:19
  8.5 2.1 collective-permute-start.1
  10.6 5.5 %collective-permute-done.1.other = f32[16,32]{1,0:T(8,128)S(1)} collective-permute-done((f32[16,32]{1,0:T(8,128)S(1)}, f32[16,32]{1,0:T(8,128)S(1)}, u32[]{:S(2)}, u32[]{:S(2)}) %collective-permute-start.1) | collective-permute-done | bytes 2080 | tf_op jit(solution)/shard_map/ppermute | solution.py:19
  19.1 2.9 %collective-permute-start.6 = (bf16[144,896]{1,0:T(8,128)(2,1)S(1)}, bf16[144,896]{1,0:T(8,128)(2,1)S(1)}, u32[]{:S(2)}, u32[]{:S(2)}) collective-permute-start(bf16[144,896]{1,0:T(8,128)(2,1)S(1)} %get-tuple-element.112), channel_id=1, source_target_pairs={{0,4},{1,5},{2,6},{3,7},{4,0},{5,1},{6,2},{7,3},{8,12},{9,13},{10,... | collective-permute-start | bytes 774152 | tf_op jit(solution)/shard_map/ppermute | solution.py:555
  28.9 3.1 %copy-done = bf16[1,1,1024,3584]{3,2,1,0:T(8,128)(2,1)S(1)} copy-done((bf16[1,1,1024,3584]{3,2,1,0:T(8,128)(2,1)S(1)}, bf16[1,1,1024,3584]{3,2,1,0:T(8,128)(2,1)}, u32[]{:S(2)}) %copy-start) | copy-done | bytes 7340056
  32.0 5.7 %load.1 = (bf16[3584,2048]{1,0:T(8,128)(2,1)S(1)}, bf16[1024,3584]{1,0:T(8,128)(2,1)S(1)}) custom-call(s32[4]{0:T(128)S(1)} %pad_add_fusion.me.refs_0_, bf16[3584,2048]{1,0:T(8,128)(2,1)} %bitcast.53, bf16[1024,3584]{1,0:T(8,128)(2,1)S(1)} %bitcast.44, bf16[64,3584]{1,0:T(8,128)(2,1)S(1)} %get-tuple-element.104.refs_3_.refs_1_), custom_call_target="tpu_custom_call" | custom-call | tf_op jit(solution)/shard_map/load/pallas_call | solution.py:349
  39.6 6.9 %collective-permute-start.12 = (bf16[144,896]{1,0:T(8,128)(2,1)S(1)}, bf16[144,896]{1,0:T(8,128)(2,1)S(1)}, u32[]{:S(2)}, u32[]{:S(2)}) collective-permute-start(bf16[144,896]{1,0:T(8,128)(2,1)S(1)} %get-tuple-element.127), channel_id=1, source_target_pairs={{0,4},{1,5},{2,6},{3,7},{4,0},{5,1},{6,2},{7,3},{8,12},{9,13},{10,... | collective-permute-start | bytes 774152 | tf_op jit(solution)/shard_map/ppermute | solution.py:555
  47.0 2.6 %first.4 = (bf16[160,512]{1,0:T(8,128)(2,1)S(1)}, bf16[144,3584]{1,0:T(8,128)(2,1)S(1)}, f32[144,128]{1,0:T(8,128)S(1)}) custom-call(s32[4]{0:T(128)S(1)} %pad_add_fusion.me.refs_0_, bf16[144,896]{1,0:T(8,128)(2,1)S(1)} %get-tuple-element.106.refs_1_, bf16[144,896]{1,0:T(8,128)(2,1)S(1)} %collective-permute-done.2.refs_2_, ...), custom_call_target="tpu_custom_call" | custom-call | tf_op jit(solution)/shard_map/first/pallas_call | solution.py:194
  53.2 1.8 own.4
  55.0 3.4 %collective-permute-done.9.ups = bf16[144,512]{1,0:T(8,128)(2,1)S(1)} collective-permute-done((bf16[144,512]{1,0:T(8,128)(2,1)S(1)}, bf16[144,512]{1,0:T(8,128)(2,1)S(1)}, u32[]{:S(2)}, u32[]{:S(2)}) %collective-permute-start.9) | collective-permute-done | bytes 147488 | tf_op jit(solution)/shard_map/ppermute | solution.py:19
  61.5 2.3 %collective-permute-done.10.t0 = bf16[144,256]{1,0:T(8,128)(2,1)S(1)} collective-permute-done((bf16[144,256]{1,0:T(8,128)(2,1)S(1)}, bf16[144,256]{1,0:T(8,128)(2,1)S(1)}, u32[]{:S(2)}, u32[]{:S(2)}) %collective-permute-start.10) | collective-permute-done | bytes 73760 | tf_op jit(solution)/shard_map/ppermute | solution.py:19
  65.3 2.9 %third.4 = (bf16[144,896]{1,0:T(8,128)(2,1)S(1)}, bf16[144,896]{1,0:T(8,128)(2,1)S(1)}, bf16[144,896]{1,0:T(8,128)(2,1)S(1)}, bf16[144,896]{1,0:T(8,128)(2,1)S(1)}) custom-call(s32[4]{0:T(128)S(1)} %pad_add_fusion.me.refs_0_, bf16[144,256]{1,0:T(8,128)(2,1)S(1)} %get-tuple-element.120.h0, bf16[144,256]{1,0:T(8,128)(2,1)S(1)} %get-tuple-element.121.h1, ...), custom_call_target="tpu_custom_call" | custom-call | tf_op jit(solution)/shard_map/third/pallas_call | solution.py:194
  68.2 2.6 %collective-permute-start.20 = (bf16[144,896]{1,0:T(8,128)(2,1)S(1)}, bf16[144,896]{1,0:T(8,128)(2,1)S(1)}, u32[]{:S(2)}, u32[]{:S(2)}) collective-permute-start(bf16[144,896]{1,0:T(8,128)(2,1)S(1)} %get-tuple-element.142), channel_id=1, source_target_pairs={{0,4},{1,5},{2,6},{3,7},{4,0},{5,1},{6,2},{7,3},{8,12},{9,13},{10,... | collective-permute-start | bytes 774152 | tf_op jit(solution)/shard_map/ppermute | solution.py:555
  70.8 1.7 collective-permute-start.21
  72.5 2.6 %first.5 = (bf16[160,512]{1,0:T(8,128)(2,1)S(1)}, bf16[144,3584]{1,0:T(8,128)(2,1)S(1)}, f32[144,128]{1,0:T(8,128)S(1)}) custom-call(s32[4]{0:T(128)S(1)} %pad_add_fusion.me.refs_0_, bf16[144,896]{1,0:T(8,128)(2,1)S(1)} %get-tuple-element.130.refs_1_, bf16[144,896]{1,0:T(8,128)(2,1)S(1)} %collective-permute-done.15.refs_2_, ...), custom_call_target="tpu_custom_call" | custom-call | tf_op jit(solution)/shard_map/first/pallas_call | solution.py:194
  78.6 1.8 own.5
  80.4 3.3 %collective-permute-done.17.ups = bf16[144,512]{1,0:T(8,128)(2,1)S(1)} collective-permute-done((bf16[144,512]{1,0:T(8,128)(2,1)S(1)}, bf16[144,512]{1,0:T(8,128)(2,1)S(1)}, u32[]{:S(2)}, u32[]{:S(2)}) %collective-permute-start.17) | collective-permute-done | bytes 147488 | tf_op jit(solution)/shard_map/ppermute | solution.py:19
  86.8 2.3 %collective-permute-done.18.t0 = bf16[144,256]{1,0:T(8,128)(2,1)S(1)} collective-permute-done((bf16[144,256]{1,0:T(8,128)(2,1)S(1)}, bf16[144,256]{1,0:T(8,128)(2,1)S(1)}, u32[]{:S(2)}, u32[]{:S(2)}) %collective-permute-start.18) | collective-permute-done | bytes 73760 | tf_op jit(solution)/shard_map/ppermute | solution.py:19
  90.6 3.1 %third.5 = (bf16[144,896]{1,0:T(8,128)(2,1)S(1)}, bf16[144,896]{1,0:T(8,128)(2,1)S(1)}, bf16[144,896]{1,0:T(8,128)(2,1)S(1)}, bf16[144,896]{1,0:T(8,128)(2,1)S(1)}) custom-call(s32[4]{0:T(128)S(1)} %pad_add_fusion.me.refs_0_, bf16[144,256]{1,0:T(8,128)(2,1)S(1)} %get-tuple-element.137.h0, bf16[144,256]{1,0:T(8,128)(2,1)S(1)} %get-tuple-element.138.h1, ...), custom_call_target="tpu_custom_call" | custom-call | tf_op jit(solution)/shard_map/third/pallas_call | solution.py:194
  95.0 2.0 collective-permute-start.25
  97.0 2.3 %mix.2 = (bf16[32,3584]{1,0:T(8,128)(2,1)S(1)}, bf16[32,3584]{1,0:T(8,128)(2,1)S(1)}) custom-call(s32[4]{0:T(128)S(1)} %pad_add_fusion.me.refs_0_, bf16[64,3584]{1,0:T(8,128)(2,1)S(1)} %get-tuple-element.104.refs_3_.refs_1_, f32[256,16]{1,0:T(8,128)S(1)} %get-tuple-element.105.refs_2_, bf16[144,896]{1,0:T(8,128)(2,1)S(1)} %get-tuple-element.123.refs_7_.refs_3_, ...), custom_call_target="tpu_custom_call" | custom-call | tf_op jit(solution)/shard_map/mix/pallas_call | solution.py:194
  100.6 4.2 %collective-permute-start.23 = (bf16[32,3584]{1,0:T(8,128)(2,1)S(1)}, bf16[32,3584]{1,0:T(8,128)(2,1)S(1)}, u32[]{:S(2)}, u32[]{:S(2)}) collective-permute-start(bf16[32,3584]{1,0:T(8,128)(2,1)S(1)} %get-tuple-element.148), channel_id=1, source_target_pairs={{0,8},{8,16},{16,24},{1,9},{9,17},{17,25},{2,10},{10,18},{18,26},{... | collective-permute-start | bytes 688136 | tf_op jit(solution)/shard_map/ppermute | solution.py:25
  107.1 5.1 %collective-permute-done.24.refs_5_ = bf16[144,896]{1,0:T(8,128)(2,1)S(1)} collective-permute-done((bf16[144,896]{1,0:T(8,128)(2,1)S(1)}, bf16[144,896]{1,0:T(8,128)(2,1)S(1)}, u32[]{:S(2)}, u32[]{:S(2)}) %collective-permute-start.24) | collective-permute-done | bytes 258080 | tf_op jit(solution)/shard_map/ppermute | solution.py:555
  112.2 4.7 %collective-permute-start.30 = (bf16[144,896]{1,0:T(8,128)(2,1)S(1)}, bf16[144,896]{1,0:T(8,128)(2,1)S(1)}, u32[]{:S(2)}, u32[]{:S(2)}) collective-permute-start(bf16[144,896]{1,0:T(8,128)(2,1)S(1)} %get-tuple-element.163), channel_id=1, source_target_pairs={{0,4},{1,5},{2,6},{3,7},{4,0},{5,1},{6,2},{7,3},{8,12},{9,13},{10,... | collective-permute-start | bytes 774152 | tf_op jit(solution)/shard_map/ppermute | solution.py:555
  116.9 3.4 %collective-permute-start.31 = (bf16[144,896]{1,0:T(8,128)(2,1)S(1)}, bf16[144,896]{1,0:T(8,128)(2,1)S(1)}, u32[]{:S(2)}, u32[]{:S(2)}) collective-permute-start(bf16[144,896]{1,0:T(8,128)(2,1)S(1)} %get-tuple-element.164), channel_id=1, source_target_pairs={{0,6},{1,7},{2,4},{3,5},{4,2},{5,3},{6,0},{7,1},{8,14},{9,15},{10,... | collective-permute-start | bytes 774152 | tf_op jit(solution)/shard_map/ppermute | solution.py:555
  120.3 2.3 %mix.3 = (bf16[32,3584]{1,0:T(8,128)(2,1)S(1)}, bf16[32,3584]{1,0:T(8,128)(2,1)S(1)}) custom-call(s32[4]{0:T(128)S(1)} %pad_add_fusion.me.refs_0_, bf16[64,3584]{1,0:T(8,128)(2,1)S(1)} %get-tuple-element.116.refs_7_.refs_1_, f32[256,16]{1,0:T(8,128)S(1)} %get-tuple-element.105.refs_2_, bf16[144,896]{1,0:T(8,128)(2,1)S(1)} %get-tuple-element.146.refs_7_.refs_3_, ...), custom_call_target="tpu_custom_call" | custom-call | tf_op jit(solution)/shard_map/mix/pallas_call | solution.py:194
  125.9 1.9 collective-permute-done.29.moved_rest
  129.1 6.0 %collective-permute-done.30.refs_3_ = bf16[144,896]{1,0:T(8,128)(2,1)S(1)} collective-permute-done((bf16[144,896]{1,0:T(8,128)(2,1)S(1)}, bf16[144,896]{1,0:T(8,128)(2,1)S(1)}, u32[]{:S(2)}, u32[]{:S(2)}) %collective-permute-start.30) | collective-permute-done | bytes 258080 | tf_op jit(solution)/shard_map/ppermute | solution.py:555
  135.1 7.1 %collective-permute-start.36 = (bf16[144,896]{1,0:T(8,128)(2,1)S(1)}, bf16[144,896]{1,0:T(8,128)(2,1)S(1)}, u32[]{:S(2)}, u32[]{:S(2)}) collective-permute-start(bf16[144,896]{1,0:T(8,128)(2,1)S(1)} %get-tuple-element.177), channel_id=1, source_target_pairs={{0,4},{1,5},{2,6},{3,7},{4,0},{5,1},{6,2},{7,3},{8,12},{9,13},{10,... | collective-permute-start | bytes 774152 | tf_op jit(solution)/shard_map/ppermute | solution.py:555
  142.6 2.6 %first.6 = (bf16[160,512]{1,0:T(8,128)(2,1)S(1)}, bf16[144,3584]{1,0:T(8,128)(2,1)S(1)}, f32[144,128]{1,0:T(8,128)S(1)}) custom-call(s32[4]{0:T(128)S(1)} %pad_add_fusion.me.refs_0_, bf16[144,896]{1,0:T(8,128)(2,1)S(1)} %get-tuple-element.150.refs_7_.refs_1_, bf16[144,896]{1,0:T(8,128)(2,1)S(1)} %collective-permute-done.26.refs_2_, ...), custom_call_target="tpu_custom_call" | custom-call | tf_op jit(solution)/shard_map/first/pallas_call | solution.py:194
  148.8 1.8 own.6
  150.6 3.2 %collective-permute-done.33.ups = bf16[144,512]{1,0:T(8,128)(2,1)S(1)} collective-permute-done((bf16[144,512]{1,0:T(8,128)(2,1)S(1)}, bf16[144,512]{1,0:T(8,128)(2,1)S(1)}, u32[]{:S(2)}, u32[]{:S(2)}) %collective-permute-start.33) | collective-permute-done | bytes 147488 | tf_op jit(solution)/shard_map/ppermute | solution.py:19
  154.8 1.6 collective-permute-start.34
  156.9 2.3 %collective-permute-done.34.t0 = bf16[144,256]{1,0:T(8,128)(2,1)S(1)} collective-permute-done((bf16[144,256]{1,0:T(8,128)(2,1)S(1)}, bf16[144,256]{1,0:T(8,128)(2,1)S(1)}, u32[]{:S(2)}, u32[]{:S(2)}) %collective-permute-start.34) | collective-permute-done | bytes 73760 | tf_op jit(solution)/shard_map/ppermute | solution.py:19
  160.8 2.9 %third.6 = (bf16[144,896]{1,0:T(8,128)(2,1)S(1)}, bf16[144,896]{1,0:T(8,128)(2,1)S(1)}, bf16[144,896]{1,0:T(8,128)(2,1)S(1)}, bf16[144,896]{1,0:T(8,128)(2,1)S(1)}) custom-call(s32[4]{0:T(128)S(1)} %pad_add_fusion.me.refs_0_, bf16[144,256]{1,0:T(8,128)(2,1)S(1)} %get-tuple-element.171.h0, bf16[144,256]{1,0:T(8,128)(2,1)S(1)} %get-tuple-element.172.h1, ...), custom_call_target="tpu_custom_call" | custom-call | tf_op jit(solution)/shard_map/third/pallas_call | solution.py:194
  163.7 2.8 %collective-permute-start.44 = (bf16[144,896]{1,0:T(8,128)(2,1)S(1)}, bf16[144,896]{1,0:T(8,128)(2,1)S(1)}, u32[]{:S(2)}, u32[]{:S(2)}) collective-permute-start(bf16[144,896]{1,0:T(8,128)(2,1)S(1)} %get-tuple-element.192), channel_id=1, source_target_pairs={{0,4},{1,5},{2,6},{3,7},{4,0},{5,1},{6,2},{7,3},{8,12},{9,13},{10,... | collective-permute-start | bytes 774152 | tf_op jit(solution)/shard_map/ppermute | solution.py:555
  168.0 2.6 %first.7 = (bf16[160,512]{1,0:T(8,128)(2,1)S(1)}, bf16[144,3584]{1,0:T(8,128)(2,1)S(1)}, f32[144,128]{1,0:T(8,128)S(1)}) custom-call(s32[4]{0:T(128)S(1)} %pad_add_fusion.me.refs_0_, bf16[144,896]{1,0:T(8,128)(2,1)S(1)} %get-tuple-element.180.refs_1_, bf16[144,896]{1,0:T(8,128)(2,1)S(1)} %collective-permute-done.39.refs_2_, ...), custom_call_target="tpu_custom_call" | custom-call | tf_op jit(solution)/shard_map/first/pallas_call | solution.py:194
  174.0 1.8 own.7
  175.9 3.3 %collective-permute-done.41.ups = bf16[144,512]{1,0:T(8,128)(2,1)S(1)} collective-permute-done((bf16[144,512]{1,0:T(8,128)(2,1)S(1)}, bf16[144,512]{1,0:T(8,128)(2,1)S(1)}, u32[]{:S(2)}, u32[]{:S(2)}) %collective-permute-start.41) | collective-permute-done | bytes 147488 | tf_op jit(solution)/shard_map/ppermute | solution.py:19
  180.2 1.6 collective-permute-start.42
  182.3 2.3 %collective-permute-done.42.t0 = bf16[144,256]{1,0:T(8,128)(2,1)S(1)} collective-permute-done((bf16[144,256]{1,0:T(8,128)(2,1)S(1)}, bf16[144,256]{1,0:T(8,128)(2,1)S(1)}, u32[]{:S(2)}, u32[]{:S(2)}) %collective-permute-start.42) | collective-permute-done | bytes 73760 | tf_op jit(solution)/shard_map/ppermute | solution.py:19
  186.2 3.1 %third.7 = (bf16[144,896]{1,0:T(8,128)(2,1)S(1)}, bf16[144,896]{1,0:T(8,128)(2,1)S(1)}, bf16[144,896]{1,0:T(8,128)(2,1)S(1)}, bf16[144,896]{1,0:T(8,128)(2,1)S(1)}) custom-call(s32[4]{0:T(128)S(1)} %pad_add_fusion.me.refs_0_, bf16[144,256]{1,0:T(8,128)(2,1)S(1)} %get-tuple-element.187.h0, bf16[144,256]{1,0:T(8,128)(2,1)S(1)} %get-tuple-element.188.h1, ...), custom_call_target="tpu_custom_call" | custom-call | tf_op jit(solution)/shard_map/third/pallas_call | solution.py:194
  190.7 3.1 %collective-permute-start.49 = (bf16[144,896]{1,0:T(8,128)(2,1)S(1)}, bf16[144,896]{1,0:T(8,128)(2,1)S(1)}, u32[]{:S(2)}, u32[]{:S(2)}) collective-permute-start(bf16[144,896]{1,0:T(8,128)(2,1)S(1)} %get-tuple-element.201), channel_id=1, source_target_pairs={{0,6},{1,7},{2,4},{3,5},{4,2},{5,3},{6,0},{7,1},{8,14},{9,15},{10,... | collective-permute-start | bytes 774152 | tf_op jit(solution)/shard_map/ppermute | solution.py:555
  193.8 2.3 %last.2 = (bf16[32,3584]{1,0:T(8,128)(2,1)S(1)}, bf16[32,3584]{1,0:T(8,128)(2,1)S(1)}) custom-call(s32[4]{0:T(128)S(1)} %pad_add_fusion.me.refs_0_, bf16[64,3584]{1,0:T(8,128)(2,1)S(1)} %get-tuple-element.149.refs_1_, f32[256,16]{1,0:T(8,128)S(1)} %get-tuple-element.105.refs_2_, bf16[144,896]{1,0:T(8,128)(2,1)S(1)} %get-tuple-element.173.refs_7_.refs_3_, ...), custom_call_target="tpu_custom_call" | custom-call | tf_op jit(solution)/shard_map/last/pallas_call | solution.py:194
  196.9 2.7 %collective-permute-done.47.refs_4_ = bf16[144,896]{1,0:T(8,128)(2,1)S(1)} collective-permute-done((bf16[144,896]{1,0:T(8,128)(2,1)S(1)}, bf16[144,896]{1,0:T(8,128)(2,1)S(1)}, u32[]{:S(2)}, u32[]{:S(2)}) %collective-permute-start.47) | collective-permute-done | bytes 258080 | tf_op jit(solution)/shard_map/ppermute | solution.py:555
  199.6 10.9 %collective-permute-done.48.refs_5_ = bf16[144,896]{1,0:T(8,128)(2,1)S(1)} collective-permute-done((bf16[144,896]{1,0:T(8,128)(2,1)S(1)}, bf16[144,896]{1,0:T(8,128)(2,1)S(1)}, u32[]{:S(2)}, u32[]{:S(2)}) %collective-permute-start.48) | collective-permute-done | bytes 258080 | tf_op jit(solution)/shard_map/ppermute | solution.py:555
  210.5 2.2 %last.3 = (bf16[32,3584]{1,0:T(8,128)(2,1)S(1)}, bf16[32,3584]{1,0:T(8,128)(2,1)S(1)}) custom-call(s32[4]{0:T(128)S(1)} %pad_add_fusion.me.refs_0_, bf16[64,3584]{1,0:T(8,128)(2,1)S(1)} %get-tuple-element.167.refs_7_.refs_1_, f32[256,16]{1,0:T(8,128)S(1)} %get-tuple-element.105.refs_2_, bf16[144,896]{1,0:T(8,128)(2,1)S(1)} %get-tuple-element.196.refs_7_.refs_3_, ...), custom_call_target="tpu_custom_call" | custom-call | tf_op jit(solution)/shard_map/last/pallas_call | solution.py:194
  215.1 3.8 %collective-permute-done.50.other = bf16[32,3584]{1,0:T(8,128)(2,1)S(1)} collective-permute-done((bf16[32,3584]{1,0:T(8,128)(2,1)S(1)}, bf16[32,3584]{1,0:T(8,128)(2,1)S(1)}, u32[]{:S(2)}, u32[]{:S(2)}) %collective-permute-start.50) | collective-permute-done | bytes 229408 | tf_op jit(solution)/shard_map/ppermute | solution.py:19
  (114 shorter events, 63.6 us)
Async XLA Ops:
  2.3 25.9 %collective-permute-start.5 = (bf16[32,3584]{1,0:T(8,128)(2,1)S(1)}, bf16[32,3584]{1,0:T(8,128)(2,1)S(1)}, u32[]{:S(2)}, u32[]{:S(2)}) collective-permute-start(bf16[32,3584]{1,0:T(8,128)(2,1)S(1)} %cut.7), channel_id=1, source_target_pairs={{0,1},{1,0},{2,3},{3,2},{4,5},{5,4},{6,7},{7,6},{8,9},{9,8},{10,11... | collective-permute-start | bytes 688136 | tf_op jit(solution)/shard_map/ppermute | solution.py:19
  6.9 9.9 %collective-permute-start = (bf16[32,3584]{1,0:T(8,128)(2,1)S(1)}, bf16[32,3584]{1,0:T(8,128)(2,1)S(1)}, u32[]{:S(2)}, u32[]{:S(2)}) collective-permute-start(bf16[32,3584]{1,0:T(8,128)(2,1)S(1)} %cut.4), channel_id=1, source_target_pairs={{0,1},{1,0},{2,3},{3,2},{4,5},{5,4},{6,7},{7,6},{8,9},{9,8},{10,11... | collective-permute-start | bytes 688136 | tf_op jit(solution)/shard_map/ppermute | solution.py:19
  8.5 7.5 %collective-permute-start.1 = (f32[16,32]{1,0:T(8,128)S(1)}, f32[16,32]{1,0:T(8,128)S(1)}, u32[]{:S(2)}, u32[]{:S(2)}) collective-permute-start(f32[16,32]{1,0:T(8,128)S(1)} %concatenate.3.own), channel_id=1, source_target_pairs={{0,1},{1,0},{2,3},{3,2},{4,5},{5,4},{6,7},{7,6},{8,9},{9,8},{10,11... | collective-permute-start | bytes 6152 | tf_op jit(solution)/shard_map/ppermute | solution.py:19
  19.1 20.6 %collective-permute-start.6 = (bf16[144,896]{1,0:T(8,128)(2,1)S(1)}, bf16[144,896]{1,0:T(8,128)(2,1)S(1)}, u32[]{:S(2)}, u32[]{:S(2)}) collective-permute-start(bf16[144,896]{1,0:T(8,128)(2,1)S(1)} %get-tuple-element.112), channel_id=1, source_target_pairs={{0,4},{1,5},{2,6},{3,7},{4,0},{5,1},{6,2},{7,3},{8,12},{9,13},{10,... | collective-permute-start | bytes 774152 | tf_op jit(solution)/shard_map/ppermute | solution.py:555
  22.0 17.7 %collective-permute-start.7 = (bf16[144,896]{1,0:T(8,128)(2,1)S(1)}, bf16[144,896]{1,0:T(8,128)(2,1)S(1)}, u32[]{:S(2)}, u32[]{:S(2)}) collective-permute-start(bf16[144,896]{1,0:T(8,128)(2,1)S(1)} %get-tuple-element.113), channel_id=1, source_target_pairs={{0,6},{1,7},{2,4},{3,5},{4,2},{5,3},{6,0},{7,1},{8,14},{9,15},{10,... | collective-permute-start | bytes 774152 | tf_op jit(solution)/shard_map/ppermute | solution.py:555
  23.3 23.7 %collective-permute-start.2 = (bf16[144,896]{1,0:T(8,128)(2,1)S(1)}, bf16[144,896]{1,0:T(8,128)(2,1)S(1)}, u32[]{:S(2)}, u32[]{:S(2)}) collective-permute-start(bf16[144,896]{1,0:T(8,128)(2,1)S(1)} %get-tuple-element.107), channel_id=1, source_target_pairs={{0,2},{1,3},{2,0},{3,1},{4,6},{5,7},{6,4},{7,5},{8,10},{9,11},{10,... | collective-permute-start | bytes 774152 | tf_op jit(solution)/shard_map/ppermute | solution.py:555
  25.1 12.6 %collective-permute-start.4 = (bf16[32,3584]{1,0:T(8,128)(2,1)S(1)}, bf16[32,3584]{1,0:T(8,128)(2,1)S(1)}, u32[]{:S(2)}, u32[]{:S(2)}) collective-permute-start(bf16[32,3584]{1,0:T(8,128)(2,1)S(1)} %cut.6), channel_id=1, source_target_pairs={{0,1},{1,0},{2,3},{3,2},{4,5},{5,4},{6,7},{7,6},{8,9},{9,8},{10,11... | collective-permute-start | bytes 688136 | tf_op jit(solution)/shard_map/ppermute | solution.py:19
  28.3 9.4 %collective-permute-start.3 = (bf16[32,3584]{1,0:T(8,128)(2,1)S(1)}, bf16[32,3584]{1,0:T(8,128)(2,1)S(1)}, u32[]{:S(2)}, u32[]{:S(2)}) collective-permute-start(bf16[32,3584]{1,0:T(8,128)(2,1)S(1)} %cut.5), channel_id=1, source_target_pairs={{0,1},{1,0},{2,3},{3,2},{4,5},{5,4},{6,7},{7,6},{8,9},{9,8},{10,11... | collective-permute-start | bytes 688136 | tf_op jit(solution)/shard_map/ppermute | solution.py:19
  39.6 28.6 %collective-permute-start.12 = (bf16[144,896]{1,0:T(8,128)(2,1)S(1)}, bf16[144,896]{1,0:T(8,128)(2,1)S(1)}, u32[]{:S(2)}, u32[]{:S(2)}) collective-permute-start(bf16[144,896]{1,0:T(8,128)(2,1)S(1)} %get-tuple-element.127), channel_id=1, source_target_pairs={{0,4},{1,5},{2,6},{3,7},{4,0},{5,1},{6,2},{7,3},{8,12},{9,13},{10,... | collective-permute-start | bytes 774152 | tf_op jit(solution)/shard_map/ppermute | solution.py:555
  46.6 21.6 %collective-permute-start.13 = (bf16[144,896]{1,0:T(8,128)(2,1)S(1)}, bf16[144,896]{1,0:T(8,128)(2,1)S(1)}, u32[]{:S(2)}, u32[]{:S(2)}) collective-permute-start(bf16[144,896]{1,0:T(8,128)(2,1)S(1)} %get-tuple-element.128), channel_id=1, source_target_pairs={{0,6},{1,7},{2,4},{3,5},{4,2},{5,3},{6,0},{7,1},{8,14},{9,15},{10,... | collective-permute-start | bytes 774152 | tf_op jit(solution)/shard_map/ppermute | solution.py:555
  49.6 8.8 %collective-permute-start.8 = (bf16[160,512]{1,0:T(8,128)(2,1)S(1)}, bf16[160,512]{1,0:T(8,128)(2,1)S(1)}, u32[]{:S(2)}, u32[]{:S(2)}) collective-permute-start(bf16[160,512]{1,0:T(8,128)(2,1)S(1)} %get-tuple-element.118), channel_id=1, source_target_pairs={{0,1},{1,0},{2,3},{3,2},{4,5},{5,4},{6,7},{7,6},{8,9},{9,8},{10,11... | collective-permute-start | bytes 491528 | tf_op jit(solution)/shard_map/ppermute | solution.py:19
  51.2 21.4 %collective-permute-start.15 = (bf16[144,896]{1,0:T(8,128)(2,1)S(1)}, bf16[144,896]{1,0:T(8,128)(2,1)S(1)}, u32[]{:S(2)}, u32[]{:S(2)}) collective-permute-start(bf16[144,896]{1,0:T(8,128)(2,1)S(1)} %get-tuple-element.131), channel_id=1, source_target_pairs={{0,2},{1,3},{2,0},{3,1},{4,6},{5,7},{6,4},{7,5},{8,10},{9,11},{10,... | collective-permute-start | bytes 774152 | tf_op jit(solution)/shard_map/ppermute | solution.py:555
  52.6 5.8 %collective-permute-start.9 = (bf16[144,512]{1,0:T(8,128)(2,1)S(1)}, bf16[144,512]{1,0:T(8,128)(2,1)S(1)}, u32[]{:S(2)}, u32[]{:S(2)}) collective-permute-start(bf16[144,512]{1,0:T(8,128)(2,1)S(1)} %second.4), channel_id=1, source_target_pairs={{0,1},{1,0},{2,3},{3,2},{4,5},{5,4},{6,7},{7,6},{8,9},{9,8},{10,11... | collective-permute-start | bytes 442376 | tf_op jit(solution)/shard_map/ppermute | solution.py:19
  59.4 4.4 %collective-permute-start.10 = (bf16[144,256]{1,0:T(8,128)(2,1)S(1)}, bf16[144,256]{1,0:T(8,128)(2,1)S(1)}, u32[]{:S(2)}, u32[]{:S(2)}) collective-permute-start(bf16[144,256]{1,0:T(8,128)(2,1)S(1)} %get-tuple-element.120.h0), channel_id=1, source_target_pairs={{0,1},{1,0},{2,3},{3,2},{4,5},{5,4},{6,7},{7,6},{8,9},{9,8},{10,11... | collective-permute-start | bytes 221192 | tf_op jit(solution)/shard_map/ppermute | solution.py:19
  60.9 4.4 %collective-permute-start.11 = (bf16[144,256]{1,0:T(8,128)(2,1)S(1)}, bf16[144,256]{1,0:T(8,128)(2,1)S(1)}, u32[]{:S(2)}, u32[]{:S(2)}) collective-permute-start(bf16[144,256]{1,0:T(8,128)(2,1)S(1)} %get-tuple-element.121.h1), channel_id=1, source_target_pairs={{0,1},{1,0},{2,3},{3,2},{4,5},{5,4},{6,7},{7,6},{8,9},{9,8},{10,11... | collective-permute-start | bytes 221192 | tf_op jit(solution)/shard_map/ppermute | solution.py:19
  68.2 25.5 %collective-permute-start.20 = (bf16[144,896]{1,0:T(8,128)(2,1)S(1)}, bf16[144,896]{1,0:T(8,128)(2,1)S(1)}, u32[]{:S(2)}, u32[]{:S(2)}) collective-permute-start(bf16[144,896]{1,0:T(8,128)(2,1)S(1)} %get-tuple-element.142), channel_id=1, source_target_pairs={{0,4},{1,5},{2,6},{3,7},{4,0},{5,1},{6,2},{7,3},{8,12},{9,13},{10,... | collective-permute-start | bytes 774152 | tf_op jit(solution)/shard_map/ppermute | solution.py:555
  70.8 23.0 %collective-permute-start.21 = (bf16[144,896]{1,0:T(8,128)(2,1)S(1)}, bf16[144,896]{1,0:T(8,128)(2,1)S(1)}, u32[]{:S(2)}, u32[]{:S(2)}) collective-permute-start(bf16[144,896]{1,0:T(8,128)(2,1)S(1)} %get-tuple-element.143), channel_id=1, source_target_pairs={{0,6},{1,7},{2,4},{3,5},{4,2},{5,3},{6,0},{7,1},{8,14},{9,15},{10,... | collective-permute-start | bytes 774152 | tf_op jit(solution)/shard_map/ppermute | solution.py:555
  75.1 8.6 %collective-permute-start.16 = (bf16[160,512]{1,0:T(8,128)(2,1)S(1)}, bf16[160,512]{1,0:T(8,128)(2,1)S(1)}, u32[]{:S(2)}, u32[]{:S(2)}) collective-permute-start(bf16[160,512]{1,0:T(8,128)(2,1)S(1)} %get-tuple-element.135), channel_id=1, source_target_pairs={{0,1},{1,0},{2,3},{3,2},{4,5},{5,4},{6,7},{7,6},{8,9},{9,8},{10,11... | collective-permute-start | bytes 491528 | tf_op jit(solution)/shard_map/ppermute | solution.py:19
  76.7 20.3 %collective-permute-start.14 = (bf16[144,896]{1,0:T(8,128)(2,1)S(1)}, bf16[144,896]{1,0:T(8,128)(2,1)S(1)}, u32[]{:S(2)}, u32[]{:S(2)}) collective-permute-start(bf16[144,896]{1,0:T(8,128)(2,1)S(1)} %get-tuple-element.129), channel_id=1, source_target_pairs={{0,2},{1,3},{2,0},{3,1},{4,6},{5,7},{6,4},{7,5},{8,10},{9,11},{10,... | collective-permute-start | bytes 774152 | tf_op jit(solution)/shard_map/ppermute | solution.py:555
  78.0 5.7 %collective-permute-start.17 = (bf16[144,512]{1,0:T(8,128)(2,1)S(1)}, bf16[144,512]{1,0:T(8,128)(2,1)S(1)}, u32[]{:S(2)}, u32[]{:S(2)}) collective-permute-start(bf16[144,512]{1,0:T(8,128)(2,1)S(1)} %second.5), channel_id=1, source_target_pairs={{0,1},{1,0},{2,3},{3,2},{4,5},{5,4},{6,7},{7,6},{8,9},{9,8},{10,11... | collective-permute-start | bytes 442376 | tf_op jit(solution)/shard_map/ppermute | solution.py:19
  84.7 4.4 %collective-permute-start.18 = (bf16[144,256]{1,0:T(8,128)(2,1)S(1)}, bf16[144,256]{1,0:T(8,128)(2,1)S(1)}, u32[]{:S(2)}, u32[]{:S(2)}) collective-permute-start(bf16[144,256]{1,0:T(8,128)(2,1)S(1)} %get-tuple-element.137.h0), channel_id=1, source_target_pairs={{0,1},{1,0},{2,3},{3,2},{4,5},{5,4},{6,7},{7,6},{8,9},{9,8},{10,11... | collective-permute-start | bytes 221192 | tf_op jit(solution)/shard_map/ppermute | solution.py:19
  86.3 4.4 %collective-permute-start.19 = (bf16[144,256]{1,0:T(8,128)(2,1)S(1)}, bf16[144,256]{1,0:T(8,128)(2,1)S(1)}, u32[]{:S(2)}, u32[]{:S(2)}) collective-permute-start(bf16[144,256]{1,0:T(8,128)(2,1)S(1)} %get-tuple-element.138.h1), channel_id=1, source_target_pairs={{0,1},{1,0},{2,3},{3,2},{4,5},{5,4},{6,7},{7,6},{8,9},{9,8},{10,11... | collective-permute-start | bytes 221192 | tf_op jit(solution)/shard_map/ppermute | solution.py:19
  93.8 18.4 %collective-permute-start.24 = (bf16[144,896]{1,0:T(8,128)(2,1)S(1)}, bf16[144,896]{1,0:T(8,128)(2,1)S(1)}, u32[]{:S(2)}, u32[]{:S(2)}) collective-permute-start(bf16[144,896]{1,0:T(8,128)(2,1)S(1)} %get-tuple-element.154), channel_id=1, source_target_pairs={{0,4},{1,5},{2,6},{3,7},{4,0},{5,1},{6,2},{7,3},{8,12},{9,13},{10,... | collective-permute-start | bytes 774152 | tf_op jit(solution)/shard_map/ppermute | solution.py:555
  95.0 17.1 %collective-permute-start.25 = (bf16[144,896]{1,0:T(8,128)(2,1)S(1)}, bf16[144,896]{1,0:T(8,128)(2,1)S(1)}, u32[]{:S(2)}, u32[]{:S(2)}) collective-permute-start(bf16[144,896]{1,0:T(8,128)(2,1)S(1)} %get-tuple-element.155), channel_id=1, source_target_pairs={{0,6},{1,7},{2,4},{3,5},{4,2},{5,3},{6,0},{7,1},{8,14},{9,15},{10,... | collective-permute-start | bytes 774152 | tf_op jit(solution)/shard_map/ppermute | solution.py:555
  99.3 5.9 %collective-permute-start.22 = (bf16[32,3584]{1,0:T(8,128)(2,1)S(1)}, bf16[32,3584]{1,0:T(8,128)(2,1)S(1)}, u32[]{:S(2)}, u32[]{:S(2)}) collective-permute-start(bf16[32,3584]{1,0:T(8,128)(2,1)S(1)} %get-tuple-element.147), channel_id=1, source_target_pairs={{0,8},{8,16},{16,24},{1,9},{9,17},{17,25},{2,10},{10,18},{18,26},{... | collective-permute-start | bytes 688136 | tf_op jit(solution)/shard_map/ppermute | solution.py:25
  100.6 5.2 %collective-permute-start.23 = (bf16[32,3584]{1,0:T(8,128)(2,1)S(1)}, bf16[32,3584]{1,0:T(8,128)(2,1)S(1)}, u32[]{:S(2)}, u32[]{:S(2)}) collective-permute-start(bf16[32,3584]{1,0:T(8,128)(2,1)S(1)} %get-tuple-element.148), channel_id=1, source_target_pairs={{0,8},{8,16},{16,24},{1,9},{9,17},{17,25},{2,10},{10,18},{18,26},{... | collective-permute-start | bytes 688136 | tf_op jit(solution)/shard_map/ppermute | solution.py:25
  104.7 15.6 %collective-permute-start.27 = (bf16[144,896]{1,0:T(8,128)(2,1)S(1)}, bf16[144,896]{1,0:T(8,128)(2,1)S(1)}, u32[]{:S(2)}, u32[]{:S(2)}) collective-permute-start(bf16[144,896]{1,0:T(8,128)(2,1)S(1)} %get-tuple-element.157), channel_id=1, source_target_pairs={{0,2},{1,3},{2,0},{3,1},{4,6},{5,7},{6,4},{7,5},{8,10},{9,11},{10,... | collective-permute-start | bytes 774152 | tf_op jit(solution)/shard_map/ppermute | solution.py:555
  112.2 22.9 %collective-permute-start.30 = (bf16[144,896]{1,0:T(8,128)(2,1)S(1)}, bf16[144,896]{1,0:T(8,128)(2,1)S(1)}, u32[]{:S(2)}, u32[]{:S(2)}) collective-permute-start(bf16[144,896]{1,0:T(8,128)(2,1)S(1)} %get-tuple-element.163), channel_id=1, source_target_pairs={{0,4},{1,5},{2,6},{3,7},{4,0},{5,1},{6,2},{7,3},{8,12},{9,13},{10,... | collective-permute-start | bytes 774152 | tf_op jit(solution)/shard_map/ppermute | solution.py:555
  116.9 18.2 %collective-permute-start.31 = (bf16[144,896]{1,0:T(8,128)(2,1)S(1)}, bf16[144,896]{1,0:T(8,128)(2,1)S(1)}, u32[]{:S(2)}, u32[]{:S(2)}) collective-permute-start(bf16[144,896]{1,0:T(8,128)(2,1)S(1)} %get-tuple-element.164), channel_id=1, source_target_pairs={{0,6},{1,7},{2,4},{3,5},{4,2},{5,3},{6,0},{7,1},{8,14},{9,15},{10,... | collective-permute-start | bytes 774152 | tf_op jit(solution)/shard_map/ppermute | solution.py:555
  120.3 22.3 %collective-permute-start.26 = (bf16[144,896]{1,0:T(8,128)(2,1)S(1)}, bf16[144,896]{1,0:T(8,128)(2,1)S(1)}, u32[]{:S(2)}, u32[]{:S(2)}) collective-permute-start(bf16[144,896]{1,0:T(8,128)(2,1)S(1)} %get-tuple-element.156), channel_id=1, source_target_pairs={{0,2},{1,3},{2,0},{3,1},{4,6},{5,7},{6,4},{7,5},{8,10},{9,11},{10,... | collective-permute-start | bytes 774152 | tf_op jit(solution)/shard_map/ppermute | solution.py:555
  135.1 28.6 %collective-permute-start.36 = (bf16[144,896]{1,0:T(8,128)(2,1)S(1)}, bf16[144,896]{1,0:T(8,128)(2,1)S(1)}, u32[]{:S(2)}, u32[]{:S(2)}) collective-permute-start(bf16[144,896]{1,0:T(8,128)(2,1)S(1)} %get-tuple-element.177), channel_id=1, source_target_pairs={{0,4},{1,5},{2,6},{3,7},{4,0},{5,1},{6,2},{7,3},{8,12},{9,13},{10,... | collective-permute-start | bytes 774152 | tf_op jit(solution)/shard_map/ppermute | solution.py:555
  142.2 21.5 %collective-permute-start.37 = (bf16[144,896]{1,0:T(8,128)(2,1)S(1)}, bf16[144,896]{1,0:T(8,128)(2,1)S(1)}, u32[]{:S(2)}, u32[]{:S(2)}) collective-permute-start(bf16[144,896]{1,0:T(8,128)(2,1)S(1)} %get-tuple-element.178), channel_id=1, source_target_pairs={{0,6},{1,7},{2,4},{3,5},{4,2},{5,3},{6,0},{7,1},{8,14},{9,15},{10,... | collective-permute-start | bytes 774152 | tf_op jit(solution)/shard_map/ppermute | solution.py:555
  145.2 8.6 %collective-permute-start.32 = (bf16[160,512]{1,0:T(8,128)(2,1)S(1)}, bf16[160,512]{1,0:T(8,128)(2,1)S(1)}, u32[]{:S(2)}, u32[]{:S(2)}) collective-permute-start(bf16[160,512]{1,0:T(8,128)(2,1)S(1)} %get-tuple-element.169), channel_id=1, source_target_pairs={{0,1},{1,0},{2,3},{3,2},{4,5},{5,4},{6,7},{7,6},{8,9},{9,8},{10,11... | collective-permute-start | bytes 491528 | tf_op jit(solution)/shard_map/ppermute | solution.py:19
  146.8 21.2 %collective-permute-start.39 = (bf16[144,896]{1,0:T(8,128)(2,1)S(1)}, bf16[144,896]{1,0:T(8,128)(2,1)S(1)}, u32[]{:S(2)}, u32[]{:S(2)}) collective-permute-start(bf16[144,896]{1,0:T(8,128)(2,1)S(1)} %get-tuple-element.181), channel_id=1, source_target_pairs={{0,2},{1,3},{2,0},{3,1},{4,6},{5,7},{6,4},{7,5},{8,10},{9,11},{10,... | collective-permute-start | bytes 774152 | tf_op jit(solution)/shard_map/ppermute | solution.py:555
  148.3 5.6 %collective-permute-start.33 = (bf16[144,512]{1,0:T(8,128)(2,1)S(1)}, bf16[144,512]{1,0:T(8,128)(2,1)S(1)}, u32[]{:S(2)}, u32[]{:S(2)}) collective-permute-start(bf16[144,512]{1,0:T(8,128)(2,1)S(1)} %second.6), channel_id=1, source_target_pairs={{0,1},{1,0},{2,3},{3,2},{4,5},{5,4},{6,7},{7,6},{8,9},{9,8},{10,11... | collective-permute-start | bytes 442376 | tf_op jit(solution)/shard_map/ppermute | solution.py:19
  154.8 4.4 %collective-permute-start.34 = (bf16[144,256]{1,0:T(8,128)(2,1)S(1)}, bf16[144,256]{1,0:T(8,128)(2,1)S(1)}, u32[]{:S(2)}, u32[]{:S(2)}) collective-permute-start(bf16[144,256]{1,0:T(8,128)(2,1)S(1)} %get-tuple-element.171.h0), channel_id=1, source_target_pairs={{0,1},{1,0},{2,3},{3,2},{4,5},{5,4},{6,7},{7,6},{8,9},{9,8},{10,11... | collective-permute-start | bytes 221192 | tf_op jit(solution)/shard_map/ppermute | solution.py:19
  156.5 4.4 %collective-permute-start.35 = (bf16[144,256]{1,0:T(8,128)(2,1)S(1)}, bf16[144,256]{1,0:T(8,128)(2,1)S(1)}, u32[]{:S(2)}, u32[]{:S(2)}) collective-permute-start(bf16[144,256]{1,0:T(8,128)(2,1)S(1)} %get-tuple-element.172.h1), channel_id=1, source_target_pairs={{0,1},{1,0},{2,3},{3,2},{4,5},{5,4},{6,7},{7,6},{8,9},{9,8},{10,11... | collective-permute-start | bytes 221192 | tf_op jit(solution)/shard_map/ppermute | solution.py:19
  163.7 25.6 %collective-permute-start.44 = (bf16[144,896]{1,0:T(8,128)(2,1)S(1)}, bf16[144,896]{1,0:T(8,128)(2,1)S(1)}, u32[]{:S(2)}, u32[]{:S(2)}) collective-permute-start(bf16[144,896]{1,0:T(8,128)(2,1)S(1)} %get-tuple-element.192), channel_id=1, source_target_pairs={{0,4},{1,5},{2,6},{3,7},{4,0},{5,1},{6,2},{7,3},{8,12},{9,13},{10,... | collective-permute-start | bytes 774152 | tf_op jit(solution)/shard_map/ppermute | solution.py:555
  166.5 22.8 %collective-permute-start.45 = (bf16[144,896]{1,0:T(8,128)(2,1)S(1)}, bf16[144,896]{1,0:T(8,128)(2,1)S(1)}, u32[]{:S(2)}, u32[]{:S(2)}) collective-permute-start(bf16[144,896]{1,0:T(8,128)(2,1)S(1)} %get-tuple-element.193), channel_id=1, source_target_pairs={{0,6},{1,7},{2,4},{3,5},{4,2},{5,3},{6,0},{7,1},{8,14},{9,15},{10,... | collective-permute-start | bytes 774152 | tf_op jit(solution)/shard_map/ppermute | solution.py:555
  170.6 8.6 %collective-permute-start.40 = (bf16[160,512]{1,0:T(8,128)(2,1)S(1)}, bf16[160,512]{1,0:T(8,128)(2,1)S(1)}, u32[]{:S(2)}, u32[]{:S(2)}) collective-permute-start(bf16[160,512]{1,0:T(8,128)(2,1)S(1)} %get-tuple-element.185), channel_id=1, source_target_pairs={{0,1},{1,0},{2,3},{3,2},{4,5},{5,4},{6,7},{7,6},{8,9},{9,8},{10,11... | collective-permute-start | bytes 491528 | tf_op jit(solution)/shard_map/ppermute | solution.py:19
  173.5 5.7 %collective-permute-start.41 = (bf16[144,512]{1,0:T(8,128)(2,1)S(1)}, bf16[144,512]{1,0:T(8,128)(2,1)S(1)}, u32[]{:S(2)}, u32[]{:S(2)}) collective-permute-start(bf16[144,512]{1,0:T(8,128)(2,1)S(1)} %second.7), channel_id=1, source_target_pairs={{0,1},{1,0},{2,3},{3,2},{4,5},{5,4},{6,7},{7,6},{8,9},{9,8},{10,11... | collective-permute-start | bytes 442376 | tf_op jit(solution)/shard_map/ppermute | solution.py:19
  180.2 4.4 %collective-permute-start.42 = (bf16[144,256]{1,0:T(8,128)(2,1)S(1)}, bf16[144,256]{1,0:T(8,128)(2,1)S(1)}, u32[]{:S(2)}, u32[]{:S(2)}) collective-permute-start(bf16[144,256]{1,0:T(8,128)(2,1)S(1)} %get-tuple-element.187.h0), channel_id=1, source_target_pairs={{0,1},{1,0},{2,3},{3,2},{4,5},{5,4},{6,7},{7,6},{8,9},{9,8},{10,11... | collective-permute-start | bytes 221192 | tf_op jit(solution)/shard_map/ppermute | solution.py:19
  182.3 11.5 %collective-permute-start.38 = (bf16[144,896]{1,0:T(8,128)(2,1)S(1)}, bf16[144,896]{1,0:T(8,128)(2,1)S(1)}, u32[]{:S(2)}, u32[]{:S(2)}) collective-permute-start(bf16[144,896]{1,0:T(8,128)(2,1)S(1)} %get-tuple-element.179), channel_id=1, source_target_pairs={{0,2},{1,3},{2,0},{3,1},{4,6},{5,7},{6,4},{7,5},{8,10},{9,11},{10,... | collective-permute-start | bytes 774152 | tf_op jit(solution)/shard_map/ppermute | solution.py:555
  189.3 10.3 %collective-permute-start.47 = (bf16[144,896]{1,0:T(8,128)(2,1)S(1)}, bf16[144,896]{1,0:T(8,128)(2,1)S(1)}, u32[]{:S(2)}, u32[]{:S(2)}) collective-permute-start(bf16[144,896]{1,0:T(8,128)(2,1)S(1)} %get-tuple-element.199), channel_id=1, source_target_pairs={{0,2},{1,3},{2,0},{3,1},{4,6},{5,7},{6,4},{7,5},{8,10},{9,11},{10,... | collective-permute-start | bytes 774152 | tf_op jit(solution)/shard_map/ppermute | solution.py:555
  189.4 21.1 %collective-permute-start.48 = (bf16[144,896]{1,0:T(8,128)(2,1)S(1)}, bf16[144,896]{1,0:T(8,128)(2,1)S(1)}, u32[]{:S(2)}, u32[]{:S(2)}) collective-permute-start(bf16[144,896]{1,0:T(8,128)(2,1)S(1)} %get-tuple-element.200), channel_id=1, source_target_pairs={{0,4},{1,5},{2,6},{3,7},{4,0},{5,1},{6,2},{7,3},{8,12},{9,13},{10,... | collective-permute-start | bytes 774152 | tf_op jit(solution)/shard_map/ppermute | solution.py:555
  190.7 19.8 %collective-permute-start.49 = (bf16[144,896]{1,0:T(8,128)(2,1)S(1)}, bf16[144,896]{1,0:T(8,128)(2,1)S(1)}, u32[]{:S(2)}, u32[]{:S(2)}) collective-permute-start(bf16[144,896]{1,0:T(8,128)(2,1)S(1)} %get-tuple-element.201), channel_id=1, source_target_pairs={{0,6},{1,7},{2,4},{3,5},{4,2},{5,3},{6,0},{7,1},{8,14},{9,15},{10,... | collective-permute-start | bytes 774152 | tf_op jit(solution)/shard_map/ppermute | solution.py:555
  196.1 17.7 %collective-permute-start.46 = (bf16[32,3584]{1,0:T(8,128)(2,1)S(1)}, bf16[32,3584]{1,0:T(8,128)(2,1)S(1)}, u32[]{:S(2)}, u32[]{:S(2)}) collective-permute-start(bf16[32,3584]{1,0:T(8,128)(2,1)S(1)} %get-tuple-element.198), channel_id=1, source_target_pairs={{0,1},{1,0},{2,3},{3,2},{4,5},{5,4},{6,7},{7,6},{8,9},{9,8},{10,11... | collective-permute-start | bytes 688136 | tf_op jit(solution)/shard_map/ppermute | solution.py:19
  212.8 6.1 %collective-permute-start.50 = (bf16[32,3584]{1,0:T(8,128)(2,1)S(1)}, bf16[32,3584]{1,0:T(8,128)(2,1)S(1)}, u32[]{:S(2)}, u32[]{:S(2)}) collective-permute-start(bf16[32,3584]{1,0:T(8,128)(2,1)S(1)} %get-tuple-element.203), channel_id=1, source_target_pairs={{0,1},{1,0},{2,3},{3,2},{4,5},{5,4},{6,7},{7,6},{8,9},{9,8},{10,11... | collective-permute-start | bytes 688136 | tf_op jit(solution)/shard_map/ppermute | solution.py:19
  (13 other events, 148.7 us)

commit v4 on v3

--- a/solution.py
+++ b/solution.py
@@ -359,24 +359,19 @@
     )(me, *arrays, *after)
 
 
-def first_kernel(me, r0, r1, r2, r3, gain, weight, message, rows_out, squares, stacked):
+def first_kernel(me, r0, r1, r2, r3, gain, weight, gates, ups, rows_out, squares):
     slots = 2 * CAP
-    block = PARTS * slots
-    width = r0.shape[1]
-    for apart, ref in enumerate((r0, r1, r2, r3)):
-        stacked[apart * block:(apart + 1) * block, :] = ref[...]
-    row = iota((block, EXPERTS * block), 0)
-    column = iota((block, EXPERTS * block), 1)
+    block, width = r0.shape
+    units = weight.shape[1] // 4
+    held = [ref[...].astype(jnp.float32) for ref in (r0, r1, r2, r3)]
     total = jnp.zeros((block, 1), jnp.float32)
     for part in range(PARTS):
-        source = row // slots * block + part * slots + row % slots
-        values = matmul(ones_where(column == source), stacked[...])
+        values = jnp.concatenate([rows[part * slots:(part + 1) * slots, :] for rows in held], axis=0)
         total = total + jnp.sum(values * values, axis=1, keepdims=True)
         start = pl.multiple_of(me[1] * PARTS * width + part * width, width)
         scaled = values * gain[:, pl.ds(start, width)]
         rows_out[:, part * width:(part + 1) * width] = scaled.astype(jnp.bfloat16)
     squares[...] = jnp.broadcast_to(total, squares.shape)
-    units = weight.shape[1] // 4
     lane = iota(squares.shape, 1)
     high, middle, low = [piece.astype(jnp.float32) for piece in pieces(total)]
     sent = jnp.where(lane == 0, high, jnp.where(lane == 1, middle, jnp.where(lane == 2, low, 0.0)))
@@ -386,28 +381,20 @@
         (((0,), (0,)), ((), ())),
         preferred_element_type=jnp.float32,
     )
-    message[block:, :] = jnp.zeros((message.shape[0] - block, units), jnp.bfloat16)
-    message[block:, :block] = turned[:message.shape[0] - block, :].astype(jnp.bfloat16)
-    start = pl.multiple_of(units * (1 - me[1]), units)
-    message[:block, :] = matmul(rows_out[...], weight[:, pl.ds(start, units)]).astype(jnp.bfloat16)
+    extra = gates.shape[0] - block
+    gates[block:, :] = jnp.zeros((extra, units), jnp.bfloat16)
+    gates[block:, :block] = turned[:extra, :].astype(jnp.bfloat16)
+    for kind in range(2):
+        start = pl.multiple_of(units * (2 * kind + 1 - me[1]), units)
+        columns = matmul(rows_out[...], weight[:, pl.ds(start, units)]).astype(jnp.bfloat16)
+        (gates, ups)[kind][:block, :] = columns
 
 
 def first(me, received, gain, weight, after):
     block, width = received[0].shape
     half, both = weight.shape
-    outs = [bf16(block + 16, both // 4), bf16(block, half), f32(block, 128)]
-    scratch = [pltpu.VMEM((EXPERTS * block, width), jnp.bfloat16)]
-    return call(first_kernel, "first", outs, me, *received, gain, weight, after=after, scratch=scratch)
-
-
-def second_kernel(me, rows_in, weight, message):
-    units = weight.shape[1] // 4
-    start = pl.multiple_of(units * (3 - me[1]), units)
-    message[...] = matmul(rows_in[...], weight[:, pl.ds(start, units)]).astype(jnp.bfloat16)
-
-
-def second(me, rows_in, weight):
-    return call(second_kernel, "second", bf16(rows_in.shape[0], weight.shape[1] // 4), me, rows_in, weight)
+    outs = [bf16(block + 16, both // 4), bf16(block, both // 4), bf16(block, half), f32(block, 128)]
+    return call(first_kernel, "first", outs, me, *received, gain, weight, after=after)
 
 
 def own_kernel(me, rows_in, weight, own):
@@ -445,32 +432,29 @@
     return call(functools.partial(act_kernel, model_width), "act", outs, me, own, gates, ups, squares)
 
 
-def third_kernel(me, h0, h1, t0, t1, weight, *refs):
-    o0, o1, o2, o3, hidden, stacked = refs
+def third_kernel(me, h0, h1, t0, t1, weight, o0, o1, o2, o3, hidden):
     slots = 2 * CAP
     block, units = hidden.shape
     size = units // 4
     width = o0.shape[1]
-    for index, refs in enumerate(((h0, h1), (t0, t1))):
-        for place, ref in enumerate(refs):
+    for index, pair in enumerate(((h0, h1), (t0, t1))):
+        for place, ref in enumerate(pair):
             start = ((me[1] ^ index) * 2 + place) * size
             hidden[:, pl.ds(pl.multiple_of(start, size), size)] = ref[...]
+    results = []
     for part in range(PARTS):
-        result = matmul(hidden[...], weight[:, part * width:(part + 1) * width])
-        stacked[part * block:(part + 1) * block, :] = result.astype(jnp.bfloat16)
-    row = iota((block, PARTS * block), 0)
-    column = iota((block, PARTS * block), 1)
+        columns = slice(part * width, (part + 1) * width)
+        results.append(matmul(hidden[...], weight[:, columns]))
     for apart, out in enumerate((o0, o1, o2, o3)):
-        source = row // slots * block + apart * slots + row % slots
-        out[...] = matmul(ones_where(column == source), stacked[...]).astype(jnp.bfloat16)
+        rows = [result[apart * slots:(apart + 1) * slots, :] for result in results]
+        out[...] = jnp.concatenate(rows, axis=0).astype(jnp.bfloat16)
 
 
 def third(me, hidden, hidden_other, weight):
     block = hidden[0].shape[0]
     units, half = weight.shape
-    width = half // PARTS
-    outs = [bf16(block, width)] * EXPERTS
-    scratch = [pltpu.VMEM((block, units), jnp.bfloat16), pltpu.VMEM((PARTS * block, width), jnp.bfloat16)]
+    outs = [bf16(block, half // PARTS)] * EXPERTS
+    scratch = [pltpu.VMEM((block, units), jnp.bfloat16)]
     return call(third_kernel, "third", outs, me, *hidden, *hidden_other, weight, scratch=scratch)
 
 
@@ -558,7 +542,8 @@
 def across(blocks, behind=None):
     own, near, two, three = blocks
     if behind is not None:
-        near, two, three, *behind[2:] = lax.optimization_barrier((near, two, three, *behind[2:]))
+        two, three, *behind[2:] = lax.optimization_barrier((two, three, *behind[2:]))
+        near, behind[1] = lax.optimization_barrier((near, behind[1]))
     two, three = along(two, 2), along(three, 3)
     return [own, along(near, 1), two, three]
 
@@ -622,13 +607,11 @@
         behind = states[1]
         for stream in range(2):
             turn = stream * TICKS + tick
-            message, scaled, squares = first(me, arrived[stream], norm_gain, weight_in, [behind])
-            gates = partner(message, "expert", 0)
-            ups = partner(second(me, scaled, weight_in), "expert", 0)
+            gates, ups, scaled, squares = first(me, arrived[stream], norm_gain, weight_in, [behind])
+            gates, ups = partner(gates, "expert", 0), partner(ups, "expert", 0)
             own = own_half(me, scaled, weight_in)
             hidden = act(me, own, gates, ups, squares, model_width)
-            hidden_other = [partner(half, "expert", 0) for half in hidden]
-            result = third(me, hidden, hidden_other, weight_out)
+            result = third(me, hidden, [partner(half, "expert", 0) for half in hidden], weight_out)
             behind = result[0]
             arrived[stream] = across(result, ahead)
             ahead = arrived[stream]

time: 222 us -> 212 us (0.955)
  Pallas kernels: 64.1 us -> 54 us
    pallas_call x35 -> x31, Pallas kernels: 58.3 us -> 48.3 us  [call(): pl.pallas_call(kernel, out_shape=out_shape, in_specs=[pl.BlockSpec(memory...]
  transfers between devices with their start and end apart: 51 -> 51, of which waited for: 22 -> 22; matrix products, arithmetic and copies ran while one was open for 1% -> 1% of each run, Pallas kernels for 28% -> 25%
where the time goes in v4:
time: 212 us; the launch traced here: 209 us
  starting transfers between devices  78.5 us (37%)
  waiting for transfers between devices  65.3 us (31%)
  Pallas kernels  54 us (25%)
  local copies, waits for them, and re-layouts  8.96 us (4%)
    pallas_call x31, Pallas kernels, call(): pl.pallas_call(kernel, out_shape=out_shape, in_specs=[pl.BlockSpec(memory...  48.3 us
    ppermute x24, starting transfers between devices, along(): lax.ppermute(block, 'expert', [(i, i ^ 2 * apart) for i in range(lax.axis...  43.2 us
    ppermute x23, waiting for transfers between devices, partner(): lax.ppermute(shard, axis, [(i, i ^ 1 << apart) for i in range(lax.axis_si...  36 us
    ppermute x23, starting transfers between devices, partner(): lax.ppermute(shard, axis, [(i, i ^ 1 << apart) for i in range(lax.axis_si...  27.1 us
    ppermute x24, waiting for transfers between devices, along(): lax.ppermute(block, 'expert', [(i, i ^ 2 * apart) for i in range(lax.axis...  25.7 us
    ppermute x4, starting transfers between devices, shifted(): return lax.ppermute(block, axis, route)  8.24 us
    unnamed x20, local copies, waits for them, and re-layouts  8.19 us
    pallas_call x1, Pallas kernels, load(): pl.pallas_call(kernel, out_shape=[bf16(*array.shape) for array in arrays]...  5.73 us
  transfers between devices with their start and end apart: 51, of which 22 were waited for; matrix products, arithmetic and copies ran while one was open for 1% of the time, Pallas kernels for 25%

profile of v4, /device:TPU:0, one launch (start us, length us, event | category | flops | bytes accessed | tf_op | source)
XLA Modules:
  0.0 208.6 jit_solution(3331228231843992606)
XLA Ops:
  2.3 3.0 %collective-permute-start.4 = (bf16[32,3584]{1,0:T(8,128)(2,1)S(1)}, bf16[32,3584]{1,0:T(8,128)(2,1)S(1)}, u32[]{:S(2)}, u32[]{:S(2)}) collective-permute-start(bf16[32,3584]{1,0:T(8,128)(2,1)S(1)} %cut.7), channel_id=1, source_target_pairs={{0,1},{1,0},{2,3},{3,2},{4,5},{5,4},{6,7},{7,6},{8,9},{9,8},{10,11... | collective-permute-start | bytes 688136 | tf_op jit(solution)/shard_map/ppermute | solution.py:19
  8.5 2.1 collective-permute-start.1
  10.6 5.5 %collective-permute-done.1.other = f32[16,32]{1,0:T(8,128)S(1)} collective-permute-done((f32[16,32]{1,0:T(8,128)S(1)}, f32[16,32]{1,0:T(8,128)S(1)}, u32[]{:S(2)}, u32[]{:S(2)}) %collective-permute-start.1) | collective-permute-done | bytes 2080 | tf_op jit(solution)/shard_map/ppermute | solution.py:19
  19.1 1.9 collective-permute-start.5
  20.9 2.6 %collective-permute-start.6 = (bf16[144,896]{1,0:T(8,128)(2,1)S(1)}, bf16[144,896]{1,0:T(8,128)(2,1)S(1)}, u32[]{:S(2)}, u32[]{:S(2)}) collective-permute-start(bf16[144,896]{1,0:T(8,128)(2,1)S(1)} %get-tuple-element.123), channel_id=1, source_target_pairs={{0,4},{1,5},{2,6},{3,7},{4,0},{5,1},{6,2},{7,3},{8,12},{9,13},{10,... | collective-permute-start | bytes 774152 | tf_op jit(solution)/shard_map/ppermute | solution.py:539
  28.9 3.1 %copy-done = bf16[1,1,1024,3584]{3,2,1,0:T(8,128)(2,1)S(1)} copy-done((bf16[1,1,1024,3584]{3,2,1,0:T(8,128)(2,1)S(1)}, bf16[1,1,1024,3584]{3,2,1,0:T(8,128)(2,1)}, u32[]{:S(2)}) %copy-start) | copy-done | bytes 7340056
  32.0 5.7 %load.1 = (bf16[3584,2048]{1,0:T(8,128)(2,1)S(1)}, bf16[1024,3584]{1,0:T(8,128)(2,1)S(1)}) custom-call(s32[4]{0:T(128)S(1)} %pad_add_fusion.me.refs_0_, bf16[3584,2048]{1,0:T(8,128)(2,1)} %bitcast.53, bf16[1024,3584]{1,0:T(8,128)(2,1)S(1)} %bitcast.44, bf16[64,3584]{1,0:T(8,128)(2,1)S(1)} %get-tuple-element.114.refs_3_.refs_1_), custom_call_target="tpu_custom_call" | custom-call | tf_op jit(solution)/shard_map/load/pallas_call | solution.py:349
  39.9 2.2 %collective-permute-done.6.refs_3_ = bf16[144,896]{1,0:T(8,128)(2,1)S(1)} collective-permute-done((bf16[144,896]{1,0:T(8,128)(2,1)S(1)}, bf16[144,896]{1,0:T(8,128)(2,1)S(1)}, u32[]{:S(2)}, u32[]{:S(2)}) %collective-permute-start.6) | collective-permute-done | bytes 258080 | tf_op jit(solution)/shard_map/ppermute | solution.py:539
  42.1 5.6 %collective-permute-start.13 = (bf16[144,896]{1,0:T(8,128)(2,1)S(1)}, bf16[144,896]{1,0:T(8,128)(2,1)S(1)}, u32[]{:S(2)}, u32[]{:S(2)}) collective-permute-start(bf16[144,896]{1,0:T(8,128)(2,1)S(1)} %get-tuple-element.142), channel_id=1, source_target_pairs={{0,4},{1,5},{2,6},{3,7},{4,0},{5,1},{6,2},{7,3},{8,12},{9,13},{10,... | collective-permute-start | bytes 774152 | tf_op jit(solution)/shard_map/ppermute | solution.py:539
  48.2 2.4 %first.4 = (bf16[160,512]{1,0:T(8,128)(2,1)S(1)}, bf16[144,512]{1,0:T(8,128)(2,1)S(1)}, bf16[144,3584]{1,0:T(8,128)(2,1)S(1)}, f32[144,128]{1,0:T(8,128)S(1)}) custom-call(s32[4]{0:T(128)S(1)} %pad_add_fusion.me.refs_0_, bf16[144,896]{1,0:T(8,128)(2,1)S(1)} %get-tuple-element.116.refs_1_, bf16[144,896]{1,0:T(8,128)(2,1)S(1)} %collective-permute-done.5.refs_2_, ...), custom_call_target="tpu_custom_call" | custom-call | tf_op jit(solution)/shard_map/first/pallas_call | solution.py:194
  52.8 1.9 own.4
  54.6 3.2 %collective-permute-done.9.ups = bf16[144,512]{1,0:T(8,128)(2,1)S(1)} collective-permute-done((bf16[144,512]{1,0:T(8,128)(2,1)S(1)}, bf16[144,512]{1,0:T(8,128)(2,1)S(1)}, u32[]{:S(2)}, u32[]{:S(2)}) %collective-permute-start.9) | collective-permute-done | bytes 147488 | tf_op jit(solution)/shard_map/ppermute | solution.py:19
  60.9 2.3 %collective-permute-done.10.t0 = bf16[144,256]{1,0:T(8,128)(2,1)S(1)} collective-permute-done((bf16[144,256]{1,0:T(8,128)(2,1)S(1)}, bf16[144,256]{1,0:T(8,128)(2,1)S(1)}, u32[]{:S(2)}, u32[]{:S(2)}) %collective-permute-start.10) | collective-permute-done | bytes 73760 | tf_op jit(solution)/shard_map/ppermute | solution.py:19
  64.7 2.0 third.4
  67.0 4.4 %collective-permute-start.20 = (bf16[144,896]{1,0:T(8,128)(2,1)S(1)}, bf16[144,896]{1,0:T(8,128)(2,1)S(1)}, u32[]{:S(2)}, u32[]{:S(2)}) collective-permute-start(bf16[144,896]{1,0:T(8,128)(2,1)S(1)} %get-tuple-element.157), channel_id=1, source_target_pairs={{0,4},{1,5},{2,6},{3,7},{4,0},{5,1},{6,2},{7,3},{8,12},{9,13},{10,... | collective-permute-start | bytes 774152 | tf_op jit(solution)/shard_map/ppermute | solution.py:539
  71.4 2.4 %first.5 = (bf16[160,512]{1,0:T(8,128)(2,1)S(1)}, bf16[144,512]{1,0:T(8,128)(2,1)S(1)}, bf16[144,3584]{1,0:T(8,128)(2,1)S(1)}, f32[144,128]{1,0:T(8,128)S(1)}) custom-call(s32[4]{0:T(128)S(1)} %pad_add_fusion.me.refs_0_, bf16[144,896]{1,0:T(8,128)(2,1)S(1)} %get-tuple-element.136.refs_1_, bf16[144,896]{1,0:T(8,128)(2,1)S(1)} %collective-permute-done.12.refs_2_, ...), custom_call_target="tpu_custom_call" | custom-call | tf_op jit(solution)/shard_map/first/pallas_call | solution.py:194
  75.9 1.9 own.5
  77.8 3.0 %collective-permute-done.16.ups = bf16[144,512]{1,0:T(8,128)(2,1)S(1)} collective-permute-done((bf16[144,512]{1,0:T(8,128)(2,1)S(1)}, bf16[144,512]{1,0:T(8,128)(2,1)S(1)}, u32[]{:S(2)}, u32[]{:S(2)}) %collective-permute-start.16) | collective-permute-done | bytes 147488 | tf_op jit(solution)/shard_map/ppermute | solution.py:19
  83.9 2.3 %collective-permute-done.17.t0 = bf16[144,256]{1,0:T(8,128)(2,1)S(1)} collective-permute-done((bf16[144,256]{1,0:T(8,128)(2,1)S(1)}, bf16[144,256]{1,0:T(8,128)(2,1)S(1)}, u32[]{:S(2)}, u32[]{:S(2)}) %collective-permute-start.17) | collective-permute-done | bytes 73760 | tf_op jit(solution)/shard_map/ppermute | solution.py:19
  87.3 2.0 third.5
  89.2 2.0 collective-permute-start.24
  91.3 3.7 %collective-permute-start.25 = (bf16[144,896]{1,0:T(8,128)(2,1)S(1)}, bf16[144,896]{1,0:T(8,128)(2,1)S(1)}, u32[]{:S(2)}, u32[]{:S(2)}) collective-permute-start(bf16[144,896]{1,0:T(8,128)(2,1)S(1)} %get-tuple-element.167), channel_id=1, source_target_pairs={{0,4},{1,5},{2,6},{3,7},{4,0},{5,1},{6,2},{7,3},{8,12},{9,13},{10,... | collective-permute-start | bytes 774152 | tf_op jit(solution)/shard_map/ppermute | solution.py:539
  95.0 2.3 %mix.2 = (bf16[32,3584]{1,0:T(8,128)(2,1)S(1)}, bf16[32,3584]{1,0:T(8,128)(2,1)S(1)}) custom-call(s32[4]{0:T(128)S(1)} %pad_add_fusion.me.refs_0_, bf16[64,3584]{1,0:T(8,128)(2,1)S(1)} %get-tuple-element.114.refs_3_.refs_1_, f32[256,16]{1,0:T(8,128)S(1)} %get-tuple-element.115.refs_2_, bf16[144,896]{1,0:T(8,128)(2,1)S(1)} %get-tuple-element.135.refs_7_.refs_3_, ...), custom_call_target="tpu_custom_call" | custom-call | tf_op jit(solution)/shard_map/mix/pallas_call | solution.py:194
  98.6 4.3 %collective-permute-start.23 = (bf16[32,3584]{1,0:T(8,128)(2,1)S(1)}, bf16[32,3584]{1,0:T(8,128)(2,1)S(1)}, u32[]{:S(2)}, u32[]{:S(2)}) collective-permute-start(bf16[32,3584]{1,0:T(8,128)(2,1)S(1)} %get-tuple-element.163), channel_id=1, source_target_pairs={{0,8},{8,16},{16,24},{1,9},{9,17},{17,25},{2,10},{10,18},{18,26},{... | collective-permute-start | bytes 688136 | tf_op jit(solution)/shard_map/ppermute | solution.py:25
  105.8 3.7 %collective-permute-done.25.refs_5_ = bf16[144,896]{1,0:T(8,128)(2,1)S(1)} collective-permute-done((bf16[144,896]{1,0:T(8,128)(2,1)S(1)}, bf16[144,896]{1,0:T(8,128)(2,1)S(1)}, u32[]{:S(2)}, u32[]{:S(2)}) %collective-permute-start.25) | collective-permute-done | bytes 258080 | tf_op jit(solution)/shard_map/ppermute | solution.py:539
  109.5 4.6 %collective-permute-start.30 = (bf16[144,896]{1,0:T(8,128)(2,1)S(1)}, bf16[144,896]{1,0:T(8,128)(2,1)S(1)}, u32[]{:S(2)}, u32[]{:S(2)}) collective-permute-start(bf16[144,896]{1,0:T(8,128)(2,1)S(1)} %get-tuple-element.179), channel_id=1, source_target_pairs={{0,4},{1,5},{2,6},{3,7},{4,0},{5,1},{6,2},{7,3},{8,12},{9,13},{10,... | collective-permute-start | bytes 774152 | tf_op jit(solution)/shard_map/ppermute | solution.py:539
  115.7 2.3 %mix.3 = (bf16[32,3584]{1,0:T(8,128)(2,1)S(1)}, bf16[32,3584]{1,0:T(8,128)(2,1)S(1)}) custom-call(s32[4]{0:T(128)S(1)} %pad_add_fusion.me.refs_0_, bf16[64,3584]{1,0:T(8,128)(2,1)S(1)} %get-tuple-element.127.refs_7_.refs_1_, f32[256,16]{1,0:T(8,128)S(1)} %get-tuple-element.115.refs_2_, bf16[144,896]{1,0:T(8,128)(2,1)S(1)} %get-tuple-element.161.refs_7_.refs_3_, ...), custom_call_target="tpu_custom_call" | custom-call | tf_op jit(solution)/shard_map/mix/pallas_call | solution.py:194
  121.3 1.9 collective-permute-done.28.moved_rest
  124.5 7.8 %collective-permute-done.30.refs_3_ = bf16[144,896]{1,0:T(8,128)(2,1)S(1)} collective-permute-done((bf16[144,896]{1,0:T(8,128)(2,1)S(1)}, bf16[144,896]{1,0:T(8,128)(2,1)S(1)}, u32[]{:S(2)}, u32[]{:S(2)}) %collective-permute-start.30) | collective-permute-done | bytes 258080 | tf_op jit(solution)/shard_map/ppermute | solution.py:539
  132.3 4.0 %collective-permute-start.37 = (bf16[144,896]{1,0:T(8,128)(2,1)S(1)}, bf16[144,896]{1,0:T(8,128)(2,1)S(1)}, u32[]{:S(2)}, u32[]{:S(2)}) collective-permute-start(bf16[144,896]{1,0:T(8,128)(2,1)S(1)} %get-tuple-element.197), channel_id=1, source_target_pairs={{0,4},{1,5},{2,6},{3,7},{4,0},{5,1},{6,2},{7,3},{8,12},{9,13},{10,... | collective-permute-start | bytes 774152 | tf_op jit(solution)/shard_map/ppermute | solution.py:539
  136.3 2.2 %collective-permute-start.38 = (bf16[144,896]{1,0:T(8,128)(2,1)S(1)}, bf16[144,896]{1,0:T(8,128)(2,1)S(1)}, u32[]{:S(2)}, u32[]{:S(2)}) collective-permute-start(bf16[144,896]{1,0:T(8,128)(2,1)S(1)} %get-tuple-element.198), channel_id=1, source_target_pairs={{0,6},{1,7},{2,4},{3,5},{4,2},{5,3},{6,0},{7,1},{8,14},{9,15},{10,... | collective-permute-start | bytes 774152 | tf_op jit(solution)/shard_map/ppermute | solution.py:539
  138.5 2.4 %first.6 = (bf16[160,512]{1,0:T(8,128)(2,1)S(1)}, bf16[144,512]{1,0:T(8,128)(2,1)S(1)}, bf16[144,3584]{1,0:T(8,128)(2,1)S(1)}, f32[144,128]{1,0:T(8,128)S(1)}) custom-call(s32[4]{0:T(128)S(1)} %pad_add_fusion.me.refs_0_, bf16[144,896]{1,0:T(8,128)(2,1)S(1)} %get-tuple-element.165.refs_7_.refs_1_, bf16[144,896]{1,0:T(8,128)(2,1)S(1)} %collective-permute-done.29.refs_2_, ...), custom_call_target="tpu_custom_call" | custom-call | tf_op jit(solution)/shard_map/first/pallas_call | solution.py:194
  143.1 1.8 own.6
  145.0 3.4 %collective-permute-done.33.ups = bf16[144,512]{1,0:T(8,128)(2,1)S(1)} collective-permute-done((bf16[144,512]{1,0:T(8,128)(2,1)S(1)}, bf16[144,512]{1,0:T(8,128)(2,1)S(1)}, u32[]{:S(2)}, u32[]{:S(2)}) %collective-permute-start.33) | collective-permute-done | bytes 147488 | tf_op jit(solution)/shard_map/ppermute | solution.py:19
  149.4 1.9 collective-permute-start.34
  151.4 2.3 %collective-permute-done.34.t0 = bf16[144,256]{1,0:T(8,128)(2,1)S(1)} collective-permute-done((bf16[144,256]{1,0:T(8,128)(2,1)S(1)}, bf16[144,256]{1,0:T(8,128)(2,1)S(1)}, u32[]{:S(2)}, u32[]{:S(2)}) %collective-permute-start.34) | collective-permute-done | bytes 73760 | tf_op jit(solution)/shard_map/ppermute | solution.py:19
  153.8 1.8 collective-permute-done.35.t1
  155.6 2.0 third.6
  159.4 2.7 %collective-permute-start.45 = (bf16[144,896]{1,0:T(8,128)(2,1)S(1)}, bf16[144,896]{1,0:T(8,128)(2,1)S(1)}, u32[]{:S(2)}, u32[]{:S(2)}) collective-permute-start(bf16[144,896]{1,0:T(8,128)(2,1)S(1)} %get-tuple-element.213), channel_id=1, source_target_pairs={{0,6},{1,7},{2,4},{3,5},{4,2},{5,3},{6,0},{7,1},{8,14},{9,15},{10,... | collective-permute-start | bytes 774152 | tf_op jit(solution)/shard_map/ppermute | solution.py:539
  162.0 2.3 %first.7 = (bf16[160,512]{1,0:T(8,128)(2,1)S(1)}, bf16[144,512]{1,0:T(8,128)(2,1)S(1)}, bf16[144,3584]{1,0:T(8,128)(2,1)S(1)}, f32[144,128]{1,0:T(8,128)S(1)}) custom-call(s32[4]{0:T(128)S(1)} %pad_add_fusion.me.refs_0_, bf16[144,896]{1,0:T(8,128)(2,1)S(1)} %get-tuple-element.191.refs_1_, bf16[144,896]{1,0:T(8,128)(2,1)S(1)} %collective-permute-done.36.refs_2_, ...), custom_call_target="tpu_custom_call" | custom-call | tf_op jit(solution)/shard_map/first/pallas_call | solution.py:194
  168.2 3.5 %collective-permute-done.40.ups = bf16[144,512]{1,0:T(8,128)(2,1)S(1)} collective-permute-done((bf16[144,512]{1,0:T(8,128)(2,1)S(1)}, bf16[144,512]{1,0:T(8,128)(2,1)S(1)}, u32[]{:S(2)}, u32[]{:S(2)}) %collective-permute-start.40) | collective-permute-done | bytes 147488 | tf_op jit(solution)/shard_map/ppermute | solution.py:19
  174.8 2.3 %collective-permute-done.41.t0 = bf16[144,256]{1,0:T(8,128)(2,1)S(1)} collective-permute-done((bf16[144,256]{1,0:T(8,128)(2,1)S(1)}, bf16[144,256]{1,0:T(8,128)(2,1)S(1)}, u32[]{:S(2)}, u32[]{:S(2)}) %collective-permute-start.41) | collective-permute-done | bytes 73760 | tf_op jit(solution)/shard_map/ppermute | solution.py:19
  177.9 2.0 third.7
  179.9 2.3 %collective-permute-start.48 = (bf16[144,896]{1,0:T(8,128)(2,1)S(1)}, bf16[144,896]{1,0:T(8,128)(2,1)S(1)}, u32[]{:S(2)}, u32[]{:S(2)}) collective-permute-start(bf16[144,896]{1,0:T(8,128)(2,1)S(1)} %get-tuple-element.220), channel_id=1, source_target_pairs={{0,4},{1,5},{2,6},{3,7},{4,0},{5,1},{6,2},{7,3},{8,12},{9,13},{10,... | collective-permute-start | bytes 774152 | tf_op jit(solution)/shard_map/ppermute | solution.py:539
  183.4 2.2 %last.2 = (bf16[32,3584]{1,0:T(8,128)(2,1)S(1)}, bf16[32,3584]{1,0:T(8,128)(2,1)S(1)}) custom-call(s32[4]{0:T(128)S(1)} %pad_add_fusion.me.refs_0_, bf16[64,3584]{1,0:T(8,128)(2,1)S(1)} %get-tuple-element.164.refs_1_, f32[256,16]{1,0:T(8,128)S(1)} %get-tuple-element.115.refs_2_, bf16[144,896]{1,0:T(8,128)(2,1)S(1)} %get-tuple-element.190.refs_7_.refs_3_, ...), custom_call_target="tpu_custom_call" | custom-call | tf_op jit(solution)/shard_map/last/pallas_call | solution.py:194
  187.0 11.1 %collective-permute-done.48.refs_5_ = bf16[144,896]{1,0:T(8,128)(2,1)S(1)} collective-permute-done((bf16[144,896]{1,0:T(8,128)(2,1)S(1)}, bf16[144,896]{1,0:T(8,128)(2,1)S(1)}, u32[]{:S(2)}, u32[]{:S(2)}) %collective-permute-start.48) | collective-permute-done | bytes 258080 | tf_op jit(solution)/shard_map/ppermute | solution.py:539
  199.0 2.2 %last.3 = (bf16[32,3584]{1,0:T(8,128)(2,1)S(1)}, bf16[32,3584]{1,0:T(8,128)(2,1)S(1)}) custom-call(s32[4]{0:T(128)S(1)} %pad_add_fusion.me.refs_0_, bf16[64,3584]{1,0:T(8,128)(2,1)S(1)} %get-tuple-element.183.refs_7_.refs_1_, f32[256,16]{1,0:T(8,128)S(1)} %get-tuple-element.115.refs_2_, bf16[144,896]{1,0:T(8,128)(2,1)S(1)} %get-tuple-element.216.refs_7_.refs_3_, ...), custom_call_target="tpu_custom_call" | custom-call | tf_op jit(solution)/shard_map/last/pallas_call | solution.py:194
  204.3 3.0 %collective-permute-done.50.other = bf16[32,3584]{1,0:T(8,128)(2,1)S(1)} collective-permute-done((bf16[32,3584]{1,0:T(8,128)(2,1)S(1)}, bf16[32,3584]{1,0:T(8,128)(2,1)S(1)}, u32[]{:S(2)}, u32[]{:S(2)}) %collective-permute-start.50) | collective-permute-done | bytes 229408 | tf_op jit(solution)/shard_map/ppermute | solution.py:19
  (110 shorter events, 60.0 us)
Async XLA Ops:
  2.3 26.2 %collective-permute-start.4 = (bf16[32,3584]{1,0:T(8,128)(2,1)S(1)}, bf16[32,3584]{1,0:T(8,128)(2,1)S(1)}, u32[]{:S(2)}, u32[]{:S(2)}) collective-permute-start(bf16[32,3584]{1,0:T(8,128)(2,1)S(1)} %cut.7), channel_id=1, source_target_pairs={{0,1},{1,0},{2,3},{3,2},{4,5},{5,4},{6,7},{7,6},{8,9},{9,8},{10,11... | collective-permute-start | bytes 688136 | tf_op jit(solution)/shard_map/ppermute | solution.py:19
  6.9 9.9 %collective-permute-start = (bf16[32,3584]{1,0:T(8,128)(2,1)S(1)}, bf16[32,3584]{1,0:T(8,128)(2,1)S(1)}, u32[]{:S(2)}, u32[]{:S(2)}) collective-permute-start(bf16[32,3584]{1,0:T(8,128)(2,1)S(1)} %cut.4), channel_id=1, source_target_pairs={{0,1},{1,0},{2,3},{3,2},{4,5},{5,4},{6,7},{7,6},{8,9},{9,8},{10,11... | collective-permute-start | bytes 688136 | tf_op jit(solution)/shard_map/ppermute | solution.py:19
  8.5 7.5 %collective-permute-start.1 = (f32[16,32]{1,0:T(8,128)S(1)}, f32[16,32]{1,0:T(8,128)S(1)}, u32[]{:S(2)}, u32[]{:S(2)}) collective-permute-start(f32[16,32]{1,0:T(8,128)S(1)} %concatenate.3.own), channel_id=1, source_target_pairs={{0,1},{1,0},{2,3},{3,2},{4,5},{5,4},{6,7},{7,6},{8,9},{9,8},{10,11... | collective-permute-start | bytes 6152 | tf_op jit(solution)/shard_map/ppermute | solution.py:19
  19.1 19.9 %collective-permute-start.5 = (bf16[144,896]{1,0:T(8,128)(2,1)S(1)}, bf16[144,896]{1,0:T(8,128)(2,1)S(1)}, u32[]{:S(2)}, u32[]{:S(2)}) collective-permute-start(bf16[144,896]{1,0:T(8,128)(2,1)S(1)} %get-tuple-element.119), channel_id=1, source_target_pairs={{0,2},{1,3},{2,0},{3,1},{4,6},{5,7},{6,4},{7,5},{8,10},{9,11},{10,... | collective-permute-start | bytes 774152 | tf_op jit(solution)/shard_map/ppermute | solution.py:539
  20.9 21.1 %collective-permute-start.6 = (bf16[144,896]{1,0:T(8,128)(2,1)S(1)}, bf16[144,896]{1,0:T(8,128)(2,1)S(1)}, u32[]{:S(2)}, u32[]{:S(2)}) collective-permute-start(bf16[144,896]{1,0:T(8,128)(2,1)S(1)} %get-tuple-element.123), channel_id=1, source_target_pairs={{0,4},{1,5},{2,6},{3,7},{4,0},{5,1},{6,2},{7,3},{8,12},{9,13},{10,... | collective-permute-start | bytes 774152 | tf_op jit(solution)/shard_map/ppermute | solution.py:539
  23.5 18.5 %collective-permute-start.7 = (bf16[144,896]{1,0:T(8,128)(2,1)S(1)}, bf16[144,896]{1,0:T(8,128)(2,1)S(1)}, u32[]{:S(2)}, u32[]{:S(2)}) collective-permute-start(bf16[144,896]{1,0:T(8,128)(2,1)S(1)} %get-tuple-element.124), channel_id=1, source_target_pairs={{0,6},{1,7},{2,4},{3,5},{4,2},{5,3},{6,0},{7,1},{8,14},{9,15},{10,... | collective-permute-start | bytes 774152 | tf_op jit(solution)/shard_map/ppermute | solution.py:539
  25.1 12.6 %collective-permute-start.3 = (bf16[32,3584]{1,0:T(8,128)(2,1)S(1)}, bf16[32,3584]{1,0:T(8,128)(2,1)S(1)}, u32[]{:S(2)}, u32[]{:S(2)}) collective-permute-start(bf16[32,3584]{1,0:T(8,128)(2,1)S(1)} %cut.6), channel_id=1, source_target_pairs={{0,1},{1,0},{2,3},{3,2},{4,5},{5,4},{6,7},{7,6},{8,9},{9,8},{10,11... | collective-permute-start | bytes 688136 | tf_op jit(solution)/shard_map/ppermute | solution.py:19
  28.5 9.2 %collective-permute-start.2 = (bf16[32,3584]{1,0:T(8,128)(2,1)S(1)}, bf16[32,3584]{1,0:T(8,128)(2,1)S(1)}, u32[]{:S(2)}, u32[]{:S(2)}) collective-permute-start(bf16[32,3584]{1,0:T(8,128)(2,1)S(1)} %cut.5), channel_id=1, source_target_pairs={{0,1},{1,0},{2,3},{3,2},{4,5},{5,4},{6,7},{7,6},{8,9},{9,8},{10,11... | collective-permute-start | bytes 688136 | tf_op jit(solution)/shard_map/ppermute | solution.py:19
  38.9 27.8 %collective-permute-start.12 = (bf16[144,896]{1,0:T(8,128)(2,1)S(1)}, bf16[144,896]{1,0:T(8,128)(2,1)S(1)}, u32[]{:S(2)}, u32[]{:S(2)}) collective-permute-start(bf16[144,896]{1,0:T(8,128)(2,1)S(1)} %get-tuple-element.138), channel_id=1, source_target_pairs={{0,2},{1,3},{2,0},{3,1},{4,6},{5,7},{6,4},{7,5},{8,10},{9,11},{10,... | collective-permute-start | bytes 774152 | tf_op jit(solution)/shard_map/ppermute | solution.py:539
  42.1 24.9 %collective-permute-start.13 = (bf16[144,896]{1,0:T(8,128)(2,1)S(1)}, bf16[144,896]{1,0:T(8,128)(2,1)S(1)}, u32[]{:S(2)}, u32[]{:S(2)}) collective-permute-start(bf16[144,896]{1,0:T(8,128)(2,1)S(1)} %get-tuple-element.142), channel_id=1, source_target_pairs={{0,4},{1,5},{2,6},{3,7},{4,0},{5,1},{6,2},{7,3},{8,12},{9,13},{10,... | collective-permute-start | bytes 774152 | tf_op jit(solution)/shard_map/ppermute | solution.py:539
  47.7 19.3 %collective-permute-start.14 = (bf16[144,896]{1,0:T(8,128)(2,1)S(1)}, bf16[144,896]{1,0:T(8,128)(2,1)S(1)}, u32[]{:S(2)}, u32[]{:S(2)}) collective-permute-start(bf16[144,896]{1,0:T(8,128)(2,1)S(1)} %get-tuple-element.143), channel_id=1, source_target_pairs={{0,6},{1,7},{2,4},{3,5},{4,2},{5,3},{6,0},{7,1},{8,14},{9,15},{10,... | collective-permute-start | bytes 774152 | tf_op jit(solution)/shard_map/ppermute | solution.py:539
  50.7 7.1 %collective-permute-start.8 = (bf16[160,512]{1,0:T(8,128)(2,1)S(1)}, bf16[160,512]{1,0:T(8,128)(2,1)S(1)}, u32[]{:S(2)}, u32[]{:S(2)}) collective-permute-start(bf16[160,512]{1,0:T(8,128)(2,1)S(1)} %get-tuple-element.129), channel_id=1, source_target_pairs={{0,1},{1,0},{2,3},{3,2},{4,5},{5,4},{6,7},{7,6},{8,9},{9,8},{10,11... | collective-permute-start | bytes 491528 | tf_op jit(solution)/shard_map/ppermute | solution.py:19
  52.2 5.6 %collective-permute-start.9 = (bf16[144,512]{1,0:T(8,128)(2,1)S(1)}, bf16[144,512]{1,0:T(8,128)(2,1)S(1)}, u32[]{:S(2)}, u32[]{:S(2)}) collective-permute-start(bf16[144,512]{1,0:T(8,128)(2,1)S(1)} %get-tuple-element.130), channel_id=1, source_target_pairs={{0,1},{1,0},{2,3},{3,2},{4,5},{5,4},{6,7},{7,6},{8,9},{9,8},{10,11... | collective-permute-start | bytes 442376 | tf_op jit(solution)/shard_map/ppermute | solution.py:19
  58.8 4.4 %collective-permute-start.10 = (bf16[144,256]{1,0:T(8,128)(2,1)S(1)}, bf16[144,256]{1,0:T(8,128)(2,1)S(1)}, u32[]{:S(2)}, u32[]{:S(2)}) collective-permute-start(bf16[144,256]{1,0:T(8,128)(2,1)S(1)} %get-tuple-element.132.h0), channel_id=1, source_target_pairs={{0,1},{1,0},{2,3},{3,2},{4,5},{5,4},{6,7},{7,6},{8,9},{9,8},{10,11... | collective-permute-start | bytes 221192 | tf_op jit(solution)/shard_map/ppermute | solution.py:19
  60.4 4.4 %collective-permute-start.11 = (bf16[144,256]{1,0:T(8,128)(2,1)S(1)}, bf16[144,256]{1,0:T(8,128)(2,1)S(1)}, u32[]{:S(2)}, u32[]{:S(2)}) collective-permute-start(bf16[144,256]{1,0:T(8,128)(2,1)S(1)} %get-tuple-element.133.h1), channel_id=1, source_target_pairs={{0,1},{1,0},{2,3},{3,2},{4,5},{5,4},{6,7},{7,6},{8,9},{9,8},{10,11... | collective-permute-start | bytes 221192 | tf_op jit(solution)/shard_map/ppermute | solution.py:19
  66.7 22.5 %collective-permute-start.19 = (bf16[144,896]{1,0:T(8,128)(2,1)S(1)}, bf16[144,896]{1,0:T(8,128)(2,1)S(1)}, u32[]{:S(2)}, u32[]{:S(2)}) collective-permute-start(bf16[144,896]{1,0:T(8,128)(2,1)S(1)} %get-tuple-element.153), channel_id=1, source_target_pairs={{0,2},{1,3},{2,0},{3,1},{4,6},{5,7},{6,4},{7,5},{8,10},{9,11},{10,... | collective-permute-start | bytes 774152 | tf_op jit(solution)/shard_map/ppermute | solution.py:539
  67.0 24.3 %collective-permute-start.20 = (bf16[144,896]{1,0:T(8,128)(2,1)S(1)}, bf16[144,896]{1,0:T(8,128)(2,1)S(1)}, u32[]{:S(2)}, u32[]{:S(2)}) collective-permute-start(bf16[144,896]{1,0:T(8,128)(2,1)S(1)} %get-tuple-element.157), channel_id=1, source_target_pairs={{0,4},{1,5},{2,6},{3,7},{4,0},{5,1},{6,2},{7,3},{8,12},{9,13},{10,... | collective-permute-start | bytes 774152 | tf_op jit(solution)/shard_map/ppermute | solution.py:539
  71.4 19.9 %collective-permute-start.21 = (bf16[144,896]{1,0:T(8,128)(2,1)S(1)}, bf16[144,896]{1,0:T(8,128)(2,1)S(1)}, u32[]{:S(2)}, u32[]{:S(2)}) collective-permute-start(bf16[144,896]{1,0:T(8,128)(2,1)S(1)} %get-tuple-element.158), channel_id=1, source_target_pairs={{0,6},{1,7},{2,4},{3,5},{4,2},{5,3},{6,0},{7,1},{8,14},{9,15},{10,... | collective-permute-start | bytes 774152 | tf_op jit(solution)/shard_map/ppermute | solution.py:539
  73.9 7.0 %collective-permute-start.15 = (bf16[160,512]{1,0:T(8,128)(2,1)S(1)}, bf16[160,512]{1,0:T(8,128)(2,1)S(1)}, u32[]{:S(2)}, u32[]{:S(2)}) collective-permute-start(bf16[160,512]{1,0:T(8,128)(2,1)S(1)} %get-tuple-element.147), channel_id=1, source_target_pairs={{0,1},{1,0},{2,3},{3,2},{4,5},{5,4},{6,7},{7,6},{8,9},{9,8},{10,11... | collective-permute-start | bytes 491528 | tf_op jit(solution)/shard_map/ppermute | solution.py:19
  74.7 6.1 %collective-permute-start.16 = (bf16[144,512]{1,0:T(8,128)(2,1)S(1)}, bf16[144,512]{1,0:T(8,128)(2,1)S(1)}, u32[]{:S(2)}, u32[]{:S(2)}) collective-permute-start(bf16[144,512]{1,0:T(8,128)(2,1)S(1)} %get-tuple-element.148), channel_id=1, source_target_pairs={{0,1},{1,0},{2,3},{3,2},{4,5},{5,4},{6,7},{7,6},{8,9},{9,8},{10,11... | collective-permute-start | bytes 442376 | tf_op jit(solution)/shard_map/ppermute | solution.py:19
  81.8 4.4 %collective-permute-start.17 = (bf16[144,256]{1,0:T(8,128)(2,1)S(1)}, bf16[144,256]{1,0:T(8,128)(2,1)S(1)}, u32[]{:S(2)}, u32[]{:S(2)}) collective-permute-start(bf16[144,256]{1,0:T(8,128)(2,1)S(1)} %get-tuple-element.150.h0), channel_id=1, source_target_pairs={{0,1},{1,0},{2,3},{3,2},{4,5},{5,4},{6,7},{7,6},{8,9},{9,8},{10,11... | collective-permute-start | bytes 221192 | tf_op jit(solution)/shard_map/ppermute | solution.py:19
  82.9 4.4 %collective-permute-start.18 = (bf16[144,256]{1,0:T(8,128)(2,1)S(1)}, bf16[144,256]{1,0:T(8,128)(2,1)S(1)}, u32[]{:S(2)}, u32[]{:S(2)}) collective-permute-start(bf16[144,256]{1,0:T(8,128)(2,1)S(1)} %get-tuple-element.151.h1), channel_id=1, source_target_pairs={{0,1},{1,0},{2,3},{3,2},{4,5},{5,4},{6,7},{7,6},{8,9},{9,8},{10,11... | collective-permute-start | bytes 221192 | tf_op jit(solution)/shard_map/ppermute | solution.py:19
  89.2 15.8 %collective-permute-start.24 = (bf16[144,896]{1,0:T(8,128)(2,1)S(1)}, bf16[144,896]{1,0:T(8,128)(2,1)S(1)}, u32[]{:S(2)}, u32[]{:S(2)}) collective-permute-start(bf16[144,896]{1,0:T(8,128)(2,1)S(1)} %get-tuple-element.166), channel_id=1, source_target_pairs={{0,2},{1,3},{2,0},{3,1},{4,6},{5,7},{6,4},{7,5},{8,10},{9,11},{10,... | collective-permute-start | bytes 774152 | tf_op jit(solution)/shard_map/ppermute | solution.py:539
  91.3 18.2 %collective-permute-start.25 = (bf16[144,896]{1,0:T(8,128)(2,1)S(1)}, bf16[144,896]{1,0:T(8,128)(2,1)S(1)}, u32[]{:S(2)}, u32[]{:S(2)}) collective-permute-start(bf16[144,896]{1,0:T(8,128)(2,1)S(1)} %get-tuple-element.167), channel_id=1, source_target_pairs={{0,4},{1,5},{2,6},{3,7},{4,0},{5,1},{6,2},{7,3},{8,12},{9,13},{10,... | collective-permute-start | bytes 774152 | tf_op jit(solution)/shard_map/ppermute | solution.py:539
  95.0 14.5 %collective-permute-start.26 = (bf16[144,896]{1,0:T(8,128)(2,1)S(1)}, bf16[144,896]{1,0:T(8,128)(2,1)S(1)}, u32[]{:S(2)}, u32[]{:S(2)}) collective-permute-start(bf16[144,896]{1,0:T(8,128)(2,1)S(1)} %get-tuple-element.168), channel_id=1, source_target_pairs={{0,6},{1,7},{2,4},{3,5},{4,2},{5,3},{6,0},{7,1},{8,14},{9,15},{10,... | collective-permute-start | bytes 774152 | tf_op jit(solution)/shard_map/ppermute | solution.py:539
  97.2 5.7 %collective-permute-start.22 = (bf16[32,3584]{1,0:T(8,128)(2,1)S(1)}, bf16[32,3584]{1,0:T(8,128)(2,1)S(1)}, u32[]{:S(2)}, u32[]{:S(2)}) collective-permute-start(bf16[32,3584]{1,0:T(8,128)(2,1)S(1)} %get-tuple-element.162), channel_id=1, source_target_pairs={{0,8},{8,16},{16,24},{1,9},{9,17},{17,25},{2,10},{10,18},{18,26},{... | collective-permute-start | bytes 688136 | tf_op jit(solution)/shard_map/ppermute | solution.py:25
  98.6 5.3 %collective-permute-start.23 = (bf16[32,3584]{1,0:T(8,128)(2,1)S(1)}, bf16[32,3584]{1,0:T(8,128)(2,1)S(1)}, u32[]{:S(2)}, u32[]{:S(2)}) collective-permute-start(bf16[32,3584]{1,0:T(8,128)(2,1)S(1)} %get-tuple-element.163), channel_id=1, source_target_pairs={{0,8},{8,16},{16,24},{1,9},{9,17},{17,25},{2,10},{10,18},{18,26},{... | collective-permute-start | bytes 688136 | tf_op jit(solution)/shard_map/ppermute | solution.py:25
  105.1 19.4 %collective-permute-start.29 = (bf16[144,896]{1,0:T(8,128)(2,1)S(1)}, bf16[144,896]{1,0:T(8,128)(2,1)S(1)}, u32[]{:S(2)}, u32[]{:S(2)}) collective-permute-start(bf16[144,896]{1,0:T(8,128)(2,1)S(1)} %get-tuple-element.173), channel_id=1, source_target_pairs={{0,2},{1,3},{2,0},{3,1},{4,6},{5,7},{6,4},{7,5},{8,10},{9,11},{10,... | collective-permute-start | bytes 774152 | tf_op jit(solution)/shard_map/ppermute | solution.py:539
  109.5 22.8 %collective-permute-start.30 = (bf16[144,896]{1,0:T(8,128)(2,1)S(1)}, bf16[144,896]{1,0:T(8,128)(2,1)S(1)}, u32[]{:S(2)}, u32[]{:S(2)}) collective-permute-start(bf16[144,896]{1,0:T(8,128)(2,1)S(1)} %get-tuple-element.179), channel_id=1, source_target_pairs={{0,4},{1,5},{2,6},{3,7},{4,0},{5,1},{6,2},{7,3},{8,12},{9,13},{10,... | collective-permute-start | bytes 774152 | tf_op jit(solution)/shard_map/ppermute | solution.py:539
  114.1 18.2 %collective-permute-start.31 = (bf16[144,896]{1,0:T(8,128)(2,1)S(1)}, bf16[144,896]{1,0:T(8,128)(2,1)S(1)}, u32[]{:S(2)}, u32[]{:S(2)}) collective-permute-start(bf16[144,896]{1,0:T(8,128)(2,1)S(1)} %get-tuple-element.180), channel_id=1, source_target_pairs={{0,6},{1,7},{2,4},{3,5},{4,2},{5,3},{6,0},{7,1},{8,14},{9,15},{10,... | collective-permute-start | bytes 774152 | tf_op jit(solution)/shard_map/ppermute | solution.py:539
  124.5 33.1 %collective-permute-start.36 = (bf16[144,896]{1,0:T(8,128)(2,1)S(1)}, bf16[144,896]{1,0:T(8,128)(2,1)S(1)}, u32[]{:S(2)}, u32[]{:S(2)}) collective-permute-start(bf16[144,896]{1,0:T(8,128)(2,1)S(1)} %get-tuple-element.193), channel_id=1, source_target_pairs={{0,2},{1,3},{2,0},{3,1},{4,6},{5,7},{6,4},{7,5},{8,10},{9,11},{10,... | collective-permute-start | bytes 774152 | tf_op jit(solution)/shard_map/ppermute | solution.py:539
  132.3 25.3 %collective-permute-start.37 = (bf16[144,896]{1,0:T(8,128)(2,1)S(1)}, bf16[144,896]{1,0:T(8,128)(2,1)S(1)}, u32[]{:S(2)}, u32[]{:S(2)}) collective-permute-start(bf16[144,896]{1,0:T(8,128)(2,1)S(1)} %get-tuple-element.197), channel_id=1, source_target_pairs={{0,4},{1,5},{2,6},{3,7},{4,0},{5,1},{6,2},{7,3},{8,12},{9,13},{10,... | collective-permute-start | bytes 774152 | tf_op jit(solution)/shard_map/ppermute | solution.py:539
  136.3 21.3 %collective-permute-start.38 = (bf16[144,896]{1,0:T(8,128)(2,1)S(1)}, bf16[144,896]{1,0:T(8,128)(2,1)S(1)}, u32[]{:S(2)}, u32[]{:S(2)}) collective-permute-start(bf16[144,896]{1,0:T(8,128)(2,1)S(1)} %get-tuple-element.198), channel_id=1, source_target_pairs={{0,6},{1,7},{2,4},{3,5},{4,2},{5,3},{6,0},{7,1},{8,14},{9,15},{10,... | collective-permute-start | bytes 774152 | tf_op jit(solution)/shard_map/ppermute | solution.py:539
  141.0 7.4 %collective-permute-start.32 = (bf16[160,512]{1,0:T(8,128)(2,1)S(1)}, bf16[160,512]{1,0:T(8,128)(2,1)S(1)}, u32[]{:S(2)}, u32[]{:S(2)}) collective-permute-start(bf16[160,512]{1,0:T(8,128)(2,1)S(1)} %get-tuple-element.185), channel_id=1, source_target_pairs={{0,1},{1,0},{2,3},{3,2},{4,5},{5,4},{6,7},{7,6},{8,9},{9,8},{10,11... | collective-permute-start | bytes 491528 | tf_op jit(solution)/shard_map/ppermute | solution.py:19
  142.6 5.7 %collective-permute-start.33 = (bf16[144,512]{1,0:T(8,128)(2,1)S(1)}, bf16[144,512]{1,0:T(8,128)(2,1)S(1)}, u32[]{:S(2)}, u32[]{:S(2)}) collective-permute-start(bf16[144,512]{1,0:T(8,128)(2,1)S(1)} %get-tuple-element.186), channel_id=1, source_target_pairs={{0,1},{1,0},{2,3},{3,2},{4,5},{5,4},{6,7},{7,6},{8,9},{9,8},{10,11... | collective-permute-start | bytes 442376 | tf_op jit(solution)/shard_map/ppermute | solution.py:19
  149.4 4.4 %collective-permute-start.34 = (bf16[144,256]{1,0:T(8,128)(2,1)S(1)}, bf16[144,256]{1,0:T(8,128)(2,1)S(1)}, u32[]{:S(2)}, u32[]{:S(2)}) collective-permute-start(bf16[144,256]{1,0:T(8,128)(2,1)S(1)} %get-tuple-element.188.h0), channel_id=1, source_target_pairs={{0,1},{1,0},{2,3},{3,2},{4,5},{5,4},{6,7},{7,6},{8,9},{9,8},{10,11... | collective-permute-start | bytes 221192 | tf_op jit(solution)/shard_map/ppermute | solution.py:19
  157.6 22.3 %collective-permute-start.43 = (bf16[144,896]{1,0:T(8,128)(2,1)S(1)}, bf16[144,896]{1,0:T(8,128)(2,1)S(1)}, u32[]{:S(2)}, u32[]{:S(2)}) collective-permute-start(bf16[144,896]{1,0:T(8,128)(2,1)S(1)} %get-tuple-element.208), channel_id=1, source_target_pairs={{0,2},{1,3},{2,0},{3,1},{4,6},{5,7},{6,4},{7,5},{8,10},{9,11},{10,... | collective-permute-start | bytes 774152 | tf_op jit(solution)/shard_map/ppermute | solution.py:539
  157.7 22.2 %collective-permute-start.44 = (bf16[144,896]{1,0:T(8,128)(2,1)S(1)}, bf16[144,896]{1,0:T(8,128)(2,1)S(1)}, u32[]{:S(2)}, u32[]{:S(2)}) collective-permute-start(bf16[144,896]{1,0:T(8,128)(2,1)S(1)} %get-tuple-element.212), channel_id=1, source_target_pairs={{0,4},{1,5},{2,6},{3,7},{4,0},{5,1},{6,2},{7,3},{8,12},{9,13},{10,... | collective-permute-start | bytes 774152 | tf_op jit(solution)/shard_map/ppermute | solution.py:539
  159.4 20.5 %collective-permute-start.45 = (bf16[144,896]{1,0:T(8,128)(2,1)S(1)}, bf16[144,896]{1,0:T(8,128)(2,1)S(1)}, u32[]{:S(2)}, u32[]{:S(2)}) collective-permute-start(bf16[144,896]{1,0:T(8,128)(2,1)S(1)} %get-tuple-element.213), channel_id=1, source_target_pairs={{0,6},{1,7},{2,4},{3,5},{4,2},{5,3},{6,0},{7,1},{8,14},{9,15},{10,... | collective-permute-start | bytes 774152 | tf_op jit(solution)/shard_map/ppermute | solution.py:539
  164.3 7.4 %collective-permute-start.39 = (bf16[160,512]{1,0:T(8,128)(2,1)S(1)}, bf16[160,512]{1,0:T(8,128)(2,1)S(1)}, u32[]{:S(2)}, u32[]{:S(2)}) collective-permute-start(bf16[160,512]{1,0:T(8,128)(2,1)S(1)} %get-tuple-element.202), channel_id=1, source_target_pairs={{0,1},{1,0},{2,3},{3,2},{4,5},{5,4},{6,7},{7,6},{8,9},{9,8},{10,11... | collective-permute-start | bytes 491528 | tf_op jit(solution)/shard_map/ppermute | solution.py:19
  165.2 6.5 %collective-permute-start.40 = (bf16[144,512]{1,0:T(8,128)(2,1)S(1)}, bf16[144,512]{1,0:T(8,128)(2,1)S(1)}, u32[]{:S(2)}, u32[]{:S(2)}) collective-permute-start(bf16[144,512]{1,0:T(8,128)(2,1)S(1)} %get-tuple-element.203), channel_id=1, source_target_pairs={{0,1},{1,0},{2,3},{3,2},{4,5},{5,4},{6,7},{7,6},{8,9},{9,8},{10,11... | collective-permute-start | bytes 442376 | tf_op jit(solution)/shard_map/ppermute | solution.py:19
  172.7 4.4 %collective-permute-start.41 = (bf16[144,256]{1,0:T(8,128)(2,1)S(1)}, bf16[144,256]{1,0:T(8,128)(2,1)S(1)}, u32[]{:S(2)}, u32[]{:S(2)}) collective-permute-start(bf16[144,256]{1,0:T(8,128)(2,1)S(1)} %get-tuple-element.205.h0), channel_id=1, source_target_pairs={{0,1},{1,0},{2,3},{3,2},{4,5},{5,4},{6,7},{7,6},{8,9},{9,8},{10,11... | collective-permute-start | bytes 221192 | tf_op jit(solution)/shard_map/ppermute | solution.py:19
  173.1 4.8 %collective-permute-start.42 = (bf16[144,256]{1,0:T(8,128)(2,1)S(1)}, bf16[144,256]{1,0:T(8,128)(2,1)S(1)}, u32[]{:S(2)}, u32[]{:S(2)}) collective-permute-start(bf16[144,256]{1,0:T(8,128)(2,1)S(1)} %get-tuple-element.206.h1), channel_id=1, source_target_pairs={{0,1},{1,0},{2,3},{3,2},{4,5},{5,4},{6,7},{7,6},{8,9},{9,8},{10,11... | collective-permute-start | bytes 221192 | tf_op jit(solution)/shard_map/ppermute | solution.py:19
  179.9 18.2 %collective-permute-start.48 = (bf16[144,896]{1,0:T(8,128)(2,1)S(1)}, bf16[144,896]{1,0:T(8,128)(2,1)S(1)}, u32[]{:S(2)}, u32[]{:S(2)}) collective-permute-start(bf16[144,896]{1,0:T(8,128)(2,1)S(1)} %get-tuple-element.220), channel_id=1, source_target_pairs={{0,4},{1,5},{2,6},{3,7},{4,0},{5,1},{6,2},{7,3},{8,12},{9,13},{10,... | collective-permute-start | bytes 774152 | tf_op jit(solution)/shard_map/ppermute | solution.py:539
  182.2 15.9 %collective-permute-start.49 = (bf16[144,896]{1,0:T(8,128)(2,1)S(1)}, bf16[144,896]{1,0:T(8,128)(2,1)S(1)}, u32[]{:S(2)}, u32[]{:S(2)}) collective-permute-start(bf16[144,896]{1,0:T(8,128)(2,1)S(1)} %get-tuple-element.221), channel_id=1, source_target_pairs={{0,6},{1,7},{2,4},{3,5},{4,2},{5,3},{6,0},{7,1},{8,14},{9,15},{10,... | collective-permute-start | bytes 774152 | tf_op jit(solution)/shard_map/ppermute | solution.py:539
  182.7 16.3 %collective-permute-start.47 = (bf16[144,896]{1,0:T(8,128)(2,1)S(1)}, bf16[144,896]{1,0:T(8,128)(2,1)S(1)}, u32[]{:S(2)}, u32[]{:S(2)}) collective-permute-start(bf16[144,896]{1,0:T(8,128)(2,1)S(1)} %get-tuple-element.219), channel_id=1, source_target_pairs={{0,2},{1,3},{2,0},{3,1},{4,6},{5,7},{6,4},{7,5},{8,10},{9,11},{10,... | collective-permute-start | bytes 774152 | tf_op jit(solution)/shard_map/ppermute | solution.py:539
  185.7 17.3 %collective-permute-start.46 = (bf16[32,3584]{1,0:T(8,128)(2,1)S(1)}, bf16[32,3584]{1,0:T(8,128)(2,1)S(1)}, u32[]{:S(2)}, u32[]{:S(2)}) collective-permute-start(bf16[32,3584]{1,0:T(8,128)(2,1)S(1)} %get-tuple-element.218), channel_id=1, source_target_pairs={{0,1},{1,0},{2,3},{3,2},{4,5},{5,4},{6,7},{7,6},{8,9},{9,8},{10,11... | collective-permute-start | bytes 688136 | tf_op jit(solution)/shard_map/ppermute | solution.py:19
  201.2 6.1 %collective-permute-start.50 = (bf16[32,3584]{1,0:T(8,128)(2,1)S(1)}, bf16[32,3584]{1,0:T(8,128)(2,1)S(1)}, u32[]{:S(2)}, u32[]{:S(2)}) collective-permute-start(bf16[32,3584]{1,0:T(8,128)(2,1)S(1)} %get-tuple-element.223), channel_id=1, source_target_pairs={{0,1},{1,0},{2,3},{3,2},{4,5},{5,4},{6,7},{7,6},{8,9},{9,8},{10,11... | collective-permute-start | bytes 688136 | tf_op jit(solution)/shard_map/ppermute | solution.py:19
  (13 other events, 149.4 us)

commit v5 on v4

--- a/solution.py
+++ b/solution.py
@@ -230,14 +230,19 @@
     return high, middle, (rest - middle.astype(jnp.float32)).astype(jnp.bfloat16)
 
 
-def cut_kernel(me, batch, sent):
+def cut_kernel(me, batch, kept, sent):
     half = sent.shape[1]
+    kept[...] = batch[:, pl.ds(pl.multiple_of(me[1] * half, half), half)]
     sent[...] = batch[:, pl.ds(pl.multiple_of((1 - me[1]) * half, half), half)]
 
 
-def cut(me, batch):
+def cut(me, batch, after=()):
     rows, model_width = batch.shape
-    return call(cut_kernel, "cut", bf16(rows, model_width // 2), me, batch)
+    return call(cut_kernel, "cut", [bf16(rows, model_width // 2)] * 2, me, batch, after=after)
+
+
+def crossed(halves):
+    return halves[0], partner(halves[1], "expert", 0)
 
 
 def tables_kernel(me, own, other, as_rows, as_columns):
@@ -267,10 +272,9 @@
     return call(tables_kernel, "tables", [f32(kinds, total), f32(total, kinds)], me, own, other)
 
 
-def joined(me, batch, other, state):
-    rows, half = other.shape
-    kept = batch[:, pl.ds(pl.multiple_of(me[1] * half, half), half)]
-    state[pl.ds(pl.multiple_of(me[1] * rows, rows), rows), :] = kept
+def joined(me, kept, other, state):
+    rows = kept.shape[0]
+    state[pl.ds(pl.multiple_of(me[1] * rows, rows), rows), :] = kept[...]
     state[pl.ds(pl.multiple_of((1 - me[1]) * rows, rows), rows), :] = other[...]
 
 
@@ -297,18 +301,18 @@
         outs[apart][...] = matmul(ones_where(hit), stacked[...]).astype(jnp.bfloat16)
 
 
-def enter_kernel(turn, me, batch, other, table, o0, o1, o2, o3, state, stacked):
-    joined(me, batch, other, state)
+def enter_kernel(turn, me, kept, other, table, o0, o1, o2, o3, state, stacked):
+    joined(me, kept, other, state)
     packed(me, state, table, turn, (o0, o1, o2, o3), stacked)
 
 
-def relay_kernel(turn, edge, me, moved, moved_rest, batch, other, table, o0, o1, o2, o3, state, stacked):
+def relay_kernel(turn, edge, me, moved, moved_rest, kept, other, table, o0, o1, o2, o3, state, stacked):
     state[:moved.shape[0], :] = moved[...]
     state[moved.shape[0]:, :] = moved_rest[...]
 
     @pl.when(me[2 + edge] == 1)
     def _():
-        joined(me, batch, other, state)
+        joined(me, kept, other, state)
 
     packed(me, state, table, turn, (o0, o1, o2, o3), stacked)
 
@@ -319,16 +323,16 @@
     return outs, [pltpu.VMEM((PARTS * 2 * rows, width), jnp.bfloat16)]
 
 
-def enter(me, turn, batch, other, table, after):
+def enter(me, turn, kept, other, table, after):
     outs, scratch = pack_shapes(*other.shape)
-    made = call(functools.partial(enter_kernel, turn), "enter", outs, me, batch, other, table, after=after, scratch=scratch)
+    made = call(functools.partial(enter_kernel, turn), "enter", outs, me, kept, other, table, after=after, scratch=scratch)
     return made[:EXPERTS], made[EXPERTS]
 
 
-def relay(me, turn, edge, moved, batch, other, table):
+def relay(me, turn, edge, moved, kept, other, table):
     outs, scratch = pack_shapes(*other.shape)
     kernel = functools.partial(relay_kernel, turn, edge)
-    made = call(kernel, "relay", outs, me, *moved, batch, other, table, scratch=scratch)
+    made = call(kernel, "relay", outs, me, *moved, kept, other, table, scratch=scratch)
     return made[:EXPERTS], made[EXPERTS]
 
 
@@ -458,10 +462,8 @@
     return call(third_kernel, "third", outs, me, *hidden, *hidden_other, weight, scratch=scratch)
 
 
-def mixed_parts(me, table, turn, received, tokens):
-    rows = tokens // 2
-    width = received[0].shape[1]
-    total = PARTS * tokens
+def spread_gates(me, table, turn, rows, start):
+    total = table.shape[0]
     slots = 2 * CAP
     expert = me[0] ^ iota((total, 128), 1)
     chosen = table[:, 4 * turn:4 * turn + 2].astype(jnp.int32)
@@ -473,17 +475,28 @@
         iota((total, total), 0) > iota((total, total), 1)
     )
     before = matmul(ones_where(earlier), ones_where(named))
-    line = iota((total, 128), 0)
-    start = line // tokens * slots + line // rows % 2 * CAP
     place = jnp.where(named, start + before.astype(jnp.int32), -1)
-    mixed = jnp.zeros((total, width), jnp.float32)
-    for apart, ref in enumerate(received):
+    spreads = []
+    for apart in range(EXPERTS):
         hit = iota((total, PARTS * slots), 1) == place[:, apart:apart + 1]
-        spread = jnp.where(hit, weight[:, apart:apart + 1], 0.0)
+        spreads.append(jnp.where(hit, weight[:, apart:apart + 1], 0.0))
+    return spreads
+
+
+def combined(spreads, received):
+    mixed = jnp.zeros((spreads[0].shape[0], received[0].shape[1]), jnp.float32)
+    for spread, ref in zip(spreads, received):
         high = spread.astype(jnp.bfloat16)
         low = (spread - high.astype(jnp.float32)).astype(jnp.bfloat16)
         mixed = mixed + matmul(high, ref[...]) + matmul(low, ref[...])
     return mixed
+
+
+def mixed_parts(me, table, turn, received, tokens):
+    rows = tokens // 2
+    line = iota((PARTS * tokens, 128), 0)
+    start = line // tokens * 2 * CAP + line // rows % 2 * CAP
+    return combined(spread_gates(me, table, turn, rows, start), received)
 
 
 def mix_kernel(turn, me, state, table, r0, r1, r2, r3, out):
@@ -511,18 +524,30 @@
     return call(kernel, "mix", outs, me, state, table, *received, after=after, scratch=scratch)
 
 
-def last_kernel(turn, me, state, table, r0, r1, r2, r3, kept, sent, result):
-    rows = kept.shape[0]
-    mix_kernel(turn, me, state, table, r0, r1, r2, r3, result)
-    kept[...] = result[pl.ds(pl.multiple_of(me[1] * rows, rows), rows), :]
-    sent[...] = result[pl.ds(pl.multiple_of((1 - me[1]) * rows, rows), rows), :]
-
-
-def last(me, turn, state, table, received, after):
+def last_kernel(turn, side, me, state, table, r0, r1, r2, r3, out, lines):
+    rows, half = out.shape
+    width = r0.shape[1]
+    slots = 2 * CAP
+    total = PARTS * rows
+    source = me[1] ^ side
+    for part in range(PARTS):
+        start = pl.multiple_of((2 * part + source) * rows, rows)
+        lines[part * rows:(part + 1) * rows, :] = table[pl.ds(start, rows), :]
+    spreads = spread_gates(me, lines, turn, rows, iota((total, 128), 0) // rows * slots + source * CAP)
+    mixed = combined(spreads, (r0, r1, r2, r3))
+    start = pl.multiple_of(source * rows, rows)
+    for part in range(PARTS):
+        span = slice(part * width, (part + 1) * width)
+        values = state[pl.ds(start, rows), span].astype(jnp.float32)
+        out[:, span] = (values + mixed[part * rows:(part + 1) * rows, :]).astype(jnp.bfloat16)
+
+
+def last(me, turn, side, state, table, received, after):
     tokens, half = state.shape
-    outs = [bf16(tokens // 2, half)] * 2
-    scratch = [pltpu.VMEM(state.shape, jnp.bfloat16)]
-    return call(functools.partial(last_kernel, turn), "last", outs, me, state, table, *received, after=after, scratch=scratch)
+    rows = tokens // 2
+    scratch = [pltpu.VMEM((PARTS * rows, table.shape[1]), jnp.float32)]
+    kernel = functools.partial(last_kernel, turn, side)
+    return call(kernel, "last", bf16(rows, half), me, state, table, *received, after=after, scratch=scratch)
 
 
 def finish_kernel(me, kept, other, out):
@@ -539,13 +564,12 @@
     return lax.ppermute(block, "expert", [(i, i ^ 2 * apart) for i in range(lax.axis_size("expert"))])
 
 
-def across(blocks, behind=None):
+def across(blocks, behind=None, hold=False):
     own, near, two, three = blocks
     if behind is not None:
         two, three, *behind[2:] = lax.optimization_barrier((two, three, *behind[2:]))
         near, behind[1] = lax.optimization_barrier((near, behind[1]))
-    two, three = along(two, 2), along(three, 3)
-    return [own, along(near, 1), two, three]
+    return [own, along(near, 1), along(two, 2), three if hold else along(three, 3)]
 
 
 def paired_shards(
@@ -577,9 +601,9 @@
 
     batches = [east_batch[0], west_batch[0]]
     entering = [east_entering[0], west_entering[0]]
-    batches_other = [partner(cut(me, batch), "expert", 0) for batch in batches]
+    east_halves = cut(me, batches[0])
     as_rows, as_columns = tables(me, lists, partner(lists, "expert", 0))
-    entering_other = [partner(cut(me, batch), "expert", 0) for batch in entering]
+    east_halves = crossed(east_halves)
     moved = [None, None]
     results = [None, None]
     states = [None, None]
@@ -590,36 +614,45 @@
         for stream in range(2):
             turn = stream * TICKS + tick
             if tick == 0:
-                after = []
+                after, west_halves = [], None
                 if stream == 1:
+                    west_halves = crossed(cut(me, batches[1], [states[0]]))
+                    entering_halves = [crossed(cut(me, batch, [states[0]])) for batch in entering]
                     weight_in, weight_out = load(me, expert_in[0, 0], expert_down[0, 0], [states[0]])
-                    after = [weight_in, *entering_other]
-                sent, states[stream] = enter(me, turn, batches[stream], batches_other[stream], as_rows, after)
+                    after = [weight_in]
+                sent, states[stream] = enter(me, turn, *(east_halves, west_halves)[stream], as_rows, after)
             else:
                 sent, states[stream] = relay(
-                    me, turn, stream, moved[stream], entering[stream], entering_other[stream], as_rows
+                    me, turn, stream, moved[stream], *entering_halves[stream], as_rows
                 )
                 if stream == 0:
                     pieces_now = mix(me, turn_before, state_before, as_columns, ahead, [sent[0]])
                     moved[1] = [shifted(piece, "pipe", -1) for piece in pieces_now]
-            arrived[stream] = across(sent, ahead)
+            arrived[stream] = across(sent, ahead, stream == 1)
             ahead = arrived[stream]
         behind = states[1]
+        crossings = [halves[1] for halves in entering_halves] if tick == 0 else []
         for stream in range(2):
             turn = stream * TICKS + tick
-            gates, ups, scaled, squares = first(me, arrived[stream], norm_gain, weight_in, [behind])
+            gates, ups, scaled, squares = first(me, arrived[stream], norm_gain, weight_in, [behind, *crossings])
+            crossings = []
+            held = arrived[1 - stream]
+            scaled, held[3] = lax.optimization_barrier((scaled, held[3]))
+            held[3] = along(held[3], 3)
             gates, ups = partner(gates, "expert", 0), partner(ups, "expert", 0)
             own = own_half(me, scaled, weight_in)
             hidden = act(me, own, gates, ups, squares, model_width)
             result = third(me, hidden, [partner(half, "expert", 0) for half in hidden], weight_out)
             behind = result[0]
-            arrived[stream] = across(result, ahead)
+            arrived[stream] = across(result, ahead, stream == 0)
             ahead = arrived[stream]
         if final:
             for stream in range(2):
                 turn = stream * TICKS + tick
-                kept, sent = last(me, turn, states[stream], as_columns, arrived[stream], [behind])
-                results[stream] = finish(me, kept, partner(sent, "expert", 0))
+                sent = last(me, turn, 1, states[stream], as_columns, arrived[stream], [behind])
+                other = partner(sent, "expert", 0)
+                kept = last(me, turn, 0, states[stream], as_columns, arrived[stream], [sent])
+                results[stream] = finish(me, kept, other)
         else:
             pieces_now = mix(me, tick, states[0], as_columns, arrived[0], [behind])
             moved[0] = [shifted(piece, "pipe", 1) for piece in pieces_now]

time: 212 us -> 208 us (0.981)
  starting transfers between devices: 78.5 us -> 76 us
  waiting for transfers between devices: 65.3 us -> 63 us
    ppermute x23, waiting for transfers between devices: 36 us -> 33.7 us  [partner(): lax.ppermute(shard, axis, [(i, i ^ 1 << apart) for i in range(lax.axis_si...]
    pallas_call x31 -> x33, Pallas kernels: 48.3 us -> 50.1 us  [call(): pl.pallas_call(kernel, out_shape=out_shape, in_specs=[pl.BlockSpec(memory...]
    unnamed x20 -> x12, local copies, waits for them, and re-layouts: 8.19 us -> 7.16 us
where the time goes in v5:
time: 208 us; the launch traced here: 205 us
  starting transfers between devices  76 us (37%)
  waiting for transfers between devices  63 us (30%)
  Pallas kernels  55.9 us (27%)
  local copies, waits for them, and re-layouts  7.93 us (4%)
    pallas_call x33, Pallas kernels, call(): pl.pallas_call(kernel, out_shape=out_shape, in_specs=[pl.BlockSpec(memory...  50.1 us
    ppermute x24, starting transfers between devices, along(): lax.ppermute(block, 'expert', [(i, i ^ 2 * apart) for i in range(lax.axis...  42.9 us
    ppermute x23, waiting for transfers between devices, partner(): lax.ppermute(shard, axis, [(i, i ^ 1 << apart) for i in range(lax.axis_si...  33.7 us
    ppermute x24, waiting for transfers between devices, along(): lax.ppermute(block, 'expert', [(i, i ^ 2 * apart) for i in range(lax.axis...  25.5 us
    ppermute x23, starting transfers between devices, partner(): lax.ppermute(shard, axis, [(i, i ^ 1 << apart) for i in range(lax.axis_si...  25.1 us
    ppermute x4, starting transfers between devices, shifted(): return lax.ppermute(block, axis, route)  8.03 us
    unnamed x12, local copies, waits for them, and re-layouts  7.16 us
    pallas_call x1, Pallas kernels, load(): pl.pallas_call(kernel, out_shape=[bf16(*array.shape) for array in arrays]...  5.73 us
  transfers between devices with their start and end apart: 51, of which 22 were waited for; matrix products, arithmetic and copies ran while one was open for 1% of the time, Pallas kernels for 25%

profile of v5, /device:TPU:0, one launch (start us, length us, event | category | flops | bytes accessed | tf_op | source)
XLA Modules:
  0.0 204.7 jit_solution(9041634458625666115)
XLA Ops:
  2.3 3.0 %collective-permute-start = (bf16[32,3584]{1,0:T(8,128)(2,1)S(1)}, bf16[32,3584]{1,0:T(8,128)(2,1)S(1)}, u32[]{:S(2)}, u32[]{:S(2)}) collective-permute-start(bf16[32,3584]{1,0:T(8,128)(2,1)S(1)} %get-tuple-element.126), channel_id=1, source_target_pairs={{0,1},{1,0},{2,3},{3,2},{4,5},{5,4},{6,7},{7,6},{8,9},{9,8},{10,11... | collective-permute-start | bytes 688136 | tf_op jit(solution)/shard_map/ppermute | solution.py:19
  6.9 4.2 %collective-permute-done.1.other = f32[16,32]{1,0:T(8,128)S(1)} collective-permute-done((f32[16,32]{1,0:T(8,128)S(1)}, f32[16,32]{1,0:T(8,128)S(1)}, u32[]{:S(2)}, u32[]{:S(2)}) %collective-permute-start.1) | collective-permute-done | bytes 2080 | tf_op jit(solution)/shard_map/ppermute | solution.py:19
  14.7 1.8 collective-permute-start.2
  18.1 2.6 %collective-permute-start.4 = (bf16[144,896]{1,0:T(8,128)(2,1)S(1)}, bf16[144,896]{1,0:T(8,128)(2,1)S(1)}, u32[]{:S(2)}, u32[]{:S(2)}) collective-permute-start(bf16[144,896]{1,0:T(8,128)(2,1)S(1)} %get-tuple-element.139), channel_id=1, source_target_pairs={{0,4},{1,5},{2,6},{3,7},{4,0},{5,1},{6,2},{7,3},{8,12},{9,13},{10,... | collective-permute-start | bytes 774152 | tf_op jit(solution)/shard_map/ppermute | solution.py:564
  24.5 1.8 collective-permute-start.6
  26.3 3.1 %copy-done = bf16[1,1,1024,3584]{3,2,1,0:T(8,128)(2,1)S(1)} copy-done((bf16[1,1,1024,3584]{3,2,1,0:T(8,128)(2,1)S(1)}, bf16[1,1,1024,3584]{3,2,1,0:T(8,128)(2,1)}, u32[]{:S(2)}) %copy-start) | copy-done | bytes 7340056
  29.4 5.7 %load.1 = (bf16[3584,2048]{1,0:T(8,128)(2,1)S(1)}, bf16[1024,3584]{1,0:T(8,128)(2,1)S(1)}) custom-call(s32[4]{0:T(128)S(1)} %pad_add_fusion.me.refs_0_, bf16[3584,2048]{1,0:T(8,128)(2,1)} %bitcast.49, bf16[1024,3584]{1,0:T(8,128)(2,1)S(1)} %bitcast.44, bf16[64,3584]{1,0:T(8,128)(2,1)S(1)} %get-tuple-element.128.refs_2_.refs_3_.refs_1_), custom_call_target="tpu_custom_call" | custom-call | tf_op jit(solution)/shard_map/load/pallas_call | solution.py:353
  36.3 2.9 %collective-permute-done.4.refs_3_ = bf16[144,896]{1,0:T(8,128)(2,1)S(1)} collective-permute-done((bf16[144,896]{1,0:T(8,128)(2,1)S(1)}, bf16[144,896]{1,0:T(8,128)(2,1)S(1)}, u32[]{:S(2)}, u32[]{:S(2)}) %collective-permute-start.4) | collective-permute-done | bytes 258080 | tf_op jit(solution)/shard_map/ppermute | solution.py:564
  39.2 5.6 %collective-permute-start.13 = (bf16[144,896]{1,0:T(8,128)(2,1)S(1)}, bf16[144,896]{1,0:T(8,128)(2,1)S(1)}, u32[]{:S(2)}, u32[]{:S(2)}) collective-permute-start(bf16[144,896]{1,0:T(8,128)(2,1)S(1)} %get-tuple-element.162), channel_id=1, source_target_pairs={{0,4},{1,5},{2,6},{3,7},{4,0},{5,1},{6,2},{7,3},{8,12},{9,13},{10,... | collective-permute-start | bytes 774152 | tf_op jit(solution)/shard_map/ppermute | solution.py:564
  44.9 2.5 %first.4 = (bf16[160,512]{1,0:T(8,128)(2,1)S(1)}, bf16[144,512]{1,0:T(8,128)(2,1)S(1)}, bf16[144,3584]{1,0:T(8,128)(2,1)S(1)}, f32[144,128]{1,0:T(8,128)S(1)}) custom-call(s32[4]{0:T(128)S(1)} %pad_add_fusion.me.refs_0_, bf16[144,896]{1,0:T(8,128)(2,1)S(1)} %get-tuple-element.130.refs_1_, bf16[144,896]{1,0:T(8,128)(2,1)S(1)} %collective-permute-done.3.refs_2_, ...), custom_call_target="tpu_custom_call" | custom-call | tf_op jit(solution)/shard_map/first/pallas_call | solution.py:194
  50.9 1.8 own.4
  52.7 3.9 %collective-permute-done.9.ups = bf16[144,512]{1,0:T(8,128)(2,1)S(1)} collective-permute-done((bf16[144,512]{1,0:T(8,128)(2,1)S(1)}, bf16[144,512]{1,0:T(8,128)(2,1)S(1)}, u32[]{:S(2)}, u32[]{:S(2)}) %collective-permute-start.9) | collective-permute-done | bytes 147488 | tf_op jit(solution)/shard_map/ppermute | solution.py:19
  59.8 2.3 %collective-permute-done.10.t0 = bf16[144,256]{1,0:T(8,128)(2,1)S(1)} collective-permute-done((bf16[144,256]{1,0:T(8,128)(2,1)S(1)}, bf16[144,256]{1,0:T(8,128)(2,1)S(1)}, u32[]{:S(2)}, u32[]{:S(2)}) %collective-permute-start.10) | collective-permute-done | bytes 73760 | tf_op jit(solution)/shard_map/ppermute | solution.py:19
  62.9 2.0 third.4
  64.9 2.4 %collective-permute-start.20 = (bf16[144,896]{1,0:T(8,128)(2,1)S(1)}, bf16[144,896]{1,0:T(8,128)(2,1)S(1)}, u32[]{:S(2)}, u32[]{:S(2)}) collective-permute-start(bf16[144,896]{1,0:T(8,128)(2,1)S(1)} %get-tuple-element.179), channel_id=1, source_target_pairs={{0,4},{1,5},{2,6},{3,7},{4,0},{5,1},{6,2},{7,3},{8,12},{9,13},{10,... | collective-permute-start | bytes 774152 | tf_op jit(solution)/shard_map/ppermute | solution.py:564
  67.9 2.3 %first.5 = (bf16[160,512]{1,0:T(8,128)(2,1)S(1)}, bf16[144,512]{1,0:T(8,128)(2,1)S(1)}, bf16[144,3584]{1,0:T(8,128)(2,1)S(1)}, f32[144,128]{1,0:T(8,128)S(1)}) custom-call(s32[4]{0:T(128)S(1)} %pad_add_fusion.me.refs_0_, bf16[144,896]{1,0:T(8,128)(2,1)S(1)} %get-tuple-element.156.refs_1_, bf16[144,896]{1,0:T(8,128)(2,1)S(1)} %collective-permute-done.12.refs_2_, ...), custom_call_target="tpu_custom_call" | custom-call | tf_op jit(solution)/shard_map/first/pallas_call | solution.py:194
  73.7 1.8 own.5
  75.5 3.7 %collective-permute-done.16.ups = bf16[144,512]{1,0:T(8,128)(2,1)S(1)} collective-permute-done((bf16[144,512]{1,0:T(8,128)(2,1)S(1)}, bf16[144,512]{1,0:T(8,128)(2,1)S(1)}, u32[]{:S(2)}, u32[]{:S(2)}) %collective-permute-start.16) | collective-permute-done | bytes 147488 | tf_op jit(solution)/shard_map/ppermute | solution.py:19
  80.2 2.0 collective-permute-start.17
  82.3 2.3 %collective-permute-done.17.t0 = bf16[144,256]{1,0:T(8,128)(2,1)S(1)} collective-permute-done((bf16[144,256]{1,0:T(8,128)(2,1)S(1)}, bf16[144,256]{1,0:T(8,128)(2,1)S(1)}, u32[]{:S(2)}, u32[]{:S(2)}) %collective-permute-start.17) | collective-permute-done | bytes 73760 | tf_op jit(solution)/shard_map/ppermute | solution.py:19
  84.6 1.9 collective-permute-done.18.t1
  86.6 2.0 third.5
  88.7 3.2 %collective-permute-start.25 = (bf16[144,896]{1,0:T(8,128)(2,1)S(1)}, bf16[144,896]{1,0:T(8,128)(2,1)S(1)}, u32[]{:S(2)}, u32[]{:S(2)}) collective-permute-start(bf16[144,896]{1,0:T(8,128)(2,1)S(1)} %get-tuple-element.190), channel_id=1, source_target_pairs={{0,4},{1,5},{2,6},{3,7},{4,0},{5,1},{6,2},{7,3},{8,12},{9,13},{10,... | collective-permute-start | bytes 774152 | tf_op jit(solution)/shard_map/ppermute | solution.py:564
  93.0 2.3 %mix.2 = (bf16[32,3584]{1,0:T(8,128)(2,1)S(1)}, bf16[32,3584]{1,0:T(8,128)(2,1)S(1)}) custom-call(s32[4]{0:T(128)S(1)} %pad_add_fusion.me.refs_0_, bf16[64,3584]{1,0:T(8,128)(2,1)S(1)} %get-tuple-element.128.refs_2_.refs_3_.refs_1_, f32[256,16]{1,0:T(8,128)S(1)} %get-tuple-element.129.refs_2_, bf16[144,896]{1,0:T(8,128)(2,1)S(1)} %get-tuple-element.155.refs_7_.refs_3_, ...), custom_call_target="tpu_custom_call" | custom-call | tf_op jit(solution)/shard_map/mix/pallas_call | solution.py:194
  96.6 4.1 %collective-permute-start.23 = (bf16[32,3584]{1,0:T(8,128)(2,1)S(1)}, bf16[32,3584]{1,0:T(8,128)(2,1)S(1)}, u32[]{:S(2)}, u32[]{:S(2)}) collective-permute-start(bf16[32,3584]{1,0:T(8,128)(2,1)S(1)} %get-tuple-element.185), channel_id=1, source_target_pairs={{0,8},{8,16},{16,24},{1,9},{9,17},{17,25},{2,10},{10,18},{18,26},{... | collective-permute-start | bytes 688136 | tf_op jit(solution)/shard_map/ppermute | solution.py:25
  103.4 2.7 %collective-permute-done.25.refs_5_ = bf16[144,896]{1,0:T(8,128)(2,1)S(1)} collective-permute-done((bf16[144,896]{1,0:T(8,128)(2,1)S(1)}, bf16[144,896]{1,0:T(8,128)(2,1)S(1)}, u32[]{:S(2)}, u32[]{:S(2)}) %collective-permute-start.25) | collective-permute-done | bytes 258080 | tf_op jit(solution)/shard_map/ppermute | solution.py:564
  106.1 4.8 %collective-permute-start.30 = (bf16[144,896]{1,0:T(8,128)(2,1)S(1)}, bf16[144,896]{1,0:T(8,128)(2,1)S(1)}, u32[]{:S(2)}, u32[]{:S(2)}) collective-permute-start(bf16[144,896]{1,0:T(8,128)(2,1)S(1)} %get-tuple-element.203), channel_id=1, source_target_pairs={{0,4},{1,5},{2,6},{3,7},{4,0},{5,1},{6,2},{7,3},{8,12},{9,13},{10,... | collective-permute-start | bytes 774152 | tf_op jit(solution)/shard_map/ppermute | solution.py:564
  110.9 2.1 %collective-permute-start.31 = (bf16[144,896]{1,0:T(8,128)(2,1)S(1)}, bf16[144,896]{1,0:T(8,128)(2,1)S(1)}, u32[]{:S(2)}, u32[]{:S(2)}) collective-permute-start(bf16[144,896]{1,0:T(8,128)(2,1)S(1)} %get-tuple-element.204), channel_id=1, source_target_pairs={{0,6},{1,7},{2,4},{3,5},{4,2},{5,3},{6,0},{7,1},{8,14},{9,15},{10,... | collective-permute-start | bytes 774152 | tf_op jit(solution)/shard_map/ppermute | solution.py:564
  113.0 2.3 %mix.3 = (bf16[32,3584]{1,0:T(8,128)(2,1)S(1)}, bf16[32,3584]{1,0:T(8,128)(2,1)S(1)}) custom-call(s32[4]{0:T(128)S(1)} %pad_add_fusion.me.refs_0_, bf16[64,3584]{1,0:T(8,128)(2,1)S(1)} %get-tuple-element.143.refs_7_.refs_1_, f32[256,16]{1,0:T(8,128)S(1)} %get-tuple-element.129.refs_2_, bf16[144,896]{1,0:T(8,128)(2,1)S(1)} %get-tuple-element.183.refs_7_.refs_3_, ...), custom_call_target="tpu_custom_call" | custom-call | tf_op jit(solution)/shard_map/mix/pallas_call | solution.py:194
  118.7 1.9 collective-permute-done.28.moved_rest
  121.8 7.2 %collective-permute-done.30.refs_3_ = bf16[144,896]{1,0:T(8,128)(2,1)S(1)} collective-permute-done((bf16[144,896]{1,0:T(8,128)(2,1)S(1)}, bf16[144,896]{1,0:T(8,128)(2,1)S(1)}, u32[]{:S(2)}, u32[]{:S(2)}) %collective-permute-start.30) | collective-permute-done | bytes 258080 | tf_op jit(solution)/shard_map/ppermute | solution.py:564
  129.1 4.9 %collective-permute-start.37 = (bf16[144,896]{1,0:T(8,128)(2,1)S(1)}, bf16[144,896]{1,0:T(8,128)(2,1)S(1)}, u32[]{:S(2)}, u32[]{:S(2)}) collective-permute-start(bf16[144,896]{1,0:T(8,128)(2,1)S(1)} %get-tuple-element.223), channel_id=1, source_target_pairs={{0,4},{1,5},{2,6},{3,7},{4,0},{5,1},{6,2},{7,3},{8,12},{9,13},{10,... | collective-permute-start | bytes 774152 | tf_op jit(solution)/shard_map/ppermute | solution.py:564
  134.0 2.4 %first.6 = (bf16[160,512]{1,0:T(8,128)(2,1)S(1)}, bf16[144,512]{1,0:T(8,128)(2,1)S(1)}, bf16[144,3584]{1,0:T(8,128)(2,1)S(1)}, f32[144,128]{1,0:T(8,128)S(1)}) custom-call(s32[4]{0:T(128)S(1)} %pad_add_fusion.me.refs_0_, bf16[144,896]{1,0:T(8,128)(2,1)S(1)} %get-tuple-element.188.refs_7_.refs_1_, bf16[144,896]{1,0:T(8,128)(2,1)S(1)} %collective-permute-done.29.refs_2_, ...), custom_call_target="tpu_custom_call" | custom-call | tf_op jit(solution)/shard_map/first/pallas_call | solution.py:194
  140.0 1.9 own.6
  141.8 3.7 %collective-permute-done.33.ups = bf16[144,512]{1,0:T(8,128)(2,1)S(1)} collective-permute-done((bf16[144,512]{1,0:T(8,128)(2,1)S(1)}, bf16[144,512]{1,0:T(8,128)(2,1)S(1)}, u32[]{:S(2)}, u32[]{:S(2)}) %collective-permute-start.33) | collective-permute-done | bytes 147488 | tf_op jit(solution)/shard_map/ppermute | solution.py:19
  148.6 2.3 %collective-permute-done.34.t0 = bf16[144,256]{1,0:T(8,128)(2,1)S(1)} collective-permute-done((bf16[144,256]{1,0:T(8,128)(2,1)S(1)}, bf16[144,256]{1,0:T(8,128)(2,1)S(1)}, u32[]{:S(2)}, u32[]{:S(2)}) %collective-permute-start.34) | collective-permute-done | bytes 73760 | tf_op jit(solution)/shard_map/ppermute | solution.py:19
  151.8 2.0 third.6
  153.8 2.4 %collective-permute-start.44 = (bf16[144,896]{1,0:T(8,128)(2,1)S(1)}, bf16[144,896]{1,0:T(8,128)(2,1)S(1)}, u32[]{:S(2)}, u32[]{:S(2)}) collective-permute-start(bf16[144,896]{1,0:T(8,128)(2,1)S(1)} %get-tuple-element.240), channel_id=1, source_target_pairs={{0,4},{1,5},{2,6},{3,7},{4,0},{5,1},{6,2},{7,3},{8,12},{9,13},{10,... | collective-permute-start | bytes 774152 | tf_op jit(solution)/shard_map/ppermute | solution.py:564
  156.8 2.3 %first.7 = (bf16[160,512]{1,0:T(8,128)(2,1)S(1)}, bf16[144,512]{1,0:T(8,128)(2,1)S(1)}, bf16[144,3584]{1,0:T(8,128)(2,1)S(1)}, f32[144,128]{1,0:T(8,128)S(1)}) custom-call(s32[4]{0:T(128)S(1)} %pad_add_fusion.me.refs_0_, bf16[144,896]{1,0:T(8,128)(2,1)S(1)} %get-tuple-element.217.refs_1_, bf16[144,896]{1,0:T(8,128)(2,1)S(1)} %collective-permute-done.36.refs_2_, ...), custom_call_target="tpu_custom_call" | custom-call | tf_op jit(solution)/shard_map/first/pallas_call | solution.py:194
  162.7 1.8 own.7
  164.5 3.1 %collective-permute-done.40.ups = bf16[144,512]{1,0:T(8,128)(2,1)S(1)} collective-permute-done((bf16[144,512]{1,0:T(8,128)(2,1)S(1)}, bf16[144,512]{1,0:T(8,128)(2,1)S(1)}, u32[]{:S(2)}, u32[]{:S(2)}) %collective-permute-start.40) | collective-permute-done | bytes 147488 | tf_op jit(solution)/shard_map/ppermute | solution.py:19
  170.7 2.3 %collective-permute-done.41.t0 = bf16[144,256]{1,0:T(8,128)(2,1)S(1)} collective-permute-done((bf16[144,256]{1,0:T(8,128)(2,1)S(1)}, bf16[144,256]{1,0:T(8,128)(2,1)S(1)}, u32[]{:S(2)}, u32[]{:S(2)}) %collective-permute-start.41) | collective-permute-done | bytes 73760 | tf_op jit(solution)/shard_map/ppermute | solution.py:19
  174.1 2.0 third.7
  176.6 3.4 %collective-permute-start.48 = (bf16[144,896]{1,0:T(8,128)(2,1)S(1)}, bf16[144,896]{1,0:T(8,128)(2,1)S(1)}, u32[]{:S(2)}, u32[]{:S(2)}) collective-permute-start(bf16[144,896]{1,0:T(8,128)(2,1)S(1)} %get-tuple-element.246), channel_id=1, source_target_pairs={{0,4},{1,5},{2,6},{3,7},{4,0},{5,1},{6,2},{7,3},{8,12},{9,13},{10,... | collective-permute-start | bytes 774152 | tf_op jit(solution)/shard_map/ppermute | solution.py:564
  183.1 4.4 %collective-permute-done.47.refs_4_ = bf16[144,896]{1,0:T(8,128)(2,1)S(1)} collective-permute-done((bf16[144,896]{1,0:T(8,128)(2,1)S(1)}, bf16[144,896]{1,0:T(8,128)(2,1)S(1)}, u32[]{:S(2)}, u32[]{:S(2)}) %collective-permute-start.47) | collective-permute-done | bytes 258080 | tf_op jit(solution)/shard_map/ppermute | solution.py:564
  187.5 8.2 %collective-permute-done.48.refs_5_ = bf16[144,896]{1,0:T(8,128)(2,1)S(1)} collective-permute-done((bf16[144,896]{1,0:T(8,128)(2,1)S(1)}, bf16[144,896]{1,0:T(8,128)(2,1)S(1)}, u32[]{:S(2)}, u32[]{:S(2)}) %collective-permute-start.48) | collective-permute-done | bytes 258080 | tf_op jit(solution)/shard_map/ppermute | solution.py:564
  197.9 1.6 last.5.kept
  200.9 1.6 last.7.kept
  (104 shorter events, 61.1 us)
Async XLA Ops:
  2.3 9.6 %collective-permute-start = (bf16[32,3584]{1,0:T(8,128)(2,1)S(1)}, bf16[32,3584]{1,0:T(8,128)(2,1)S(1)}, u32[]{:S(2)}, u32[]{:S(2)}) collective-permute-start(bf16[32,3584]{1,0:T(8,128)(2,1)S(1)} %get-tuple-element.126), channel_id=1, source_target_pairs={{0,1},{1,0},{2,3},{3,2},{4,5},{5,4},{6,7},{7,6},{8,9},{9,8},{10,11... | collective-permute-start | bytes 688136 | tf_op jit(solution)/shard_map/ppermute | solution.py:19
  14.7 9.8 %collective-permute-start.2 = (bf16[32,3584]{1,0:T(8,128)(2,1)S(1)}, bf16[32,3584]{1,0:T(8,128)(2,1)S(1)}, u32[]{:S(2)}, u32[]{:S(2)}) collective-permute-start(bf16[32,3584]{1,0:T(8,128)(2,1)S(1)} %get-tuple-element.132), channel_id=1, source_target_pairs={{0,1},{1,0},{2,3},{3,2},{4,5},{5,4},{6,7},{7,6},{8,9},{9,8},{10,11... | collective-permute-start | bytes 688136 | tf_op jit(solution)/shard_map/ppermute | solution.py:19
  16.5 19.8 %collective-permute-start.3 = (bf16[144,896]{1,0:T(8,128)(2,1)S(1)}, bf16[144,896]{1,0:T(8,128)(2,1)S(1)}, u32[]{:S(2)}, u32[]{:S(2)}) collective-permute-start(bf16[144,896]{1,0:T(8,128)(2,1)S(1)} %get-tuple-element.135), channel_id=1, source_target_pairs={{0,2},{1,3},{2,0},{3,1},{4,6},{5,7},{6,4},{7,5},{8,10},{9,11},{10,... | collective-permute-start | bytes 774152 | tf_op jit(solution)/shard_map/ppermute | solution.py:564
  18.1 21.1 %collective-permute-start.4 = (bf16[144,896]{1,0:T(8,128)(2,1)S(1)}, bf16[144,896]{1,0:T(8,128)(2,1)S(1)}, u32[]{:S(2)}, u32[]{:S(2)}) collective-permute-start(bf16[144,896]{1,0:T(8,128)(2,1)S(1)} %get-tuple-element.139), channel_id=1, source_target_pairs={{0,4},{1,5},{2,6},{3,7},{4,0},{5,1},{6,2},{7,3},{8,12},{9,13},{10,... | collective-permute-start | bytes 774152 | tf_op jit(solution)/shard_map/ppermute | solution.py:564
  20.7 18.5 %collective-permute-start.5 = (bf16[144,896]{1,0:T(8,128)(2,1)S(1)}, bf16[144,896]{1,0:T(8,128)(2,1)S(1)}, u32[]{:S(2)}, u32[]{:S(2)}) collective-permute-start(bf16[144,896]{1,0:T(8,128)(2,1)S(1)} %get-tuple-element.140), channel_id=1, source_target_pairs={{0,6},{1,7},{2,4},{3,5},{4,2},{5,3},{6,0},{7,1},{8,14},{9,15},{10,... | collective-permute-start | bytes 774152 | tf_op jit(solution)/shard_map/ppermute | solution.py:564
  22.5 22.3 %collective-permute-start.7 = (bf16[32,3584]{1,0:T(8,128)(2,1)S(1)}, bf16[32,3584]{1,0:T(8,128)(2,1)S(1)}, u32[]{:S(2)}, u32[]{:S(2)}) collective-permute-start(bf16[32,3584]{1,0:T(8,128)(2,1)S(1)} %get-tuple-element.145), channel_id=1, source_target_pairs={{0,1},{1,0},{2,3},{3,2},{4,5},{5,4},{6,7},{7,6},{8,9},{9,8},{10,11... | collective-permute-start | bytes 688136 | tf_op jit(solution)/shard_map/ppermute | solution.py:19
  24.5 20.4 %collective-permute-start.6 = (bf16[32,3584]{1,0:T(8,128)(2,1)S(1)}, bf16[32,3584]{1,0:T(8,128)(2,1)S(1)}, u32[]{:S(2)}, u32[]{:S(2)}) collective-permute-start(bf16[32,3584]{1,0:T(8,128)(2,1)S(1)} %get-tuple-element.144), channel_id=1, source_target_pairs={{0,1},{1,0},{2,3},{3,2},{4,5},{5,4},{6,7},{7,6},{8,9},{9,8},{10,11... | collective-permute-start | bytes 688136 | tf_op jit(solution)/shard_map/ppermute | solution.py:19
  39.2 25.6 %collective-permute-start.13 = (bf16[144,896]{1,0:T(8,128)(2,1)S(1)}, bf16[144,896]{1,0:T(8,128)(2,1)S(1)}, u32[]{:S(2)}, u32[]{:S(2)}) collective-permute-start(bf16[144,896]{1,0:T(8,128)(2,1)S(1)} %get-tuple-element.162), channel_id=1, source_target_pairs={{0,4},{1,5},{2,6},{3,7},{4,0},{5,1},{6,2},{7,3},{8,12},{9,13},{10,... | collective-permute-start | bytes 774152 | tf_op jit(solution)/shard_map/ppermute | solution.py:564
  44.9 20.0 %collective-permute-start.12 = (bf16[144,896]{1,0:T(8,128)(2,1)S(1)}, bf16[144,896]{1,0:T(8,128)(2,1)S(1)}, u32[]{:S(2)}, u32[]{:S(2)}) collective-permute-start(bf16[144,896]{1,0:T(8,128)(2,1)S(1)} %get-tuple-element.158), channel_id=1, source_target_pairs={{0,2},{1,3},{2,0},{3,1},{4,6},{5,7},{6,4},{7,5},{8,10},{9,11},{10,... | collective-permute-start | bytes 774152 | tf_op jit(solution)/shard_map/ppermute | solution.py:564
  47.3 17.5 %collective-permute-start.14 = (bf16[144,896]{1,0:T(8,128)(2,1)S(1)}, bf16[144,896]{1,0:T(8,128)(2,1)S(1)}, u32[]{:S(2)}, u32[]{:S(2)}) collective-permute-start(bf16[144,896]{1,0:T(8,128)(2,1)S(1)} %get-tuple-element.163), channel_id=1, source_target_pairs={{0,6},{1,7},{2,4},{3,5},{4,2},{5,3},{6,0},{7,1},{8,14},{9,15},{10,... | collective-permute-start | bytes 774152 | tf_op jit(solution)/shard_map/ppermute | solution.py:564
  48.9 7.8 %collective-permute-start.8 = (bf16[160,512]{1,0:T(8,128)(2,1)S(1)}, bf16[160,512]{1,0:T(8,128)(2,1)S(1)}, u32[]{:S(2)}, u32[]{:S(2)}) collective-permute-start(bf16[160,512]{1,0:T(8,128)(2,1)S(1)} %get-tuple-element.149), channel_id=1, source_target_pairs={{0,1},{1,0},{2,3},{3,2},{4,5},{5,4},{6,7},{7,6},{8,9},{9,8},{10,11... | collective-permute-start | bytes 491528 | tf_op jit(solution)/shard_map/ppermute | solution.py:19
  49.4 7.3 %collective-permute-start.9 = (bf16[144,512]{1,0:T(8,128)(2,1)S(1)}, bf16[144,512]{1,0:T(8,128)(2,1)S(1)}, u32[]{:S(2)}, u32[]{:S(2)}) collective-permute-start(bf16[144,512]{1,0:T(8,128)(2,1)S(1)} %get-tuple-element.150), channel_id=1, source_target_pairs={{0,1},{1,0},{2,3},{3,2},{4,5},{5,4},{6,7},{7,6},{8,9},{9,8},{10,11... | collective-permute-start | bytes 442376 | tf_op jit(solution)/shard_map/ppermute | solution.py:19
  57.7 4.4 %collective-permute-start.10 = (bf16[144,256]{1,0:T(8,128)(2,1)S(1)}, bf16[144,256]{1,0:T(8,128)(2,1)S(1)}, u32[]{:S(2)}, u32[]{:S(2)}) collective-permute-start(bf16[144,256]{1,0:T(8,128)(2,1)S(1)} %get-tuple-element.152.h0), channel_id=1, source_target_pairs={{0,1},{1,0},{2,3},{3,2},{4,5},{5,4},{6,7},{7,6},{8,9},{9,8},{10,11... | collective-permute-start | bytes 221192 | tf_op jit(solution)/shard_map/ppermute | solution.py:19
  58.3 4.6 %collective-permute-start.11 = (bf16[144,256]{1,0:T(8,128)(2,1)S(1)}, bf16[144,256]{1,0:T(8,128)(2,1)S(1)}, u32[]{:S(2)}, u32[]{:S(2)}) collective-permute-start(bf16[144,256]{1,0:T(8,128)(2,1)S(1)} %get-tuple-element.153.h1), channel_id=1, source_target_pairs={{0,1},{1,0},{2,3},{3,2},{4,5},{5,4},{6,7},{7,6},{8,9},{9,8},{10,11... | collective-permute-start | bytes 221192 | tf_op jit(solution)/shard_map/ppermute | solution.py:19
  64.9 23.8 %collective-permute-start.20 = (bf16[144,896]{1,0:T(8,128)(2,1)S(1)}, bf16[144,896]{1,0:T(8,128)(2,1)S(1)}, u32[]{:S(2)}, u32[]{:S(2)}) collective-permute-start(bf16[144,896]{1,0:T(8,128)(2,1)S(1)} %get-tuple-element.179), channel_id=1, source_target_pairs={{0,4},{1,5},{2,6},{3,7},{4,0},{5,1},{6,2},{7,3},{8,12},{9,13},{10,... | collective-permute-start | bytes 774152 | tf_op jit(solution)/shard_map/ppermute | solution.py:564
  67.3 21.3 %collective-permute-start.19 = (bf16[144,896]{1,0:T(8,128)(2,1)S(1)}, bf16[144,896]{1,0:T(8,128)(2,1)S(1)}, u32[]{:S(2)}, u32[]{:S(2)}) collective-permute-start(bf16[144,896]{1,0:T(8,128)(2,1)S(1)} %get-tuple-element.175), channel_id=1, source_target_pairs={{0,2},{1,3},{2,0},{3,1},{4,6},{5,7},{6,4},{7,5},{8,10},{9,11},{10,... | collective-permute-start | bytes 774152 | tf_op jit(solution)/shard_map/ppermute | solution.py:564
  70.2 18.5 %collective-permute-start.21 = (bf16[144,896]{1,0:T(8,128)(2,1)S(1)}, bf16[144,896]{1,0:T(8,128)(2,1)S(1)}, u32[]{:S(2)}, u32[]{:S(2)}) collective-permute-start(bf16[144,896]{1,0:T(8,128)(2,1)S(1)} %get-tuple-element.180), channel_id=1, source_target_pairs={{0,6},{1,7},{2,4},{3,5},{4,2},{5,3},{6,0},{7,1},{8,14},{9,15},{10,... | collective-permute-start | bytes 774152 | tf_op jit(solution)/shard_map/ppermute | solution.py:564
  71.7 7.5 %collective-permute-start.15 = (bf16[160,512]{1,0:T(8,128)(2,1)S(1)}, bf16[160,512]{1,0:T(8,128)(2,1)S(1)}, u32[]{:S(2)}, u32[]{:S(2)}) collective-permute-start(bf16[160,512]{1,0:T(8,128)(2,1)S(1)} %get-tuple-element.169), channel_id=1, source_target_pairs={{0,1},{1,0},{2,3},{3,2},{4,5},{5,4},{6,7},{7,6},{8,9},{9,8},{10,11... | collective-permute-start | bytes 491528 | tf_op jit(solution)/shard_map/ppermute | solution.py:19
  72.9 6.3 %collective-permute-start.16 = (bf16[144,512]{1,0:T(8,128)(2,1)S(1)}, bf16[144,512]{1,0:T(8,128)(2,1)S(1)}, u32[]{:S(2)}, u32[]{:S(2)}) collective-permute-start(bf16[144,512]{1,0:T(8,128)(2,1)S(1)} %get-tuple-element.170), channel_id=1, source_target_pairs={{0,1},{1,0},{2,3},{3,2},{4,5},{5,4},{6,7},{7,6},{8,9},{9,8},{10,11... | collective-permute-start | bytes 442376 | tf_op jit(solution)/shard_map/ppermute | solution.py:19
  80.2 4.4 %collective-permute-start.17 = (bf16[144,256]{1,0:T(8,128)(2,1)S(1)}, bf16[144,256]{1,0:T(8,128)(2,1)S(1)}, u32[]{:S(2)}, u32[]{:S(2)}) collective-permute-start(bf16[144,256]{1,0:T(8,128)(2,1)S(1)} %get-tuple-element.172.h0), channel_id=1, source_target_pairs={{0,1},{1,0},{2,3},{3,2},{4,5},{5,4},{6,7},{7,6},{8,9},{9,8},{10,11... | collective-permute-start | bytes 221192 | tf_op jit(solution)/shard_map/ppermute | solution.py:19
  82.2 4.4 %collective-permute-start.18 = (bf16[144,256]{1,0:T(8,128)(2,1)S(1)}, bf16[144,256]{1,0:T(8,128)(2,1)S(1)}, u32[]{:S(2)}, u32[]{:S(2)}) collective-permute-start(bf16[144,256]{1,0:T(8,128)(2,1)S(1)} %get-tuple-element.173.h1), channel_id=1, source_target_pairs={{0,1},{1,0},{2,3},{3,2},{4,5},{5,4},{6,7},{7,6},{8,9},{9,8},{10,11... | collective-permute-start | bytes 221192 | tf_op jit(solution)/shard_map/ppermute | solution.py:19
  88.6 14.7 %collective-permute-start.24 = (bf16[144,896]{1,0:T(8,128)(2,1)S(1)}, bf16[144,896]{1,0:T(8,128)(2,1)S(1)}, u32[]{:S(2)}, u32[]{:S(2)}) collective-permute-start(bf16[144,896]{1,0:T(8,128)(2,1)S(1)} %get-tuple-element.189), channel_id=1, source_target_pairs={{0,2},{1,3},{2,0},{3,1},{4,6},{5,7},{6,4},{7,5},{8,10},{9,11},{10,... | collective-permute-start | bytes 774152 | tf_op jit(solution)/shard_map/ppermute | solution.py:564
  88.7 17.4 %collective-permute-start.25 = (bf16[144,896]{1,0:T(8,128)(2,1)S(1)}, bf16[144,896]{1,0:T(8,128)(2,1)S(1)}, u32[]{:S(2)}, u32[]{:S(2)}) collective-permute-start(bf16[144,896]{1,0:T(8,128)(2,1)S(1)} %get-tuple-element.190), channel_id=1, source_target_pairs={{0,4},{1,5},{2,6},{3,7},{4,0},{5,1},{6,2},{7,3},{8,12},{9,13},{10,... | collective-permute-start | bytes 774152 | tf_op jit(solution)/shard_map/ppermute | solution.py:564
  91.8 14.3 %collective-permute-start.26 = (bf16[144,896]{1,0:T(8,128)(2,1)S(1)}, bf16[144,896]{1,0:T(8,128)(2,1)S(1)}, u32[]{:S(2)}, u32[]{:S(2)}) collective-permute-start(bf16[144,896]{1,0:T(8,128)(2,1)S(1)} %get-tuple-element.191), channel_id=1, source_target_pairs={{0,6},{1,7},{2,4},{3,5},{4,2},{5,3},{6,0},{7,1},{8,14},{9,15},{10,... | collective-permute-start | bytes 774152 | tf_op jit(solution)/shard_map/ppermute | solution.py:564
  95.3 5.5 %collective-permute-start.22 = (bf16[32,3584]{1,0:T(8,128)(2,1)S(1)}, bf16[32,3584]{1,0:T(8,128)(2,1)S(1)}, u32[]{:S(2)}, u32[]{:S(2)}) collective-permute-start(bf16[32,3584]{1,0:T(8,128)(2,1)S(1)} %get-tuple-element.184), channel_id=1, source_target_pairs={{0,8},{8,16},{16,24},{1,9},{9,17},{17,25},{2,10},{10,18},{18,26},{... | collective-permute-start | bytes 688136 | tf_op jit(solution)/shard_map/ppermute | solution.py:25
  96.6 5.2 %collective-permute-start.23 = (bf16[32,3584]{1,0:T(8,128)(2,1)S(1)}, bf16[32,3584]{1,0:T(8,128)(2,1)S(1)}, u32[]{:S(2)}, u32[]{:S(2)}) collective-permute-start(bf16[32,3584]{1,0:T(8,128)(2,1)S(1)} %get-tuple-element.185), channel_id=1, source_target_pairs={{0,8},{8,16},{16,24},{1,9},{9,17},{17,25},{2,10},{10,18},{18,26},{... | collective-permute-start | bytes 688136 | tf_op jit(solution)/shard_map/ppermute | solution.py:25
  103.3 18.5 %collective-permute-start.29 = (bf16[144,896]{1,0:T(8,128)(2,1)S(1)}, bf16[144,896]{1,0:T(8,128)(2,1)S(1)}, u32[]{:S(2)}, u32[]{:S(2)}) collective-permute-start(bf16[144,896]{1,0:T(8,128)(2,1)S(1)} %get-tuple-element.197), channel_id=1, source_target_pairs={{0,2},{1,3},{2,0},{3,1},{4,6},{5,7},{6,4},{7,5},{8,10},{9,11},{10,... | collective-permute-start | bytes 774152 | tf_op jit(solution)/shard_map/ppermute | solution.py:564
  106.1 23.0 %collective-permute-start.30 = (bf16[144,896]{1,0:T(8,128)(2,1)S(1)}, bf16[144,896]{1,0:T(8,128)(2,1)S(1)}, u32[]{:S(2)}, u32[]{:S(2)}) collective-permute-start(bf16[144,896]{1,0:T(8,128)(2,1)S(1)} %get-tuple-element.203), channel_id=1, source_target_pairs={{0,4},{1,5},{2,6},{3,7},{4,0},{5,1},{6,2},{7,3},{8,12},{9,13},{10,... | collective-permute-start | bytes 774152 | tf_op jit(solution)/shard_map/ppermute | solution.py:564
  110.9 18.2 %collective-permute-start.31 = (bf16[144,896]{1,0:T(8,128)(2,1)S(1)}, bf16[144,896]{1,0:T(8,128)(2,1)S(1)}, u32[]{:S(2)}, u32[]{:S(2)}) collective-permute-start(bf16[144,896]{1,0:T(8,128)(2,1)S(1)} %get-tuple-element.204), channel_id=1, source_target_pairs={{0,6},{1,7},{2,4},{3,5},{4,2},{5,3},{6,0},{7,1},{8,14},{9,15},{10,... | collective-permute-start | bytes 774152 | tf_op jit(solution)/shard_map/ppermute | solution.py:564
  129.1 24.8 %collective-permute-start.37 = (bf16[144,896]{1,0:T(8,128)(2,1)S(1)}, bf16[144,896]{1,0:T(8,128)(2,1)S(1)}, u32[]{:S(2)}, u32[]{:S(2)}) collective-permute-start(bf16[144,896]{1,0:T(8,128)(2,1)S(1)} %get-tuple-element.223), channel_id=1, source_target_pairs={{0,4},{1,5},{2,6},{3,7},{4,0},{5,1},{6,2},{7,3},{8,12},{9,13},{10,... | collective-permute-start | bytes 774152 | tf_op jit(solution)/shard_map/ppermute | solution.py:564
  134.0 19.9 %collective-permute-start.36 = (bf16[144,896]{1,0:T(8,128)(2,1)S(1)}, bf16[144,896]{1,0:T(8,128)(2,1)S(1)}, u32[]{:S(2)}, u32[]{:S(2)}) collective-permute-start(bf16[144,896]{1,0:T(8,128)(2,1)S(1)} %get-tuple-element.219), channel_id=1, source_target_pairs={{0,2},{1,3},{2,0},{3,1},{4,6},{5,7},{6,4},{7,5},{8,10},{9,11},{10,... | collective-permute-start | bytes 774152 | tf_op jit(solution)/shard_map/ppermute | solution.py:564
  136.4 17.4 %collective-permute-start.38 = (bf16[144,896]{1,0:T(8,128)(2,1)S(1)}, bf16[144,896]{1,0:T(8,128)(2,1)S(1)}, u32[]{:S(2)}, u32[]{:S(2)}) collective-permute-start(bf16[144,896]{1,0:T(8,128)(2,1)S(1)} %get-tuple-element.224), channel_id=1, source_target_pairs={{0,6},{1,7},{2,4},{3,5},{4,2},{5,3},{6,0},{7,1},{8,14},{9,15},{10,... | collective-permute-start | bytes 774152 | tf_op jit(solution)/shard_map/ppermute | solution.py:564
  137.9 7.6 %collective-permute-start.32 = (bf16[160,512]{1,0:T(8,128)(2,1)S(1)}, bf16[160,512]{1,0:T(8,128)(2,1)S(1)}, u32[]{:S(2)}, u32[]{:S(2)}) collective-permute-start(bf16[160,512]{1,0:T(8,128)(2,1)S(1)} %get-tuple-element.211), channel_id=1, source_target_pairs={{0,1},{1,0},{2,3},{3,2},{4,5},{5,4},{6,7},{7,6},{8,9},{9,8},{10,11... | collective-permute-start | bytes 491528 | tf_op jit(solution)/shard_map/ppermute | solution.py:19
  139.0 6.6 %collective-permute-start.33 = (bf16[144,512]{1,0:T(8,128)(2,1)S(1)}, bf16[144,512]{1,0:T(8,128)(2,1)S(1)}, u32[]{:S(2)}, u32[]{:S(2)}) collective-permute-start(bf16[144,512]{1,0:T(8,128)(2,1)S(1)} %get-tuple-element.212), channel_id=1, source_target_pairs={{0,1},{1,0},{2,3},{3,2},{4,5},{5,4},{6,7},{7,6},{8,9},{9,8},{10,11... | collective-permute-start | bytes 442376 | tf_op jit(solution)/shard_map/ppermute | solution.py:19
  146.5 4.4 %collective-permute-start.34 = (bf16[144,256]{1,0:T(8,128)(2,1)S(1)}, bf16[144,256]{1,0:T(8,128)(2,1)S(1)}, u32[]{:S(2)}, u32[]{:S(2)}) collective-permute-start(bf16[144,256]{1,0:T(8,128)(2,1)S(1)} %get-tuple-element.214.h0), channel_id=1, source_target_pairs={{0,1},{1,0},{2,3},{3,2},{4,5},{5,4},{6,7},{7,6},{8,9},{9,8},{10,11... | collective-permute-start | bytes 221192 | tf_op jit(solution)/shard_map/ppermute | solution.py:19
  147.5 4.4 %collective-permute-start.35 = (bf16[144,256]{1,0:T(8,128)(2,1)S(1)}, bf16[144,256]{1,0:T(8,128)(2,1)S(1)}, u32[]{:S(2)}, u32[]{:S(2)}) collective-permute-start(bf16[144,256]{1,0:T(8,128)(2,1)S(1)} %get-tuple-element.215.h1), channel_id=1, source_target_pairs={{0,1},{1,0},{2,3},{3,2},{4,5},{5,4},{6,7},{7,6},{8,9},{9,8},{10,11... | collective-permute-start | bytes 221192 | tf_op jit(solution)/shard_map/ppermute | solution.py:19
  153.8 22.8 %collective-permute-start.44 = (bf16[144,896]{1,0:T(8,128)(2,1)S(1)}, bf16[144,896]{1,0:T(8,128)(2,1)S(1)}, u32[]{:S(2)}, u32[]{:S(2)}) collective-permute-start(bf16[144,896]{1,0:T(8,128)(2,1)S(1)} %get-tuple-element.240), channel_id=1, source_target_pairs={{0,4},{1,5},{2,6},{3,7},{4,0},{5,1},{6,2},{7,3},{8,12},{9,13},{10,... | collective-permute-start | bytes 774152 | tf_op jit(solution)/shard_map/ppermute | solution.py:564
  156.2 19.9 %collective-permute-start.43 = (bf16[144,896]{1,0:T(8,128)(2,1)S(1)}, bf16[144,896]{1,0:T(8,128)(2,1)S(1)}, u32[]{:S(2)}, u32[]{:S(2)}) collective-permute-start(bf16[144,896]{1,0:T(8,128)(2,1)S(1)} %get-tuple-element.236), channel_id=1, source_target_pairs={{0,2},{1,3},{2,0},{3,1},{4,6},{5,7},{6,4},{7,5},{8,10},{9,11},{10,... | collective-permute-start | bytes 774152 | tf_op jit(solution)/shard_map/ppermute | solution.py:564
  159.1 17.5 %collective-permute-start.45 = (bf16[144,896]{1,0:T(8,128)(2,1)S(1)}, bf16[144,896]{1,0:T(8,128)(2,1)S(1)}, u32[]{:S(2)}, u32[]{:S(2)}) collective-permute-start(bf16[144,896]{1,0:T(8,128)(2,1)S(1)} %get-tuple-element.241), channel_id=1, source_target_pairs={{0,6},{1,7},{2,4},{3,5},{4,2},{5,3},{6,0},{7,1},{8,14},{9,15},{10,... | collective-permute-start | bytes 774152 | tf_op jit(solution)/shard_map/ppermute | solution.py:564
  160.7 6.9 %collective-permute-start.39 = (bf16[160,512]{1,0:T(8,128)(2,1)S(1)}, bf16[160,512]{1,0:T(8,128)(2,1)S(1)}, u32[]{:S(2)}, u32[]{:S(2)}) collective-permute-start(bf16[160,512]{1,0:T(8,128)(2,1)S(1)} %get-tuple-element.230), channel_id=1, source_target_pairs={{0,1},{1,0},{2,3},{3,2},{4,5},{5,4},{6,7},{7,6},{8,9},{9,8},{10,11... | collective-permute-start | bytes 491528 | tf_op jit(solution)/shard_map/ppermute | solution.py:19
  161.8 5.8 %collective-permute-start.40 = (bf16[144,512]{1,0:T(8,128)(2,1)S(1)}, bf16[144,512]{1,0:T(8,128)(2,1)S(1)}, u32[]{:S(2)}, u32[]{:S(2)}) collective-permute-start(bf16[144,512]{1,0:T(8,128)(2,1)S(1)} %get-tuple-element.231), channel_id=1, source_target_pairs={{0,1},{1,0},{2,3},{3,2},{4,5},{5,4},{6,7},{7,6},{8,9},{9,8},{10,11... | collective-permute-start | bytes 442376 | tf_op jit(solution)/shard_map/ppermute | solution.py:19
  168.6 4.4 %collective-permute-start.41 = (bf16[144,256]{1,0:T(8,128)(2,1)S(1)}, bf16[144,256]{1,0:T(8,128)(2,1)S(1)}, u32[]{:S(2)}, u32[]{:S(2)}) collective-permute-start(bf16[144,256]{1,0:T(8,128)(2,1)S(1)} %get-tuple-element.233.h0), channel_id=1, source_target_pairs={{0,1},{1,0},{2,3},{3,2},{4,5},{5,4},{6,7},{7,6},{8,9},{9,8},{10,11... | collective-permute-start | bytes 221192 | tf_op jit(solution)/shard_map/ppermute | solution.py:19
  169.8 4.4 %collective-permute-start.42 = (bf16[144,256]{1,0:T(8,128)(2,1)S(1)}, bf16[144,256]{1,0:T(8,128)(2,1)S(1)}, u32[]{:S(2)}, u32[]{:S(2)}) collective-permute-start(bf16[144,256]{1,0:T(8,128)(2,1)S(1)} %get-tuple-element.234.h1), channel_id=1, source_target_pairs={{0,1},{1,0},{2,3},{3,2},{4,5},{5,4},{6,7},{7,6},{8,9},{9,8},{10,11... | collective-permute-start | bytes 221192 | tf_op jit(solution)/shard_map/ppermute | solution.py:19
  176.1 11.4 %collective-permute-start.47 = (bf16[144,896]{1,0:T(8,128)(2,1)S(1)}, bf16[144,896]{1,0:T(8,128)(2,1)S(1)}, u32[]{:S(2)}, u32[]{:S(2)}) collective-permute-start(bf16[144,896]{1,0:T(8,128)(2,1)S(1)} %get-tuple-element.245), channel_id=1, source_target_pairs={{0,2},{1,3},{2,0},{3,1},{4,6},{5,7},{6,4},{7,5},{8,10},{9,11},{10,... | collective-permute-start | bytes 774152 | tf_op jit(solution)/shard_map/ppermute | solution.py:564
  176.6 19.1 %collective-permute-start.48 = (bf16[144,896]{1,0:T(8,128)(2,1)S(1)}, bf16[144,896]{1,0:T(8,128)(2,1)S(1)}, u32[]{:S(2)}, u32[]{:S(2)}) collective-permute-start(bf16[144,896]{1,0:T(8,128)(2,1)S(1)} %get-tuple-element.246), channel_id=1, source_target_pairs={{0,4},{1,5},{2,6},{3,7},{4,0},{5,1},{6,2},{7,3},{8,12},{9,13},{10,... | collective-permute-start | bytes 774152 | tf_op jit(solution)/shard_map/ppermute | solution.py:564
  180.0 15.7 %collective-permute-start.49 = (bf16[144,896]{1,0:T(8,128)(2,1)S(1)}, bf16[144,896]{1,0:T(8,128)(2,1)S(1)}, u32[]{:S(2)}, u32[]{:S(2)}) collective-permute-start(bf16[144,896]{1,0:T(8,128)(2,1)S(1)} %get-tuple-element.247), channel_id=1, source_target_pairs={{0,6},{1,7},{2,4},{3,5},{4,2},{5,3},{6,0},{7,1},{8,14},{9,15},{10,... | collective-permute-start | bytes 774152 | tf_op jit(solution)/shard_map/ppermute | solution.py:564
  182.1 17.4 %collective-permute-start.46 = (bf16[32,3584]{1,0:T(8,128)(2,1)S(1)}, bf16[32,3584]{1,0:T(8,128)(2,1)S(1)}, u32[]{:S(2)}, u32[]{:S(2)}) collective-permute-start(bf16[32,3584]{1,0:T(8,128)(2,1)S(1)} %last.4.refs_7_), channel_id=1, source_target_pairs={{0,1},{1,0},{2,3},{3,2},{4,5},{5,4},{6,7},{7,6},{8,9},{9,8},{10,11... | collective-permute-start | bytes 688136 | tf_op jit(solution)/shard_map/ppermute | solution.py:19
  197.3 6.1 %collective-permute-start.50 = (bf16[32,3584]{1,0:T(8,128)(2,1)S(1)}, bf16[32,3584]{1,0:T(8,128)(2,1)S(1)}, u32[]{:S(2)}, u32[]{:S(2)}) collective-permute-start(bf16[32,3584]{1,0:T(8,128)(2,1)S(1)} %last.6.refs_7_), channel_id=1, source_target_pairs={{0,1},{1,0},{2,3},{3,2},{4,5},{5,4},{6,7},{7,6},{8,9},{9,8},{10,11... | collective-permute-start | bytes 688136 | tf_op jit(solution)/shard_map/ppermute | solution.py:19
  (9 other events, 34.3 us)

commit v6 on v5

--- a/solution.py
+++ b/solution.py
@@ -230,15 +230,40 @@
     return high, middle, (rest - middle.astype(jnp.float32)).astype(jnp.bfloat16)
 
 
-def cut_kernel(me, batch, kept, sent):
-    half = sent.shape[1]
-    kept[...] = batch[:, pl.ds(pl.multiple_of(me[1] * half, half), half)]
-    sent[...] = batch[:, pl.ds(pl.multiple_of((1 - me[1]) * half, half), half)]
-
-
-def cut(me, batch, after=()):
-    rows, model_width = batch.shape
-    return call(cut_kernel, "cut", [bf16(rows, model_width // 2)] * 2, me, batch, after=after)
+def cut_kernel(count, me, *refs):
+    batches, outs, done = refs[:count], refs[count:-1], refs[-1]
+    half = outs[0].shape[1]
+    copies = []
+    for index, batch in enumerate(batches):
+        for side in range(2):
+            start = pl.multiple_of((me[1] ^ side) * half, half)
+            place = 2 * index + side
+            copies.append(pltpu.make_async_copy(batch.at[:, pl.ds(start, half)], outs[place], done.at[place]))
+    for copy in copies:
+        copy.start()
+    for copy in copies:
+        copy.wait()
+
+
+def cut(me, batches, after=()):
+    count = len(batches)
+    rows, model_width = batches[0].shape
+    kernel = functools.partial(cut_kernel, count)
+    if after:
+        kernel = functools.partial(without, kernel, 1 + count, len(after))
+    made = pl.pallas_call(
+        kernel,
+        out_shape=[bf16(rows, model_width // 2)] * (2 * count),
+        in_specs=[pl.BlockSpec(memory_space=pltpu.SMEM)]
+        + [pl.BlockSpec(memory_space=pltpu.HBM)] * count
+        + [pl.BlockSpec(memory_space=pl.ANY)] * len(after),
+        out_specs=whole(2 * count),
+        scratch_shapes=[pltpu.SemaphoreType.DMA((2 * count,))],
+        compiler_params=pltpu.CompilerParams(vmem_limit_bytes=LIMIT),
+        cost_estimate=pl.CostEstimate(flops=0, bytes_accessed=0, transcendentals=0),
+        name="cut",
+    )(me, *batches, *after)
+    return [made[2 * index:2 * index + 2] for index in range(count)]
 
 
 def crossed(halves):
@@ -336,31 +361,27 @@
     return made[:EXPERTS], made[EXPERTS]
 
 
-def load_kernel(me, source, other_source, out, other_out, done):
-    copies = [
-        pltpu.make_async_copy(source, out, done.at[0]),
-        pltpu.make_async_copy(other_source, other_out, done.at[1]),
-    ]
-    for copy in copies:
-        copy.start()
-    for copy in copies:
-        copy.wait()
-
-
-def load(me, weight, other_weight, after):
-    arrays = [weight, other_weight]
-    kernel = functools.partial(without, load_kernel, 3, len(after))
+def load_kernel(me, source, unread, out, done):
+    copy = pltpu.make_async_copy(source, out, done.at[0])
+    copy.start()
+    copy.wait()
+
+
+def load(me, weight, after):
     return pl.pallas_call(
-        kernel,
-        out_shape=[bf16(*array.shape) for array in arrays],
-        in_specs=[pl.BlockSpec(memory_space=pltpu.SMEM)] + [pl.BlockSpec(memory_space=pltpu.HBM)] * 2
-        + [pl.BlockSpec(memory_space=pl.ANY)] * len(after),
-        out_specs=whole(2),
-        scratch_shapes=[pltpu.SemaphoreType.DMA((2,))],
+        load_kernel,
+        out_shape=bf16(*weight.shape),
+        in_specs=[
+            pl.BlockSpec(memory_space=pltpu.SMEM),
+            pl.BlockSpec(memory_space=pltpu.HBM),
+            pl.BlockSpec(memory_space=pl.ANY),
+        ],
+        out_specs=whole(1)[0],
+        scratch_shapes=[pltpu.SemaphoreType.DMA((1,))],
         compiler_params=pltpu.CompilerParams(vmem_limit_bytes=LIMIT),
         cost_estimate=pl.CostEstimate(flops=0, bytes_accessed=0, transcendentals=0),
         name="load",
-    )(me, *arrays, *after)
+    )(me, weight, after)
 
 
 def first_kernel(me, r0, r1, r2, r3, gain, weight, gates, ups, rows_out, squares):
@@ -601,7 +622,7 @@
 
     batches = [east_batch[0], west_batch[0]]
     entering = [east_entering[0], west_entering[0]]
-    east_halves = cut(me, batches[0])
+    east_halves = cut(me, batches[:1])[0]
     as_rows, as_columns = tables(me, lists, partner(lists, "expert", 0))
     east_halves = crossed(east_halves)
     moved = [None, None]
@@ -616,9 +637,10 @@
             if tick == 0:
                 after, west_halves = [], None
                 if stream == 1:
-                    west_halves = crossed(cut(me, batches[1], [states[0]]))
-                    entering_halves = [crossed(cut(me, batch, [states[0]])) for batch in entering]
-                    weight_in, weight_out = load(me, expert_in[0, 0], expert_down[0, 0], [states[0]])
+                    west_halves = crossed(cut(me, batches[1:], [states[0]])[0])
+                    entering_halves = [crossed(halves) for halves in cut(me, entering, [west_halves[0]])]
+                    weight_in = load(me, expert_in[0, 0], states[0])
+                    weight_out = expert_down[0, 0]
                     after = [weight_in]
                 sent, states[stream] = enter(me, turn, *(east_halves, west_halves)[stream], as_rows, after)
             else:

time: 208 us -> 207 us (level)
  Pallas kernels: 55.9 us -> 51.5 us
  waiting for transfers between devices: 63 us -> 65.4 us
    ppermute x24, waiting for transfers between devices: 25.5 us -> 28.7 us  [along(): lax.ppermute(block, 'expert', [(i, i ^ 2 * apart) for i in range(lax.axis...]
    pallas_call x33 -> x29, Pallas kernels: 50.1 us -> 47.6 us  [call(): pl.pallas_call(kernel, out_shape=out_shape, in_specs=[pl.BlockSpec(memory...]
    unnamed x12 -> x16, local copies, waits for them, and re-layouts: 7.16 us -> 9.26 us
    pallas_call x1 -> x4, Pallas kernels: 5.73 us -> 3.83 us  [the longest x3 2.31 us: cut(): pl.pallas_call(kernel, out_shape=[bf16(rows, model_width // 2)] * (2 * co...]
  transfers between devices with their start and end apart: 51 -> 51, of which waited for: 22 -> 22; matrix products, arithmetic and copies ran while one was open for 1% -> 1% of each run, Pallas kernels for 25% -> 23%
where the time goes in v6:
time: 207 us; the launch traced here: 205 us
  starting transfers between devices  75.9 us (37%)
  waiting for transfers between devices  65.4 us (32%)
  Pallas kernels  51.5 us (25%)
  local copies, waits for them, and re-layouts  10 us (5%)
    pallas_call x29, Pallas kernels, call(): pl.pallas_call(kernel, out_shape=out_shape, in_specs=[pl.BlockSpec(memory...  47.6 us
    ppermute x24, starting transfers between devices, along(): lax.ppermute(block, 'expert', [(i, i ^ 2 * apart) for i in range(lax.axis...  42.4 us
    ppermute x23, waiting for transfers between devices, partner(): lax.ppermute(shard, axis, [(i, i ^ 1 << apart) for i in range(lax.axis_si...  33.1 us
    ppermute x24, waiting for transfers between devices, along(): lax.ppermute(block, 'expert', [(i, i ^ 2 * apart) for i in range(lax.axis...  28.7 us
    ppermute x23, starting transfers between devices, partner(): lax.ppermute(shard, axis, [(i, i ^ 1 << apart) for i in range(lax.axis_si...  25.3 us
    unnamed x16, local copies, waits for them, and re-layouts  9.26 us
    ppermute x4, starting transfers between devices, shifted(): return lax.ppermute(block, axis, route)  8.2 us
  transfers between devices with their start and end apart: 51, of which 22 were waited for; matrix products, arithmetic and copies ran while one was open for 1% of the time, Pallas kernels for 23%

profile of v6, /device:TPU:0, one launch (start us, length us, event | category | flops | bytes accessed | tf_op | source)
XLA Modules:
  0.0 204.7 jit_solution(3458302029698963797)
XLA Ops:
  2.5 3.0 %collective-permute-start = (bf16[32,3584]{1,0:T(8,128)(2,1)S(1)}, bf16[32,3584]{1,0:T(8,128)(2,1)S(1)}, u32[]{:S(2)}, u32[]{:S(2)}) collective-permute-start(bf16[32,3584]{1,0:T(8,128)(2,1)S(1)} %get-tuple-element.124), channel_id=1, source_target_pairs={{0,1},{1,0},{2,3},{3,2},{4,5},{5,4},{6,7},{7,6},{8,9},{9,8},{10,11... | collective-permute-start | bytes 688136 | tf_op jit(solution)/shard_map/ppermute | solution.py:19
  7.1 4.2 %collective-permute-done.1.other = f32[16,32]{1,0:T(8,128)S(1)} collective-permute-done((f32[16,32]{1,0:T(8,128)S(1)}, f32[16,32]{1,0:T(8,128)S(1)}, u32[]{:S(2)}, u32[]{:S(2)}) %collective-permute-start.1) | collective-permute-done | bytes 2080 | tf_op jit(solution)/shard_map/ppermute | solution.py:19
  15.0 1.8 collective-permute-start.2
  18.4 2.6 %collective-permute-start.4 = (bf16[144,896]{1,0:T(8,128)(2,1)S(1)}, bf16[144,896]{1,0:T(8,128)(2,1)S(1)}, u32[]{:S(2)}, u32[]{:S(2)}) collective-permute-start(bf16[144,896]{1,0:T(8,128)(2,1)S(1)} %get-tuple-element.136), channel_id=1, source_target_pairs={{0,4},{1,5},{2,6},{3,7},{4,0},{5,1},{6,2},{7,3},{8,12},{9,13},{10,... | collective-permute-start | bytes 774152 | tf_op jit(solution)/shard_map/ppermute | solution.py:585
  24.5 1.7 collective-permute-start.7
  26.2 5.2 %copy-done = bf16[1,1,3584,2048]{3,2,1,0:T(8,128)(2,1)S(1)} copy-done((bf16[1,1,3584,2048]{3,2,1,0:T(8,128)(2,1)S(1)}, bf16[1,1,3584,2048]{3,2,1,0:T(8,128)(2,1)}, u32[]{:S(2)}) %copy-start) | copy-done | bytes 14680088
  34.1 5.4 %collective-permute-done.4.refs_3_ = bf16[144,896]{1,0:T(8,128)(2,1)S(1)} collective-permute-done((bf16[144,896]{1,0:T(8,128)(2,1)S(1)}, bf16[144,896]{1,0:T(8,128)(2,1)S(1)}, u32[]{:S(2)}, u32[]{:S(2)}) %collective-permute-start.4) | collective-permute-done | bytes 258080 | tf_op jit(solution)/shard_map/ppermute | solution.py:585
  39.5 5.6 %collective-permute-start.13 = (bf16[144,896]{1,0:T(8,128)(2,1)S(1)}, bf16[144,896]{1,0:T(8,128)(2,1)S(1)}, u32[]{:S(2)}, u32[]{:S(2)}) collective-permute-start(bf16[144,896]{1,0:T(8,128)(2,1)S(1)} %get-tuple-element.158), channel_id=1, source_target_pairs={{0,4},{1,5},{2,6},{3,7},{4,0},{5,1},{6,2},{7,3},{8,12},{9,13},{10,... | collective-permute-start | bytes 774152 | tf_op jit(solution)/shard_map/ppermute | solution.py:585
  45.2 2.3 %first.4 = (bf16[160,512]{1,0:T(8,128)(2,1)S(1)}, bf16[144,512]{1,0:T(8,128)(2,1)S(1)}, bf16[144,3584]{1,0:T(8,128)(2,1)S(1)}, f32[144,128]{1,0:T(8,128)S(1)}) custom-call(s32[4]{0:T(128)S(1)} %pad_add_fusion.me.refs_0_, bf16[144,896]{1,0:T(8,128)(2,1)S(1)} %get-tuple-element.128.refs_1_, bf16[144,896]{1,0:T(8,128)(2,1)S(1)} %collective-permute-done.3.refs_2_, ...), custom_call_target="tpu_custom_call" | custom-call | tf_op jit(solution)/shard_map/first/pallas_call | solution.py:194
  51.0 1.8 own.4
  52.8 4.0 %collective-permute-done.9.ups = bf16[144,512]{1,0:T(8,128)(2,1)S(1)} collective-permute-done((bf16[144,512]{1,0:T(8,128)(2,1)S(1)}, bf16[144,512]{1,0:T(8,128)(2,1)S(1)}, u32[]{:S(2)}, u32[]{:S(2)}) %collective-permute-start.9) | collective-permute-done | bytes 147488 | tf_op jit(solution)/shard_map/ppermute | solution.py:19
  59.9 2.3 %collective-permute-done.10.t0 = bf16[144,256]{1,0:T(8,128)(2,1)S(1)} collective-permute-done((bf16[144,256]{1,0:T(8,128)(2,1)S(1)}, bf16[144,256]{1,0:T(8,128)(2,1)S(1)}, u32[]{:S(2)}, u32[]{:S(2)}) %collective-permute-start.10) | collective-permute-done | bytes 73760 | tf_op jit(solution)/shard_map/ppermute | solution.py:19
  63.0 2.0 third.4
  65.0 2.4 %collective-permute-start.20 = (bf16[144,896]{1,0:T(8,128)(2,1)S(1)}, bf16[144,896]{1,0:T(8,128)(2,1)S(1)}, u32[]{:S(2)}, u32[]{:S(2)}) collective-permute-start(bf16[144,896]{1,0:T(8,128)(2,1)S(1)} %get-tuple-element.175), channel_id=1, source_target_pairs={{0,4},{1,5},{2,6},{3,7},{4,0},{5,1},{6,2},{7,3},{8,12},{9,13},{10,... | collective-permute-start | bytes 774152 | tf_op jit(solution)/shard_map/ppermute | solution.py:585
  68.0 2.4 %first.5 = (bf16[160,512]{1,0:T(8,128)(2,1)S(1)}, bf16[144,512]{1,0:T(8,128)(2,1)S(1)}, bf16[144,3584]{1,0:T(8,128)(2,1)S(1)}, f32[144,128]{1,0:T(8,128)S(1)}) custom-call(s32[4]{0:T(128)S(1)} %pad_add_fusion.me.refs_0_, bf16[144,896]{1,0:T(8,128)(2,1)S(1)} %get-tuple-element.152.refs_1_, bf16[144,896]{1,0:T(8,128)(2,1)S(1)} %collective-permute-done.12.refs_2_, ...), custom_call_target="tpu_custom_call" | custom-call | tf_op jit(solution)/shard_map/first/pallas_call | solution.py:194
  74.0 1.8 own.5
  75.9 3.5 %collective-permute-done.16.ups = bf16[144,512]{1,0:T(8,128)(2,1)S(1)} collective-permute-done((bf16[144,512]{1,0:T(8,128)(2,1)S(1)}, bf16[144,512]{1,0:T(8,128)(2,1)S(1)}, u32[]{:S(2)}, u32[]{:S(2)}) %collective-permute-start.16) | collective-permute-done | bytes 147488 | tf_op jit(solution)/shard_map/ppermute | solution.py:19
  80.4 2.0 collective-permute-start.17
  82.5 2.3 %collective-permute-done.17.t0 = bf16[144,256]{1,0:T(8,128)(2,1)S(1)} collective-permute-done((bf16[144,256]{1,0:T(8,128)(2,1)S(1)}, bf16[144,256]{1,0:T(8,128)(2,1)S(1)}, u32[]{:S(2)}, u32[]{:S(2)}) %collective-permute-start.17) | collective-permute-done | bytes 73760 | tf_op jit(solution)/shard_map/ppermute | solution.py:19
  84.8 2.0 collective-permute-done.18.t1
  86.8 2.0 third.5
  88.8 3.3 %collective-permute-start.25 = (bf16[144,896]{1,0:T(8,128)(2,1)S(1)}, bf16[144,896]{1,0:T(8,128)(2,1)S(1)}, u32[]{:S(2)}, u32[]{:S(2)}) collective-permute-start(bf16[144,896]{1,0:T(8,128)(2,1)S(1)} %get-tuple-element.186), channel_id=1, source_target_pairs={{0,4},{1,5},{2,6},{3,7},{4,0},{5,1},{6,2},{7,3},{8,12},{9,13},{10,... | collective-permute-start | bytes 774152 | tf_op jit(solution)/shard_map/ppermute | solution.py:585
  93.2 2.3 %mix.2 = (bf16[32,3584]{1,0:T(8,128)(2,1)S(1)}, bf16[32,3584]{1,0:T(8,128)(2,1)S(1)}) custom-call(s32[4]{0:T(128)S(1)} %pad_add_fusion.me.refs_0_, bf16[64,3584]{1,0:T(8,128)(2,1)S(1)} %get-tuple-element.126.refs_2_.unread.refs_1_, f32[256,16]{1,0:T(8,128)S(1)} %get-tuple-element.127.refs_2_, bf16[144,896]{1,0:T(8,128)(2,1)S(1)} %get-tuple-element.151.refs_7_.refs_3_, ...), custom_call_target="tpu_custom_call" | custom-call | tf_op jit(solution)/shard_map/mix/pallas_call | solution.py:194
  96.8 4.3 %collective-permute-start.23 = (bf16[32,3584]{1,0:T(8,128)(2,1)S(1)}, bf16[32,3584]{1,0:T(8,128)(2,1)S(1)}, u32[]{:S(2)}, u32[]{:S(2)}) collective-permute-start(bf16[32,3584]{1,0:T(8,128)(2,1)S(1)} %get-tuple-element.181), channel_id=1, source_target_pairs={{0,8},{8,16},{16,24},{1,9},{9,17},{17,25},{2,10},{10,18},{18,26},{... | collective-permute-start | bytes 688136 | tf_op jit(solution)/shard_map/ppermute | solution.py:25
  103.3 3.1 %collective-permute-done.25.refs_5_ = bf16[144,896]{1,0:T(8,128)(2,1)S(1)} collective-permute-done((bf16[144,896]{1,0:T(8,128)(2,1)S(1)}, bf16[144,896]{1,0:T(8,128)(2,1)S(1)}, u32[]{:S(2)}, u32[]{:S(2)}) %collective-permute-start.25) | collective-permute-done | bytes 258080 | tf_op jit(solution)/shard_map/ppermute | solution.py:585
  106.4 4.7 %collective-permute-start.30 = (bf16[144,896]{1,0:T(8,128)(2,1)S(1)}, bf16[144,896]{1,0:T(8,128)(2,1)S(1)}, u32[]{:S(2)}, u32[]{:S(2)}) collective-permute-start(bf16[144,896]{1,0:T(8,128)(2,1)S(1)} %get-tuple-element.199), channel_id=1, source_target_pairs={{0,4},{1,5},{2,6},{3,7},{4,0},{5,1},{6,2},{7,3},{8,12},{9,13},{10,... | collective-permute-start | bytes 774152 | tf_op jit(solution)/shard_map/ppermute | solution.py:585
  111.1 2.4 %collective-permute-start.31 = (bf16[144,896]{1,0:T(8,128)(2,1)S(1)}, bf16[144,896]{1,0:T(8,128)(2,1)S(1)}, u32[]{:S(2)}, u32[]{:S(2)}) collective-permute-start(bf16[144,896]{1,0:T(8,128)(2,1)S(1)} %get-tuple-element.200), channel_id=1, source_target_pairs={{0,6},{1,7},{2,4},{3,5},{4,2},{5,3},{6,0},{7,1},{8,14},{9,15},{10,... | collective-permute-start | bytes 774152 | tf_op jit(solution)/shard_map/ppermute | solution.py:585
  113.5 2.3 %mix.3 = (bf16[32,3584]{1,0:T(8,128)(2,1)S(1)}, bf16[32,3584]{1,0:T(8,128)(2,1)S(1)}) custom-call(s32[4]{0:T(128)S(1)} %pad_add_fusion.me.refs_0_, bf16[64,3584]{1,0:T(8,128)(2,1)S(1)} %get-tuple-element.140.refs_7_.refs_1_, f32[256,16]{1,0:T(8,128)S(1)} %get-tuple-element.127.refs_2_, bf16[144,896]{1,0:T(8,128)(2,1)S(1)} %get-tuple-element.179.refs_7_.refs_3_, ...), custom_call_target="tpu_custom_call" | custom-call | tf_op jit(solution)/shard_map/mix/pallas_call | solution.py:194
  119.1 1.9 collective-permute-done.28.moved_rest
  122.3 7.0 %collective-permute-done.30.refs_3_ = bf16[144,896]{1,0:T(8,128)(2,1)S(1)} collective-permute-done((bf16[144,896]{1,0:T(8,128)(2,1)S(1)}, bf16[144,896]{1,0:T(8,128)(2,1)S(1)}, u32[]{:S(2)}, u32[]{:S(2)}) %collective-permute-start.30) | collective-permute-done | bytes 258080 | tf_op jit(solution)/shard_map/ppermute | solution.py:585
  129.3 4.8 %collective-permute-start.37 = (bf16[144,896]{1,0:T(8,128)(2,1)S(1)}, bf16[144,896]{1,0:T(8,128)(2,1)S(1)}, u32[]{:S(2)}, u32[]{:S(2)}) collective-permute-start(bf16[144,896]{1,0:T(8,128)(2,1)S(1)} %get-tuple-element.219), channel_id=1, source_target_pairs={{0,4},{1,5},{2,6},{3,7},{4,0},{5,1},{6,2},{7,3},{8,12},{9,13},{10,... | collective-permute-start | bytes 774152 | tf_op jit(solution)/shard_map/ppermute | solution.py:585
  134.1 2.3 %first.6 = (bf16[160,512]{1,0:T(8,128)(2,1)S(1)}, bf16[144,512]{1,0:T(8,128)(2,1)S(1)}, bf16[144,3584]{1,0:T(8,128)(2,1)S(1)}, f32[144,128]{1,0:T(8,128)S(1)}) custom-call(s32[4]{0:T(128)S(1)} %pad_add_fusion.me.refs_0_, bf16[144,896]{1,0:T(8,128)(2,1)S(1)} %get-tuple-element.184.refs_7_.refs_1_, bf16[144,896]{1,0:T(8,128)(2,1)S(1)} %collective-permute-done.29.refs_2_, ...), custom_call_target="tpu_custom_call" | custom-call | tf_op jit(solution)/shard_map/first/pallas_call | solution.py:194
  139.9 1.8 own.6
  141.7 3.5 %collective-permute-done.33.ups = bf16[144,512]{1,0:T(8,128)(2,1)S(1)} collective-permute-done((bf16[144,512]{1,0:T(8,128)(2,1)S(1)}, bf16[144,512]{1,0:T(8,128)(2,1)S(1)}, u32[]{:S(2)}, u32[]{:S(2)}) %collective-permute-start.33) | collective-permute-done | bytes 147488 | tf_op jit(solution)/shard_map/ppermute | solution.py:19
  148.3 2.3 %collective-permute-done.34.t0 = bf16[144,256]{1,0:T(8,128)(2,1)S(1)} collective-permute-done((bf16[144,256]{1,0:T(8,128)(2,1)S(1)}, bf16[144,256]{1,0:T(8,128)(2,1)S(1)}, u32[]{:S(2)}, u32[]{:S(2)}) %collective-permute-start.34) | collective-permute-done | bytes 73760 | tf_op jit(solution)/shard_map/ppermute | solution.py:19
  152.0 2.0 third.6
  154.0 2.4 %collective-permute-start.44 = (bf16[144,896]{1,0:T(8,128)(2,1)S(1)}, bf16[144,896]{1,0:T(8,128)(2,1)S(1)}, u32[]{:S(2)}, u32[]{:S(2)}) collective-permute-start(bf16[144,896]{1,0:T(8,128)(2,1)S(1)} %get-tuple-element.236), channel_id=1, source_target_pairs={{0,4},{1,5},{2,6},{3,7},{4,0},{5,1},{6,2},{7,3},{8,12},{9,13},{10,... | collective-permute-start | bytes 774152 | tf_op jit(solution)/shard_map/ppermute | solution.py:585
  157.0 2.4 %first.7 = (bf16[160,512]{1,0:T(8,128)(2,1)S(1)}, bf16[144,512]{1,0:T(8,128)(2,1)S(1)}, bf16[144,3584]{1,0:T(8,128)(2,1)S(1)}, f32[144,128]{1,0:T(8,128)S(1)}) custom-call(s32[4]{0:T(128)S(1)} %pad_add_fusion.me.refs_0_, bf16[144,896]{1,0:T(8,128)(2,1)S(1)} %get-tuple-element.213.refs_1_, bf16[144,896]{1,0:T(8,128)(2,1)S(1)} %collective-permute-done.36.refs_2_, ...), custom_call_target="tpu_custom_call" | custom-call | tf_op jit(solution)/shard_map/first/pallas_call | solution.py:194
  163.0 1.8 own.7
  164.8 3.0 %collective-permute-done.40.ups = bf16[144,512]{1,0:T(8,128)(2,1)S(1)} collective-permute-done((bf16[144,512]{1,0:T(8,128)(2,1)S(1)}, bf16[144,512]{1,0:T(8,128)(2,1)S(1)}, u32[]{:S(2)}, u32[]{:S(2)}) %collective-permute-start.40) | collective-permute-done | bytes 147488 | tf_op jit(solution)/shard_map/ppermute | solution.py:19
  171.0 2.3 %collective-permute-done.41.t0 = bf16[144,256]{1,0:T(8,128)(2,1)S(1)} collective-permute-done((bf16[144,256]{1,0:T(8,128)(2,1)S(1)}, bf16[144,256]{1,0:T(8,128)(2,1)S(1)}, u32[]{:S(2)}, u32[]{:S(2)}) %collective-permute-start.41) | collective-permute-done | bytes 73760 | tf_op jit(solution)/shard_map/ppermute | solution.py:19
  174.1 2.0 third.7
  176.1 2.5 %collective-permute-start.48 = (bf16[144,896]{1,0:T(8,128)(2,1)S(1)}, bf16[144,896]{1,0:T(8,128)(2,1)S(1)}, u32[]{:S(2)}, u32[]{:S(2)}) collective-permute-start(bf16[144,896]{1,0:T(8,128)(2,1)S(1)} %get-tuple-element.242), channel_id=1, source_target_pairs={{0,4},{1,5},{2,6},{3,7},{4,0},{5,1},{6,2},{7,3},{8,12},{9,13},{10,... | collective-permute-start | bytes 774152 | tf_op jit(solution)/shard_map/ppermute | solution.py:585
  180.0 1.6 last.4.refs_7_
  182.5 12.8 %collective-permute-done.48.refs_5_ = bf16[144,896]{1,0:T(8,128)(2,1)S(1)} collective-permute-done((bf16[144,896]{1,0:T(8,128)(2,1)S(1)}, bf16[144,896]{1,0:T(8,128)(2,1)S(1)}, u32[]{:S(2)}, u32[]{:S(2)}) %collective-permute-start.48) | collective-permute-done | bytes 258080 | tf_op jit(solution)/shard_map/ppermute | solution.py:585
  195.7 1.6 last.6.refs_7_
  198.1 1.6 last.5.kept
  201.1 1.6 last.7.kept
  (108 shorter events, 59.9 us)
Async XLA Ops:
  2.5 9.6 %collective-permute-start = (bf16[32,3584]{1,0:T(8,128)(2,1)S(1)}, bf16[32,3584]{1,0:T(8,128)(2,1)S(1)}, u32[]{:S(2)}, u32[]{:S(2)}) collective-permute-start(bf16[32,3584]{1,0:T(8,128)(2,1)S(1)} %get-tuple-element.124), channel_id=1, source_target_pairs={{0,1},{1,0},{2,3},{3,2},{4,5},{5,4},{6,7},{7,6},{8,9},{9,8},{10,11... | collective-permute-start | bytes 688136 | tf_op jit(solution)/shard_map/ppermute | solution.py:19
  15.0 9.5 %collective-permute-start.2 = (bf16[32,3584]{1,0:T(8,128)(2,1)S(1)}, bf16[32,3584]{1,0:T(8,128)(2,1)S(1)}, u32[]{:S(2)}, u32[]{:S(2)}) collective-permute-start(bf16[32,3584]{1,0:T(8,128)(2,1)S(1)} %get-tuple-element.130), channel_id=1, source_target_pairs={{0,1},{1,0},{2,3},{3,2},{4,5},{5,4},{6,7},{7,6},{8,9},{9,8},{10,11... | collective-permute-start | bytes 688136 | tf_op jit(solution)/shard_map/ppermute | solution.py:19
  16.8 17.3 %collective-permute-start.3 = (bf16[144,896]{1,0:T(8,128)(2,1)S(1)}, bf16[144,896]{1,0:T(8,128)(2,1)S(1)}, u32[]{:S(2)}, u32[]{:S(2)}) collective-permute-start(bf16[144,896]{1,0:T(8,128)(2,1)S(1)} %get-tuple-element.132), channel_id=1, source_target_pairs={{0,2},{1,3},{2,0},{3,1},{4,6},{5,7},{6,4},{7,5},{8,10},{9,11},{10,... | collective-permute-start | bytes 774152 | tf_op jit(solution)/shard_map/ppermute | solution.py:585
  18.4 21.1 %collective-permute-start.4 = (bf16[144,896]{1,0:T(8,128)(2,1)S(1)}, bf16[144,896]{1,0:T(8,128)(2,1)S(1)}, u32[]{:S(2)}, u32[]{:S(2)}) collective-permute-start(bf16[144,896]{1,0:T(8,128)(2,1)S(1)} %get-tuple-element.136), channel_id=1, source_target_pairs={{0,4},{1,5},{2,6},{3,7},{4,0},{5,1},{6,2},{7,3},{8,12},{9,13},{10,... | collective-permute-start | bytes 774152 | tf_op jit(solution)/shard_map/ppermute | solution.py:585
  21.0 18.5 %collective-permute-start.5 = (bf16[144,896]{1,0:T(8,128)(2,1)S(1)}, bf16[144,896]{1,0:T(8,128)(2,1)S(1)}, u32[]{:S(2)}, u32[]{:S(2)}) collective-permute-start(bf16[144,896]{1,0:T(8,128)(2,1)S(1)} %get-tuple-element.137), channel_id=1, source_target_pairs={{0,6},{1,7},{2,4},{3,5},{4,2},{5,3},{6,0},{7,1},{8,14},{9,15},{10,... | collective-permute-start | bytes 774152 | tf_op jit(solution)/shard_map/ppermute | solution.py:585
  24.1 21.0 %collective-permute-start.6 = (bf16[32,3584]{1,0:T(8,128)(2,1)S(1)}, bf16[32,3584]{1,0:T(8,128)(2,1)S(1)}, u32[]{:S(2)}, u32[]{:S(2)}) collective-permute-start(bf16[32,3584]{1,0:T(8,128)(2,1)S(1)} %get-tuple-element.141), channel_id=1, source_target_pairs={{0,1},{1,0},{2,3},{3,2},{4,5},{5,4},{6,7},{7,6},{8,9},{9,8},{10,11... | collective-permute-start | bytes 688136 | tf_op jit(solution)/shard_map/ppermute | solution.py:19
  24.5 20.6 %collective-permute-start.7 = (bf16[32,3584]{1,0:T(8,128)(2,1)S(1)}, bf16[32,3584]{1,0:T(8,128)(2,1)S(1)}, u32[]{:S(2)}, u32[]{:S(2)}) collective-permute-start(bf16[32,3584]{1,0:T(8,128)(2,1)S(1)} %get-tuple-element.142), channel_id=1, source_target_pairs={{0,1},{1,0},{2,3},{3,2},{4,5},{5,4},{6,7},{7,6},{8,9},{9,8},{10,11... | collective-permute-start | bytes 688136 | tf_op jit(solution)/shard_map/ppermute | solution.py:19
  39.5 25.5 %collective-permute-start.13 = (bf16[144,896]{1,0:T(8,128)(2,1)S(1)}, bf16[144,896]{1,0:T(8,128)(2,1)S(1)}, u32[]{:S(2)}, u32[]{:S(2)}) collective-permute-start(bf16[144,896]{1,0:T(8,128)(2,1)S(1)} %get-tuple-element.158), channel_id=1, source_target_pairs={{0,4},{1,5},{2,6},{3,7},{4,0},{5,1},{6,2},{7,3},{8,12},{9,13},{10,... | collective-permute-start | bytes 774152 | tf_op jit(solution)/shard_map/ppermute | solution.py:585
  45.1 19.9 %collective-permute-start.12 = (bf16[144,896]{1,0:T(8,128)(2,1)S(1)}, bf16[144,896]{1,0:T(8,128)(2,1)S(1)}, u32[]{:S(2)}, u32[]{:S(2)}) collective-permute-start(bf16[144,896]{1,0:T(8,128)(2,1)S(1)} %get-tuple-element.154), channel_id=1, source_target_pairs={{0,2},{1,3},{2,0},{3,1},{4,6},{5,7},{6,4},{7,5},{8,10},{9,11},{10,... | collective-permute-start | bytes 774152 | tf_op jit(solution)/shard_map/ppermute | solution.py:585
  47.5 17.6 %collective-permute-start.14 = (bf16[144,896]{1,0:T(8,128)(2,1)S(1)}, bf16[144,896]{1,0:T(8,128)(2,1)S(1)}, u32[]{:S(2)}, u32[]{:S(2)}) collective-permute-start(bf16[144,896]{1,0:T(8,128)(2,1)S(1)} %get-tuple-element.159), channel_id=1, source_target_pairs={{0,6},{1,7},{2,4},{3,5},{4,2},{5,3},{6,0},{7,1},{8,14},{9,15},{10,... | collective-permute-start | bytes 774152 | tf_op jit(solution)/shard_map/ppermute | solution.py:585
  49.0 7.8 %collective-permute-start.8 = (bf16[160,512]{1,0:T(8,128)(2,1)S(1)}, bf16[160,512]{1,0:T(8,128)(2,1)S(1)}, u32[]{:S(2)}, u32[]{:S(2)}) collective-permute-start(bf16[160,512]{1,0:T(8,128)(2,1)S(1)} %get-tuple-element.146), channel_id=1, source_target_pairs={{0,1},{1,0},{2,3},{3,2},{4,5},{5,4},{6,7},{7,6},{8,9},{9,8},{10,11... | collective-permute-start | bytes 491528 | tf_op jit(solution)/shard_map/ppermute | solution.py:19
  49.5 7.3 %collective-permute-start.9 = (bf16[144,512]{1,0:T(8,128)(2,1)S(1)}, bf16[144,512]{1,0:T(8,128)(2,1)S(1)}, u32[]{:S(2)}, u32[]{:S(2)}) collective-permute-start(bf16[144,512]{1,0:T(8,128)(2,1)S(1)} %get-tuple-element.147), channel_id=1, source_target_pairs={{0,1},{1,0},{2,3},{3,2},{4,5},{5,4},{6,7},{7,6},{8,9},{9,8},{10,11... | collective-permute-start | bytes 442376 | tf_op jit(solution)/shard_map/ppermute | solution.py:19
  57.8 4.4 %collective-permute-start.10 = (bf16[144,256]{1,0:T(8,128)(2,1)S(1)}, bf16[144,256]{1,0:T(8,128)(2,1)S(1)}, u32[]{:S(2)}, u32[]{:S(2)}) collective-permute-start(bf16[144,256]{1,0:T(8,128)(2,1)S(1)} %get-tuple-element.149.h0), channel_id=1, source_target_pairs={{0,1},{1,0},{2,3},{3,2},{4,5},{5,4},{6,7},{7,6},{8,9},{9,8},{10,11... | collective-permute-start | bytes 221192 | tf_op jit(solution)/shard_map/ppermute | solution.py:19
  58.4 4.6 %collective-permute-start.11 = (bf16[144,256]{1,0:T(8,128)(2,1)S(1)}, bf16[144,256]{1,0:T(8,128)(2,1)S(1)}, u32[]{:S(2)}, u32[]{:S(2)}) collective-permute-start(bf16[144,256]{1,0:T(8,128)(2,1)S(1)} %get-tuple-element.150.h1), channel_id=1, source_target_pairs={{0,1},{1,0},{2,3},{3,2},{4,5},{5,4},{6,7},{7,6},{8,9},{9,8},{10,11... | collective-permute-start | bytes 221192 | tf_op jit(solution)/shard_map/ppermute | solution.py:19
  65.0 23.8 %collective-permute-start.20 = (bf16[144,896]{1,0:T(8,128)(2,1)S(1)}, bf16[144,896]{1,0:T(8,128)(2,1)S(1)}, u32[]{:S(2)}, u32[]{:S(2)}) collective-permute-start(bf16[144,896]{1,0:T(8,128)(2,1)S(1)} %get-tuple-element.175), channel_id=1, source_target_pairs={{0,4},{1,5},{2,6},{3,7},{4,0},{5,1},{6,2},{7,3},{8,12},{9,13},{10,... | collective-permute-start | bytes 774152 | tf_op jit(solution)/shard_map/ppermute | solution.py:585
  67.4 21.3 %collective-permute-start.19 = (bf16[144,896]{1,0:T(8,128)(2,1)S(1)}, bf16[144,896]{1,0:T(8,128)(2,1)S(1)}, u32[]{:S(2)}, u32[]{:S(2)}) collective-permute-start(bf16[144,896]{1,0:T(8,128)(2,1)S(1)} %get-tuple-element.171), channel_id=1, source_target_pairs={{0,2},{1,3},{2,0},{3,1},{4,6},{5,7},{6,4},{7,5},{8,10},{9,11},{10,... | collective-permute-start | bytes 774152 | tf_op jit(solution)/shard_map/ppermute | solution.py:585
  70.5 18.3 %collective-permute-start.21 = (bf16[144,896]{1,0:T(8,128)(2,1)S(1)}, bf16[144,896]{1,0:T(8,128)(2,1)S(1)}, u32[]{:S(2)}, u32[]{:S(2)}) collective-permute-start(bf16[144,896]{1,0:T(8,128)(2,1)S(1)} %get-tuple-element.176), channel_id=1, source_target_pairs={{0,6},{1,7},{2,4},{3,5},{4,2},{5,3},{6,0},{7,1},{8,14},{9,15},{10,... | collective-permute-start | bytes 774152 | tf_op jit(solution)/shard_map/ppermute | solution.py:585
  72.0 7.4 %collective-permute-start.15 = (bf16[160,512]{1,0:T(8,128)(2,1)S(1)}, bf16[160,512]{1,0:T(8,128)(2,1)S(1)}, u32[]{:S(2)}, u32[]{:S(2)}) collective-permute-start(bf16[160,512]{1,0:T(8,128)(2,1)S(1)} %get-tuple-element.165), channel_id=1, source_target_pairs={{0,1},{1,0},{2,3},{3,2},{4,5},{5,4},{6,7},{7,6},{8,9},{9,8},{10,11... | collective-permute-start | bytes 491528 | tf_op jit(solution)/shard_map/ppermute | solution.py:19
  73.2 6.1 %collective-permute-start.16 = (bf16[144,512]{1,0:T(8,128)(2,1)S(1)}, bf16[144,512]{1,0:T(8,128)(2,1)S(1)}, u32[]{:S(2)}, u32[]{:S(2)}) collective-permute-start(bf16[144,512]{1,0:T(8,128)(2,1)S(1)} %get-tuple-element.166), channel_id=1, source_target_pairs={{0,1},{1,0},{2,3},{3,2},{4,5},{5,4},{6,7},{7,6},{8,9},{9,8},{10,11... | collective-permute-start | bytes 442376 | tf_op jit(solution)/shard_map/ppermute | solution.py:19
  80.4 4.4 %collective-permute-start.17 = (bf16[144,256]{1,0:T(8,128)(2,1)S(1)}, bf16[144,256]{1,0:T(8,128)(2,1)S(1)}, u32[]{:S(2)}, u32[]{:S(2)}) collective-permute-start(bf16[144,256]{1,0:T(8,128)(2,1)S(1)} %get-tuple-element.168.h0), channel_id=1, source_target_pairs={{0,1},{1,0},{2,3},{3,2},{4,5},{5,4},{6,7},{7,6},{8,9},{9,8},{10,11... | collective-permute-start | bytes 221192 | tf_op jit(solution)/shard_map/ppermute | solution.py:19
  82.4 4.4 %collective-permute-start.18 = (bf16[144,256]{1,0:T(8,128)(2,1)S(1)}, bf16[144,256]{1,0:T(8,128)(2,1)S(1)}, u32[]{:S(2)}, u32[]{:S(2)}) collective-permute-start(bf16[144,256]{1,0:T(8,128)(2,1)S(1)} %get-tuple-element.169.h1), channel_id=1, source_target_pairs={{0,1},{1,0},{2,3},{3,2},{4,5},{5,4},{6,7},{7,6},{8,9},{9,8},{10,11... | collective-permute-start | bytes 221192 | tf_op jit(solution)/shard_map/ppermute | solution.py:19
  88.7 14.5 %collective-permute-start.24 = (bf16[144,896]{1,0:T(8,128)(2,1)S(1)}, bf16[144,896]{1,0:T(8,128)(2,1)S(1)}, u32[]{:S(2)}, u32[]{:S(2)}) collective-permute-start(bf16[144,896]{1,0:T(8,128)(2,1)S(1)} %get-tuple-element.185), channel_id=1, source_target_pairs={{0,2},{1,3},{2,0},{3,1},{4,6},{5,7},{6,4},{7,5},{8,10},{9,11},{10,... | collective-permute-start | bytes 774152 | tf_op jit(solution)/shard_map/ppermute | solution.py:585
  88.8 17.6 %collective-permute-start.25 = (bf16[144,896]{1,0:T(8,128)(2,1)S(1)}, bf16[144,896]{1,0:T(8,128)(2,1)S(1)}, u32[]{:S(2)}, u32[]{:S(2)}) collective-permute-start(bf16[144,896]{1,0:T(8,128)(2,1)S(1)} %get-tuple-element.186), channel_id=1, source_target_pairs={{0,4},{1,5},{2,6},{3,7},{4,0},{5,1},{6,2},{7,3},{8,12},{9,13},{10,... | collective-permute-start | bytes 774152 | tf_op jit(solution)/shard_map/ppermute | solution.py:585
  92.1 14.3 %collective-permute-start.26 = (bf16[144,896]{1,0:T(8,128)(2,1)S(1)}, bf16[144,896]{1,0:T(8,128)(2,1)S(1)}, u32[]{:S(2)}, u32[]{:S(2)}) collective-permute-start(bf16[144,896]{1,0:T(8,128)(2,1)S(1)} %get-tuple-element.187), channel_id=1, source_target_pairs={{0,6},{1,7},{2,4},{3,5},{4,2},{5,3},{6,0},{7,1},{8,14},{9,15},{10,... | collective-permute-start | bytes 774152 | tf_op jit(solution)/shard_map/ppermute | solution.py:585
  95.5 5.6 %collective-permute-start.22 = (bf16[32,3584]{1,0:T(8,128)(2,1)S(1)}, bf16[32,3584]{1,0:T(8,128)(2,1)S(1)}, u32[]{:S(2)}, u32[]{:S(2)}) collective-permute-start(bf16[32,3584]{1,0:T(8,128)(2,1)S(1)} %get-tuple-element.180), channel_id=1, source_target_pairs={{0,8},{8,16},{16,24},{1,9},{9,17},{17,25},{2,10},{10,18},{18,26},{... | collective-permute-start | bytes 688136 | tf_op jit(solution)/shard_map/ppermute | solution.py:25
  96.8 5.2 %collective-permute-start.23 = (bf16[32,3584]{1,0:T(8,128)(2,1)S(1)}, bf16[32,3584]{1,0:T(8,128)(2,1)S(1)}, u32[]{:S(2)}, u32[]{:S(2)}) collective-permute-start(bf16[32,3584]{1,0:T(8,128)(2,1)S(1)} %get-tuple-element.181), channel_id=1, source_target_pairs={{0,8},{8,16},{16,24},{1,9},{9,17},{17,25},{2,10},{10,18},{18,26},{... | collective-permute-start | bytes 688136 | tf_op jit(solution)/shard_map/ppermute | solution.py:25
  103.3 19.0 %collective-permute-start.29 = (bf16[144,896]{1,0:T(8,128)(2,1)S(1)}, bf16[144,896]{1,0:T(8,128)(2,1)S(1)}, u32[]{:S(2)}, u32[]{:S(2)}) collective-permute-start(bf16[144,896]{1,0:T(8,128)(2,1)S(1)} %get-tuple-element.193), channel_id=1, source_target_pairs={{0,2},{1,3},{2,0},{3,1},{4,6},{5,7},{6,4},{7,5},{8,10},{9,11},{10,... | collective-permute-start | bytes 774152 | tf_op jit(solution)/shard_map/ppermute | solution.py:585
  106.4 22.9 %collective-permute-start.30 = (bf16[144,896]{1,0:T(8,128)(2,1)S(1)}, bf16[144,896]{1,0:T(8,128)(2,1)S(1)}, u32[]{:S(2)}, u32[]{:S(2)}) collective-permute-start(bf16[144,896]{1,0:T(8,128)(2,1)S(1)} %get-tuple-element.199), channel_id=1, source_target_pairs={{0,4},{1,5},{2,6},{3,7},{4,0},{5,1},{6,2},{7,3},{8,12},{9,13},{10,... | collective-permute-start | bytes 774152 | tf_op jit(solution)/shard_map/ppermute | solution.py:585
  111.1 18.2 %collective-permute-start.31 = (bf16[144,896]{1,0:T(8,128)(2,1)S(1)}, bf16[144,896]{1,0:T(8,128)(2,1)S(1)}, u32[]{:S(2)}, u32[]{:S(2)}) collective-permute-start(bf16[144,896]{1,0:T(8,128)(2,1)S(1)} %get-tuple-element.200), channel_id=1, source_target_pairs={{0,6},{1,7},{2,4},{3,5},{4,2},{5,3},{6,0},{7,1},{8,14},{9,15},{10,... | collective-permute-start | bytes 774152 | tf_op jit(solution)/shard_map/ppermute | solution.py:585
  129.3 24.7 %collective-permute-start.37 = (bf16[144,896]{1,0:T(8,128)(2,1)S(1)}, bf16[144,896]{1,0:T(8,128)(2,1)S(1)}, u32[]{:S(2)}, u32[]{:S(2)}) collective-permute-start(bf16[144,896]{1,0:T(8,128)(2,1)S(1)} %get-tuple-element.219), channel_id=1, source_target_pairs={{0,4},{1,5},{2,6},{3,7},{4,0},{5,1},{6,2},{7,3},{8,12},{9,13},{10,... | collective-permute-start | bytes 774152 | tf_op jit(solution)/shard_map/ppermute | solution.py:585
  134.1 19.9 %collective-permute-start.36 = (bf16[144,896]{1,0:T(8,128)(2,1)S(1)}, bf16[144,896]{1,0:T(8,128)(2,1)S(1)}, u32[]{:S(2)}, u32[]{:S(2)}) collective-permute-start(bf16[144,896]{1,0:T(8,128)(2,1)S(1)} %get-tuple-element.215), channel_id=1, source_target_pairs={{0,2},{1,3},{2,0},{3,1},{4,6},{5,7},{6,4},{7,5},{8,10},{9,11},{10,... | collective-permute-start | bytes 774152 | tf_op jit(solution)/shard_map/ppermute | solution.py:585
  136.4 17.6 %collective-permute-start.38 = (bf16[144,896]{1,0:T(8,128)(2,1)S(1)}, bf16[144,896]{1,0:T(8,128)(2,1)S(1)}, u32[]{:S(2)}, u32[]{:S(2)}) collective-permute-start(bf16[144,896]{1,0:T(8,128)(2,1)S(1)} %get-tuple-element.220), channel_id=1, source_target_pairs={{0,6},{1,7},{2,4},{3,5},{4,2},{5,3},{6,0},{7,1},{8,14},{9,15},{10,... | collective-permute-start | bytes 774152 | tf_op jit(solution)/shard_map/ppermute | solution.py:585
  137.9 7.3 %collective-permute-start.32 = (bf16[160,512]{1,0:T(8,128)(2,1)S(1)}, bf16[160,512]{1,0:T(8,128)(2,1)S(1)}, u32[]{:S(2)}, u32[]{:S(2)}) collective-permute-start(bf16[160,512]{1,0:T(8,128)(2,1)S(1)} %get-tuple-element.207), channel_id=1, source_target_pairs={{0,1},{1,0},{2,3},{3,2},{4,5},{5,4},{6,7},{7,6},{8,9},{9,8},{10,11... | collective-permute-start | bytes 491528 | tf_op jit(solution)/shard_map/ppermute | solution.py:19
  138.9 6.3 %collective-permute-start.33 = (bf16[144,512]{1,0:T(8,128)(2,1)S(1)}, bf16[144,512]{1,0:T(8,128)(2,1)S(1)}, u32[]{:S(2)}, u32[]{:S(2)}) collective-permute-start(bf16[144,512]{1,0:T(8,128)(2,1)S(1)} %get-tuple-element.208), channel_id=1, source_target_pairs={{0,1},{1,0},{2,3},{3,2},{4,5},{5,4},{6,7},{7,6},{8,9},{9,8},{10,11... | collective-permute-start | bytes 442376 | tf_op jit(solution)/shard_map/ppermute | solution.py:19
  146.2 4.4 %collective-permute-start.34 = (bf16[144,256]{1,0:T(8,128)(2,1)S(1)}, bf16[144,256]{1,0:T(8,128)(2,1)S(1)}, u32[]{:S(2)}, u32[]{:S(2)}) collective-permute-start(bf16[144,256]{1,0:T(8,128)(2,1)S(1)} %get-tuple-element.210.h0), channel_id=1, source_target_pairs={{0,1},{1,0},{2,3},{3,2},{4,5},{5,4},{6,7},{7,6},{8,9},{9,8},{10,11... | collective-permute-start | bytes 221192 | tf_op jit(solution)/shard_map/ppermute | solution.py:19
  147.6 4.4 %collective-permute-start.35 = (bf16[144,256]{1,0:T(8,128)(2,1)S(1)}, bf16[144,256]{1,0:T(8,128)(2,1)S(1)}, u32[]{:S(2)}, u32[]{:S(2)}) collective-permute-start(bf16[144,256]{1,0:T(8,128)(2,1)S(1)} %get-tuple-element.211.h1), channel_id=1, source_target_pairs={{0,1},{1,0},{2,3},{3,2},{4,5},{5,4},{6,7},{7,6},{8,9},{9,8},{10,11... | collective-permute-start | bytes 221192 | tf_op jit(solution)/shard_map/ppermute | solution.py:19
  154.0 22.1 %collective-permute-start.44 = (bf16[144,896]{1,0:T(8,128)(2,1)S(1)}, bf16[144,896]{1,0:T(8,128)(2,1)S(1)}, u32[]{:S(2)}, u32[]{:S(2)}) collective-permute-start(bf16[144,896]{1,0:T(8,128)(2,1)S(1)} %get-tuple-element.236), channel_id=1, source_target_pairs={{0,4},{1,5},{2,6},{3,7},{4,0},{5,1},{6,2},{7,3},{8,12},{9,13},{10,... | collective-permute-start | bytes 774152 | tf_op jit(solution)/shard_map/ppermute | solution.py:585
  156.4 19.7 %collective-permute-start.43 = (bf16[144,896]{1,0:T(8,128)(2,1)S(1)}, bf16[144,896]{1,0:T(8,128)(2,1)S(1)}, u32[]{:S(2)}, u32[]{:S(2)}) collective-permute-start(bf16[144,896]{1,0:T(8,128)(2,1)S(1)} %get-tuple-element.232), channel_id=1, source_target_pairs={{0,2},{1,3},{2,0},{3,1},{4,6},{5,7},{6,4},{7,5},{8,10},{9,11},{10,... | collective-permute-start | bytes 774152 | tf_op jit(solution)/shard_map/ppermute | solution.py:585
  159.4 16.6 %collective-permute-start.45 = (bf16[144,896]{1,0:T(8,128)(2,1)S(1)}, bf16[144,896]{1,0:T(8,128)(2,1)S(1)}, u32[]{:S(2)}, u32[]{:S(2)}) collective-permute-start(bf16[144,896]{1,0:T(8,128)(2,1)S(1)} %get-tuple-element.237), channel_id=1, source_target_pairs={{0,6},{1,7},{2,4},{3,5},{4,2},{5,3},{6,0},{7,1},{8,14},{9,15},{10,... | collective-permute-start | bytes 774152 | tf_op jit(solution)/shard_map/ppermute | solution.py:585
  161.0 6.9 %collective-permute-start.39 = (bf16[160,512]{1,0:T(8,128)(2,1)S(1)}, bf16[160,512]{1,0:T(8,128)(2,1)S(1)}, u32[]{:S(2)}, u32[]{:S(2)}) collective-permute-start(bf16[160,512]{1,0:T(8,128)(2,1)S(1)} %get-tuple-element.226), channel_id=1, source_target_pairs={{0,1},{1,0},{2,3},{3,2},{4,5},{5,4},{6,7},{7,6},{8,9},{9,8},{10,11... | collective-permute-start | bytes 491528 | tf_op jit(solution)/shard_map/ppermute | solution.py:19
  161.8 6.1 %collective-permute-start.40 = (bf16[144,512]{1,0:T(8,128)(2,1)S(1)}, bf16[144,512]{1,0:T(8,128)(2,1)S(1)}, u32[]{:S(2)}, u32[]{:S(2)}) collective-permute-start(bf16[144,512]{1,0:T(8,128)(2,1)S(1)} %get-tuple-element.227), channel_id=1, source_target_pairs={{0,1},{1,0},{2,3},{3,2},{4,5},{5,4},{6,7},{7,6},{8,9},{9,8},{10,11... | collective-permute-start | bytes 442376 | tf_op jit(solution)/shard_map/ppermute | solution.py:19
  168.9 4.4 %collective-permute-start.41 = (bf16[144,256]{1,0:T(8,128)(2,1)S(1)}, bf16[144,256]{1,0:T(8,128)(2,1)S(1)}, u32[]{:S(2)}, u32[]{:S(2)}) collective-permute-start(bf16[144,256]{1,0:T(8,128)(2,1)S(1)} %get-tuple-element.229.h0), channel_id=1, source_target_pairs={{0,1},{1,0},{2,3},{3,2},{4,5},{5,4},{6,7},{7,6},{8,9},{9,8},{10,11... | collective-permute-start | bytes 221192 | tf_op jit(solution)/shard_map/ppermute | solution.py:19
  169.7 4.4 %collective-permute-start.42 = (bf16[144,256]{1,0:T(8,128)(2,1)S(1)}, bf16[144,256]{1,0:T(8,128)(2,1)S(1)}, u32[]{:S(2)}, u32[]{:S(2)}) collective-permute-start(bf16[144,256]{1,0:T(8,128)(2,1)S(1)} %get-tuple-element.230.h1), channel_id=1, source_target_pairs={{0,1},{1,0},{2,3},{3,2},{4,5},{5,4},{6,7},{7,6},{8,9},{9,8},{10,11... | collective-permute-start | bytes 221192 | tf_op jit(solution)/shard_map/ppermute | solution.py:19
  176.1 19.3 %collective-permute-start.48 = (bf16[144,896]{1,0:T(8,128)(2,1)S(1)}, bf16[144,896]{1,0:T(8,128)(2,1)S(1)}, u32[]{:S(2)}, u32[]{:S(2)}) collective-permute-start(bf16[144,896]{1,0:T(8,128)(2,1)S(1)} %get-tuple-element.242), channel_id=1, source_target_pairs={{0,4},{1,5},{2,6},{3,7},{4,0},{5,1},{6,2},{7,3},{8,12},{9,13},{10,... | collective-permute-start | bytes 774152 | tf_op jit(solution)/shard_map/ppermute | solution.py:585
  178.5 16.8 %collective-permute-start.49 = (bf16[144,896]{1,0:T(8,128)(2,1)S(1)}, bf16[144,896]{1,0:T(8,128)(2,1)S(1)}, u32[]{:S(2)}, u32[]{:S(2)}) collective-permute-start(bf16[144,896]{1,0:T(8,128)(2,1)S(1)} %get-tuple-element.243), channel_id=1, source_target_pairs={{0,6},{1,7},{2,4},{3,5},{4,2},{5,3},{6,0},{7,1},{8,14},{9,15},{10,... | collective-permute-start | bytes 774152 | tf_op jit(solution)/shard_map/ppermute | solution.py:585
  180.0 15.7 %collective-permute-start.47 = (bf16[144,896]{1,0:T(8,128)(2,1)S(1)}, bf16[144,896]{1,0:T(8,128)(2,1)S(1)}, u32[]{:S(2)}, u32[]{:S(2)}) collective-permute-start(bf16[144,896]{1,0:T(8,128)(2,1)S(1)} %get-tuple-element.241), channel_id=1, source_target_pairs={{0,2},{1,3},{2,0},{3,1},{4,6},{5,7},{6,4},{7,5},{8,10},{9,11},{10,... | collective-permute-start | bytes 774152 | tf_op jit(solution)/shard_map/ppermute | solution.py:585
  181.6 18.2 %collective-permute-start.46 = (bf16[32,3584]{1,0:T(8,128)(2,1)S(1)}, bf16[32,3584]{1,0:T(8,128)(2,1)S(1)}, u32[]{:S(2)}, u32[]{:S(2)}) collective-permute-start(bf16[32,3584]{1,0:T(8,128)(2,1)S(1)} %last.4.refs_7_), channel_id=1, source_target_pairs={{0,1},{1,0},{2,3},{3,2},{4,5},{5,4},{6,7},{7,6},{8,9},{9,8},{10,11... | collective-permute-start | bytes 688136 | tf_op jit(solution)/shard_map/ppermute | solution.py:19
  197.3 6.1 %collective-permute-start.50 = (bf16[32,3584]{1,0:T(8,128)(2,1)S(1)}, bf16[32,3584]{1,0:T(8,128)(2,1)S(1)}, u32[]{:S(2)}, u32[]{:S(2)}) collective-permute-start(bf16[32,3584]{1,0:T(8,128)(2,1)S(1)} %last.6.refs_7_), channel_id=1, source_target_pairs={{0,1},{1,0},{2,3},{3,2},{4,5},{5,4},{6,7},{7,6},{8,9},{9,8},{10,11... | collective-permute-start | bytes 688136 | tf_op jit(solution)/shard_map/ppermute | solution.py:19
  (11 other events, 64.5 us)
